TPU v7x, 32 devices: a whole 2x2x4 slice. The times are simulated.
32 devices in a mesh: groups: 2 (over x), expert: 16 (over z, y, core).
Axes of the slice: x: 2, y: 2, z: 4, core: 2. Of those that a mesh axis runs over, the one named last changes fastest.
Arguments:
- resid: bfloat16 [2048, 4096], P(('groups', 'expert')), parts along dimension 0, may hold values from -6 to 6
- queries: bfloat16 [2048, 4096], P(('groups', 'expert')), parts along dimension 0, may hold values from -120 to 120
- keys: bfloat16 [2048, 4096], P(('groups', 'expert')), parts along dimension 0, may hold values from -6 to 6
- values: bfloat16 [2048, 4096], P(('groups', 'expert')), parts along dimension 0, may hold values from -6 to 6
- segment_ids: int32 [2048], P(('groups', 'expert')), parts along dimension 0, may hold values from 0 to 3, never falling along the last dimension, each value on 1 to 512 neighbouring positions
- norm_gain: float32 [4096], replicated, may hold values from 0.1 to 1.9
- routes: int32 [2048, 2], P(('groups', 'expert')), parts along dimension 0, may hold values from 0 to 7, all different within a row; in each aligned block of 64 rows (0 to 63, 64 to 127, ...) at most 20 rows name the same one
- route_gates: bfloat16 [2048, 2], P(('groups', 'expert')), parts along dimension 0, may hold values from 0.19921875 to 1
- w_gate: bfloat16 [4096, 16384], P(None, 'expert'), may hold values from -0.09375 to 0.09375
- w_up: bfloat16 [4096, 16384], P(None, 'expert'), may hold values from -0.09375 to 0.09375
- w_down: bfloat16 [16384, 4096], P('expert'), may hold values from -0.0625 to 0.0625
Outputs:
- layer_out: bfloat16 [2048, 4096], P(('groups', 'expert')), parts along dimension 0
There are 2 independent parts, one for each index of `groups`. A program takes and returns all parts, laid end to end along the dimension named above; an argument that names none is the same for every part. Nothing has to cross between parts.
Inputs may be any that keep to these rules, and one draw needn't show every extreme that they name: `routes`: in each token's row the experts differ; in the rows of one device no expert is named more than 20 times, a bound that some block reaches.
All inputs are finite; a program needn't handle non-finite values.
Results may differ from a plain program's by a relative error of at most 0.0037.
Values may be sent and summed in bfloat16 or wider, within the bound.
No kernel may reach another device: no remote copies, remote signals or barrier semaphores. Data moves between devices by JAX's collectives and lax.ppermute only.
A program may use at most 128 MiB of HBM per device.

v0:
```python
import jax
import jax.numpy as jnp
from jax import lax
from jax.sharding import PartitionSpec as P

HEAD_DIM = 128
E_WIN = 2
WIN_DEV = 3
CAP = 20


def shifted(value, axis, steps):
    count = lax.axis_size(axis)
    leading, last = (max(0, -steps), min(count, count - steps))
    return lax.ppermute(value, axis, [(source, source + steps) for source in range(leading, last)])


def shards(
    resid, queries, keys, values, segment_ids, norm_gain, routes, route_gates, w_gate, w_up, w_down
):
    tok_rows = resid.shape[0]
    model_width = resid.shape[1]
    head_count = model_width // HEAD_DIM
    device_count = lax.axis_size("expert")
    own_index = lax.axis_index("expert")
    shard_count = device_count // E_WIN
    softmax_scale = 1.0 / HEAD_DIM**0.5
    query_pos = own_index * tok_rows + jnp.arange(tok_rows)
    query_heads = queries.reshape(tok_rows, head_count, HEAD_DIM)
    reach = WIN_DEV * tok_rows
    key_list = [keys]
    value_list = [values]
    seg_list = [segment_ids]
    pos_list = [query_pos]
    for behind in range(1, WIN_DEV + 1):
        moved_keys, moved_values, moved_segs = shifted(
            (keys, values, segment_ids), "expert", behind
        )
        key_list.append(moved_keys)
        value_list.append(moved_values)
        seg_list.append(moved_segs)
        pos_list.append((own_index - behind) * tok_rows + jnp.arange(tok_rows))
    key_all = jnp.concatenate(key_list, axis=0)
    value_all = jnp.concatenate(value_list, axis=0)
    seg_all = jnp.concatenate(seg_list, axis=0)
    pos_all = jnp.concatenate(pos_list, axis=0)
    key_rows = key_all.shape[0]
    key_heads = key_all.reshape(key_rows, head_count, HEAD_DIM)
    value_heads = value_all.reshape(key_rows, head_count, HEAD_DIM)
    distance = query_pos[:, None] - pos_all[None, :]
    allowed = (
        (distance >= 0)
        & (distance <= reach)
        & (pos_all[None, :] >= 0)
        & (segment_ids[:, None] == seg_all[None, :])
    )
    scores = (
        jnp.einsum("qhd,khd->hqk", query_heads, key_heads, preferred_element_type=jnp.float32)
        * softmax_scale
    )
    scores = jnp.where(allowed[None], scores, -1e30)
    rowmax = jnp.max(scores, axis=2, keepdims=True)
    expo = jnp.where(allowed[None], jnp.exp(scores - rowmax), 0.0)
    denom = jnp.sum(expo, axis=2)
    numer = jnp.einsum(
        "hqk,khd->hqd", expo.astype(jnp.bfloat16), value_heads, preferred_element_type=jnp.float32
    )
    attended = (numer / denom[..., None]).transpose(1, 0, 2).reshape(tok_rows, model_width)
    mixed = resid.astype(jnp.float32) + attended
    normed = (
        mixed * lax.rsqrt(jnp.mean(mixed * mixed, axis=1, keepdims=True) + 1e-05) * norm_gain
    ).astype(jnp.bfloat16)
    top_count = routes.shape[1]
    capacity = CAP
    flat_routes = routes.reshape(-1)
    flat_gates = route_gates.reshape(-1).astype(jnp.float32)
    is_valid = flat_routes < E_WIN
    member = (flat_routes[:, None] == jnp.arange(E_WIN)[None, :]).astype(jnp.int32)
    earlier = jnp.cumsum(member, axis=0) - member
    rank = jnp.sum(earlier * member, axis=1)
    destination = flat_routes * capacity + rank
    places = jnp.arange(E_WIN * capacity)
    select = ((destination[:, None] == places[None, :]) & is_valid[:, None]).astype(jnp.float32)
    picker = select.reshape(tok_rows, top_count, E_WIN * capacity).sum(axis=1)
    gate_matrix = (
        (select * flat_gates[:, None]).reshape(tok_rows, top_count, E_WIN * capacity).sum(axis=1)
    )
    packed = jnp.dot(
        picker.T.astype(jnp.bfloat16), normed, preferred_element_type=jnp.float32
    ).astype(jnp.bfloat16)
    outgoing = jnp.repeat(packed.reshape(E_WIN, capacity, model_width), shard_count, axis=0)
    arrived = lax.all_to_all(outgoing, "expert", split_axis=0, concat_axis=0, tiled=True)
    in_rows = arrived.reshape(device_count * capacity, model_width)
    gate_proj = jnp.dot(in_rows, w_gate, preferred_element_type=jnp.float32)
    up_proj = jnp.dot(in_rows, w_up, preferred_element_type=jnp.float32)
    hidden = (jax.nn.silu(gate_proj) * up_proj).astype(jnp.bfloat16)
    partial_out = jnp.dot(hidden, w_down, preferred_element_type=jnp.float32).astype(jnp.bfloat16)
    partial_out = partial_out.reshape(device_count, capacity, model_width)
    back_home = lax.all_to_all(partial_out, "expert", split_axis=0, concat_axis=0, tiled=True)
    expert_out = (
        back_home.reshape(E_WIN, shard_count, capacity, model_width).astype(jnp.float32).sum(axis=1)
    )
    expert_out = expert_out.reshape(E_WIN * capacity, model_width)
    combined = jnp.dot(gate_matrix, expert_out, precision=lax.Precision.HIGHEST)
    return (mixed + combined).astype(jnp.bfloat16)


def solution(mesh):
    placed = (
        P(("groups", "expert"), None),
        P(("groups", "expert"), None),
        P(("groups", "expert"), None),
        P(("groups", "expert"), None),
        P(("groups", "expert")),
        P(),
        P(("groups", "expert"), None),
        P(("groups", "expert"), None),
        P(None, "expert"),
        P(None, "expert"),
        P("expert", None),
    )
    return jax.shard_map(
        shards, mesh=mesh, in_specs=placed, out_specs=P(("groups", "expert"), None), check_vma=False
    )
```

profile of v0, /device:TPU:0, one launch (start us, length us, event | category | flops | bytes accessed | tf_op | source)
XLA Modules:
  0.0 257.3 jit_solution(1411332996577728565)
XLA Ops:
  0.0 2.5 collective-permute-start
  2.5 4.4 %collective-permute-start.1 = (s32[64]{0:T(128)}, s32[64]{0:T(128)S(1)}, u32[]{:S(2)}, u32[]{:S(2)}) collective-permute-start(s32[64]{0:T(128)} %param.15), channel_id=1, source_target_pairs={{0,2},{1,3},{2,4},{3,5},{4,6},{5,7},{6,8},{7,9},{8,10},{9,11},{10,... | collective-permute-start | bytes 776 | tf_op jit(solution)/shard_map/ppermute | solution.py:15
  7.0 4.1 %collective-permute-start.3 = (bf16[64,4096]{1,0:T(8,128)(2,1)}, bf16[64,4096]{1,0:T(8,128)(2,1)}, u32[]{:S(2)}, u32[]{:S(2)}) collective-permute-start(bf16[64,4096]{1,0:T(8,128)(2,1)} %param.13), channel_id=1, source_target_pairs={{0,1},{1,2},{2,3},{3,4},{4,5},{5,6},{6,7},{7,8},{8,9},{9,10},{10,1... | collective-permute-start | bytes 1572872 | tf_op jit(solution)/shard_map/ppermute | solution.py:15
  11.0 3.4 %collective-permute-start.4 = (bf16[64,4096]{1,0:T(8,128)(2,1)}, bf16[64,4096]{1,0:T(8,128)(2,1)}, u32[]{:S(2)}, u32[]{:S(2)}) collective-permute-start(bf16[64,4096]{1,0:T(8,128)(2,1)} %param.13), channel_id=1, source_target_pairs={{0,2},{1,3},{2,4},{3,5},{4,6},{5,7},{6,8},{7,9},{8,10},{9,11},{10,... | collective-permute-start | bytes 1572872 | tf_op jit(solution)/shard_map/ppermute | solution.py:15
  14.4 3.0 %collective-permute-start.5 = (bf16[64,4096]{1,0:T(8,128)(2,1)}, bf16[64,4096]{1,0:T(8,128)(2,1)}, u32[]{:S(2)}, u32[]{:S(2)}) collective-permute-start(bf16[64,4096]{1,0:T(8,128)(2,1)} %param.13), channel_id=1, source_target_pairs={{0,3},{1,4},{2,5},{3,6},{4,7},{5,8},{6,9},{7,10},{8,11},{9,12},{10... | collective-permute-start | bytes 1572872 | tf_op jit(solution)/shard_map/ppermute | solution.py:15
  21.8 2.8 %collective-permute-start.2 = (s32[64]{0:T(128)}, s32[64]{0:T(128)S(1)}, u32[]{:S(2)}, u32[]{:S(2)}) collective-permute-start(s32[64]{0:T(128)} %param.15), channel_id=1, source_target_pairs={{0,3},{1,4},{2,5},{3,6},{4,7},{5,8},{6,9},{7,10},{8,11},{9,12},{10... | collective-permute-start | bytes 776 | tf_op jit(solution)/shard_map/ppermute | solution.py:15
  27.7 2.7 %collective-permute-start.6 = (bf16[64,4096]{1,0:T(8,128)(2,1)S(1)}, bf16[64,4096]{1,0:T(8,128)(2,1)}, u32[]{:S(2)}, u32[]{:S(2)}) collective-permute-start(bf16[64,4096]{1,0:T(8,128)(2,1)S(1)} %copy-done.7), channel_id=1, source_target_pairs={{0,1},{1,2},{2,3},{3,4},{4,5},{5,6},{6,7},{7,8},{8,9},{9,10},{10,1... | collective-permute-start | bytes 1572872 | tf_op jit(solution)/shard_map/ppermute | solution.py:15
  30.4 5.1 %collective-permute-done.2 = s32[64]{0:T(128)S(1)} collective-permute-done((s32[64]{0:T(128)}, s32[64]{0:T(128)S(1)}, u32[]{:S(2)}, u32[]{:S(2)}) %collective-permute-start.2) | collective-permute-done | bytes 288 | tf_op jit(solution)/shard_map/ppermute | solution.py:15
  35.5 6.3 %collective-permute-start.7 = (bf16[64,4096]{1,0:T(8,128)(2,1)S(1)}, bf16[64,4096]{1,0:T(8,128)(2,1)}, u32[]{:S(2)}, u32[]{:S(2)}) collective-permute-start(bf16[64,4096]{1,0:T(8,128)(2,1)S(1)} %copy-done.7), channel_id=1, source_target_pairs={{0,2},{1,3},{2,4},{3,5},{4,6},{5,7},{6,8},{7,9},{8,10},{9,11},{10,... | collective-permute-start | bytes 1572872 | tf_op jit(solution)/shard_map/ppermute | solution.py:15
  42.0 4.4 %collective-permute-start.8 = (bf16[64,4096]{1,0:T(8,128)(2,1)S(1)}, bf16[64,4096]{1,0:T(8,128)(2,1)}, u32[]{:S(2)}, u32[]{:S(2)}) collective-permute-start(bf16[64,4096]{1,0:T(8,128)(2,1)S(1)} %copy-done.7), channel_id=1, source_target_pairs={{0,3},{1,4},{2,5},{3,6},{4,7},{5,8},{6,9},{7,10},{8,11},{9,12},{10... | collective-permute-start | bytes 1572872 | tf_op jit(solution)/shard_map/ppermute | solution.py:15
  46.4 2.4 copy.69
  48.8 2.4 copy.70
  51.2 2.4 copy.71
  53.6 4.5 %pad_maximum_fusion = bf16[256,4096]{0,1:T(8,128)(2,1)} fusion(bf16[64,4096]{0,1:T(8,128)(2,1)} %copy.71, bf16[64,4096]{0,1:T(8,128)(2,1)} %copy.70, bf16[64,4096]{0,1:T(8,128)(2,1)} %copy.69, bf16[64,4096]{0,1:T(8,128)(2,1)S(1)} %copy.68), kind=kLoop, calls=%fused_computation.6 | loop fusion | flops 8388608 | bytes 4194304 | tf_op jit(solution)/shard_map/concatenate | solution.py:43
  59.6 2.4 copy.76
  62.0 3.5 %fusion.24 = (f32[32,64]{1,0:T(8,128)S(1)}, bf16[32,64,256]{2,1,0:T(8,128)(2,1)}) fusion(pred[64,256]{1,0:T(8,128)(4,1)S(1)} %fusion.18, bf16[256,32,128]{0,2,1:T(8,128)(2,1)} %bitcast.55, bf16[64,4096]{1,0:T(8,128)(2,1)S(1)} %copy-done), kind=kOutput, calls=%fused_computation.54 | convolution fusion | flops 137363712 | bytes 3694592 | tf_op jit(solution)/shard_map/sub | solution.py:63
  65.5 2.4 copy.77
  67.9 3.0 %pad_maximum_fusion.1 = bf16[256,4096]{0,1:T(8,128)(2,1)S(1)} fusion(bf16[64,4096]{0,1:T(8,128)(2,1)} %copy.77, bf16[64,4096]{0,1:T(8,128)(2,1)} %copy.76, bf16[64,4096]{0,1:T(8,128)(2,1)S(1)} %copy.75, bf16[64,4096]{0,1:T(8,128)(2,1)S(1)} %copy.74), kind=kLoop, calls=%fused_computation.7 | loop fusion | flops 8388608 | bytes 4194304 | tf_op jit(solution)/shard_map/concatenate | solution.py:44
  73.6 78.3 %all_to_all.10 = bf16[16,20,4096]{2,1,0:T(8,128)(2,1)S(1)} all-to-all(bf16[16,20,4096]{2,1,0:T(8,128)(2,1)S(1)} %bitcast.54), channel_id=1, replica_groups=mesh['groups'=2,'expert'=16] {'expert'}, dimensions={0} | all-to-all | bytes 5242880 | tf_op jit(solution)/shard_map/all_to_all | solution.py:92
  154.2 8.3 %fusion.29 = f32[320,1024]{1,0:T(8,128)} fusion(bf16[320,4096]{1,0:T(8,128)(2,1)} %reshape.203, bf16[4096,1024]{1,0:T(8,128)(2,1)} %param.19), kind=kOutput, calls=%fused_computation.55 | convolution fusion | flops 2684354560 | bytes 12320768 | tf_op jit(solution)/shard_map/dot_general | solution.py:94
  162.5 13.4 %convolution_convert_fusion = bf16[320,4096]{1,0:T(8,128)(2,1)} fusion(bf16[1024,4096]{1,0:T(8,128)(2,1)} %param.21, bf16[320,4096]{1,0:T(8,128)(2,1)S(1)} %copy-done.6, bf16[4096,1024]{1,0:T(8,128)(2,1)} %param.20, f32[320,1024]{1,0:T(8,128)} %fusion.29), kind=kOutput, calls=%fused_computation.2 | convolution fusion | flops 5371985920 | bytes 23330816 | tf_op jit(solution)/shard_map/dot_general | solution.py:97
  175.8 2.7 %reshape.204 = bf16[16,20,4096]{2,1,0:T(8,128)(2,1)S(1)} reshape(bf16[320,4096]{1,0:T(8,128)(2,1)} %convolution_convert_fusion) | data formatting | bytes 5242880 | tf_op jit(solution)/shard_map/reshape | solution.py:98
  178.6 74.8 %all_to_all.11 = bf16[16,20,4096]{2,1,0:T(8,128)(2,1)S(1)} all-to-all(bf16[16,20,4096]{2,1,0:T(8,128)(2,1)S(1)} %reshape.204), channel_id=1, replica_groups=mesh['groups'=2,'expert'=16] {'expert'}, dimensions={0} | all-to-all | bytes 5242880 | tf_op jit(solution)/shard_map/all_to_all | solution.py:99
  254.7 2.6 fusion.1
  (59 shorter events, 15.4 us)
Async XLA Ops:
  0.0 62.0 %copy-start = (bf16[64,4096]{1,0:T(8,128)(2,1)S(1)}, bf16[64,4096]{1,0:T(8,128)(2,1)}, u32[]{:S(2)}) copy-start(bf16[64,4096]{1,0:T(8,128)(2,1)} %param.12) | copy-start | bytes 1572868
  0.0 41.8 %copy-start.9 = (s32[64]{0:T(128)S(1)}, s32[64]{0:T(128)}, u32[]{:S(2)}) copy-start(s32[64]{0:T(128)} %param.15) | copy-start | bytes 772
  0.0 27.7 %copy-start.7 = (bf16[64,4096]{1,0:T(8,128)(2,1)S(1)}, bf16[64,4096]{1,0:T(8,128)(2,1)}, u32[]{:S(2)}) copy-start(bf16[64,4096]{1,0:T(8,128)(2,1)} %param.14) | copy-start | bytes 1572868
  0.0 21.8 %collective-permute-start = (s32[64]{0:T(128)}, s32[64]{0:T(128)S(1)}, u32[]{:S(2)}, u32[]{:S(2)}) collective-permute-start(s32[64]{0:T(128)} %param.15), channel_id=1, source_target_pairs={{0,1},{1,2},{2,3},{3,4},{4,5},{5,6},{6,7},{7,8},{8,9},{9,10},{10,1... | collective-permute-start | bytes 776 | tf_op jit(solution)/shard_map/ppermute | solution.py:15
  2.5 25.2 %collective-permute-start.1 = (s32[64]{0:T(128)}, s32[64]{0:T(128)S(1)}, u32[]{:S(2)}, u32[]{:S(2)}) collective-permute-start(s32[64]{0:T(128)} %param.15), channel_id=1, source_target_pairs={{0,2},{1,3},{2,4},{3,5},{4,6},{5,7},{6,8},{7,9},{8,10},{9,11},{10,... | collective-permute-start | bytes 776 | tf_op jit(solution)/shard_map/ppermute | solution.py:15
  7.0 35.0 %collective-permute-start.3 = (bf16[64,4096]{1,0:T(8,128)(2,1)}, bf16[64,4096]{1,0:T(8,128)(2,1)}, u32[]{:S(2)}, u32[]{:S(2)}) collective-permute-start(bf16[64,4096]{1,0:T(8,128)(2,1)} %param.13), channel_id=1, source_target_pairs={{0,1},{1,2},{2,3},{3,4},{4,5},{5,6},{6,7},{7,8},{8,9},{9,10},{10,1... | collective-permute-start | bytes 1572872 | tf_op jit(solution)/shard_map/ppermute | solution.py:15
  11.0 37.8 %collective-permute-start.4 = (bf16[64,4096]{1,0:T(8,128)(2,1)}, bf16[64,4096]{1,0:T(8,128)(2,1)}, u32[]{:S(2)}, u32[]{:S(2)}) collective-permute-start(bf16[64,4096]{1,0:T(8,128)(2,1)} %param.13), channel_id=1, source_target_pairs={{0,2},{1,3},{2,4},{3,5},{4,6},{5,7},{6,8},{7,9},{8,10},{9,11},{10,... | collective-permute-start | bytes 1572872 | tf_op jit(solution)/shard_map/ppermute | solution.py:15
  14.4 36.7 %collective-permute-start.5 = (bf16[64,4096]{1,0:T(8,128)(2,1)}, bf16[64,4096]{1,0:T(8,128)(2,1)}, u32[]{:S(2)}, u32[]{:S(2)}) collective-permute-start(bf16[64,4096]{1,0:T(8,128)(2,1)} %param.13), channel_id=1, source_target_pairs={{0,3},{1,4},{2,5},{3,6},{4,7},{5,8},{6,9},{7,10},{8,11},{9,12},{10... | collective-permute-start | bytes 1572872 | tf_op jit(solution)/shard_map/ppermute | solution.py:15
  21.8 13.7 %collective-permute-start.2 = (s32[64]{0:T(128)}, s32[64]{0:T(128)S(1)}, u32[]{:S(2)}, u32[]{:S(2)}) collective-permute-start(s32[64]{0:T(128)} %param.15), channel_id=1, source_target_pairs={{0,3},{1,4},{2,5},{3,6},{4,7},{5,8},{6,9},{7,10},{8,11},{9,12},{10... | collective-permute-start | bytes 776 | tf_op jit(solution)/shard_map/ppermute | solution.py:15
  27.7 30.4 %collective-permute-start.6 = (bf16[64,4096]{1,0:T(8,128)(2,1)S(1)}, bf16[64,4096]{1,0:T(8,128)(2,1)}, u32[]{:S(2)}, u32[]{:S(2)}) collective-permute-start(bf16[64,4096]{1,0:T(8,128)(2,1)S(1)} %copy-done.7), channel_id=1, source_target_pairs={{0,1},{1,2},{2,3},{3,4},{4,5},{5,6},{6,7},{7,8},{8,9},{9,10},{10,1... | collective-permute-start | bytes 1572872 | tf_op jit(solution)/shard_map/ppermute | solution.py:15
  35.5 24.1 %collective-permute-start.7 = (bf16[64,4096]{1,0:T(8,128)(2,1)S(1)}, bf16[64,4096]{1,0:T(8,128)(2,1)}, u32[]{:S(2)}, u32[]{:S(2)}) collective-permute-start(bf16[64,4096]{1,0:T(8,128)(2,1)S(1)} %copy-done.7), channel_id=1, source_target_pairs={{0,2},{1,3},{2,4},{3,5},{4,6},{5,7},{6,8},{7,9},{8,10},{9,11},{10,... | collective-permute-start | bytes 1572872 | tf_op jit(solution)/shard_map/ppermute | solution.py:15
  42.0 23.5 %collective-permute-start.8 = (bf16[64,4096]{1,0:T(8,128)(2,1)S(1)}, bf16[64,4096]{1,0:T(8,128)(2,1)}, u32[]{:S(2)}, u32[]{:S(2)}) collective-permute-start(bf16[64,4096]{1,0:T(8,128)(2,1)S(1)} %copy-done.7), channel_id=1, source_target_pairs={{0,3},{1,4},{2,5},{3,6},{4,7},{5,8},{6,9},{7,10},{8,11},{9,12},{10... | collective-permute-start | bytes 1572872 | tf_op jit(solution)/shard_map/ppermute | solution.py:15
  67.8 3.0 %copy-start.10 = (bf16[32,64,256]{2,1,0:T(8,128)(2,1)S(1)}, bf16[32,64,256]{2,1,0:T(8,128)(2,1)}, u32[]{:S(2)}) copy-start(bf16[32,64,256]{2,1,0:T(8,128)(2,1)} %get-tuple-element.10) | copy-start | bytes 3145732
  70.8 1.0 copy-start.4
  70.8 2.0 copy-start.8
  71.9 1.0 copy-start.2
  154.2 8.3 %copy-start.6 = (bf16[320,4096]{1,0:T(8,128)(2,1)S(1)}, bf16[320,4096]{1,0:T(8,128)(2,1)}, u32[]{:S(2)}) copy-start(bf16[320,4096]{1,0:T(8,128)(2,1)} %reshape.203) | copy-start | bytes 7864324
  253.3 1.2 copy-start.3
  253.3 1.4 copy-start.5
  253.3 3.9 %copy-start.1 = (bf16[64,4096]{1,0:T(8,128)(2,1)S(1)}, bf16[64,4096]{1,0:T(8,128)(2,1)}, u32[]{:S(2)}) copy-start(bf16[64,4096]{1,0:T(8,128)(2,1)} %param.12) | copy-start | bytes 1572868
where the time goes:
time: 259 us; the launch traced here: 257 us
  blocking collectives  153 us (59%)
  starting transfers between devices  33.7 us (13%)
  matrix products  28.8 us (11%)
  local copies, waits for them, and re-layouts  24.7 us (10%)
  other arithmetic  11.6 us (4%)
  waiting for transfers between devices  5.15 us (2%)
    all_to_all x1, blocking collectives, shards(): lax.all_to_all(outgoing, 'expert', split_axis=0, concat_axis=0, tiled=True)  78.3 us
    all_to_all x1, blocking collectives, shards(): lax.all_to_all(partial_out, 'expert', split_axis=0, concat_axis=0, tiled=...  74.8 us
    ppermute x9, starting transfers between devices, shifted(): lax.ppermute(value, axis, [(source, source + steps) for source in range(l...  33.7 us
    ppermute x6, local copies, waits for them, and re-layouts, shifted(): lax.ppermute(value, axis, [(source, source + steps) for source in range(l...  13.4 us
    dot_general x1, matrix products, shards(): jnp.dot(hidden, w_down, preferred_element_type=jnp.float32)  13.4 us
    dot_general x1, matrix products, shards(): gate_proj = jnp.dot(in_rows, w_gate, preferred_element_type=jnp.float32)  8.26 us
    unnamed x25, local copies, waits for them, and re-layouts  5.51 us
  transfers between devices with their start and end apart: 9, of which 1 were waited for; matrix products, arithmetic and copies ran while one was open for 10% of the time, Pallas kernels for 0%

commit v1 on v0

v1 whole, which is shorter than its diff:
```python
import functools

import jax
import jax.numpy as jnp
from jax import lax
from jax.experimental import pallas as pl
from jax.experimental.pallas import tpu as pltpu
from jax.sharding import PartitionSpec as P

HEAD_DIM = 128
E_WIN = 2
WIN_DEV = 3
CAP = 20
HEADS_STEP = 4
MASKED = -1e30


def attention_kernel(
    deltas, q, k0, v0, k1, v1, k2, v2, k3, v3, segs, resid, gain, routes, gates,
    mixed_out, keep_out, send_out, weight_out, mask,
):
    step = pl.program_id(0)
    steps = pl.num_programs(0)
    rows = q.shape[0]
    keys = (WIN_DEV + 1) * rows

    @pl.when(step == 0)
    def _():
        seg_row = segs[...]
        eye = lax.broadcasted_iota(jnp.int32, (rows, rows), 0) == lax.broadcasted_iota(
            jnp.int32, (rows, rows), 1
        )
        seg_col = jnp.sum(jnp.where(eye, seg_row[:, :rows], 0), axis=1, keepdims=True)
        lane = lax.broadcasted_iota(jnp.int32, (rows, keys), 1)
        sub = lax.broadcasted_iota(jnp.int32, (rows, keys), 0)
        block = lane // rows
        back = jnp.where(
            block == 0,
            deltas[0],
            jnp.where(block == 1, deltas[1], jnp.where(block == 2, deltas[2], deltas[3])),
        )
        distance = sub - (lane - block * rows) + back * rows
        allowed = (distance >= 0) & (distance <= WIN_DEV * rows) & (seg_col == seg_row)
        mask[...] = jnp.where(allowed, 1.0, 0.0)

    allowed = mask[...] > 0.5
    scale = 1.0 / HEAD_DIM**0.5
    outs = []
    for head in range(HEADS_STEP):
        cols = slice(head * HEAD_DIM, (head + 1) * HEAD_DIM)
        key_h = jnp.concatenate([k0[:, cols], k1[:, cols], k2[:, cols], k3[:, cols]], axis=0)
        value_h = jnp.concatenate([v0[:, cols], v1[:, cols], v2[:, cols], v3[:, cols]], axis=0)
        scores = (
            lax.dot_general(
                q[:, cols], key_h, (((1,), (1,)), ((), ())), preferred_element_type=jnp.float32
            )
            * scale
        )
        scores = jnp.where(allowed, scores, MASKED)
        rowmax = jnp.max(scores, axis=1, keepdims=True)
        expo = jnp.where(allowed, jnp.exp(scores - rowmax), 0.0)
        denom = jnp.sum(expo, axis=1, keepdims=True)
        numer = jnp.dot(expo.astype(jnp.bfloat16), value_h, preferred_element_type=jnp.float32)
        outs.append(numer / denom)
    attended = jnp.concatenate(outs, axis=1)
    width = HEADS_STEP * HEAD_DIM
    at = pl.ds(pl.multiple_of(step * width, width), width)
    mixed_out[:, at] = resid[...].astype(jnp.float32) + attended

    @pl.when(step == steps - 1)
    def _():
        mixed = mixed_out[...]
        normed = (
            mixed * lax.rsqrt(jnp.mean(mixed * mixed, axis=1, keepdims=True) + 1e-05) * gain[...]
        ).astype(jnp.bfloat16)
        upper = (
            lax.broadcasted_iota(jnp.int32, (rows, rows), 0)
            < lax.broadcasted_iota(jnp.int32, (rows, rows), 1)
        ).astype(jnp.float32).astype(jnp.bfloat16)
        slot = lax.broadcasted_iota(jnp.int32, (CAP, rows), 0)
        for place, out in ((0, keep_out), (1, send_out)):
            expert = jnp.where(place == 0, deltas[4], 1 - deltas[4])
            hit = routes[...] == expert
            member = jnp.max(jnp.where(hit, 1.0, 0.0), axis=0, keepdims=True)
            weight = jnp.sum(
                jnp.where(hit, gates[...].astype(jnp.float32), 0.0), axis=0, keepdims=True
            )
            rank = jnp.dot(
                jnp.broadcast_to(member, (8, rows)).astype(jnp.bfloat16),
                upper,
                preferred_element_type=jnp.float32,
            )[0:1].astype(jnp.int32)
            pick = jnp.where((slot == rank) & (member > 0.5), 1.0, 0.0)
            out[...] = jnp.dot(
                pick.astype(jnp.bfloat16), normed, preferred_element_type=jnp.float32
            ).astype(jnp.bfloat16)
            weight_out[place] = (pick * weight).astype(jnp.bfloat16)


def attention(deltas, q, k_own, v_own, arrived, segs, resid, gain, routes, gates):
    rows, width = q.shape
    cols = HEADS_STEP * HEAD_DIM
    steps = width // cols
    top = routes.shape[0]
    first = pl.BlockSpec((rows, cols), lambda j, *_: (0, j))
    second = pl.BlockSpec((rows, cols), lambda j, *_: (1, j))

    def whole(shape):
        return pl.BlockSpec(shape, lambda j, *_: (0,) * len(shape))

    pairs = []
    pair_specs = []
    for block in arrived:
        pairs += [block, block]
        pair_specs += [first, second]
    return pl.pallas_call(
        attention_kernel,
        grid_spec=pltpu.PrefetchScalarGridSpec(
            num_scalar_prefetch=1,
            grid=(steps,),
            in_specs=[first, first, first]
            + pair_specs
            + [
                whole((1, (WIN_DEV + 1) * rows)),
                first,
                whole((1, width)),
                whole((top, rows)),
                whole((top, rows)),
            ],
            out_specs=[
                whole((rows, width)),
                whole((CAP, width)),
                whole((CAP, width)),
                whole((E_WIN, CAP, rows)),
            ],
            scratch_shapes=[pltpu.VMEM((rows, (WIN_DEV + 1) * rows), jnp.float32)],
        ),
        out_shape=[
            jax.ShapeDtypeStruct((rows, width), jnp.float32),
            jax.ShapeDtypeStruct((CAP, width), jnp.bfloat16),
            jax.ShapeDtypeStruct((CAP, width), jnp.bfloat16),
            jax.ShapeDtypeStruct((E_WIN, CAP, rows), jnp.bfloat16),
        ],
        compiler_params=pltpu.CompilerParams(vmem_limit_bytes=24 * 1024 * 1024),
        cost_estimate=pl.CostEstimate(
            flops=4 * rows * 4 * rows * width, bytes_accessed=8 * rows * width * 4,
            transcendentals=rows * 4 * rows * (width // HEAD_DIM),
        ),
        name="attention",
    )(deltas, q, k_own, v_own, *pairs, segs, resid, gain, routes, gates)


def experts_kernel(first_steps, x, w_gate, w_up, w_down, out, hidden):
    step = pl.program_id(0)
    cols = w_gate.shape[1]

    @pl.when(step < first_steps)
    def _():
        rows = x[...]
        gate = jnp.dot(rows, w_gate[...], preferred_element_type=jnp.float32)
        up = jnp.dot(rows, w_up[...], preferred_element_type=jnp.float32)
        at = pl.ds(pl.multiple_of(step * cols, cols), cols)
        hidden[:, at] = (jax.nn.silu(gate) * up).astype(jnp.bfloat16)

    @pl.when(step >= first_steps)
    def _():
        out[...] = jnp.dot(
            hidden[...], w_down[...], preferred_element_type=jnp.float32
        ).astype(jnp.bfloat16)


def experts(x, w_gate, w_up, w_down):
    rows, width = x.shape
    units = w_gate.shape[1]
    cols = min(256, units)
    first_steps = units // cols
    out_cols = 1024
    second_steps = width // out_cols
    return pl.pallas_call(
        functools.partial(experts_kernel, first_steps),
        grid=(first_steps + second_steps,),
        in_specs=[
            pl.BlockSpec((rows, width), lambda j: (0, 0)),
            pl.BlockSpec((width, cols), lambda j: (0, jnp.minimum(j, first_steps - 1))),
            pl.BlockSpec((width, cols), lambda j: (0, jnp.minimum(j, first_steps - 1))),
            pl.BlockSpec((units, out_cols), lambda j: (0, jnp.maximum(j - first_steps, 0))),
        ],
        out_specs=pl.BlockSpec((rows, out_cols), lambda j: (0, jnp.maximum(j - first_steps, 0))),
        out_shape=jax.ShapeDtypeStruct((rows, width), jnp.bfloat16),
        scratch_shapes=[pltpu.VMEM((rows, units), jnp.bfloat16)],
        compiler_params=pltpu.CompilerParams(vmem_limit_bytes=48 * 1024 * 1024),
        cost_estimate=pl.CostEstimate(
            flops=6 * rows * width * units,
            bytes_accessed=6 * width * units + 4 * rows * width,
            transcendentals=rows * units,
        ),
        name="experts",
    )(x, w_gate, w_up, w_down)


def combine_kernel(mixed, weight, own, other, out):
    total = mixed[...]
    for place, part in ((0, own[...][:CAP]), (1, other[...])):
        total = total + lax.dot_general(
            weight[place], part, (((0,), (0,)), ((), ())), preferred_element_type=jnp.float32
        )
    out[...] = total.astype(jnp.bfloat16)


def combine(mixed, weight, own, other):
    rows, width = mixed.shape
    cols = 1024
    return pl.pallas_call(
        combine_kernel,
        grid=(width // cols,),
        in_specs=[
            pl.BlockSpec((rows, cols), lambda j: (0, j)),
            pl.BlockSpec(weight.shape, lambda j: (0, 0, 0)),
            pl.BlockSpec((own.shape[0], cols), lambda j: (0, j)),
            pl.BlockSpec((other.shape[0], cols), lambda j: (0, j)),
        ],
        out_specs=pl.BlockSpec((rows, cols), lambda j: (0, j)),
        out_shape=jax.ShapeDtypeStruct((rows, width), jnp.bfloat16),
        name="combine",
    )(mixed, weight, own, other)


def shards(
    resid, queries, keys, values, segment_ids, norm_gain, routes, route_gates, w_gate, w_up, w_down
):
    tok_rows = resid.shape[0]
    count = lax.axis_size("expert")
    own = lax.axis_index("expert")
    shard_count = count // E_WIN
    odd = own % 2

    both = jnp.concatenate([keys, values], axis=0)
    two_back = lax.ppermute(both, "expert", [(i, i + 2) for i in range(count - 2)])
    crossing = [(i, i + 1) for i in range(0, count, 2)]
    crossing += [(i, i + 3) for i in range(1, count - 3, 2)]
    crossed = lax.ppermute(both, "expert", crossing)
    mirrored = lax.ppermute(two_back, "expert", [(i, i ^ 1) for i in range(count)])
    delta_list = [0 * own, 0 * own + 2, 3 - 2 * odd, 1 + 2 * odd]

    seg_all = lax.all_gather(segment_ids, "expert", axis=0, tiled=True)
    segs = [
        lax.dynamic_slice_in_dim(seg_all, jnp.maximum(own - delta, 0) * tok_rows, tok_rows)
        for delta in delta_list
    ]
    segs = jnp.concatenate(segs).reshape(1, -1)
    far = 2 * WIN_DEV + 2
    my_expert = own // shard_count
    scalars = jnp.stack(
        [jnp.where(own >= delta, delta, far) for delta in delta_list] + [my_expert]
    ).astype(jnp.int32)

    mixed, keep, send, weight = attention(
        scalars, queries, keys, values, [two_back, crossed, mirrored], segs, resid,
        norm_gain.reshape(1, -1), routes.T, route_gates.T,
    )
    partner = [(i, (i + shard_count) % count) for i in range(count)]
    got = lax.ppermute(send, "expert", partner)
    pair_rows = jnp.concatenate([keep, got], axis=0)
    halves = [list(range(e * shard_count, (e + 1) * shard_count)) for e in range(E_WIN)]
    in_rows = lax.all_gather(pair_rows, "expert", axis=0, tiled=True, axis_index_groups=halves)
    partial_out = experts(in_rows, w_gate, w_up, w_down)
    summed = lax.psum_scatter(
        partial_out, "expert", scatter_dimension=0, tiled=True, axis_index_groups=halves
    )
    back = lax.ppermute(summed[CAP:], "expert", partner)
    return combine(mixed, weight, summed, back)


def solution(mesh):
    placed = (
        P(("groups", "expert"), None),
        P(("groups", "expert"), None),
        P(("groups", "expert"), None),
        P(("groups", "expert"), None),
        P(("groups", "expert")),
        P(),
        P(("groups", "expert"), None),
        P(("groups", "expert"), None),
        P(None, "expert"),
        P(None, "expert"),
        P("expert", None),
    )
    return jax.shard_map(
        shards, mesh=mesh, in_specs=placed, out_specs=P(("groups", "expert"), None), check_vma=False
    )
```

time: 259 us -> 185 us (0.71)
  blocking collectives: 153 us -> 14.5 us
  waiting for transfers between devices: 5.15 us -> 97.7 us
  Pallas kernels: 0 us -> 30.5 us
  matrix products: 28.8 us -> 0 us
  starting transfers between devices: 33.7 us -> 9.31 us
  between operations: 0.22 us -> 14.1 us
  other arithmetic: 11.6 us -> 0.87 us
  local copies, waits for them, and re-layouts: 24.7 us -> 17.3 us
    all_to_all x2 -> x0, blocking collectives: 153 us -> none  [the longest x1 78.3 us: shards(): lax.all_to_all(outgoing, 'expert', split_axis=0, concat_axis=0, tiled=True)]
    ppermute x9 -> x5, waiting for transfers between devices: 5.15 us -> 40.5 us  [the longest x1 21.1 us: shards(): lax.ppermute(both, 'expert', [(i, i + 2) for i in range(count - 2)])]
    reduce_scatter x0 -> x1, waiting for transfers between devices: none -> 34.8 us  [shards(): lax.psum_scatter(partial_out, 'expert', scatter_dimension=0, tiled=True,...]
    pallas_call x0 -> x3, Pallas kernels: none -> 30.5 us  [the longest x1 16 us: experts(): pl.pallas_call(functools.partial(experts_kernel, first_steps), grid=(firs...]
    dot_general x5 -> x0, matrix products: 25.4 us -> none  [the longest x1 13.4 us: shards(): jnp.dot(hidden, w_down, preferred_element_type=jnp.float32)]
    ppermute x9 -> x5, starting transfers between devices: 33.7 us -> 9.27 us  [the longest x1 4.92 us: shards(): lax.ppermute(both, 'expert', [(i, i + 2) for i in range(count - 2)])]
    all_gather x0 -> x1, waiting for transfers between devices: none -> 22.5 us  [shards(): lax.all_gather(pair_rows, 'expert', axis=0, tiled=True, axis_index_groups...]
    unnamed x0 -> x1, blocking collectives: none -> 14.5 us
  transfers between devices with their start and end apart: 9 -> 7, of which waited for: 1 -> 5; matrix products, arithmetic and copies ran while one was open for 10% -> 1% of each run, Pallas kernels for 0% -> 0%
where the time goes in v1:
time: 185 us; the launch traced here: 184 us
  waiting for transfers between devices  97.7 us (53%)
  Pallas kernels  30.5 us (16%)
  local copies, waits for them, and re-layouts  17.3 us (9%)
  blocking collectives  14.5 us (8%)
  between operations  14.1 us (8%)
  starting transfers between devices  9.31 us (5%)
    reduce_scatter x1, waiting for transfers between devices, shards(): lax.psum_scatter(partial_out, 'expert', scatter_dimension=0, tiled=True,...  34.8 us
    all_gather x1, waiting for transfers between devices, shards(): lax.all_gather(pair_rows, 'expert', axis=0, tiled=True, axis_index_groups...  22.5 us
    ppermute x1, waiting for transfers between devices, shards(): lax.ppermute(both, 'expert', [(i, i + 2) for i in range(count - 2)])  21.1 us
    pallas_call x1, Pallas kernels, experts(): pl.pallas_call(functools.partial(experts_kernel, first_steps), grid=(firs...  16 us
    unnamed x1, blocking collectives  14.5 us
    unnamed x26, local copies, waits for them, and re-layouts  14.2 us
    pallas_call x1, Pallas kernels, attention(): pl.pallas_call(attention_kernel, grid_spec=pltpu.PrefetchScalarGridSpec(n...  10.6 us
    ppermute x1, waiting for transfers between devices, shards(): back = lax.ppermute(summed[CAP:], 'expert', partner)  10.2 us
  transfers between devices with their start and end apart: 7, of which 5 were waited for; matrix products, arithmetic and copies ran while one was open for 1% of the time, Pallas kernels for 0%

profile of v1, /device:TPU:0, one launch (start us, length us, event | category | flops | bytes accessed | tf_op | source)
XLA Modules:
  0.0 184.3 jit_solution(8134021831965286892)
XLA Ops:
  6.5 1.9 %constant_dynamic-update-slice_fusion.1 = bf16[128,4096]{1,0:T(8,128)(2,1)} fusion(bf16[64,4096]{1,0:T(8,128)(2,1)} %k0.1), kind=kLoop, calls=%fused_computation.2 | loop fusion | bytes 1048576
  8.4 1.9 %constant_dynamic-update-slice_fusion = bf16[128,4096]{1,0:T(8,128)(2,1)} fusion(bf16[128,4096]{1,0:T(8,128)(2,1)} %constant_dynamic-update-slice_fusion.1, bf16[64,4096]{1,0:T(8,128)(2,1)} %v0.1), kind=kLoop, calls=%fused_computation.1 | loop fusion | bytes 1048576 | tf_op jit(solution)/shard_map/concatenate | solution.py:237
  10.3 4.9 %collective-permute-start = (bf16[128,4096]{1,0:T(8,128)(2,1)}, bf16[128,4096]{1,0:T(8,128)(2,1)S(1)}, u32[]{:S(2)}, u32[]{:S(2)}) collective-permute-start(bf16[128,4096]{1,0:T(8,128)(2,1)} %constant_dynamic-update-slice_fusion), channel_id=1, source_target_pairs={{0,2},{1,3},{2,4},{3,5},{4,6},{5,7},{6,8},{7,9},{8,10},{9,11},{10,... | collective-permute-start | bytes 3145736 | tf_op jit(solution)/shard_map/ppermute | solution.py:238
  15.2 1.5 collective-permute-start.1
  16.8 21.1 %collective-permute-done.k1.v1 = bf16[128,4096]{1,0:T(8,128)(2,1)S(1)} collective-permute-done((bf16[128,4096]{1,0:T(8,128)(2,1)}, bf16[128,4096]{1,0:T(8,128)(2,1)S(1)}, u32[]{:S(2)}, u32[]{:S(2)}) %collective-permute-start) | collective-permute-done | bytes 1048608 | tf_op jit(solution)/shard_map/ppermute | solution.py:238
  37.9 1.3 dynamic-slice
  39.9 0.9 dynamic-update-slice
  40.8 14.5 %all-reduce = s32[1024]{0:T(1024)S(1)} all-reduce(s32[1024]{0:T(1024)S(1)} %dynamic-update-slice), channel_id=1, replica_groups=mesh['groups'=2,'expert'=16] {'expert'}, use_global_device_ids=true, to_apply=%add | all-reduce | flops 1024 | bytes 8192
  55.5 1.0 copy-done.1
  56.6 1.0 copy-done.2
  57.6 1.0 copy-done.4
  58.6 1.0 copy-done.5
  61.7 10.6 %attention.1 = (f32[64,4096]{1,0:T(8,128)S(1)}, bf16[20,4096]{1,0:T(8,128)(2,1)S(1)}, bf16[20,4096]{1,0:T(8,128)(2,1)S(1)}, bf16[2,20,64]{2,1,0:T(8,128)(2,1)S(1)}) custom-call(s32[5]{0:T(128)S(1)} %stack.23.deltas, bf16[64,4096]{1,0:T(8,128)(2,1)S(1)} %copy-done.4, bf16[64,4096]{1,0:T(8,128)(2,1)S(1)} %copy-done.1, bf16[64,4096]{1,0:T(8,128)(2,1)S(1)} %copy-done.2, ...), custom_call_target="tpu_custom_call" | custom-call | flops 268435456 | bytes 8388608 | tf_op jit(solution)/shard_map/attention/pallas_call | solution.py:116
  72.4 1.0 copy-done.3
  74.3 9.1 %collective-permute-done.3 = bf16[20,4096]{1,0:T(8,128)(2,1)S(1)} collective-permute-done((bf16[20,4096]{1,0:T(8,128)(2,1)S(1)}, bf16[20,4096]{1,0:T(8,128)(2,1)S(1)}, u32[]{:S(2)}, u32[]{:S(2)}) %collective-permute-start.3) | collective-permute-done | bytes 163872 | tf_op jit(solution)/shard_map/ppermute | solution.py:262
  83.4 0.8 pad_maximum_fusion
  84.2 22.5 %all-gather.2.cloned.1.call-done.x = bf16[320,4096]{1,0:T(8,128)(2,1)} async-done(((bf16[40,4096]{1,0:T(8,128)(2,1)}), bf16[320,4096]{1,0:T(8,128)(2,1)}) %all-gather.2.cloned.1.call-update) | async-done | bytes 2621456 | tf_op jit(solution)/shard_map/all_gather | solution.py:265
  106.7 1.7 copy-done
  108.4 16.0 %experts.1 = bf16[320,4096]{1,0:T(8,128)(2,1)} custom-call(bf16[320,4096]{1,0:T(8,128)(2,1)S(1)} %copy-done, bf16[4096,1024]{1,0:T(8,128)(2,1)} %w_gate.1, bf16[4096,1024]{1,0:T(8,128)(2,1)} %w_up.1, bf16[1024,4096]{1,0:T(8,128)(2,1)} %w_down.1), custom_call_target="tpu_custom_call" | custom-call | flops 8053063680 | bytes 30408704 | tf_op jit(solution)/shard_map/experts/pallas_call | solution.py:179
  124.5 34.8 %reduce-scatter.2.cloned.1.call-done.own = bf16[40,4096]{1,0:T(8,128)(2,1)} async-done(((bf16[320,4096]{1,0:T(8,128)(2,1)}), bf16[40,4096]{1,0:T(8,128)(2,1)}) %reduce-scatter.2.cloned.1.call-update) | async-done | bytes 327696 | tf_op jit(solution)/shard_map/reduce_scatter | solution.py:267
  159.3 1.0 slice.4
  160.2 2.5 %collective-permute-start.4 = (bf16[20,4096]{1,0:T(8,128)(2,1)S(1)}, bf16[20,4096]{1,0:T(8,128)(2,1)S(1)}, u32[]{:S(2)}, u32[]{:S(2)}) collective-permute-start(bf16[20,4096]{1,0:T(8,128)(2,1)S(1)} %slice.4), channel_id=1, source_target_pairs={{0,8},{1,9},{2,10},{3,11},{4,12},{5,13},{6,14},{7,15},{8,0},{9,1},... | collective-permute-start | bytes 491528 | tf_op jit(solution)/shard_map/ppermute | solution.py:270
  162.7 10.2 %collective-permute-done.4.other = bf16[20,4096]{1,0:T(8,128)(2,1)S(1)} collective-permute-done((bf16[20,4096]{1,0:T(8,128)(2,1)S(1)}, bf16[20,4096]{1,0:T(8,128)(2,1)S(1)}, u32[]{:S(2)}, u32[]{:S(2)}) %collective-permute-start.4) | collective-permute-done | bytes 163872 | tf_op jit(solution)/shard_map/ppermute | solution.py:270
  173.6 3.8 %combine.1 = bf16[64,4096]{1,0:T(8,128)(2,1)} custom-call(f32[64,4096]{1,0:T(8,128)} %copy-done.3, bf16[2,20,64]{2,1,0:T(8,128)(2,1)} %copy-done.7, bf16[40,4096]{1,0:T(8,128)(2,1)} %reduce-scatter.2.cloned.1.call-done.own, bf16[20,4096]{1,0:T(8,128)(2,1)} %copy-done.10), custom_call_target="tpu_custom_call" | custom-call | tf_op jit(solution)/shard_map/combine/pallas_call | solution.py:213
  (28 shorter events, 4.0 us)
Async XLA Ops:
  6.5 100.1 %all-gather.2.cloned.1.call-start = ((), (), s32[]{:S(2)}) async-start(), calls=%async_computation.1 | async-start | bytes 2949120 | tf_op jit(solution)/shard_map/all_gather | solution.py:265
  10.3 27.6 %collective-permute-start = (bf16[128,4096]{1,0:T(8,128)(2,1)}, bf16[128,4096]{1,0:T(8,128)(2,1)S(1)}, u32[]{:S(2)}, u32[]{:S(2)}) collective-permute-start(bf16[128,4096]{1,0:T(8,128)(2,1)} %constant_dynamic-update-slice_fusion), channel_id=1, source_target_pairs={{0,2},{1,3},{2,4},{3,5},{4,6},{5,7},{6,8},{7,9},{8,10},{9,11},{10,... | collective-permute-start | bytes 3145736 | tf_op jit(solution)/shard_map/ppermute | solution.py:238
  15.2 40.3 %collective-permute-start.1 = (bf16[128,4096]{1,0:T(8,128)(2,1)}, bf16[128,4096]{1,0:T(8,128)(2,1)S(1)}, u32[]{:S(2)}, u32[]{:S(2)}) collective-permute-start(bf16[128,4096]{1,0:T(8,128)(2,1)} %constant_dynamic-update-slice_fusion), channel_id=1, source_target_pairs={{0,1},{2,3},{4,5},{6,7},{8,9},{10,11},{12,13},{14,15},{1,4},{3,6},... | collective-permute-start | bytes 3145736 | tf_op jit(solution)/shard_map/ppermute | solution.py:241
  37.9 17.6 %collective-permute-start.2 = (bf16[128,4096]{1,0:T(8,128)(2,1)S(1)}, bf16[128,4096]{1,0:T(8,128)(2,1)S(1)}, u32[]{:S(2)}, u32[]{:S(2)}) collective-permute-start(bf16[128,4096]{1,0:T(8,128)(2,1)S(1)} %collective-permute-done.k1.v1), channel_id=1, source_target_pairs={{0,1},{1,0},{2,3},{3,2},{4,5},{5,4},{6,7},{7,6},{8,9},{9,8},{10,11... | collective-permute-start | bytes 3145736 | tf_op jit(solution)/shard_map/ppermute | solution.py:242
  55.5 1.0 copy-start.1
  56.6 1.0 copy-start.2
  57.6 1.0 copy-start.4
  58.6 1.0 copy-start.5
  59.7 0.7 copy-start.6
  60.4 0.7 copy-start.8
  61.1 0.7 copy-start.9
  72.4 1.0 copy-start.3
  73.3 0.6 copy-start.7
  73.9 9.4 %collective-permute-start.3 = (bf16[20,4096]{1,0:T(8,128)(2,1)S(1)}, bf16[20,4096]{1,0:T(8,128)(2,1)S(1)}, u32[]{:S(2)}, u32[]{:S(2)}) collective-permute-start(bf16[20,4096]{1,0:T(8,128)(2,1)S(1)} %get-tuple-element.12), channel_id=1, source_target_pairs={{0,8},{1,9},{2,10},{3,11},{4,12},{5,13},{6,14},{7,15},{8,0},{9,1},... | collective-permute-start | bytes 491528 | tf_op jit(solution)/shard_map/ppermute | solution.py:262
  84.2 75.1 %reduce-scatter.2.cloned.1.call-start = ((), (), s32[]{:S(2)}) async-start(), calls=%async_computation.2 | async-start | bytes 2949120 | tf_op jit(solution)/shard_map/reduce_scatter | solution.py:267
  106.7 1.7 copy-start
  160.2 12.7 %collective-permute-start.4 = (bf16[20,4096]{1,0:T(8,128)(2,1)S(1)}, bf16[20,4096]{1,0:T(8,128)(2,1)S(1)}, u32[]{:S(2)}, u32[]{:S(2)}) collective-permute-start(bf16[20,4096]{1,0:T(8,128)(2,1)S(1)} %slice.4), channel_id=1, source_target_pairs={{0,8},{1,9},{2,10},{3,11},{4,12},{5,13},{6,14},{7,15},{8,0},{9,1},... | collective-permute-start | bytes 491528 | tf_op jit(solution)/shard_map/ppermute | solution.py:270
  173.0 0.7 copy-start.10
Sparse Core Ops, SparseCore 0:
  84.3 22.3 all-gather.1
  124.6 34.5 reduce-scatter.1

commit v2 on v1

v2 whole, which is shorter than its diff:
```python
import functools

import jax
import jax.numpy as jnp
from jax import lax
from jax.experimental import pallas as pl
from jax.experimental.pallas import tpu as pltpu
from jax.sharding import PartitionSpec as P

HEAD_DIM = 128
E_WIN = 2
WIN_DEV = 3
CAP = 20
EARLY = 16
LATE = 2 * CAP - EARLY
HEADS_STEP = 8
MASKED = -1e30
MIB = 1024 * 1024


def attention_kernel(
    deltas, q, k0, v0, k1, v1, k2, v2, k3, v3, segs, resid, gain, routes, gates,
    mixed_out, early_out, rest_out, send_out, weight_out, bias,
):
    step = pl.program_id(0)
    steps = pl.num_programs(0)
    rows = q.shape[0]
    keys = (WIN_DEV + 1) * rows

    @pl.when(step == 0)
    def _():
        seg_row = segs[...]
        eye = lax.broadcasted_iota(jnp.int32, (rows, rows), 0) == lax.broadcasted_iota(
            jnp.int32, (rows, rows), 1
        )
        seg_col = jnp.sum(jnp.where(eye, seg_row[:, :rows], 0), axis=1, keepdims=True)
        lane = lax.broadcasted_iota(jnp.int32, (rows, keys), 1)
        sub = lax.broadcasted_iota(jnp.int32, (rows, keys), 0)
        block = lane // rows
        back = jnp.where(
            block == 0,
            deltas[0],
            jnp.where(block == 1, deltas[1], jnp.where(block == 2, deltas[2], deltas[3])),
        )
        distance = sub - (lane - block * rows) + back * rows
        allowed = (distance >= 0) & (distance <= WIN_DEV * rows) & (seg_col == seg_row)
        bias[...] = jnp.where(allowed, 0.0, MASKED)

    scale = 1.0 / HEAD_DIM**0.5
    heads = [slice(head * HEAD_DIM, (head + 1) * HEAD_DIM) for head in range(HEADS_STEP)]
    scores = jnp.stack(
        [
            lax.dot_general(
                q[:, cols],
                jnp.concatenate([k0[:, cols], k1[:, cols], k2[:, cols], k3[:, cols]], axis=0),
                (((1,), (1,)), ((), ())),
                preferred_element_type=jnp.float32,
            )
            for cols in heads
        ]
    )
    scores = scores * scale + bias[...][None]
    expo = jnp.exp(scores - jnp.max(scores, axis=2, keepdims=True))
    denom = jnp.sum(expo, axis=2, keepdims=True)
    probs = expo.astype(jnp.bfloat16)
    outs = [
        jnp.dot(
            probs[head],
            jnp.concatenate([v0[:, cols], v1[:, cols], v2[:, cols], v3[:, cols]], axis=0),
            preferred_element_type=jnp.float32,
        )
        / denom[head]
        for head, cols in enumerate(heads)
    ]
    width = HEADS_STEP * HEAD_DIM
    at = pl.ds(pl.multiple_of(step * width, width), width)
    mixed_out[:, at] = resid[...].astype(jnp.float32) + jnp.concatenate(outs, axis=1)

    @pl.when(step == steps - 1)
    def _():
        mixed = mixed_out[...]
        normed = (
            mixed * lax.rsqrt(jnp.mean(mixed * mixed, axis=1, keepdims=True) + 1e-05) * gain[...]
        ).astype(jnp.bfloat16)
        across = lax.broadcasted_iota(jnp.int32, (rows, rows), 1)
        down = lax.broadcasted_iota(jnp.int32, (rows, rows), 0)
        upper = jnp.where(down < across, 1.0, 0.0).astype(jnp.bfloat16)
        eye = jnp.where(down == across, 1.0, 0.0).astype(jnp.bfloat16)
        slot = lax.broadcasted_iota(jnp.int32, (32, rows), 0)

        def picks(expert):
            hit = routes[...] == expert
            member = jnp.max(jnp.where(hit, 1.0, 0.0), axis=0, keepdims=True)
            weight = jnp.sum(
                jnp.where(hit, gates[...].astype(jnp.float32), 0.0), axis=0, keepdims=True
            )
            rank = jnp.dot(
                jnp.broadcast_to(member, (8, rows)).astype(jnp.bfloat16),
                upper,
                preferred_element_type=jnp.float32,
            )[0:1].astype(jnp.int32)
            return member > 0.5, weight, rank

        def spread(pick, weight):
            return lax.dot_general(
                eye,
                jnp.where(pick, weight, 0.0).astype(jnp.bfloat16),
                (((1,), (1,)), ((), ())),
                preferred_element_type=jnp.float32,
            ).astype(jnp.bfloat16)

        def packed(pick):
            return jnp.dot(
                jnp.where(pick, 1.0, 0.0).astype(jnp.bfloat16),
                normed,
                preferred_element_type=jnp.float32,
            ).astype(jnp.bfloat16)

        member, weight, rank = picks(deltas[4])
        pick = (slot == rank) & member
        mine = packed(pick)
        early_out[...] = mine[:EARLY]
        rest_out[...] = mine[EARLY:CAP]
        weight_out[0] = spread(pick & (slot < EARLY), weight)
        weight_out[1] = spread((slot - CAP + EARLY == rank) & (slot >= CAP) & member, weight)
        member, weight, rank = picks(1 - deltas[4])
        pick = (slot == rank) & member
        send_out[...] = packed(pick)[:CAP]
        weight_out[2] = spread(pick, weight)


def attention(deltas, q, pairs, segs, resid, gain, routes, gates):
    rows, width = q.shape
    cols = HEADS_STEP * HEAD_DIM
    top = routes.shape[0]
    piece = pl.BlockSpec((rows, cols), lambda j, *_: (0, j))

    def whole(shape):
        return pl.BlockSpec(shape, lambda j, *_: (0,) * len(shape))

    return pl.pallas_call(
        attention_kernel,
        grid_spec=pltpu.PrefetchScalarGridSpec(
            num_scalar_prefetch=1,
            grid=(width // cols,),
            in_specs=[piece] * (1 + len(pairs))
            + [
                whole((1, (WIN_DEV + 1) * rows)),
                piece,
                whole((1, width)),
                whole((top, rows)),
                whole((top, rows)),
            ],
            out_specs=[
                whole((rows, width)),
                whole((EARLY, width)),
                whole((CAP - EARLY, width)),
                whole((CAP, width)),
                whole((3, rows, 32)),
            ],
            scratch_shapes=[pltpu.VMEM((rows, (WIN_DEV + 1) * rows), jnp.float32)],
        ),
        out_shape=[
            jax.ShapeDtypeStruct((rows, width), jnp.float32),
            jax.ShapeDtypeStruct((EARLY, width), jnp.bfloat16),
            jax.ShapeDtypeStruct((CAP - EARLY, width), jnp.bfloat16),
            jax.ShapeDtypeStruct((CAP, width), jnp.bfloat16),
            jax.ShapeDtypeStruct((3, rows, 32), jnp.bfloat16),
        ],
        compiler_params=pltpu.CompilerParams(vmem_limit_bytes=56 * MIB),
        cost_estimate=pl.CostEstimate(
            flops=4 * rows * 4 * rows * width, bytes_accessed=8 * rows * width * 4,
            transcendentals=rows * 4 * rows * (width // HEAD_DIM),
        ),
        name="attention",
    )(deltas, q, *pairs, segs, resid, gain, routes, gates)


def experts_kernel(
    depth, out_cols, x, w_gate, w_up, w_down, out,
    gate_held, up_held, down_held, gate_sum, up_sum, hidden, first_sems, second_sems,
):
    width, units = gate_held.shape
    first = []
    for part in range(width // depth):
        at = pl.ds(part * depth, depth)
        first.append(
            (
                pltpu.make_async_copy(w_gate.at[at], gate_held.at[at], first_sems.at[0, part]),
                pltpu.make_async_copy(w_up.at[at], up_held.at[at], first_sems.at[1, part]),
            )
        )
    second = []
    for part in range(width // out_cols):
        at = pl.ds(part * out_cols, out_cols)
        second.append(
            pltpu.make_async_copy(w_down.at[:, at], down_held.at[:, at], second_sems.at[part])
        )
    for gate_copy, up_copy in first:
        gate_copy.start()
        up_copy.start()
    for copy in second:
        copy.start()
    for part, (gate_copy, up_copy) in enumerate(first):
        at = slice(part * depth, (part + 1) * depth)
        piece = x[:, at]
        gate_copy.wait()
        gate = jnp.dot(piece, gate_held[at], preferred_element_type=jnp.float32)
        up_copy.wait()
        up = jnp.dot(piece, up_held[at], preferred_element_type=jnp.float32)
        if part == 0:
            gate_sum[...] = gate
            up_sum[...] = up
        else:
            gate_sum[...] += gate
            up_sum[...] += up
    hidden[...] = (jax.nn.silu(gate_sum[...]) * up_sum[...]).astype(jnp.bfloat16)
    for part, copy in enumerate(second):
        at = slice(part * out_cols, (part + 1) * out_cols)
        copy.wait()
        out[:, at] = jnp.dot(
            hidden[...], down_held[:, at], preferred_element_type=jnp.float32
        ).astype(jnp.bfloat16)


def experts(x, w_gate, w_up, w_down):
    rows, width = x.shape
    units = w_gate.shape[1]
    depth = 512
    out_cols = 512
    in_place = pl.BlockSpec(memory_space=pl.ANY)
    near = pl.BlockSpec(memory_space=pltpu.VMEM)
    return pl.pallas_call(
        functools.partial(experts_kernel, depth, out_cols),
        in_specs=[near, in_place, in_place, in_place],
        out_specs=near,
        out_shape=jax.ShapeDtypeStruct((rows, width), jnp.bfloat16),
        scratch_shapes=[
            pltpu.VMEM((width, units), jnp.bfloat16),
            pltpu.VMEM((width, units), jnp.bfloat16),
            pltpu.VMEM((units, width), jnp.bfloat16),
            pltpu.VMEM((rows, units), jnp.float32),
            pltpu.VMEM((rows, units), jnp.float32),
            pltpu.VMEM((rows, units), jnp.bfloat16),
            pltpu.SemaphoreType.DMA((2, width // depth)),
            pltpu.SemaphoreType.DMA((width // out_cols,)),
        ],
        compiler_params=pltpu.CompilerParams(vmem_limit_bytes=56 * MIB),
        cost_estimate=pl.CostEstimate(
            flops=6 * rows * width * units,
            bytes_accessed=6 * width * units + 4 * rows * width,
            transcendentals=rows * units,
        ),
        name="experts",
    )(x, w_gate, w_up, w_down)


def combine_kernel(mixed, weight, early, late, other, out):
    total = mixed[...]
    for place, part in enumerate((early, late, other)):
        total = total + jnp.dot(
            weight[place][:, : part.shape[0]], part[...], preferred_element_type=jnp.float32
        )
    out[...] = total.astype(jnp.bfloat16)


def combine(mixed, weight, early, late, other):
    rows, width = mixed.shape
    cols = 2048

    def piece(count):
        return pl.BlockSpec((count, cols), lambda j: (0, j))

    return pl.pallas_call(
        combine_kernel,
        grid=(width // cols,),
        in_specs=[
            piece(rows),
            pl.BlockSpec(weight.shape, lambda j: (0, 0, 0)),
            piece(early.shape[0]),
            piece(late.shape[0]),
            piece(other.shape[0]),
        ],
        out_specs=piece(rows),
        out_shape=jax.ShapeDtypeStruct((rows, width), jnp.bfloat16),
        compiler_params=pltpu.CompilerParams(vmem_limit_bytes=56 * MIB),
        name="combine",
    )(mixed, weight, early, late, other)


def shards(
    resid, queries, keys, values, segment_ids, norm_gain, routes, route_gates, w_gate, w_up, w_down
):
    tok_rows = resid.shape[0]
    count = lax.axis_size("expert")
    own = lax.axis_index("expert")
    shard_count = count // E_WIN
    odd = own % 2

    next_chip = [(i, i + 2) for i in range(count - 2)]
    crossing = [(i, i + 1) for i in range(0, count, 2)]
    crossing += [(i, i + 3) for i in range(1, count - 3, 2)]
    mirror = [(i, i ^ 1) for i in range(count)]
    key_two = lax.ppermute(keys, "expert", next_chip)
    value_two = lax.ppermute(values, "expert", next_chip)
    key_cross = lax.ppermute(keys, "expert", crossing)
    value_cross = lax.ppermute(values, "expert", crossing)
    key_two, seg_held = lax.optimization_barrier((key_two, segment_ids))
    key_mirror = lax.ppermute(key_two, "expert", mirror)
    value_mirror = lax.ppermute(value_two, "expert", mirror)
    seg_two = lax.ppermute(seg_held, "expert", next_chip)
    seg_cross = lax.ppermute(seg_held, "expert", crossing)
    seg_mirror = lax.ppermute(seg_two, "expert", mirror)
    segs = jnp.concatenate([segment_ids, seg_two, seg_cross, seg_mirror]).reshape(1, -1)

    far = 2 * WIN_DEV + 2
    delta_list = [0 * own, 0 * own + 2, 3 - 2 * odd, 1 + 2 * odd]
    my_expert = own // shard_count
    scalars = jnp.stack(
        [jnp.where(own >= delta, delta, far) for delta in delta_list] + [my_expert]
    ).astype(jnp.int32)

    mixed, early, rest, send, weight = attention(
        scalars,
        queries,
        [keys, values, key_two, value_two, key_cross, value_cross, key_mirror, value_mirror],
        segs, resid, norm_gain.reshape(1, -1), routes.T, route_gates.T,
    )
    partner = [(i, (i + shard_count) % count) for i in range(count)]
    halves = [list(range(e * shard_count, (e + 1) * shard_count)) for e in range(E_WIN)]

    def gathered(block):
        return lax.all_gather(block, "expert", axis=0, tiled=True, axis_index_groups=halves)

    def scattered(block):
        return lax.psum_scatter(
            block, "expert", scatter_dimension=0, tiled=True, axis_index_groups=halves
        )

    early_rows = gathered(early)
    got = lax.ppermute(send, "expert", partner)
    late_rows = gathered(jnp.concatenate([got, rest], axis=0))
    early_sum = scattered(experts(early_rows, w_gate, w_up, w_down))
    late_sum = scattered(experts(late_rows, w_gate, w_up, w_down))
    back = lax.ppermute(late_sum[:CAP], "expert", partner)
    return combine(mixed, weight, early_sum, late_sum, back)


def solution(mesh):
    placed = (
        P(("groups", "expert"), None),
        P(("groups", "expert"), None),
        P(("groups", "expert"), None),
        P(("groups", "expert"), None),
        P(("groups", "expert")),
        P(),
        P(("groups", "expert"), None),
        P(("groups", "expert"), None),
        P(None, "expert"),
        P(None, "expert"),
        P("expert", None),
    )
    return jax.shard_map(
        shards, mesh=mesh, in_specs=placed, out_specs=P(("groups", "expert"), None), check_vma=False
    )
```

time: 185 us -> 193 us (1.043)
  starting transfers between devices: 9.31 us -> 34.3 us
  local copies, waits for them, and re-layouts: 17.3 us -> 2.58 us
  blocking collectives: 14.5 us -> 0 us
  Pallas kernels: 30.5 us -> 37.2 us
  waiting for transfers between devices: 97.7 us -> 102 us
    ppermute x4 -> x10, starting transfers between devices: 8.93 us -> 29.5 us  [the longest x1 6 us: shards(): seg_mirror = lax.ppermute(seg_two, 'expert', mirror)]
    ppermute x4 -> x10, waiting for transfers between devices: 31.4 us -> 16.3 us  [the longest x1 10.1 us: shards(): value_two = lax.ppermute(values, 'expert', next_chip)]
    unnamed x1 -> x0, blocking collectives: 14.5 us -> none
    reduce_scatter x1 -> x2, waiting for transfers between devices: 34.8 us -> 47.4 us  [scattered(): lax.psum_scatter(block, 'expert', scatter_dimension=0, tiled=True, axis_i...]
    unnamed x26 -> x14, local copies, waits for them, and re-layouts: 14.2 us -> 1.95 us
    pallas_call x2 -> x3, Pallas kernels: 19.9 us -> 30.2 us  [the longest x2 27.5 us: experts(): pl.pallas_call(functools.partial(experts_kernel, depth, out_cols), in_spe...]
    all_gather x1 -> x2, waiting for transfers between devices: 22.5 us -> 28.2 us  [gathered(): lax.all_gather(block, 'expert', axis=0, tiled=True, axis_index_groups=hal...]
    ppermute x1, starting transfers between devices: 0.34 us -> 4.68 us  [shards(): got = lax.ppermute(send, 'expert', partner)]
  transfers between devices with their start and end apart: 7 -> 15, of which waited for: 5 -> 10; matrix products, arithmetic and copies ran while one was open for 1% -> 1% of each run, Pallas kernels for 0% -> 14%
where the time goes in v2:
time: 193 us; the launch traced here: 192 us
  waiting for transfers between devices  102 us (53%)
  Pallas kernels  37.2 us (19%)
  starting transfers between devices  34.3 us (18%)
  between operations  13.3 us (7%)
  other arithmetic  2.74 us (1%)
  local copies, waits for them, and re-layouts  2.58 us (1%)
    reduce_scatter x2, waiting for transfers between devices, scattered(): lax.psum_scatter(block, 'expert', scatter_dimension=0, tiled=True, axis_i...  47.4 us
    all_gather x2, waiting for transfers between devices, gathered(): lax.all_gather(block, 'expert', axis=0, tiled=True, axis_index_groups=hal...  28.2 us
    pallas_call x2, Pallas kernels, experts(): pl.pallas_call(functools.partial(experts_kernel, depth, out_cols), in_spe...  27.5 us
    ppermute x1, waiting for transfers between devices, shards(): value_two = lax.ppermute(values, 'expert', next_chip)  10.1 us
    ppermute x1, waiting for transfers between devices, shards(): got = lax.ppermute(send, 'expert', partner)  9.7 us
    pallas_call x1, Pallas kernels, attention(): pl.pallas_call(attention_kernel, grid_spec=pltpu.PrefetchScalarGridSpec(n...  7.02 us
    ppermute x1, starting transfers between devices, shards(): seg_mirror = lax.ppermute(seg_two, 'expert', mirror)  6 us
    ppermute x1, starting transfers between devices, shards(): key_two = lax.ppermute(keys, 'expert', next_chip)  4.89 us
  transfers between devices with their start and end apart: 15, of which 10 were waited for; matrix products, arithmetic and copies ran while one was open for 1% of the time, Pallas kernels for 14%

profile of v2, /device:TPU:0, one launch (start us, length us, event | category | flops | bytes accessed | tf_op | source)
XLA Modules:
  0.0 192.4 jit_solution(15493172626630852941)
XLA Ops:
  6.5 4.9 %collective-permute-start = (bf16[64,4096]{1,0:T(8,128)(2,1)}, bf16[64,4096]{1,0:T(8,128)(2,1)S(1)}, u32[]{:S(2)}, u32[]{:S(2)}) collective-permute-start(bf16[64,4096]{1,0:T(8,128)(2,1)} %k0.1), channel_id=1, source_target_pairs={{0,2},{1,3},{2,4},{3,5},{4,6},{5,7},{6,8},{7,9},{8,10},{9,11},{10,... | collective-permute-start | bytes 1572872 | tf_op jit(solution)/shard_map/ppermute | solution.py:304
  11.4 3.4 %collective-permute-start.1 = (bf16[64,4096]{1,0:T(8,128)(2,1)}, bf16[64,4096]{1,0:T(8,128)(2,1)S(1)}, u32[]{:S(2)}, u32[]{:S(2)}) collective-permute-start(bf16[64,4096]{1,0:T(8,128)(2,1)} %v0.1), channel_id=1, source_target_pairs={{0,2},{1,3},{2,4},{3,5},{4,6},{5,7},{6,8},{7,9},{8,10},{9,11},{10,... | collective-permute-start | bytes 1572872 | tf_op jit(solution)/shard_map/ppermute | solution.py:305
  14.9 1.3 collective-permute-start.2
  16.2 4.2 %collective-permute-start.3 = (bf16[64,4096]{1,0:T(8,128)(2,1)}, bf16[64,4096]{1,0:T(8,128)(2,1)S(1)}, u32[]{:S(2)}, u32[]{:S(2)}) collective-permute-start(bf16[64,4096]{1,0:T(8,128)(2,1)} %v0.1), channel_id=1, source_target_pairs={{0,1},{2,3},{4,5},{6,7},{8,9},{10,11},{12,13},{14,15},{1,4},{3,6},... | collective-permute-start | bytes 1572872 | tf_op jit(solution)/shard_map/ppermute | solution.py:307
  20.4 3.6 %collective-permute-done.k1 = bf16[64,4096]{1,0:T(8,128)(2,1)S(1)} collective-permute-done((bf16[64,4096]{1,0:T(8,128)(2,1)}, bf16[64,4096]{1,0:T(8,128)(2,1)S(1)}, u32[]{:S(2)}, u32[]{:S(2)}) %collective-permute-start) | collective-permute-done | bytes 524320 | tf_op jit(solution)/shard_map/ppermute | solution.py:304
  24.0 10.1 %collective-permute-done.1.v1 = bf16[64,4096]{1,0:T(8,128)(2,1)S(1)} collective-permute-done((bf16[64,4096]{1,0:T(8,128)(2,1)}, bf16[64,4096]{1,0:T(8,128)(2,1)S(1)}, u32[]{:S(2)}, u32[]{:S(2)}) %collective-permute-start.1) | collective-permute-done | bytes 524320 | tf_op jit(solution)/shard_map/ppermute | solution.py:305
  34.1 2.4 %collective-permute-start.7 = (s32[64]{0:T(128)}, s32[64]{0:T(128)S(1)}, u32[]{:S(2)}, u32[]{:S(2)}) collective-permute-start(s32[64]{0:T(128)} %param.15), channel_id=1, source_target_pairs={{0,1},{2,3},{4,5},{6,7},{8,9},{10,11},{12,13},{14,15},{1,4},{3,6},... | collective-permute-start | bytes 776 | tf_op jit(solution)/shard_map/ppermute | solution.py:312
  36.5 0.9 collective-permute-done.7
  37.5 4.6 %collective-permute-start.6 = (s32[64]{0:T(128)}, s32[64]{0:T(128)S(1)}, u32[]{:S(2)}, u32[]{:S(2)}) collective-permute-start(s32[64]{0:T(128)} %param.15), channel_id=1, source_target_pairs={{0,2},{1,3},{2,4},{3,5},{4,6},{5,7},{6,8},{7,9},{8,10},{9,11},{10,... | collective-permute-start | bytes 776 | tf_op jit(solution)/shard_map/ppermute | solution.py:311
  42.0 1.4 collective-permute-done.6
  43.5 6.0 %collective-permute-start.8 = (s32[64]{0:T(128)S(1)}, s32[64]{0:T(128)S(1)}, u32[]{:S(2)}, u32[]{:S(2)}) collective-permute-start(s32[64]{0:T(128)S(1)} %collective-permute-done.6), channel_id=1, source_target_pairs={{0,1},{1,0},{2,3},{3,2},{4,5},{5,4},{6,7},{7,6},{8,9},{9,8},{10,11... | collective-permute-start | bytes 776 | tf_op jit(solution)/shard_map/ppermute | solution.py:313
  50.3 1.3 pad_add_fusion
  52.9 7.0 %attention.1 = (f32[64,4096]{1,0:T(8,128)}, bf16[16,4096]{1,0:T(8,128)(2,1)}, bf16[4,4096]{1,0:T(4,128)(2,1)}, bf16[20,4096]{1,0:T(8,128)(2,1)}, bf16[3,64,32]{2,1,0:T(8,128)(2,1)}) custom-call(s32[5]{0:T(128)} %stack.23.deltas, bf16[64,4096]{1,0:T(8,128)(2,1)} %q.1, bf16[64,4096]{1,0:T(8,128)(2,1)} %k0.1, bf16[64,4096]{1,0:T(8,128)(2,1)} %v0.1, ...), custom_call_target="tpu_custom_call" | custom-call | flops 268435456 | bytes 8388608 | tf_op jit(solution)/shard_map/attention/pallas_call | solution.py:141
  59.9 4.7 %collective-permute-start.9 = (bf16[20,4096]{1,0:T(8,128)(2,1)}, bf16[20,4096]{1,0:T(8,128)(2,1)S(1)}, u32[]{:S(2)}, u32[]{:S(2)}) collective-permute-start(bf16[20,4096]{1,0:T(8,128)(2,1)} %get-tuple-element.17), channel_id=1, source_target_pairs={{0,8},{1,9},{2,10},{3,11},{4,12},{5,13},{6,14},{7,15},{8,0},{9,1},... | collective-permute-start | bytes 491528 | tf_op jit(solution)/shard_map/ppermute | solution.py:341
  64.6 9.7 %collective-permute-done.9 = bf16[20,4096]{1,0:T(8,128)(2,1)S(1)} collective-permute-done((bf16[20,4096]{1,0:T(8,128)(2,1)}, bf16[20,4096]{1,0:T(8,128)(2,1)S(1)}, u32[]{:S(2)}, u32[]{:S(2)}) %collective-permute-start.9) | collective-permute-done | bytes 163872 | tf_op jit(solution)/shard_map/ppermute | solution.py:341
  74.3 1.5 pad_maximum_fusion
  76.6 21.7 %all-gather.5.cloned.1.call-done.x = bf16[192,4096]{1,0:T(8,128)(2,1)} async-done(((bf16[24,4096]{1,0:T(8,128)(2,1)}), bf16[192,4096]{1,0:T(8,128)(2,1)}) %all-gather.5.cloned.1.call-update) | async-done | bytes 1572880 | tf_op jit(solution)/shard_map/all_gather | solution.py:333
  98.3 14.3 %experts.3 = bf16[192,4096]{1,0:T(8,128)(2,1)} custom-call(bf16[192,4096]{1,0:T(8,128)(2,1)} %all-gather.5.cloned.1.call-done.x, bf16[4096,1024]{1,0:T(8,128)(2,1)} %w_gate.3, bf16[4096,1024]{1,0:T(8,128)(2,1)} %w_up.3, bf16[1024,4096]{1,0:T(8,128)(2,1)} %w_down.3), custom_call_target="tpu_custom_call" | custom-call | flops 4831838208 | bytes 28311552 | tf_op jit(solution)/shard_map/experts/pallas_call | solution.py:233
  112.7 6.4 %all-gather.3.cloned.1.call-done.x = bf16[128,4096]{1,0:T(8,128)(2,1)} async-done(((bf16[16,4096]{1,0:T(8,128)(2,1)}), bf16[128,4096]{1,0:T(8,128)(2,1)}) %all-gather.3.cloned.1.call-update) | async-done | bytes 1048592 | tf_op jit(solution)/shard_map/all_gather | solution.py:333
  119.1 13.3 %experts.2 = bf16[128,4096]{1,0:T(8,128)(2,1)} custom-call(bf16[128,4096]{1,0:T(8,128)(2,1)} %all-gather.3.cloned.1.call-done.x, bf16[4096,1024]{1,0:T(8,128)(2,1)} %w_gate.3, bf16[4096,1024]{1,0:T(8,128)(2,1)} %w_up.3, bf16[1024,4096]{1,0:T(8,128)(2,1)} %w_down.3), custom_call_target="tpu_custom_call" | custom-call | flops 3221225472 | bytes 27262976 | tf_op jit(solution)/shard_map/experts/pallas_call | solution.py:233
  132.4 18.5 %reduce-scatter.5.cloned.1.call-done.late = bf16[24,4096]{1,0:T(8,128)(2,1)} async-done(((bf16[192,4096]{1,0:T(8,128)(2,1)}), bf16[24,4096]{1,0:T(8,128)(2,1)}) %reduce-scatter.5.cloned.1.call-update) | async-done | bytes 196624 | tf_op jit(solution)/shard_map/reduce_scatter | solution.py:336
  150.9 2.7 %collective-permute-start.10 = (bf16[20,4096]{1,0:T(8,128)(2,1)}, bf16[20,4096]{1,0:T(8,128)(2,1)S(1)}, u32[]{:S(2)}, u32[]{:S(2)}) collective-permute-start(bf16[20,4096]{1,0:T(8,128)(2,1)} %bitcast.10), channel_id=1, source_target_pairs={{0,8},{1,9},{2,10},{3,11},{4,12},{5,13},{6,14},{7,15},{8,0},{9,1},... | collective-permute-start | bytes 491528 | tf_op jit(solution)/shard_map/ppermute | solution.py:345
  153.6 28.9 %reduce-scatter.3.cloned.1.call-done.early = bf16[16,4096]{1,0:T(8,128)(2,1)} async-done(((bf16[128,4096]{1,0:T(8,128)(2,1)}), bf16[16,4096]{1,0:T(8,128)(2,1)}) %reduce-scatter.3.cloned.1.call-update) | async-done | bytes 131088 | tf_op jit(solution)/shard_map/reduce_scatter | solution.py:336
  183.2 2.6 %combine.1 = bf16[64,4096]{1,0:T(8,128)(2,1)} custom-call(f32[64,4096]{1,0:T(8,128)} %get-tuple-element.14.mixed, bf16[3,64,32]{2,1,0:T(8,128)(2,1)} %get-tuple-element.15.weight, bf16[16,4096]{1,0:T(8,128)(2,1)} %reduce-scatter.3.cloned.1.call-done.early, bf16[24,4096]{1,0:T(8,128)(2,1)} %reduce-scatter.5.cloned.1.call-done.late, bf16[20,4096]{1,0:T(8,128)(2,1)} %copy-done.6), custom_call_target="tpu_custom_call" | custom-call | tf_op jit(solution)/shard_map/combine/pallas_call | solution.py:274
  (31 shorter events, 3.7 us)
Async XLA Ops:
  6.5 91.8 %all-gather.5.cloned.1.call-start = ((), (), s32[]{:S(2)}) async-start(), calls=%async_computation.4 | async-start | bytes 1769472 | tf_op jit(solution)/shard_map/all_gather | solution.py:333
  6.5 17.5 %collective-permute-start = (bf16[64,4096]{1,0:T(8,128)(2,1)}, bf16[64,4096]{1,0:T(8,128)(2,1)S(1)}, u32[]{:S(2)}, u32[]{:S(2)}) collective-permute-start(bf16[64,4096]{1,0:T(8,128)(2,1)} %k0.1), channel_id=1, source_target_pairs={{0,2},{1,3},{2,4},{3,5},{4,6},{5,7},{6,8},{7,9},{8,10},{9,11},{10,... | collective-permute-start | bytes 1572872 | tf_op jit(solution)/shard_map/ppermute | solution.py:304
  11.4 22.7 %collective-permute-start.1 = (bf16[64,4096]{1,0:T(8,128)(2,1)}, bf16[64,4096]{1,0:T(8,128)(2,1)S(1)}, u32[]{:S(2)}, u32[]{:S(2)}) collective-permute-start(bf16[64,4096]{1,0:T(8,128)(2,1)} %v0.1), channel_id=1, source_target_pairs={{0,2},{1,3},{2,4},{3,5},{4,6},{5,7},{6,8},{7,9},{8,10},{9,11},{10,... | collective-permute-start | bytes 1572872 | tf_op jit(solution)/shard_map/ppermute | solution.py:305
  14.9 36.7 %collective-permute-start.2 = (bf16[64,4096]{1,0:T(8,128)(2,1)}, bf16[64,4096]{1,0:T(8,128)(2,1)S(1)}, u32[]{:S(2)}, u32[]{:S(2)}) collective-permute-start(bf16[64,4096]{1,0:T(8,128)(2,1)} %k0.1), channel_id=1, source_target_pairs={{0,1},{2,3},{4,5},{6,7},{8,9},{10,11},{12,13},{14,15},{1,4},{3,6},... | collective-permute-start | bytes 1572872 | tf_op jit(solution)/shard_map/ppermute | solution.py:306
  16.2 35.3 %collective-permute-start.3 = (bf16[64,4096]{1,0:T(8,128)(2,1)}, bf16[64,4096]{1,0:T(8,128)(2,1)S(1)}, u32[]{:S(2)}, u32[]{:S(2)}) collective-permute-start(bf16[64,4096]{1,0:T(8,128)(2,1)} %v0.1), channel_id=1, source_target_pairs={{0,1},{2,3},{4,5},{6,7},{8,9},{10,11},{12,13},{14,15},{1,4},{3,6},... | collective-permute-start | bytes 1572872 | tf_op jit(solution)/shard_map/ppermute | solution.py:307
  24.0 27.6 %copy-start = (bf16[64,4096]{1,0:T(8,128)(2,1)}, bf16[64,4096]{1,0:T(8,128)(2,1)S(1)}, u32[]{:S(2)}) copy-start(bf16[64,4096]{1,0:T(8,128)(2,1)S(1)} %collective-permute-done.k1) | copy-start | bytes 1572868
  24.0 27.5 %collective-permute-start.4 = (bf16[64,4096]{1,0:T(8,128)(2,1)S(1)}, bf16[64,4096]{1,0:T(8,128)(2,1)S(1)}, u32[]{:S(2)}, u32[]{:S(2)}) collective-permute-start(bf16[64,4096]{1,0:T(8,128)(2,1)S(1)} %collective-permute-done.k1), channel_id=1, source_target_pairs={{0,1},{1,0},{2,3},{3,2},{4,5},{5,4},{6,7},{7,6},{8,9},{9,8},{10,11... | collective-permute-start | bytes 1572872 | tf_op jit(solution)/shard_map/ppermute | solution.py:309
  34.1 17.5 %copy-start.1 = (bf16[64,4096]{1,0:T(8,128)(2,1)}, bf16[64,4096]{1,0:T(8,128)(2,1)S(1)}, u32[]{:S(2)}) copy-start(bf16[64,4096]{1,0:T(8,128)(2,1)S(1)} %collective-permute-done.1.v1) | copy-start | bytes 1572868
  34.1 17.5 %collective-permute-start.5 = (bf16[64,4096]{1,0:T(8,128)(2,1)S(1)}, bf16[64,4096]{1,0:T(8,128)(2,1)S(1)}, u32[]{:S(2)}, u32[]{:S(2)}) collective-permute-start(bf16[64,4096]{1,0:T(8,128)(2,1)S(1)} %collective-permute-done.1.v1), channel_id=1, source_target_pairs={{0,1},{1,0},{2,3},{3,2},{4,5},{5,4},{6,7},{7,6},{8,9},{9,8},{10,11... | collective-permute-start | bytes 1572872 | tf_op jit(solution)/shard_map/ppermute | solution.py:310
  34.1 3.3 %collective-permute-start.7 = (s32[64]{0:T(128)}, s32[64]{0:T(128)S(1)}, u32[]{:S(2)}, u32[]{:S(2)}) collective-permute-start(s32[64]{0:T(128)} %param.15), channel_id=1, source_target_pairs={{0,1},{2,3},{4,5},{6,7},{8,9},{10,11},{12,13},{14,15},{1,4},{3,6},... | collective-permute-start | bytes 776 | tf_op jit(solution)/shard_map/ppermute | solution.py:312
  37.5 6.0 %collective-permute-start.6 = (s32[64]{0:T(128)}, s32[64]{0:T(128)S(1)}, u32[]{:S(2)}, u32[]{:S(2)}) collective-permute-start(s32[64]{0:T(128)} %param.15), channel_id=1, source_target_pairs={{0,2},{1,3},{2,4},{3,5},{4,6},{5,7},{6,8},{7,9},{8,10},{9,11},{10,... | collective-permute-start | bytes 776 | tf_op jit(solution)/shard_map/ppermute | solution.py:311
  43.5 6.8 %collective-permute-start.8 = (s32[64]{0:T(128)S(1)}, s32[64]{0:T(128)S(1)}, u32[]{:S(2)}, u32[]{:S(2)}) collective-permute-start(s32[64]{0:T(128)S(1)} %collective-permute-done.6), channel_id=1, source_target_pairs={{0,1},{1,0},{2,3},{3,2},{4,5},{5,4},{6,7},{7,6},{8,9},{9,8},{10,11... | collective-permute-start | bytes 776 | tf_op jit(solution)/shard_map/ppermute | solution.py:313
  51.5 0.8 copy-start.2
  51.5 1.0 copy-start.3
  51.6 1.1 copy-start.4
  51.6 1.3 copy-start.5
  59.9 14.4 %collective-permute-start.9 = (bf16[20,4096]{1,0:T(8,128)(2,1)}, bf16[20,4096]{1,0:T(8,128)(2,1)S(1)}, u32[]{:S(2)}, u32[]{:S(2)}) collective-permute-start(bf16[20,4096]{1,0:T(8,128)(2,1)} %get-tuple-element.17), channel_id=1, source_target_pairs={{0,8},{1,9},{2,10},{3,11},{4,12},{5,13},{6,14},{7,15},{8,0},{9,1},... | collective-permute-start | bytes 491528 | tf_op jit(solution)/shard_map/ppermute | solution.py:341
  75.8 43.3 %all-gather.3.cloned.1.call-start = ((), (), s32[]{:S(2)}) async-start(), calls=%async_computation.2 | async-start | bytes 1179648 | tf_op jit(solution)/shard_map/all_gather | solution.py:333
  76.5 74.4 %reduce-scatter.5.cloned.1.call-start = ((), (), s32[]{:S(2)}) async-start(), calls=%async_computation.5 | async-start | bytes 1769472 | tf_op jit(solution)/shard_map/reduce_scatter | solution.py:336
  112.6 70.0 %reduce-scatter.3.cloned.1.call-start = ((), (), s32[]{:S(2)}) async-start(), calls=%async_computation.3 | async-start | bytes 1179648 | tf_op jit(solution)/shard_map/reduce_scatter | solution.py:336
  150.9 31.7 %collective-permute-start.10 = (bf16[20,4096]{1,0:T(8,128)(2,1)}, bf16[20,4096]{1,0:T(8,128)(2,1)S(1)}, u32[]{:S(2)}, u32[]{:S(2)}) collective-permute-start(bf16[20,4096]{1,0:T(8,128)(2,1)} %bitcast.10), channel_id=1, source_target_pairs={{0,8},{1,9},{2,10},{3,11},{4,12},{5,13},{6,14},{7,15},{8,0},{9,1},... | collective-permute-start | bytes 491528 | tf_op jit(solution)/shard_map/ppermute | solution.py:345
  182.6 0.7 copy-start.6
Sparse Core Ops, SparseCore 0:
  75.9 22.3 all-gather.4
  99.9 19.1 all-gather.2
  121.4 29.4 reduce-scatter.4
  153.0 29.4 reduce-scatter.2

commit v3 on v2

v3 whole, which is shorter than its diff:
```python
import functools

import jax
import jax.numpy as jnp
from jax import lax
from jax.experimental import pallas as pl
from jax.experimental.pallas import tpu as pltpu
from jax.sharding import PartitionSpec as P

HEAD_DIM = 128
E_WIN = 2
WIN_DEV = 3
CAP = 20
SPARE = 16
HEADS_STEP = 8
MASKED = -1e30
MIB = 1024 * 1024


def bundle_kernel(keys, segs, out, row, sems):
    rows = keys.shape[0]
    spare = out.shape[0] - rows
    body = pltpu.make_async_copy(keys, out.at[pl.ds(0, rows)], sems.at[0])
    body.start()
    row[...] = jnp.zeros_like(row)
    row[:, : segs.shape[1]] = jnp.broadcast_to(
        segs[...].astype(jnp.float32), (spare, segs.shape[1])
    ).astype(jnp.bfloat16)
    tail = pltpu.make_async_copy(row, out.at[pl.ds(rows, spare)], sems.at[1])
    tail.start()
    body.wait()
    tail.wait()


def bundle(keys, segs):
    rows, width = keys.shape
    anywhere = pl.BlockSpec(memory_space=pl.ANY)
    return pl.pallas_call(
        bundle_kernel,
        in_specs=[anywhere, pl.BlockSpec(memory_space=pltpu.VMEM)],
        out_specs=anywhere,
        out_shape=jax.ShapeDtypeStruct((rows + SPARE, width), keys.dtype),
        scratch_shapes=[
            pltpu.VMEM((SPARE, width), keys.dtype),
            pltpu.SemaphoreType.DMA((2,)),
        ],
        cost_estimate=pl.CostEstimate(
            flops=0, bytes_accessed=4 * rows * width, transcendentals=0
        ),
        name="bundle",
    )(keys, segs)


def attention_kernel(
    deltas, q, k0, v0, k1, v1, k2, v2, k3, v3, seg0, seg1, seg2, seg3, resid, gain, routes, gates,
    mixed_out, keep_out, send_out, weight_out, bias,
):
    step = pl.program_id(0)
    steps = pl.num_programs(0)
    rows = q.shape[0]
    keys = (WIN_DEV + 1) * rows

    @pl.when(step == 0)
    def _():
        seg_own = seg0[...].astype(jnp.float32)
        seg_row = jnp.concatenate(
            [seg_own] + [seg[0:1, :rows].astype(jnp.float32) for seg in (seg1, seg2, seg3)],
            axis=1,
        )
        eye = lax.broadcasted_iota(jnp.int32, (rows, rows), 0) == lax.broadcasted_iota(
            jnp.int32, (rows, rows), 1
        )
        seg_col = jnp.sum(jnp.where(eye, seg_own, 0.0), axis=1, keepdims=True)
        lane = lax.broadcasted_iota(jnp.int32, (rows, keys), 1)
        sub = lax.broadcasted_iota(jnp.int32, (rows, keys), 0)
        block = lane // rows
        back = jnp.where(
            block == 0,
            deltas[0],
            jnp.where(block == 1, deltas[1], jnp.where(block == 2, deltas[2], deltas[3])),
        )
        distance = sub - (lane - block * rows) + back * rows
        allowed = (distance >= 0) & (distance <= WIN_DEV * rows) & (seg_col == seg_row)
        bias[...] = jnp.where(allowed, 0.0, MASKED)

    scale = 1.0 / HEAD_DIM**0.5
    heads = [slice(head * HEAD_DIM, (head + 1) * HEAD_DIM) for head in range(HEADS_STEP)]
    scores = jnp.stack(
        [
            lax.dot_general(
                q[:, cols],
                jnp.concatenate([k0[:, cols], k1[:, cols], k2[:, cols], k3[:, cols]], axis=0),
                (((1,), (1,)), ((), ())),
                preferred_element_type=jnp.float32,
            )
            for cols in heads
        ]
    )
    scores = scores * scale + bias[...][None]
    expo = jnp.exp(scores - jnp.max(scores, axis=2, keepdims=True))
    denom = jnp.sum(expo, axis=2, keepdims=True)
    probs = expo.astype(jnp.bfloat16)
    outs = [
        jnp.dot(
            probs[head],
            jnp.concatenate([v0[:, cols], v1[:, cols], v2[:, cols], v3[:, cols]], axis=0),
            preferred_element_type=jnp.float32,
        )
        / denom[head]
        for head, cols in enumerate(heads)
    ]
    width = HEADS_STEP * HEAD_DIM
    at = pl.ds(pl.multiple_of(step * width, width), width)
    mixed_out[:, at] = resid[...].astype(jnp.float32) + jnp.concatenate(outs, axis=1)

    @pl.when(step == steps - 1)
    def _():
        mixed = mixed_out[...]
        normed = (
            mixed * lax.rsqrt(jnp.mean(mixed * mixed, axis=1, keepdims=True) + 1e-05) * gain[...]
        ).astype(jnp.bfloat16)
        across = lax.broadcasted_iota(jnp.int32, (rows, rows), 1)
        down = lax.broadcasted_iota(jnp.int32, (rows, rows), 0)
        upper = jnp.where(down < across, 1.0, 0.0).astype(jnp.bfloat16)
        eye = jnp.where(down == across, 1.0, 0.0).astype(jnp.bfloat16)
        slot = lax.broadcasted_iota(jnp.int32, (32, rows), 0)
        for place, out in ((0, keep_out), (1, send_out)):
            expert = deltas[4] if place == 0 else 1 - deltas[4]
            hit = routes[...] == expert
            member = jnp.max(jnp.where(hit, 1.0, 0.0), axis=0, keepdims=True)
            weight = jnp.sum(
                jnp.where(hit, gates[...].astype(jnp.float32), 0.0), axis=0, keepdims=True
            )
            rank = jnp.dot(
                jnp.broadcast_to(member, (8, rows)).astype(jnp.bfloat16),
                upper,
                preferred_element_type=jnp.float32,
            )[0:1].astype(jnp.int32)
            pick = (slot == rank) & (member > 0.5)
            out[...] = jnp.dot(
                jnp.where(pick, 1.0, 0.0).astype(jnp.bfloat16),
                normed,
                preferred_element_type=jnp.float32,
            )[:CAP].astype(jnp.bfloat16)
            weight_out[place] = lax.dot_general(
                eye,
                jnp.where(pick, weight, 0.0).astype(jnp.bfloat16),
                (((1,), (1,)), ((), ())),
                preferred_element_type=jnp.float32,
            ).astype(jnp.bfloat16)


def attention(deltas, q, pairs, seg_own, resid, gain, routes, gates):
    rows, width = q.shape
    cols = HEADS_STEP * HEAD_DIM
    top = routes.shape[0]
    piece = pl.BlockSpec((rows, cols), lambda j, *_: (0, j))
    tail = pl.BlockSpec((SPARE, HEAD_DIM), lambda j, *_: (rows // SPARE, 0))

    def whole(shape):
        return pl.BlockSpec(shape, lambda j, *_: (0,) * len(shape))

    bundles = pairs[2::2]
    return pl.pallas_call(
        attention_kernel,
        grid_spec=pltpu.PrefetchScalarGridSpec(
            num_scalar_prefetch=1,
            grid=(width // cols,),
            in_specs=[piece] * (1 + len(pairs))
            + [whole((1, rows))]
            + [tail] * len(bundles)
            + [
                piece,
                whole((1, width)),
                whole((top, rows)),
                whole((top, rows)),
            ],
            out_specs=[
                whole((rows, width)),
                whole((CAP, width)),
                whole((CAP, width)),
                whole((E_WIN, rows, 32)),
            ],
            scratch_shapes=[pltpu.VMEM((rows, (WIN_DEV + 1) * rows), jnp.float32)],
        ),
        out_shape=[
            jax.ShapeDtypeStruct((rows, width), jnp.float32),
            jax.ShapeDtypeStruct((CAP, width), jnp.bfloat16),
            jax.ShapeDtypeStruct((CAP, width), jnp.bfloat16),
            jax.ShapeDtypeStruct((E_WIN, rows, 32), jnp.bfloat16),
        ],
        compiler_params=pltpu.CompilerParams(vmem_limit_bytes=20 * MIB),
        cost_estimate=pl.CostEstimate(
            flops=4 * rows * 4 * rows * width, bytes_accessed=8 * rows * width * 4,
            transcendentals=rows * 4 * rows * (width // HEAD_DIM),
        ),
        name="attention",
    )(deltas, q, *pairs, seg_own, *bundles, resid, gain, routes, gates)


def fetch_kernel(parts, source, held, sems):
    depth = source.shape[0] // parts
    copies = []
    for part in range(parts):
        at = pl.ds(part * depth, depth)
        copies.append(pltpu.make_async_copy(source.at[at], held.at[at], sems.at[part]))
    for copy in copies:
        copy.start()
    for copy in copies:
        copy.wait()


def fetch(weights):
    parts = 4
    return pl.pallas_call(
        functools.partial(fetch_kernel, parts),
        in_specs=[pl.BlockSpec(memory_space=pl.ANY)],
        out_specs=pl.BlockSpec(memory_space=pltpu.VMEM),
        out_shape=pltpu.VMEM(weights.shape, weights.dtype),
        scratch_shapes=[pltpu.SemaphoreType.DMA((parts,))],
        compiler_params=pltpu.CompilerParams(vmem_limit_bytes=2 * MIB),
        cost_estimate=pl.CostEstimate(
            flops=0, bytes_accessed=4 * weights.size, transcendentals=0
        ),
        name="fetch",
    )(weights)


def experts_kernel(x, w_gate, w_up, w_down, out, hidden):
    width, units = w_gate.shape
    tile = min(256, units)

    @pl.loop(0, units // tile)
    def _(part):
        at = pl.ds(pl.multiple_of(part * tile, tile), tile)
        gate = jnp.dot(x[...], w_gate[:, at], preferred_element_type=jnp.float32)
        up = jnp.dot(x[...], w_up[:, at], preferred_element_type=jnp.float32)
        hidden[:, at] = (jax.nn.silu(gate) * up).astype(jnp.bfloat16)

    @pl.loop(0, width // 512)
    def _(part):
        at = pl.ds(pl.multiple_of(part * 512, 512), 512)
        out[:, at] = jnp.dot(
            hidden[...], w_down[:, at], preferred_element_type=jnp.float32
        ).astype(jnp.bfloat16)


def experts(x, w_gate, w_up, w_down):
    rows, width = x.shape
    units = w_gate.shape[1]
    near = pl.BlockSpec(memory_space=pltpu.VMEM)
    held = [
        pltpu.with_memory_space_constraint(w, pltpu.VMEM) for w in (w_gate, w_up, w_down)
    ]
    return pl.pallas_call(
        experts_kernel,
        in_specs=[near] * 4,
        out_specs=near,
        out_shape=jax.ShapeDtypeStruct((rows, width), jnp.bfloat16),
        scratch_shapes=[pltpu.VMEM((rows, units), jnp.bfloat16)],
        compiler_params=pltpu.CompilerParams(vmem_limit_bytes=20 * MIB),
        cost_estimate=pl.CostEstimate(
            flops=6 * rows * width * units,
            bytes_accessed=4 * rows * width,
            transcendentals=rows * units,
        ),
        name="experts",
    )(x, *held)


def join_kernel(first, second, out):
    out[...] = jnp.concatenate(
        [first[...].astype(jnp.float32), second[...].astype(jnp.float32)], axis=0
    ).astype(out.dtype)


def join(first, second):
    width = first.shape[1]
    near = pl.BlockSpec(memory_space=pltpu.VMEM)
    return pl.pallas_call(
        join_kernel,
        in_specs=[near, near],
        out_specs=near,
        out_shape=jax.ShapeDtypeStruct((first.shape[0] + second.shape[0], width), first.dtype),
        name="join",
    )(first, second)


def pile_kernel(*refs):
    blocks, out, sems = refs[:-2], refs[-2], refs[-1]
    rows = blocks[0].shape[0]
    copies = [
        pltpu.make_async_copy(block, out.at[pl.ds(at * rows, rows)], sems.at[at])
        for at, block in enumerate(blocks)
    ]
    for copy in copies:
        copy.start()
    for copy in copies:
        copy.wait()


def pile(blocks):
    rows, width = blocks[0].shape
    anywhere = pl.BlockSpec(memory_space=pl.ANY)
    return pl.pallas_call(
        pile_kernel,
        in_specs=[anywhere] * len(blocks),
        out_specs=anywhere,
        out_shape=jax.ShapeDtypeStruct((len(blocks) * rows, width), blocks[0].dtype),
        scratch_shapes=[pltpu.SemaphoreType.DMA((len(blocks),))],
        name="pile",
    )(*blocks)


def add_kernel(first, second, *outs):
    rows = outs[0].shape[0]
    for at, out in enumerate(outs):
        part = pl.ds(at * rows, rows)
        out[...] = (
            first[part].astype(jnp.float32) + second[part].astype(jnp.float32)
        ).astype(out.dtype)


def add_split(first, second, blocks):
    rows, width = first.shape
    each = rows // blocks
    cols = 1024
    piece = pl.BlockSpec((rows, cols), lambda j: (0, j))
    small = pl.BlockSpec((each, cols), lambda j: (0, j))
    return pl.pallas_call(
        add_kernel,
        grid=(width // cols,),
        in_specs=[piece, piece],
        out_specs=[small] * blocks,
        out_shape=[jax.ShapeDtypeStruct((each, width), first.dtype)] * blocks,
        name="add_split",
    )(first, second)


def total_kernel(*refs):
    blocks, own_out, back_out = refs[:-2], refs[-2], refs[-1]
    total = blocks[0][...].astype(jnp.float32)
    for block in blocks[1:]:
        total = total + block[...].astype(jnp.float32)
    own_out[...] = total[:CAP].astype(own_out.dtype)
    back_out[...] = total[CAP:].astype(back_out.dtype)


def total_of(blocks):
    width = blocks[0].shape[1]
    cols = 2048
    return pl.pallas_call(
        total_kernel,
        grid=(width // cols,),
        in_specs=[pl.BlockSpec((2 * CAP, cols), lambda j: (0, j))] * len(blocks),
        out_specs=[pl.BlockSpec((CAP, cols), lambda j: (0, j))] * 2,
        out_shape=[jax.ShapeDtypeStruct((CAP, width), blocks[0].dtype)] * 2,
        name="total",
    )(*blocks)


def combine_kernel(mixed, weight, own, other, out):
    total = mixed[...]
    for place, part in enumerate((own, other)):
        total = total + jnp.dot(
            weight[place][:, : part.shape[0]], part[...], preferred_element_type=jnp.float32
        )
    out[...] = total.astype(jnp.bfloat16)


def combine(mixed, weight, own, other):
    rows, width = mixed.shape
    cols = 2048

    def piece(count):
        return pl.BlockSpec((count, cols), lambda j: (0, j))

    return pl.pallas_call(
        combine_kernel,
        grid=(width // cols,),
        in_specs=[
            piece(rows),
            pl.BlockSpec(weight.shape, lambda j: (0, 0, 0)),
            piece(own.shape[0]),
            piece(other.shape[0]),
        ],
        out_specs=piece(rows),
        out_shape=jax.ShapeDtypeStruct((rows, width), jnp.bfloat16),
        name="combine",
    )(mixed, weight, own, other)


def shards(
    resid, queries, keys, values, segment_ids, norm_gain, routes, route_gates, w_gate, w_up, w_down
):
    count = lax.axis_size("expert")
    own = lax.axis_index("expert")
    shard_count = count // E_WIN
    odd = own % 2

    next_chip = [(i, i + 2) for i in range(count - 2)]
    crossing = [(i, i + 1) for i in range(0, count, 2)]
    crossing += [(i, i + 3) for i in range(1, count - 3, 2)]

    def swapped(block, mask):
        return lax.ppermute(block, "expert", [(i, i ^ mask) for i in range(count)])

    seg_own = segment_ids.reshape(1, -1)
    value_two = lax.ppermute(values, "expert", next_chip)
    key_block = bundle(keys, seg_own)
    key_two = lax.ppermute(key_block, "expert", next_chip)
    value_cross = lax.ppermute(values, "expert", crossing)
    key_cross = lax.ppermute(key_block, "expert", crossing)
    value_mirror = swapped(value_two, 1)
    key_mirror = swapped(key_two, 1)
    held = [fetch(w) for w in (w_gate, w_up, w_down)]

    far = 2 * WIN_DEV + 2
    delta_list = [0 * own, 0 * own + 2, 3 - 2 * odd, 1 + 2 * odd]
    my_expert = own // shard_count
    scalars = jnp.stack(
        [jnp.where(own >= delta, delta, far) for delta in delta_list] + [my_expert]
    ).astype(jnp.int32)

    mixed, keep, send, weight = attention(
        scalars,
        queries,
        [keys, values, key_two, value_two, key_cross, value_cross, key_mirror, value_mirror],
        seg_own, resid, norm_gain.reshape(1, -1), routes.T, route_gates.T,
    )
    partner = [(i, (i + shard_count) % count) for i in range(count)]
    masks = range(2, shard_count, 2)
    pair = join(keep, lax.ppermute(send, "expert", partner))
    local = pile([pair] + [swapped(pair, mask) for mask in masks])
    remote = swapped(local, 1)
    local_part = experts(local, *held)
    remote_part = experts(remote, *held)
    blocks = add_split(local_part, swapped(remote_part, 1), 1 + len(masks))
    own_sum, back = total_of(
        [blocks[0]] + [swapped(block, mask) for block, mask in zip(blocks[1:], masks)]
    )
    return combine(mixed, weight, own_sum, lax.ppermute(back, "expert", partner))


def solution(mesh):
    placed = (
        P(("groups", "expert"), None),
        P(("groups", "expert"), None),
        P(("groups", "expert"), None),
        P(("groups", "expert"), None),
        P(("groups", "expert")),
        P(),
        P(("groups", "expert"), None),
        P(("groups", "expert"), None),
        P(None, "expert"),
        P(None, "expert"),
        P("expert", None),
    )
    return jax.shard_map(
        shards, mesh=mesh, in_specs=placed, out_specs=P(("groups", "expert"), None), check_vma=False
    )
```

time: 193 us -> 213 us (1.10)
  Pallas kernels: 37.2 us -> 87.2 us
  waiting for transfers between devices: 102 us -> 68.8 us
  local copies, waits for them, and re-layouts: 2.58 us -> 23.1 us
  between operations: 13.3 us -> 0.19 us
  other arithmetic: 2.74 us -> 0.01 us
    pallas_call x2 -> x10, Pallas kernels: 27.5 us -> 80.7 us  [the longest x1 40.8 us: pile(): pl.pallas_call(pile_kernel, in_specs=[anywhere] * len(blocks), out_specs=...]
    reduce_scatter x2 -> x0, waiting for transfers between devices: 47.4 us -> none  [scattered(): lax.psum_scatter(block, 'expert', scatter_dimension=0, tiled=True, axis_i...]
    ppermute x9 -> x14, waiting for transfers between devices: 15.9 us -> 61.2 us  [the longest x10 30.1 us: swapped(): return lax.ppermute(block, 'expert', [(i, i ^ mask) for i in range(count)])]
    all_gather x2 -> x0, waiting for transfers between devices: 28.2 us -> none  [gathered(): lax.all_gather(block, 'expert', axis=0, tiled=True, axis_index_groups=hal...]
    unnamed x14 -> x52, local copies, waits for them, and re-layouts: 1.95 us -> 23.1 us
    pallas_call x1, Pallas kernels: 7.02 us -> 4.11 us  [attention(): pl.pallas_call(attention_kernel, grid_spec=pltpu.PrefetchScalarGridSpec(n...]
    concatenate x2 -> x0, other arithmetic: 2.74 us -> none  [the longest x1 1.47 us: shards(): late_rows = gathered(jnp.concatenate([got, rest], axis=0))]
    ppermute x1, waiting for transfers between devices: 10.1 us -> 7.64 us  [shards(): value_two = lax.ppermute(values, 'expert', next_chip)]
  transfers between devices with their start and end apart: 15 -> 16, of which waited for: 10 -> 10; matrix products, arithmetic and copies ran while one was open for 1% -> 0% of each run, Pallas kernels for 14% -> 4%
where the time goes in v3:
time: 213 us; the launch traced here: 212 us
  Pallas kernels  87.2 us (41%)
  waiting for transfers between devices  68.8 us (32%)
  starting transfers between devices  32.7 us (15%)
  local copies, waits for them, and re-layouts  23.1 us (11%)
    pallas_call x1, Pallas kernels, pile(): pl.pallas_call(pile_kernel, in_specs=[anywhere] * len(blocks), out_specs=...  40.8 us
    ppermute x10, waiting for transfers between devices, swapped(): return lax.ppermute(block, 'expert', [(i, i ^ mask) for i in range(count)])  30.1 us
    unnamed x52, local copies, waits for them, and re-layouts  23.1 us
    pallas_call x1, Pallas kernels, bundle(): pl.pallas_call(bundle_kernel, in_specs=[anywhere, pl.BlockSpec(memory_spa...  17.7 us
    ppermute x10, starting transfers between devices, swapped(): return lax.ppermute(block, 'expert', [(i, i ^ mask) for i in range(count)])  15.1 us
    pallas_call x2, Pallas kernels, experts(): pl.pallas_call(experts_kernel, in_specs=[near] * 4, out_specs=near, out_s...  12.7 us
    ppermute x1, waiting for transfers between devices, shards(): lax.ppermute(back, 'expert', partner)  11 us
    ppermute x1, waiting for transfers between devices, shards(): key_two = lax.ppermute(key_block, 'expert', next_chip)  10.6 us
  transfers between devices with their start and end apart: 16, of which 10 were waited for; matrix products, arithmetic and copies ran while one was open for 0% of the time, Pallas kernels for 4%

profile of v3, /device:TPU:0, one launch (start us, length us, event | category | flops | bytes accessed | tf_op | source)
XLA Modules:
  0.0 211.9 jit_solution(365772321474583206)
XLA Ops:
  0.0 17.7 %bundle.1 = bf16[80,4096]{1,0:T(8,128)(2,1)} custom-call(bf16[64,4096]{1,0:T(8,128)(2,1)} %k0.1, s32[1,64]{1,0:T(1,128)} %bitcast.12), custom_call_target="tpu_custom_call" | custom-call | bytes 1048576 | tf_op jit(solution)/shard_map/bundle/pallas_call | solution.py:38
  17.7 4.9 %collective-permute-start = (bf16[80,4096]{1,0:T(8,128)(2,1)}, bf16[80,4096]{1,0:T(8,128)(2,1)S(1)}, u32[]{:S(2)}, u32[]{:S(2)}) collective-permute-start(bf16[80,4096]{1,0:T(8,128)(2,1)} %bundle.1), channel_id=1, source_target_pairs={{0,2},{1,3},{2,4},{3,5},{4,6},{5,7},{6,8},{7,9},{8,10},{9,11},{10,... | collective-permute-start | bytes 1966088 | tf_op jit(solution)/shard_map/ppermute | solution.py:411
  22.6 3.4 %collective-permute-start.1 = (bf16[64,4096]{1,0:T(8,128)(2,1)}, bf16[64,4096]{1,0:T(8,128)(2,1)S(1)}, u32[]{:S(2)}, u32[]{:S(2)}) collective-permute-start(bf16[64,4096]{1,0:T(8,128)(2,1)} %v0.1), channel_id=1, source_target_pairs={{0,2},{1,3},{2,4},{3,5},{4,6},{5,7},{6,8},{7,9},{8,10},{9,11},{10,... | collective-permute-start | bytes 1572872 | tf_op jit(solution)/shard_map/ppermute | solution.py:409
  27.4 10.6 %collective-permute-done.k1.seg1 = bf16[80,4096]{1,0:T(8,128)(2,1)S(1)} collective-permute-done((bf16[80,4096]{1,0:T(8,128)(2,1)}, bf16[80,4096]{1,0:T(8,128)(2,1)S(1)}, u32[]{:S(2)}, u32[]{:S(2)}) %collective-permute-start) | collective-permute-done | bytes 655392 | tf_op jit(solution)/shard_map/ppermute | solution.py:411
  38.0 2.4 %collective-permute-start.3 = (bf16[64,4096]{1,0:T(8,128)(2,1)}, bf16[64,4096]{1,0:T(8,128)(2,1)S(1)}, u32[]{:S(2)}, u32[]{:S(2)}) collective-permute-start(bf16[64,4096]{1,0:T(8,128)(2,1)} %v0.1), channel_id=1, source_target_pairs={{0,1},{2,3},{4,5},{6,7},{8,9},{10,11},{12,13},{14,15},{1,4},{3,6},... | collective-permute-start | bytes 1572872 | tf_op jit(solution)/shard_map/ppermute | solution.py:412
  40.4 7.6 %collective-permute-done.1.v1 = bf16[64,4096]{1,0:T(8,128)(2,1)S(1)} collective-permute-done((bf16[64,4096]{1,0:T(8,128)(2,1)}, bf16[64,4096]{1,0:T(8,128)(2,1)S(1)}, u32[]{:S(2)}, u32[]{:S(2)}) %collective-permute-start.1) | collective-permute-done | bytes 524320 | tf_op jit(solution)/shard_map/ppermute | solution.py:409
  56.9 4.1 %attention.1 = (f32[64,4096]{1,0:T(8,128)S(1)}, bf16[20,4096]{1,0:T(8,128)(2,1)S(1)}, bf16[20,4096]{1,0:T(8,128)(2,1)S(1)}, bf16[2,64,32]{2,1,0:T(8,128)(2,1)S(1)}) custom-call(s32[5]{0:T(128)S(1)} %stack.23.deltas, bf16[64,4096]{1,0:T(8,128)(2,1)S(1)} %copy-done.6, bf16[64,4096]{1,0:T(8,128)(2,1)S(1)} %copy-done.4, bf16[64,4096]{1,0:T(8,128)(2,1)S(1)} %copy-done.7, ...), custom_call_target="tpu_custom_call" | custom-call | flops 268435456 | bytes 8388608 | tf_op jit(solution)/shard_map/attention/pallas_call | solution.py:164
  63.2 5.5 %collective-permute-start.6 = (bf16[20,4096]{1,0:T(8,128)(2,1)S(1)}, bf16[20,4096]{1,0:T(8,128)(2,1)S(1)}, u32[]{:S(2)}, u32[]{:S(2)}) collective-permute-start(bf16[20,4096]{1,0:T(8,128)(2,1)S(1)} %get-tuple-element.18), channel_id=1, source_target_pairs={{0,8},{1,9},{2,10},{3,11},{4,12},{5,13},{6,14},{7,15},{8,0},{9,1},... | collective-permute-start | bytes 491528 | tf_op jit(solution)/shard_map/ppermute | solution.py:433
  68.7 9.4 %collective-permute-done.6.second = bf16[20,4096]{1,0:T(8,128)(2,1)S(1)} collective-permute-done((bf16[20,4096]{1,0:T(8,128)(2,1)S(1)}, bf16[20,4096]{1,0:T(8,128)(2,1)S(1)}, u32[]{:S(2)}, u32[]{:S(2)}) %collective-permute-start.6) | collective-permute-done | bytes 163872 | tf_op jit(solution)/shard_map/ppermute | solution.py:433
  80.6 7.4 %collective-permute-start.9 = (bf16[40,4096]{1,0:T(8,128)(2,1)}, bf16[40,4096]{1,0:T(8,128)(2,1)S(1)}, u32[]{:S(2)}, u32[]{:S(2)}) collective-permute-start(bf16[40,4096]{1,0:T(8,128)(2,1)} %join.1.refs_0_), channel_id=1, source_target_pairs={{0,6},{1,7},{2,4},{3,5},{4,2},{5,3},{6,0},{7,1},{8,14},{9,15},{10,... | collective-permute-start | bytes 983048 | tf_op jit(solution)/shard_map/ppermute | solution.py:406
  88.0 3.5 %collective-permute-start.8 = (bf16[40,4096]{1,0:T(8,128)(2,1)}, bf16[40,4096]{1,0:T(8,128)(2,1)S(1)}, u32[]{:S(2)}, u32[]{:S(2)}) collective-permute-start(bf16[40,4096]{1,0:T(8,128)(2,1)} %join.1.refs_0_), channel_id=1, source_target_pairs={{0,4},{1,5},{2,6},{3,7},{4,0},{5,1},{6,2},{7,3},{8,12},{9,13},{10,... | collective-permute-start | bytes 983048 | tf_op jit(solution)/shard_map/ppermute | solution.py:406
  91.6 5.1 %collective-permute-done.9.refs_3_ = bf16[40,4096]{1,0:T(8,128)(2,1)S(1)} collective-permute-done((bf16[40,4096]{1,0:T(8,128)(2,1)}, bf16[40,4096]{1,0:T(8,128)(2,1)S(1)}, u32[]{:S(2)}, u32[]{:S(2)}) %collective-permute-start.9) | collective-permute-done | bytes 327712 | tf_op jit(solution)/shard_map/ppermute | solution.py:406
  96.7 8.6 %collective-permute-done.8.refs_2_ = bf16[40,4096]{1,0:T(8,128)(2,1)S(1)} collective-permute-done((bf16[40,4096]{1,0:T(8,128)(2,1)}, bf16[40,4096]{1,0:T(8,128)(2,1)S(1)}, u32[]{:S(2)}, u32[]{:S(2)}) %collective-permute-start.8) | collective-permute-done | bytes 327712 | tf_op jit(solution)/shard_map/ppermute | solution.py:406
  106.8 40.8 %pile.1.x = bf16[160,4096]{1,0:T(8,128)(2,1)} custom-call(bf16[40,4096]{1,0:T(8,128)(2,1)} %join.1.refs_0_, bf16[40,4096]{1,0:T(8,128)(2,1)} %copy-done.21, bf16[40,4096]{1,0:T(8,128)(2,1)} %copy-done.20, bf16[40,4096]{1,0:T(8,128)(2,1)} %copy-done.18), custom_call_target="tpu_custom_call" | custom-call | tf_op jit(solution)/shard_map/pile/pallas_call | solution.py:305
  147.8 3.4 %copy-done = bf16[4096,1024]{1,0:T(8,128)(2,1)S(1)} copy-done((bf16[4096,1024]{1,0:T(8,128)(2,1)S(1)}, bf16[4096,1024]{1,0:T(8,128)(2,1)}, u32[]{:S(2)}) %copy-start) | copy-done | bytes 8388632
  151.7 2.8 %copy-done.1 = bf16[4096,1024]{1,0:T(8,128)(2,1)S(1)} copy-done((bf16[4096,1024]{1,0:T(8,128)(2,1)S(1)}, bf16[4096,1024]{1,0:T(8,128)(2,1)}, u32[]{:S(2)}) %copy-start.1) | copy-done | bytes 8388632
  157.8 6.4 %experts.3 = bf16[160,4096]{1,0:T(8,128)(2,1)S(1)} custom-call(bf16[160,4096]{1,0:T(8,128)(2,1)S(1)} %collective-permute-done.10.x, bf16[4096,1024]{1,0:T(8,128)(2,1)S(1)} %fetch.3.w_gate, bf16[4096,1024]{1,0:T(8,128)(2,1)S(1)} %fetch.4.w_up, bf16[1024,4096]{1,0:T(8,128)(2,1)S(1)} %fetch.5.w_down), custom_call_target="tpu_custom_call" | custom-call | flops 4026531840 | bytes 2621440 | tf_op jit(solution)/shard_map/experts/pallas_call | solution.py:255
  164.7 6.4 %experts.2.first = bf16[160,4096]{1,0:T(8,128)(2,1)S(1)} custom-call(bf16[160,4096]{1,0:T(8,128)(2,1)S(1)} %copy-done.2, bf16[4096,1024]{1,0:T(8,128)(2,1)S(1)} %fetch.3.w_gate, bf16[4096,1024]{1,0:T(8,128)(2,1)S(1)} %fetch.4.w_up, bf16[1024,4096]{1,0:T(8,128)(2,1)S(1)} %fetch.5.w_down), custom_call_target="tpu_custom_call" | custom-call | flops 4026531840 | bytes 2621440 | tf_op jit(solution)/shard_map/experts/pallas_call | solution.py:255
  173.3 3.7 %add_split.1 = (bf16[40,4096]{1,0:T(8,128)(2,1)}, bf16[40,4096]{1,0:T(8,128)(2,1)}, bf16[40,4096]{1,0:T(8,128)(2,1)}, bf16[40,4096]{1,0:T(8,128)(2,1)}) custom-call(bf16[160,4096]{1,0:T(8,128)(2,1)} %copy-done.3, bf16[160,4096]{1,0:T(8,128)(2,1)} %copy-done.15), custom_call_target="tpu_custom_call" | custom-call | tf_op jit(solution)/shard_map/add_split/pallas_call | solution.py:330
  177.8 2.6 %collective-permute-start.14 = (bf16[40,4096]{1,0:T(8,128)(2,1)}, bf16[40,4096]{1,0:T(8,128)(2,1)S(1)}, u32[]{:S(2)}, u32[]{:S(2)}) collective-permute-start(bf16[40,4096]{1,0:T(8,128)(2,1)} %get-tuple-element.22), channel_id=1, source_target_pairs={{0,6},{1,7},{2,4},{3,5},{4,2},{5,3},{6,0},{7,1},{8,14},{9,15},{10,... | collective-permute-start | bytes 983048 | tf_op jit(solution)/shard_map/ppermute | solution.py:406
  180.5 6.4 %collective-permute-done.12.refs_1_ = bf16[40,4096]{1,0:T(8,128)(2,1)S(1)} collective-permute-done((bf16[40,4096]{1,0:T(8,128)(2,1)}, bf16[40,4096]{1,0:T(8,128)(2,1)S(1)}, u32[]{:S(2)}, u32[]{:S(2)}) %collective-permute-start.12) | collective-permute-done | bytes 327712 | tf_op jit(solution)/shard_map/ppermute | solution.py:406
  188.5 6.5 %collective-permute-done.14.refs_3_ = bf16[40,4096]{1,0:T(8,128)(2,1)S(1)} collective-permute-done((bf16[40,4096]{1,0:T(8,128)(2,1)}, bf16[40,4096]{1,0:T(8,128)(2,1)S(1)}, u32[]{:S(2)}, u32[]{:S(2)}) %collective-permute-start.14) | collective-permute-done | bytes 327712 | tf_op jit(solution)/shard_map/ppermute | solution.py:406
  197.9 11.0 %collective-permute-done.15.other = bf16[20,4096]{1,0:T(8,128)(2,1)S(1)} collective-permute-done((bf16[20,4096]{1,0:T(8,128)(2,1)}, bf16[20,4096]{1,0:T(8,128)(2,1)S(1)}, u32[]{:S(2)}, u32[]{:S(2)}) %collective-permute-start.15) | collective-permute-done | bytes 163872 | tf_op jit(solution)/shard_map/ppermute | solution.py:442
  209.6 2.4 %combine.1 = bf16[64,4096]{1,0:T(8,128)(2,1)} custom-call(f32[64,4096]{1,0:T(8,128)} %copy-done.5, bf16[2,64,32]{2,1,0:T(8,128)(2,1)} %copy-done.10, bf16[20,4096]{1,0:T(8,128)(2,1)} %get-tuple-element.23.own, bf16[20,4096]{1,0:T(8,128)(2,1)} %copy-done.23), custom_call_target="tpu_custom_call" | custom-call | tf_op jit(solution)/shard_map/combine/pallas_call | solution.py:378
  (74 shorter events, 29.0 us)
Async XLA Ops:
  17.7 20.3 %collective-permute-start = (bf16[80,4096]{1,0:T(8,128)(2,1)}, bf16[80,4096]{1,0:T(8,128)(2,1)S(1)}, u32[]{:S(2)}, u32[]{:S(2)}) collective-permute-start(bf16[80,4096]{1,0:T(8,128)(2,1)} %bundle.1), channel_id=1, source_target_pairs={{0,2},{1,3},{2,4},{3,5},{4,6},{5,7},{6,8},{7,9},{8,10},{9,11},{10,... | collective-permute-start | bytes 1966088 | tf_op jit(solution)/shard_map/ppermute | solution.py:411
  22.6 25.5 %collective-permute-start.1 = (bf16[64,4096]{1,0:T(8,128)(2,1)}, bf16[64,4096]{1,0:T(8,128)(2,1)S(1)}, u32[]{:S(2)}, u32[]{:S(2)}) collective-permute-start(bf16[64,4096]{1,0:T(8,128)(2,1)} %v0.1), channel_id=1, source_target_pairs={{0,2},{1,3},{2,4},{3,5},{4,6},{5,7},{6,8},{7,9},{8,10},{9,11},{10,... | collective-permute-start | bytes 1572872 | tf_op jit(solution)/shard_map/ppermute | solution.py:409
  26.0 22.1 %collective-permute-start.2 = (bf16[80,4096]{1,0:T(8,128)(2,1)}, bf16[80,4096]{1,0:T(8,128)(2,1)S(1)}, u32[]{:S(2)}, u32[]{:S(2)}) collective-permute-start(bf16[80,4096]{1,0:T(8,128)(2,1)} %bundle.1), channel_id=1, source_target_pairs={{0,1},{2,3},{4,5},{6,7},{8,9},{10,11},{12,13},{14,15},{1,4},{3,6},... | collective-permute-start | bytes 1966088 | tf_op jit(solution)/shard_map/ppermute | solution.py:413
  38.0 12.0 %collective-permute-start.4 = (bf16[80,4096]{1,0:T(8,128)(2,1)S(1)}, bf16[80,4096]{1,0:T(8,128)(2,1)S(1)}, u32[]{:S(2)}, u32[]{:S(2)}) collective-permute-start(bf16[80,4096]{1,0:T(8,128)(2,1)S(1)} %collective-permute-done.k1.seg1), channel_id=1, source_target_pairs={{0,1},{1,0},{2,3},{3,2},{4,5},{5,4},{6,7},{7,6},{8,9},{9,8},{10,11... | collective-permute-start | bytes 1966088 | tf_op jit(solution)/shard_map/ppermute | solution.py:406
  38.0 10.2 %collective-permute-start.3 = (bf16[64,4096]{1,0:T(8,128)(2,1)}, bf16[64,4096]{1,0:T(8,128)(2,1)S(1)}, u32[]{:S(2)}, u32[]{:S(2)}) collective-permute-start(bf16[64,4096]{1,0:T(8,128)(2,1)} %v0.1), channel_id=1, source_target_pairs={{0,1},{2,3},{4,5},{6,7},{8,9},{10,11},{12,13},{14,15},{1,4},{3,6},... | collective-permute-start | bytes 1572872 | tf_op jit(solution)/shard_map/ppermute | solution.py:412
  48.1 1.9 collective-permute-start.5
  63.2 14.9 %collective-permute-start.6 = (bf16[20,4096]{1,0:T(8,128)(2,1)S(1)}, bf16[20,4096]{1,0:T(8,128)(2,1)S(1)}, u32[]{:S(2)}, u32[]{:S(2)}) collective-permute-start(bf16[20,4096]{1,0:T(8,128)(2,1)S(1)} %get-tuple-element.18), channel_id=1, source_target_pairs={{0,8},{1,9},{2,10},{3,11},{4,12},{5,13},{6,14},{7,15},{8,0},{9,1},... | collective-permute-start | bytes 491528 | tf_op jit(solution)/shard_map/ppermute | solution.py:433
  80.6 16.1 %collective-permute-start.9 = (bf16[40,4096]{1,0:T(8,128)(2,1)}, bf16[40,4096]{1,0:T(8,128)(2,1)S(1)}, u32[]{:S(2)}, u32[]{:S(2)}) collective-permute-start(bf16[40,4096]{1,0:T(8,128)(2,1)} %join.1.refs_0_), channel_id=1, source_target_pairs={{0,6},{1,7},{2,4},{3,5},{4,2},{5,3},{6,0},{7,1},{8,14},{9,15},{10,... | collective-permute-start | bytes 983048 | tf_op jit(solution)/shard_map/ppermute | solution.py:406
  88.0 17.3 %collective-permute-start.8 = (bf16[40,4096]{1,0:T(8,128)(2,1)}, bf16[40,4096]{1,0:T(8,128)(2,1)S(1)}, u32[]{:S(2)}, u32[]{:S(2)}) collective-permute-start(bf16[40,4096]{1,0:T(8,128)(2,1)} %join.1.refs_0_), channel_id=1, source_target_pairs={{0,4},{1,5},{2,6},{3,7},{4,0},{5,1},{6,2},{7,3},{8,12},{9,13},{10,... | collective-permute-start | bytes 983048 | tf_op jit(solution)/shard_map/ppermute | solution.py:406
  91.6 13.8 %collective-permute-start.7 = (bf16[40,4096]{1,0:T(8,128)(2,1)}, bf16[40,4096]{1,0:T(8,128)(2,1)S(1)}, u32[]{:S(2)}, u32[]{:S(2)}) collective-permute-start(bf16[40,4096]{1,0:T(8,128)(2,1)} %join.1.refs_0_), channel_id=1, source_target_pairs={{0,2},{1,3},{2,0},{3,1},{4,6},{5,7},{6,4},{7,5},{8,10},{9,11},{10,... | collective-permute-start | bytes 983048 | tf_op jit(solution)/shard_map/ppermute | solution.py:406
  96.7 8.6 %copy-start.18 = (bf16[40,4096]{1,0:T(8,128)(2,1)}, bf16[40,4096]{1,0:T(8,128)(2,1)S(1)}, u32[]{:S(2)}) copy-start(bf16[40,4096]{1,0:T(8,128)(2,1)S(1)} %collective-permute-done.9.refs_3_) | copy-start | bytes 983044
  147.7 10.1 %collective-permute-start.10 = (bf16[160,4096]{1,0:T(8,128)(2,1)}, bf16[160,4096]{1,0:T(8,128)(2,1)S(1)}, u32[]{:S(2)}, u32[]{:S(2)}) collective-permute-start(bf16[160,4096]{1,0:T(8,128)(2,1)} %pile.1.x), channel_id=1, source_target_pairs={{0,1},{1,0},{2,3},{3,2},{4,5},{5,4},{6,7},{7,6},{8,9},{9,8},{10,11... | collective-permute-start | bytes 3932168 | tf_op jit(solution)/shard_map/ppermute | solution.py:406
  147.7 3.4 %copy-start = (bf16[4096,1024]{1,0:T(8,128)(2,1)S(1)}, bf16[4096,1024]{1,0:T(8,128)(2,1)}, u32[]{:S(2)}) copy-start(bf16[4096,1024]{1,0:T(8,128)(2,1)} %source.3) | copy-start | bytes 25165828
  151.1 3.4 %copy-start.1 = (bf16[4096,1024]{1,0:T(8,128)(2,1)S(1)}, bf16[4096,1024]{1,0:T(8,128)(2,1)}, u32[]{:S(2)}) copy-start(bf16[4096,1024]{1,0:T(8,128)(2,1)} %source.4) | copy-start | bytes 25165828
  151.1 4.6 %slice-start = ((s8[8388608]{0:T(1024)(128)(4,1)}), s8[4194304]{0:T(1024)(128)(4,1)S(1)}, s32[]{:S(2)}) async-start(s8[8388608]{0:T(1024)(128)(4,1)} %bitcast.9), calls=%async_computation | async-start | bytes 8388608
  154.5 2.6 %slice-start.1 = ((s8[8388608]{0:T(1024)(128)(4,1)}), s8[4194304]{0:T(1024)(128)(4,1)S(1)}, s32[]{:S(2)}) async-start(s8[8388608]{0:T(1024)(128)(4,1)} %bitcast.9), calls=%async_computation.1 | async-start | bytes 8388608
  157.8 7.0 %copy-start.2 = (bf16[160,4096]{1,0:T(8,128)(2,1)S(1)}, bf16[160,4096]{1,0:T(8,128)(2,1)}, u32[]{:S(2)}) copy-start(bf16[160,4096]{1,0:T(8,128)(2,1)} %pile.1.x) | copy-start | bytes 3932164
  164.1 8.1 %collective-permute-start.11 = (bf16[160,4096]{1,0:T(8,128)(2,1)S(1)}, bf16[160,4096]{1,0:T(8,128)(2,1)S(1)}, u32[]{:S(2)}, u32[]{:S(2)}) collective-permute-start(bf16[160,4096]{1,0:T(8,128)(2,1)S(1)} %experts.3), channel_id=1, source_target_pairs={{0,1},{1,0},{2,3},{3,2},{4,5},{5,4},{6,7},{7,6},{8,9},{9,8},{10,11... | collective-permute-start | bytes 3932168 | tf_op jit(solution)/shard_map/ppermute | solution.py:406
  177.0 9.9 %collective-permute-start.12 = (bf16[40,4096]{1,0:T(8,128)(2,1)}, bf16[40,4096]{1,0:T(8,128)(2,1)S(1)}, u32[]{:S(2)}, u32[]{:S(2)}) collective-permute-start(bf16[40,4096]{1,0:T(8,128)(2,1)} %get-tuple-element.20), channel_id=1, source_target_pairs={{0,2},{1,3},{2,0},{3,1},{4,6},{5,7},{6,4},{7,5},{8,10},{9,11},{10,... | collective-permute-start | bytes 983048 | tf_op jit(solution)/shard_map/ppermute | solution.py:406
  177.7 10.8 %collective-permute-start.13 = (bf16[40,4096]{1,0:T(8,128)(2,1)}, bf16[40,4096]{1,0:T(8,128)(2,1)S(1)}, u32[]{:S(2)}, u32[]{:S(2)}) collective-permute-start(bf16[40,4096]{1,0:T(8,128)(2,1)} %get-tuple-element.21), channel_id=1, source_target_pairs={{0,4},{1,5},{2,6},{3,7},{4,0},{5,1},{6,2},{7,3},{8,12},{9,13},{10,... | collective-permute-start | bytes 983048 | tf_op jit(solution)/shard_map/ppermute | solution.py:406
  177.8 17.2 %collective-permute-start.14 = (bf16[40,4096]{1,0:T(8,128)(2,1)}, bf16[40,4096]{1,0:T(8,128)(2,1)S(1)}, u32[]{:S(2)}, u32[]{:S(2)}) collective-permute-start(bf16[40,4096]{1,0:T(8,128)(2,1)} %get-tuple-element.22), channel_id=1, source_target_pairs={{0,6},{1,7},{2,4},{3,5},{4,2},{5,3},{6,0},{7,1},{8,14},{9,15},{10,... | collective-permute-start | bytes 983048 | tf_op jit(solution)/shard_map/ppermute | solution.py:406
  186.9 8.1 %copy-start.16 = (bf16[40,4096]{1,0:T(8,128)(2,1)}, bf16[40,4096]{1,0:T(8,128)(2,1)S(1)}, u32[]{:S(2)}) copy-start(bf16[40,4096]{1,0:T(8,128)(2,1)S(1)} %collective-permute-done.12.refs_1_) | copy-start | bytes 983044
  188.5 6.5 %copy-start.17 = (bf16[40,4096]{1,0:T(8,128)(2,1)}, bf16[40,4096]{1,0:T(8,128)(2,1)S(1)}, u32[]{:S(2)}) copy-start(bf16[40,4096]{1,0:T(8,128)(2,1)S(1)} %collective-permute-done.13.refs_2_) | copy-start | bytes 983044
  197.9 11.0 %collective-permute-start.15 = (bf16[20,4096]{1,0:T(8,128)(2,1)}, bf16[20,4096]{1,0:T(8,128)(2,1)S(1)}, u32[]{:S(2)}, u32[]{:S(2)}) collective-permute-start(bf16[20,4096]{1,0:T(8,128)(2,1)} %get-tuple-element.24), channel_id=1, source_target_pairs={{0,8},{1,9},{2,10},{3,11},{4,12},{5,13},{6,14},{7,15},{8,0},{9,1},... | collective-permute-start | bytes 491528 | tf_op jit(solution)/shard_map/ppermute | solution.py:442
  (18 other events, 14.9 us)

commit v4 on v3

--- a/solution.py
+++ b/solution.py
@@ -17,38 +17,39 @@
 MIB = 1024 * 1024
 
 
-def bundle_kernel(keys, segs, out, row, sems):
+def far(x):
+    return pltpu.with_memory_space_constraint(x, pltpu.HBM)
+
+
+def close(x):
+    return pltpu.with_memory_space_constraint(x, pltpu.VMEM)
+
+
+NEAR = pl.BlockSpec(memory_space=pltpu.VMEM)
+
+
+def bundle_kernel(keys, segs, out):
     rows = keys.shape[0]
     spare = out.shape[0] - rows
-    body = pltpu.make_async_copy(keys, out.at[pl.ds(0, rows)], sems.at[0])
-    body.start()
-    row[...] = jnp.zeros_like(row)
-    row[:, : segs.shape[1]] = jnp.broadcast_to(
+    out[:rows] = keys[...]
+    out[rows:] = jnp.zeros((spare, keys.shape[1]), keys.dtype)
+    out[rows:, : segs.shape[1]] = jnp.broadcast_to(
         segs[...].astype(jnp.float32), (spare, segs.shape[1])
-    ).astype(jnp.bfloat16)
-    tail = pltpu.make_async_copy(row, out.at[pl.ds(rows, spare)], sems.at[1])
-    tail.start()
-    body.wait()
-    tail.wait()
+    ).astype(keys.dtype)
 
 
 def bundle(keys, segs):
     rows, width = keys.shape
-    anywhere = pl.BlockSpec(memory_space=pl.ANY)
     return pl.pallas_call(
         bundle_kernel,
-        in_specs=[anywhere, pl.BlockSpec(memory_space=pltpu.VMEM)],
-        out_specs=anywhere,
+        in_specs=[NEAR, NEAR],
+        out_specs=NEAR,
         out_shape=jax.ShapeDtypeStruct((rows + SPARE, width), keys.dtype),
-        scratch_shapes=[
-            pltpu.VMEM((SPARE, width), keys.dtype),
-            pltpu.SemaphoreType.DMA((2,)),
-        ],
         cost_estimate=pl.CostEstimate(
             flops=0, bytes_accessed=4 * rows * width, transcendentals=0
         ),
         name="bundle",
-    )(keys, segs)
+    )(far(keys), far(segs))
 
 
 def attention_kernel(
@@ -184,21 +185,24 @@
             scratch_shapes=[pltpu.VMEM((rows, (WIN_DEV + 1) * rows), jnp.float32)],
         ),
         out_shape=[
-            jax.ShapeDtypeStruct((rows, width), jnp.float32),
+            pltpu.VMEM((rows, width), jnp.float32),
             jax.ShapeDtypeStruct((CAP, width), jnp.bfloat16),
             jax.ShapeDtypeStruct((CAP, width), jnp.bfloat16),
             jax.ShapeDtypeStruct((E_WIN, rows, 32), jnp.bfloat16),
         ],
-        compiler_params=pltpu.CompilerParams(vmem_limit_bytes=20 * MIB),
+        compiler_params=pltpu.CompilerParams(vmem_limit_bytes=14 * MIB),
         cost_estimate=pl.CostEstimate(
             flops=4 * rows * 4 * rows * width, bytes_accessed=8 * rows * width * 4,
             transcendentals=rows * 4 * rows * (width // HEAD_DIM),
         ),
         name="attention",
-    )(deltas, q, *pairs, seg_own, *bundles, resid, gain, routes, gates)
-
-
-def fetch_kernel(parts, source, held, sems):
+    )(
+        deltas, far(q), far(pairs[0]), far(pairs[1]), *pairs[2:], far(seg_own), *bundles,
+        far(resid), far(gain), far(routes), far(gates),
+    )
+
+
+def fetch_kernel(parts, source, after, held, sems):
     depth = source.shape[0] // parts
     copies = []
     for part in range(parts):
@@ -210,12 +214,13 @@
         copy.wait()
 
 
-def fetch(weights):
+def fetch(weights, after):
     parts = 4
+    anywhere = pl.BlockSpec(memory_space=pl.ANY)
     return pl.pallas_call(
         functools.partial(fetch_kernel, parts),
-        in_specs=[pl.BlockSpec(memory_space=pl.ANY)],
-        out_specs=pl.BlockSpec(memory_space=pltpu.VMEM),
+        in_specs=[anywhere, anywhere],
+        out_specs=NEAR,
         out_shape=pltpu.VMEM(weights.shape, weights.dtype),
         scratch_shapes=[pltpu.SemaphoreType.DMA((parts,))],
         compiler_params=pltpu.CompilerParams(vmem_limit_bytes=2 * MIB),
@@ -223,7 +228,7 @@
             flops=0, bytes_accessed=4 * weights.size, transcendentals=0
         ),
         name="fetch",
-    )(weights)
+    )(far(weights), after)
 
 
 def experts_kernel(x, w_gate, w_up, w_down, out, hidden):
@@ -248,14 +253,10 @@
 def experts(x, w_gate, w_up, w_down):
     rows, width = x.shape
     units = w_gate.shape[1]
-    near = pl.BlockSpec(memory_space=pltpu.VMEM)
-    held = [
-        pltpu.with_memory_space_constraint(w, pltpu.VMEM) for w in (w_gate, w_up, w_down)
-    ]
     return pl.pallas_call(
         experts_kernel,
-        in_specs=[near] * 4,
-        out_specs=near,
+        in_specs=[NEAR] * 4,
+        out_specs=NEAR,
         out_shape=jax.ShapeDtypeStruct((rows, width), jnp.bfloat16),
         scratch_shapes=[pltpu.VMEM((rows, units), jnp.bfloat16)],
         compiler_params=pltpu.CompilerParams(vmem_limit_bytes=20 * MIB),
@@ -265,7 +266,7 @@
             transcendentals=rows * units,
         ),
         name="experts",
-    )(x, *held)
+    )(x, close(w_gate), close(w_up), close(w_down))
 
 
 def join_kernel(first, second, out):
@@ -276,38 +277,30 @@
 
 def join(first, second):
     width = first.shape[1]
-    near = pl.BlockSpec(memory_space=pltpu.VMEM)
     return pl.pallas_call(
         join_kernel,
-        in_specs=[near, near],
-        out_specs=near,
+        in_specs=[NEAR, NEAR],
+        out_specs=NEAR,
         out_shape=jax.ShapeDtypeStruct((first.shape[0] + second.shape[0], width), first.dtype),
         name="join",
     )(first, second)
 
 
 def pile_kernel(*refs):
-    blocks, out, sems = refs[:-2], refs[-2], refs[-1]
+    blocks, out = refs[:-1], refs[-1]
     rows = blocks[0].shape[0]
-    copies = [
-        pltpu.make_async_copy(block, out.at[pl.ds(at * rows, rows)], sems.at[at])
-        for at, block in enumerate(blocks)
-    ]
-    for copy in copies:
-        copy.start()
-    for copy in copies:
-        copy.wait()
+    for at, block in enumerate(blocks):
+        out[pl.ds(at * rows, rows)] = block[...]
 
 
 def pile(blocks):
     rows, width = blocks[0].shape
-    anywhere = pl.BlockSpec(memory_space=pl.ANY)
     return pl.pallas_call(
         pile_kernel,
-        in_specs=[anywhere] * len(blocks),
-        out_specs=anywhere,
+        in_specs=[NEAR] * len(blocks),
+        out_specs=NEAR,
         out_shape=jax.ShapeDtypeStruct((len(blocks) * rows, width), blocks[0].dtype),
-        scratch_shapes=[pltpu.SemaphoreType.DMA((len(blocks),))],
+        compiler_params=pltpu.CompilerParams(vmem_limit_bytes=24 * MIB),
         name="pile",
     )(*blocks)
 
@@ -324,15 +317,12 @@
 def add_split(first, second, blocks):
     rows, width = first.shape
     each = rows // blocks
-    cols = 1024
-    piece = pl.BlockSpec((rows, cols), lambda j: (0, j))
-    small = pl.BlockSpec((each, cols), lambda j: (0, j))
     return pl.pallas_call(
         add_kernel,
-        grid=(width // cols,),
-        in_specs=[piece, piece],
-        out_specs=[small] * blocks,
+        in_specs=[NEAR, NEAR],
+        out_specs=[NEAR] * blocks,
         out_shape=[jax.ShapeDtypeStruct((each, width), first.dtype)] * blocks,
+        compiler_params=pltpu.CompilerParams(vmem_limit_bytes=24 * MIB),
         name="add_split",
     )(first, second)
 
@@ -348,12 +338,10 @@
 
 def total_of(blocks):
     width = blocks[0].shape[1]
-    cols = 2048
     return pl.pallas_call(
         total_kernel,
-        grid=(width // cols,),
-        in_specs=[pl.BlockSpec((2 * CAP, cols), lambda j: (0, j))] * len(blocks),
-        out_specs=[pl.BlockSpec((CAP, cols), lambda j: (0, j))] * 2,
+        in_specs=[NEAR] * len(blocks),
+        out_specs=[NEAR] * 2,
         out_shape=[jax.ShapeDtypeStruct((CAP, width), blocks[0].dtype)] * 2,
         name="total",
     )(*blocks)
@@ -369,25 +357,13 @@
 
 
 def combine(mixed, weight, own, other):
-    rows, width = mixed.shape
-    cols = 2048
-
-    def piece(count):
-        return pl.BlockSpec((count, cols), lambda j: (0, j))
-
     return pl.pallas_call(
         combine_kernel,
-        grid=(width // cols,),
-        in_specs=[
-            piece(rows),
-            pl.BlockSpec(weight.shape, lambda j: (0, 0, 0)),
-            piece(own.shape[0]),
-            piece(other.shape[0]),
-        ],
-        out_specs=piece(rows),
-        out_shape=jax.ShapeDtypeStruct((rows, width), jnp.bfloat16),
+        in_specs=[NEAR] * 4,
+        out_specs=NEAR,
+        out_shape=jax.ShapeDtypeStruct(mixed.shape, jnp.bfloat16),
         name="combine",
-    )(mixed, weight, own, other)
+    )(close(mixed), weight, own, other)
 
 
 def shards(
@@ -413,13 +389,14 @@
     key_cross = lax.ppermute(key_block, "expert", crossing)
     value_mirror = swapped(value_two, 1)
     key_mirror = swapped(key_two, 1)
-    held = [fetch(w) for w in (w_gate, w_up, w_down)]
-
-    far = 2 * WIN_DEV + 2
+    held = [fetch(w, value_two) for w in (w_gate, w_up, w_down)]
+    key_cross, *held = lax.optimization_barrier((key_cross, *held))
+
+    beyond = 2 * WIN_DEV + 2
     delta_list = [0 * own, 0 * own + 2, 3 - 2 * odd, 1 + 2 * odd]
     my_expert = own // shard_count
     scalars = jnp.stack(
-        [jnp.where(own >= delta, delta, far) for delta in delta_list] + [my_expert]
+        [jnp.where(own >= delta, delta, beyond) for delta in delta_list] + [my_expert]
     ).astype(jnp.int32)
 
     mixed, keep, send, weight = attention(

time: 213 us -> 167 us (0.78)
  Pallas kernels: 87.2 us -> 37.1 us
  local copies, waits for them, and re-layouts: 23.1 us -> 33.1 us
  starting transfers between devices: 32.7 us -> 27.3 us
    pallas_call x11, Pallas kernels: 83 us -> 31.8 us  [the longest x2 12.8 us: experts(): pl.pallas_call(experts_kernel, in_specs=[NEAR] * 4, out_specs=NEAR, out_s...]
    unnamed x52 -> x44, local copies, waits for them, and re-layouts: 23.1 us -> 33 us
    ppermute x10, starting transfers between devices: 15.1 us -> 7.28 us  [swapped(): return lax.ppermute(block, 'expert', [(i, i ^ mask) for i in range(count)])]
    ppermute x1, starting transfers between devices: 0.01 us -> 2.49 us  [shards(): lax.ppermute(back, 'expert', partner)]
  transfers between devices with their start and end apart: 16 -> 16, of which waited for: 10 -> 11; matrix products, arithmetic and copies ran while one was open for 0% -> 0% of each run, Pallas kernels for 4% -> 10%
where the time goes in v4:
time: 167 us
  waiting for transfers between devices  69 us (41%)
  Pallas kernels  37.1 us (22%)
  local copies, waits for them, and re-layouts  33.1 us (20%)
  starting transfers between devices  27.3 us (16%)
    unnamed x44, local copies, waits for them, and re-layouts  33 us
    ppermute x10, waiting for transfers between devices, swapped(): return lax.ppermute(block, 'expert', [(i, i ^ mask) for i in range(count)])  31.9 us
    pallas_call x2, Pallas kernels, experts(): pl.pallas_call(experts_kernel, in_specs=[NEAR] * 4, out_specs=NEAR, out_s...  12.8 us
    ppermute x1, waiting for transfers between devices, shards(): key_two = lax.ppermute(key_block, 'expert', next_chip)  10.6 us
    pallas_call x3, Pallas kernels, fetch(): pl.pallas_call(functools.partial(fetch_kernel, parts), in_specs=[anywhere...  10.5 us
    ppermute x1, waiting for transfers between devices, shards(): pair = join(keep, lax.ppermute(send, 'expert', partner))  9.79 us
    ppermute x1, waiting for transfers between devices, shards(): lax.ppermute(back, 'expert', partner)  9.05 us
    ppermute x1, waiting for transfers between devices, shards(): value_two = lax.ppermute(values, 'expert', next_chip)  7.64 us
  transfers between devices with their start and end apart: 16, of which 11 were waited for; matrix products, arithmetic and copies ran while one was open for 0% of the time, Pallas kernels for 10%

profile of v4, /device:TPU:0, one launch (start us, length us, event | category | flops | bytes accessed | tf_op | source)
XLA Modules:
  0.0 166.8 jit_solution(17518492066032812573)
XLA Ops:
  2.0 4.9 %collective-permute-start = (bf16[80,4096]{1,0:T(8,128)(2,1)}, bf16[80,4096]{1,0:T(8,128)(2,1)S(1)}, u32[]{:S(2)}, u32[]{:S(2)}) collective-permute-start(bf16[80,4096]{1,0:T(8,128)(2,1)} %bundle.1), channel_id=1, source_target_pairs={{0,2},{1,3},{2,4},{3,5},{4,6},{5,7},{6,8},{7,9},{8,10},{9,11},{10,... | collective-permute-start | bytes 1966088 | tf_op jit(solution)/shard_map/ppermute | solution.py:387
  6.9 3.4 %collective-permute-start.1 = (bf16[64,4096]{1,0:T(8,128)(2,1)}, bf16[64,4096]{1,0:T(8,128)(2,1)S(1)}, u32[]{:S(2)}, u32[]{:S(2)}) collective-permute-start(bf16[64,4096]{1,0:T(8,128)(2,1)} %v0.1), channel_id=1, source_target_pairs={{0,2},{1,3},{2,4},{3,5},{4,6},{5,7},{6,8},{7,9},{8,10},{9,11},{10,... | collective-permute-start | bytes 1572872 | tf_op jit(solution)/shard_map/ppermute | solution.py:385
  11.6 10.6 %collective-permute-done.k1.seg1 = bf16[80,4096]{1,0:T(8,128)(2,1)S(1)} collective-permute-done((bf16[80,4096]{1,0:T(8,128)(2,1)}, bf16[80,4096]{1,0:T(8,128)(2,1)S(1)}, u32[]{:S(2)}, u32[]{:S(2)}) %collective-permute-start) | collective-permute-done | bytes 655392 | tf_op jit(solution)/shard_map/ppermute | solution.py:387
  24.7 7.6 %collective-permute-done.1.after.v1 = bf16[64,4096]{1,0:T(8,128)(2,1)S(1)} collective-permute-done((bf16[64,4096]{1,0:T(8,128)(2,1)}, bf16[64,4096]{1,0:T(8,128)(2,1)S(1)}, u32[]{:S(2)}, u32[]{:S(2)}) %collective-permute-start.1) | collective-permute-done | bytes 524320 | tf_op jit(solution)/shard_map/ppermute | solution.py:385
  32.5 3.5 %fetch.5.w_down = bf16[1024,4096]{1,0:T(8,128)(2,1)S(1)} custom-call(bf16[1024,4096]{1,0:T(8,128)(2,1)} %source.5, bf16[64,4096]{1,0:T(8,128)(2,1)S(1)} %collective-permute-done.1.after.v1), custom_call_target="tpu_custom_call" | custom-call | bytes 16777216 | tf_op jit(solution)/shard_map/fetch/pallas_call | solution.py:220
  36.0 3.3 %copy-done = bf16[1024,4096]{1,0:T(8,128)(2,1)} copy-done((bf16[1024,4096]{1,0:T(8,128)(2,1)}, bf16[1024,4096]{1,0:T(8,128)(2,1)S(1)}, u32[]{:S(2)}) %copy-start) | copy-done | bytes 8388632
  39.2 3.5 %fetch.4.w_up = bf16[4096,1024]{1,0:T(8,128)(2,1)S(1)} custom-call(bf16[4096,1024]{1,0:T(8,128)(2,1)} %source.4, bf16[64,4096]{1,0:T(8,128)(2,1)S(1)} %collective-permute-done.1.after.v1), custom_call_target="tpu_custom_call" | custom-call | bytes 16777216 | tf_op jit(solution)/shard_map/fetch/pallas_call | solution.py:220
  42.8 3.2 %copy-done.3 = bf16[4096,1024]{1,0:T(8,128)(2,1)} copy-done((bf16[4096,1024]{1,0:T(8,128)(2,1)}, bf16[4096,1024]{1,0:T(8,128)(2,1)S(1)}, u32[]{:S(2)}) %copy-start.3) | copy-done | bytes 8388632
  46.0 3.5 %fetch.3.w_gate = bf16[4096,1024]{1,0:T(8,128)(2,1)S(1)} custom-call(bf16[4096,1024]{1,0:T(8,128)(2,1)} %source.3, bf16[64,4096]{1,0:T(8,128)(2,1)S(1)} %collective-permute-done.1.after.v1), custom_call_target="tpu_custom_call" | custom-call | bytes 16777216 | tf_op jit(solution)/shard_map/fetch/pallas_call | solution.py:220
  49.5 3.3 %copy-done.6 = bf16[4096,1024]{1,0:T(8,128)(2,1)} copy-done((bf16[4096,1024]{1,0:T(8,128)(2,1)}, bf16[4096,1024]{1,0:T(8,128)(2,1)S(1)}, u32[]{:S(2)}) %copy-start.6) | copy-done | bytes 8388632
  52.8 5.3 %attention.1 = (f32[64,4096]{1,0:T(8,128)S(1)}, bf16[20,4096]{1,0:T(8,128)(2,1)S(1)}, bf16[20,4096]{1,0:T(8,128)(2,1)S(1)}, bf16[2,64,32]{2,1,0:T(8,128)(2,1)S(1)}) custom-call(s32[5]{0:T(128)S(1)} %stack.23.deltas, bf16[64,4096]{1,0:T(8,128)(2,1)} %q.1, bf16[64,4096]{1,0:T(8,128)(2,1)} %k0.1, bf16[64,4096]{1,0:T(8,128)(2,1)} %v0.1, ...), custom_call_target="tpu_custom_call" | custom-call | flops 268435456 | bytes 8388608 | tf_op jit(solution)/shard_map/attention/pallas_call | solution.py:165
  60.4 5.5 %collective-permute-start.6 = (bf16[20,4096]{1,0:T(8,128)(2,1)S(1)}, bf16[20,4096]{1,0:T(8,128)(2,1)S(1)}, u32[]{:S(2)}, u32[]{:S(2)}) collective-permute-start(bf16[20,4096]{1,0:T(8,128)(2,1)S(1)} %get-tuple-element.23), channel_id=1, source_target_pairs={{0,8},{1,9},{2,10},{3,11},{4,12},{5,13},{6,14},{7,15},{8,0},{9,1},... | collective-permute-start | bytes 491528 | tf_op jit(solution)/shard_map/ppermute | solution.py:410
  65.9 9.8 %collective-permute-done.6.second = bf16[20,4096]{1,0:T(8,128)(2,1)S(1)} collective-permute-done((bf16[20,4096]{1,0:T(8,128)(2,1)S(1)}, bf16[20,4096]{1,0:T(8,128)(2,1)S(1)}, u32[]{:S(2)}, u32[]{:S(2)}) %collective-permute-start.6) | collective-permute-done | bytes 163872 | tf_op jit(solution)/shard_map/ppermute | solution.py:410
  81.7 8.2 %collective-permute-done.9.refs_3_ = bf16[40,4096]{1,0:T(8,128)(2,1)S(1)} collective-permute-done((bf16[40,4096]{1,0:T(8,128)(2,1)}, bf16[40,4096]{1,0:T(8,128)(2,1)S(1)}, u32[]{:S(2)}, u32[]{:S(2)}) %collective-permute-start.9) | collective-permute-done | bytes 327712 | tf_op jit(solution)/shard_map/ppermute | solution.py:382
  89.9 4.2 %collective-permute-done.8.refs_2_ = bf16[40,4096]{1,0:T(8,128)(2,1)S(1)} collective-permute-done((bf16[40,4096]{1,0:T(8,128)(2,1)}, bf16[40,4096]{1,0:T(8,128)(2,1)S(1)}, u32[]{:S(2)}, u32[]{:S(2)}) %collective-permute-start.8) | collective-permute-done | bytes 327712 | tf_op jit(solution)/shard_map/ppermute | solution.py:382
  101.1 3.4 %copy-done.1 = bf16[1024,4096]{1,0:T(8,128)(2,1)S(1)} copy-done((bf16[1024,4096]{1,0:T(8,128)(2,1)S(1)}, bf16[1024,4096]{1,0:T(8,128)(2,1)}, u32[]{:S(2)}) %copy-start.1) | copy-done | bytes 8388632
  104.5 3.4 %copy-done.4 = bf16[4096,1024]{1,0:T(8,128)(2,1)S(1)} copy-done((bf16[4096,1024]{1,0:T(8,128)(2,1)S(1)}, bf16[4096,1024]{1,0:T(8,128)(2,1)}, u32[]{:S(2)}) %copy-start.4) | copy-done | bytes 8388632
  107.9 3.4 %copy-done.7 = bf16[4096,1024]{1,0:T(8,128)(2,1)S(1)} copy-done((bf16[4096,1024]{1,0:T(8,128)(2,1)S(1)}, bf16[4096,1024]{1,0:T(8,128)(2,1)}, u32[]{:S(2)}) %copy-start.7) | copy-done | bytes 8388632
  112.6 6.4 %experts.3 = bf16[160,4096]{1,0:T(8,128)(2,1)S(1)} custom-call(bf16[160,4096]{1,0:T(8,128)(2,1)S(1)} %copy-done.11, bf16[4096,1024]{1,0:T(8,128)(2,1)S(1)} %copy-done.7, bf16[4096,1024]{1,0:T(8,128)(2,1)S(1)} %copy-done.4, bf16[1024,4096]{1,0:T(8,128)(2,1)S(1)} %copy-done.1), custom_call_target="tpu_custom_call" | custom-call | flops 4026531840 | bytes 2621440 | tf_op jit(solution)/shard_map/experts/pallas_call | solution.py:256
  119.2 3.4 %copy-done.8 = bf16[4096,1024]{1,0:T(8,128)(2,1)S(1)} copy-done((bf16[4096,1024]{1,0:T(8,128)(2,1)S(1)}, bf16[4096,1024]{1,0:T(8,128)(2,1)}, u32[]{:S(2)}) %copy-start.8) | copy-done | bytes 8388632
  122.6 6.4 %experts.2.first = bf16[160,4096]{1,0:T(8,128)(2,1)S(1)} custom-call(bf16[160,4096]{1,0:T(8,128)(2,1)S(1)} %pile.1.x, bf16[4096,1024]{1,0:T(8,128)(2,1)S(1)} %copy-done.8, bf16[4096,1024]{1,0:T(8,128)(2,1)S(1)} %copy-done.5, bf16[1024,4096]{1,0:T(8,128)(2,1)S(1)} %copy-done.2), custom_call_target="tpu_custom_call" | custom-call | flops 4026531840 | bytes 2621440 | tf_op jit(solution)/shard_map/experts/pallas_call | solution.py:256
  133.5 6.5 %collective-permute-done.12.refs_1_ = bf16[40,4096]{1,0:T(8,128)(2,1)S(1)} collective-permute-done((bf16[40,4096]{1,0:T(8,128)(2,1)S(1)}, bf16[40,4096]{1,0:T(8,128)(2,1)S(1)}, u32[]{:S(2)}, u32[]{:S(2)}) %collective-permute-start.12) | collective-permute-done | bytes 327712 | tf_op jit(solution)/shard_map/ppermute | solution.py:382
  141.2 7.0 %collective-permute-done.14.refs_3_ = bf16[40,4096]{1,0:T(8,128)(2,1)S(1)} collective-permute-done((bf16[40,4096]{1,0:T(8,128)(2,1)S(1)}, bf16[40,4096]{1,0:T(8,128)(2,1)S(1)}, u32[]{:S(2)}, u32[]{:S(2)}) %collective-permute-start.14) | collective-permute-done | bytes 327712 | tf_op jit(solution)/shard_map/ppermute | solution.py:382
  153.6 9.0 %collective-permute-done.15.other = bf16[20,4096]{1,0:T(8,128)(2,1)S(1)} collective-permute-done((bf16[20,4096]{1,0:T(8,128)(2,1)}, bf16[20,4096]{1,0:T(8,128)(2,1)S(1)}, u32[]{:S(2)}, u32[]{:S(2)}) %collective-permute-start.15) | collective-permute-done | bytes 163872 | tf_op jit(solution)/shard_map/ppermute | solution.py:419
  (65 shorter events, 37.8 us)
Async XLA Ops:
  2.0 20.3 %collective-permute-start = (bf16[80,4096]{1,0:T(8,128)(2,1)}, bf16[80,4096]{1,0:T(8,128)(2,1)S(1)}, u32[]{:S(2)}, u32[]{:S(2)}) collective-permute-start(bf16[80,4096]{1,0:T(8,128)(2,1)} %bundle.1), channel_id=1, source_target_pairs={{0,2},{1,3},{2,4},{3,5},{4,6},{5,7},{6,8},{7,9},{8,10},{9,11},{10,... | collective-permute-start | bytes 1966088 | tf_op jit(solution)/shard_map/ppermute | solution.py:387
  6.9 25.5 %collective-permute-start.1 = (bf16[64,4096]{1,0:T(8,128)(2,1)}, bf16[64,4096]{1,0:T(8,128)(2,1)S(1)}, u32[]{:S(2)}, u32[]{:S(2)}) collective-permute-start(bf16[64,4096]{1,0:T(8,128)(2,1)} %v0.1), channel_id=1, source_target_pairs={{0,2},{1,3},{2,4},{3,5},{4,6},{5,7},{6,8},{7,9},{8,10},{9,11},{10,... | collective-permute-start | bytes 1572872 | tf_op jit(solution)/shard_map/ppermute | solution.py:385
  10.3 42.5 %collective-permute-start.2 = (bf16[80,4096]{1,0:T(8,128)(2,1)}, bf16[80,4096]{1,0:T(8,128)(2,1)S(1)}, u32[]{:S(2)}, u32[]{:S(2)}) collective-permute-start(bf16[80,4096]{1,0:T(8,128)(2,1)} %bundle.1), channel_id=1, source_target_pairs={{0,1},{2,3},{4,5},{6,7},{8,9},{10,11},{12,13},{14,15},{1,4},{3,6},... | collective-permute-start | bytes 1966088 | tf_op jit(solution)/shard_map/ppermute | solution.py:389
  22.3 30.5 %collective-permute-start.4 = (bf16[80,4096]{1,0:T(8,128)(2,1)S(1)}, bf16[80,4096]{1,0:T(8,128)(2,1)S(1)}, u32[]{:S(2)}, u32[]{:S(2)}) collective-permute-start(bf16[80,4096]{1,0:T(8,128)(2,1)S(1)} %collective-permute-done.k1.seg1), channel_id=1, source_target_pairs={{0,1},{1,0},{2,3},{3,2},{4,5},{5,4},{6,7},{7,6},{8,9},{9,8},{10,11... | collective-permute-start | bytes 1966088 | tf_op jit(solution)/shard_map/ppermute | solution.py:382
  22.3 30.5 %collective-permute-start.3 = (bf16[64,4096]{1,0:T(8,128)(2,1)}, bf16[64,4096]{1,0:T(8,128)(2,1)S(1)}, u32[]{:S(2)}, u32[]{:S(2)}) collective-permute-start(bf16[64,4096]{1,0:T(8,128)(2,1)} %v0.1), channel_id=1, source_target_pairs={{0,1},{2,3},{4,5},{6,7},{8,9},{10,11},{12,13},{14,15},{1,4},{3,6},... | collective-permute-start | bytes 1572872 | tf_op jit(solution)/shard_map/ppermute | solution.py:388
  32.4 20.4 %collective-permute-start.5 = (bf16[64,4096]{1,0:T(8,128)(2,1)S(1)}, bf16[64,4096]{1,0:T(8,128)(2,1)S(1)}, u32[]{:S(2)}, u32[]{:S(2)}) collective-permute-start(bf16[64,4096]{1,0:T(8,128)(2,1)S(1)} %collective-permute-done.1.after.v1), channel_id=1, source_target_pairs={{0,1},{1,0},{2,3},{3,2},{4,5},{5,4},{6,7},{7,6},{8,9},{9,8},{10,11... | collective-permute-start | bytes 1572872 | tf_op jit(solution)/shard_map/ppermute | solution.py:382
  60.4 15.3 %collective-permute-start.6 = (bf16[20,4096]{1,0:T(8,128)(2,1)S(1)}, bf16[20,4096]{1,0:T(8,128)(2,1)S(1)}, u32[]{:S(2)}, u32[]{:S(2)}) collective-permute-start(bf16[20,4096]{1,0:T(8,128)(2,1)S(1)} %get-tuple-element.23), channel_id=1, source_target_pairs={{0,8},{1,9},{2,10},{3,11},{4,12},{5,13},{6,14},{7,15},{8,0},{9,1},... | collective-permute-start | bytes 491528 | tf_op jit(solution)/shard_map/ppermute | solution.py:410
  78.2 11.7 %collective-permute-start.9 = (bf16[40,4096]{1,0:T(8,128)(2,1)}, bf16[40,4096]{1,0:T(8,128)(2,1)S(1)}, u32[]{:S(2)}, u32[]{:S(2)}) collective-permute-start(bf16[40,4096]{1,0:T(8,128)(2,1)} %join.1.refs_0_), channel_id=1, source_target_pairs={{0,6},{1,7},{2,4},{3,5},{4,2},{5,3},{6,0},{7,1},{8,14},{9,15},{10,... | collective-permute-start | bytes 983048 | tf_op jit(solution)/shard_map/ppermute | solution.py:382
  78.2 15.9 %collective-permute-start.8 = (bf16[40,4096]{1,0:T(8,128)(2,1)}, bf16[40,4096]{1,0:T(8,128)(2,1)S(1)}, u32[]{:S(2)}, u32[]{:S(2)}) collective-permute-start(bf16[40,4096]{1,0:T(8,128)(2,1)} %join.1.refs_0_), channel_id=1, source_target_pairs={{0,4},{1,5},{2,6},{3,7},{4,0},{5,1},{6,2},{7,3},{8,12},{9,13},{10,... | collective-permute-start | bytes 983048 | tf_op jit(solution)/shard_map/ppermute | solution.py:382
  79.5 16.4 %collective-permute-start.7 = (bf16[40,4096]{1,0:T(8,128)(2,1)}, bf16[40,4096]{1,0:T(8,128)(2,1)S(1)}, u32[]{:S(2)}, u32[]{:S(2)}) collective-permute-start(bf16[40,4096]{1,0:T(8,128)(2,1)} %join.1.refs_0_), channel_id=1, source_target_pairs={{0,2},{1,3},{2,0},{3,1},{4,6},{5,7},{6,4},{7,5},{8,10},{9,11},{10,... | collective-permute-start | bytes 983048 | tf_op jit(solution)/shard_map/ppermute | solution.py:382
  96.9 3.1 %collective-permute-start.10 = (bf16[160,4096]{1,0:T(8,128)(2,1)S(1)}, bf16[160,4096]{1,0:T(8,128)(2,1)S(1)}, u32[]{:S(2)}, u32[]{:S(2)}) collective-permute-start(bf16[160,4096]{1,0:T(8,128)(2,1)S(1)} %pile.1.x), channel_id=1, source_target_pairs={{0,1},{1,0},{2,3},{3,2},{4,5},{5,4},{6,7},{7,6},{8,9},{9,8},{10,11... | collective-permute-start | bytes 3932168 | tf_op jit(solution)/shard_map/ppermute | solution.py:382
  101.1 3.4 %copy-start.1 = (bf16[1024,4096]{1,0:T(8,128)(2,1)S(1)}, bf16[1024,4096]{1,0:T(8,128)(2,1)}, u32[]{:S(2)}) copy-start(bf16[1024,4096]{1,0:T(8,128)(2,1)} %copy-done) | copy-start | bytes 25165828
  104.5 3.4 %copy-start.4 = (bf16[4096,1024]{1,0:T(8,128)(2,1)S(1)}, bf16[4096,1024]{1,0:T(8,128)(2,1)}, u32[]{:S(2)}) copy-start(bf16[4096,1024]{1,0:T(8,128)(2,1)} %copy-done.3) | copy-start | bytes 25165828
  107.9 3.4 %copy-start.7 = (bf16[4096,1024]{1,0:T(8,128)(2,1)S(1)}, bf16[4096,1024]{1,0:T(8,128)(2,1)}, u32[]{:S(2)}) copy-start(bf16[4096,1024]{1,0:T(8,128)(2,1)} %copy-done.6) | copy-start | bytes 25165828
  112.6 6.6 %copy-start.2 = (bf16[1024,4096]{1,0:T(8,128)(2,1)S(1)}, bf16[1024,4096]{1,0:T(8,128)(2,1)}, u32[]{:S(2)}) copy-start(bf16[1024,4096]{1,0:T(8,128)(2,1)} %copy-done) | copy-start | bytes 25165828
  112.6 6.6 %copy-start.5 = (bf16[4096,1024]{1,0:T(8,128)(2,1)S(1)}, bf16[4096,1024]{1,0:T(8,128)(2,1)}, u32[]{:S(2)}) copy-start(bf16[4096,1024]{1,0:T(8,128)(2,1)} %copy-done.3) | copy-start | bytes 25165828
  119.0 9.9 %collective-permute-start.11 = (bf16[160,4096]{1,0:T(8,128)(2,1)S(1)}, bf16[160,4096]{1,0:T(8,128)(2,1)S(1)}, u32[]{:S(2)}, u32[]{:S(2)}) collective-permute-start(bf16[160,4096]{1,0:T(8,128)(2,1)S(1)} %experts.3), channel_id=1, source_target_pairs={{0,1},{1,0},{2,3},{3,2},{4,5},{5,4},{6,7},{7,6},{8,9},{9,8},{10,11... | collective-permute-start | bytes 3932168 | tf_op jit(solution)/shard_map/ppermute | solution.py:382
  119.2 3.4 %copy-start.8 = (bf16[4096,1024]{1,0:T(8,128)(2,1)S(1)}, bf16[4096,1024]{1,0:T(8,128)(2,1)}, u32[]{:S(2)}) copy-start(bf16[4096,1024]{1,0:T(8,128)(2,1)} %copy-done.6) | copy-start | bytes 25165828
  130.0 10.0 %collective-permute-start.12 = (bf16[40,4096]{1,0:T(8,128)(2,1)S(1)}, bf16[40,4096]{1,0:T(8,128)(2,1)S(1)}, u32[]{:S(2)}, u32[]{:S(2)}) collective-permute-start(bf16[40,4096]{1,0:T(8,128)(2,1)S(1)} %get-tuple-element.28), channel_id=1, source_target_pairs={{0,2},{1,3},{2,0},{3,1},{4,6},{5,7},{6,4},{7,5},{8,10},{9,11},{10,... | collective-permute-start | bytes 983048 | tf_op jit(solution)/shard_map/ppermute | solution.py:382
  130.6 10.6 %collective-permute-start.13 = (bf16[40,4096]{1,0:T(8,128)(2,1)S(1)}, bf16[40,4096]{1,0:T(8,128)(2,1)S(1)}, u32[]{:S(2)}, u32[]{:S(2)}) collective-permute-start(bf16[40,4096]{1,0:T(8,128)(2,1)S(1)} %get-tuple-element.29), channel_id=1, source_target_pairs={{0,4},{1,5},{2,6},{3,7},{4,0},{5,1},{6,2},{7,3},{8,12},{9,13},{10,... | collective-permute-start | bytes 983048 | tf_op jit(solution)/shard_map/ppermute | solution.py:382
  131.5 16.7 %collective-permute-start.14 = (bf16[40,4096]{1,0:T(8,128)(2,1)S(1)}, bf16[40,4096]{1,0:T(8,128)(2,1)S(1)}, u32[]{:S(2)}, u32[]{:S(2)}) collective-permute-start(bf16[40,4096]{1,0:T(8,128)(2,1)S(1)} %get-tuple-element.30), channel_id=1, source_target_pairs={{0,6},{1,7},{2,4},{3,5},{4,2},{5,3},{6,0},{7,1},{8,14},{9,15},{10,... | collective-permute-start | bytes 983048 | tf_op jit(solution)/shard_map/ppermute | solution.py:382
  140.0 8.2 %copy-start.17 = (bf16[40,4096]{1,0:T(8,128)(2,1)}, bf16[40,4096]{1,0:T(8,128)(2,1)S(1)}, u32[]{:S(2)}) copy-start(bf16[40,4096]{1,0:T(8,128)(2,1)S(1)} %collective-permute-done.12.refs_1_) | copy-start | bytes 983044
  141.2 7.0 %copy-start.18 = (bf16[40,4096]{1,0:T(8,128)(2,1)}, bf16[40,4096]{1,0:T(8,128)(2,1)S(1)}, u32[]{:S(2)}) copy-start(bf16[40,4096]{1,0:T(8,128)(2,1)S(1)} %collective-permute-done.13.refs_2_) | copy-start | bytes 983044
  151.1 11.5 %collective-permute-start.15 = (bf16[20,4096]{1,0:T(8,128)(2,1)}, bf16[20,4096]{1,0:T(8,128)(2,1)S(1)}, u32[]{:S(2)}, u32[]{:S(2)}) collective-permute-start(bf16[20,4096]{1,0:T(8,128)(2,1)} %get-tuple-element.32), channel_id=1, source_target_pairs={{0,8},{1,9},{2,10},{3,11},{4,12},{5,13},{6,14},{7,15},{8,0},{9,1},... | collective-permute-start | bytes 491528 | tf_op jit(solution)/shard_map/ppermute | solution.py:419
  (14 other events, 19.5 us)

commit v5 on v4

--- a/solution.py
+++ b/solution.py
@@ -48,6 +48,7 @@
         cost_estimate=pl.CostEstimate(
             flops=0, bytes_accessed=4 * rows * width, transcendentals=0
         ),
+        compiler_params=pltpu.CompilerParams(vmem_limit_bytes=6 * MIB),
         name="bundle",
     )(far(keys), far(segs))
 
@@ -202,7 +203,7 @@
     )
 
 
-def fetch_kernel(parts, source, after, held, sems):
+def fetch_kernel(parts, source, held, sems):
     depth = source.shape[0] // parts
     copies = []
     for part in range(parts):
@@ -214,12 +215,12 @@
         copy.wait()
 
 
-def fetch(weights, after):
+def fetch(weights):
     parts = 4
     anywhere = pl.BlockSpec(memory_space=pl.ANY)
     return pl.pallas_call(
         functools.partial(fetch_kernel, parts),
-        in_specs=[anywhere, anywhere],
+        in_specs=[anywhere],
         out_specs=NEAR,
         out_shape=pltpu.VMEM(weights.shape, weights.dtype),
         scratch_shapes=[pltpu.SemaphoreType.DMA((parts,))],
@@ -228,7 +229,7 @@
             flops=0, bytes_accessed=4 * weights.size, transcendentals=0
         ),
         name="fetch",
-    )(far(weights), after)
+    )(far(weights))
 
 
 def experts_kernel(x, w_gate, w_up, w_down, out, hidden):
@@ -282,6 +283,7 @@
         in_specs=[NEAR, NEAR],
         out_specs=NEAR,
         out_shape=jax.ShapeDtypeStruct((first.shape[0] + second.shape[0], width), first.dtype),
+        compiler_params=pltpu.CompilerParams(vmem_limit_bytes=8 * MIB),
         name="join",
     )(first, second)
 
@@ -300,7 +302,7 @@
         in_specs=[NEAR] * len(blocks),
         out_specs=NEAR,
         out_shape=jax.ShapeDtypeStruct((len(blocks) * rows, width), blocks[0].dtype),
-        compiler_params=pltpu.CompilerParams(vmem_limit_bytes=24 * MIB),
+        compiler_params=pltpu.CompilerParams(vmem_limit_bytes=(4 + len(blocks)) * MIB),
         name="pile",
     )(*blocks)
 
@@ -322,7 +324,7 @@
         in_specs=[NEAR, NEAR],
         out_specs=[NEAR] * blocks,
         out_shape=[jax.ShapeDtypeStruct((each, width), first.dtype)] * blocks,
-        compiler_params=pltpu.CompilerParams(vmem_limit_bytes=24 * MIB),
+        compiler_params=pltpu.CompilerParams(vmem_limit_bytes=(6 + blocks) * MIB),
         name="add_split",
     )(first, second)
 
@@ -343,6 +345,7 @@
         in_specs=[NEAR] * len(blocks),
         out_specs=[NEAR] * 2,
         out_shape=[jax.ShapeDtypeStruct((CAP, width), blocks[0].dtype)] * 2,
+        compiler_params=pltpu.CompilerParams(vmem_limit_bytes=(4 + len(blocks)) * MIB),
         name="total",
     )(*blocks)
 
@@ -362,6 +365,7 @@
         in_specs=[NEAR] * 4,
         out_specs=NEAR,
         out_shape=jax.ShapeDtypeStruct(mixed.shape, jnp.bfloat16),
+        compiler_params=pltpu.CompilerParams(vmem_limit_bytes=8 * MIB),
         name="combine",
     )(close(mixed), weight, own, other)
 
@@ -387,10 +391,11 @@
     key_two = lax.ppermute(key_block, "expert", next_chip)
     value_cross = lax.ppermute(values, "expert", crossing)
     key_cross = lax.ppermute(key_block, "expert", crossing)
+    held = [fetch(w) for w in (w_gate, w_up, w_down)]
+    key_two, held[0], held[1] = lax.optimization_barrier((key_two, held[0], held[1]))
+    key_mirror = swapped(key_two, 1)
+    value_two, held[2] = lax.optimization_barrier((value_two, held[2]))
     value_mirror = swapped(value_two, 1)
-    key_mirror = swapped(key_two, 1)
-    held = [fetch(w, value_two) for w in (w_gate, w_up, w_down)]
-    key_cross, *held = lax.optimization_barrier((key_cross, *held))
 
     beyond = 2 * WIN_DEV + 2
     delta_list = [0 * own, 0 * own + 2, 3 - 2 * odd, 1 + 2 * odd]

time: 167 us -> 133 us (0.80)
  local copies, waits for them, and re-layouts: 33.1 us -> 16.6 us
  waiting for transfers between devices: 69 us -> 55.5 us
  Pallas kernels: 37.1 us -> 31.9 us
    unnamed x44 -> x14, local copies, waits for them, and re-layouts: 33 us -> 16.5 us
    ppermute x1, waiting for transfers between devices: 10.6 us -> 0.01 us  [shards(): key_two = lax.ppermute(key_block, 'expert', next_chip)]
    ppermute x10, starting transfers between devices: 7.28 us -> 15.5 us  [swapped(): return lax.ppermute(block, 'expert', [(i, i ^ mask) for i in range(count)])]
    ppermute x1, waiting for transfers between devices: 7.64 us -> 0.01 us  [shards(): value_two = lax.ppermute(values, 'expert', next_chip)]
    ppermute x1, starting transfers between devices: 5.49 us -> 0.09 us  [shards(): pair = join(keep, lax.ppermute(send, 'expert', partner))]
    ppermute x1, starting transfers between devices: 2.49 us -> 0.07 us  [shards(): lax.ppermute(back, 'expert', partner)]
    ppermute x1, waiting for transfers between devices: 9.79 us -> 11.7 us  [shards(): pair = join(keep, lax.ppermute(send, 'expert', partner))]
    pallas_call x1, Pallas kernels: 2.14 us -> 0.18 us  [total_of(): pl.pallas_call(total_kernel, in_specs=[NEAR] * len(blocks), out_specs=[NE...]
  transfers between devices with their start and end apart: 16 -> 16, of which waited for: 11 -> 9; matrix products, arithmetic and copies ran while one was open for 0% -> 0% of each run, Pallas kernels for 10% -> 13%
where the time goes in v5:
time: 133 us; the launch traced here: 132 us
  waiting for transfers between devices  55.5 us (42%)
  Pallas kernels  31.9 us (24%)
  starting transfers between devices  28.1 us (21%)
  local copies, waits for them, and re-layouts  16.6 us (12%)
    ppermute x10, waiting for transfers between devices, swapped(): return lax.ppermute(block, 'expert', [(i, i ^ mask) for i in range(count)])  32.8 us
    unnamed x14, local copies, waits for them, and re-layouts  16.5 us
    ppermute x10, starting transfers between devices, swapped(): return lax.ppermute(block, 'expert', [(i, i ^ mask) for i in range(count)])  15.5 us
    pallas_call x2, Pallas kernels, experts(): pl.pallas_call(experts_kernel, in_specs=[NEAR] * 4, out_specs=NEAR, out_s...  12.8 us
    ppermute x1, waiting for transfers between devices, shards(): pair = join(keep, lax.ppermute(send, 'expert', partner))  11.7 us
    ppermute x1, waiting for transfers between devices, shards(): lax.ppermute(back, 'expert', partner)  10.9 us
    pallas_call x3, Pallas kernels, fetch(): pl.pallas_call(functools.partial(fetch_kernel, parts), in_specs=[anywhere...  10.5 us
    pallas_call x1, Pallas kernels, attention(): pl.pallas_call(attention_kernel, grid_spec=pltpu.PrefetchScalarGridSpec(n...  5.71 us
  transfers between devices with their start and end apart: 16, of which 9 were waited for; matrix products, arithmetic and copies ran while one was open for 0% of the time, Pallas kernels for 13%

profile of v5, /device:TPU:0, one launch (start us, length us, event | category | flops | bytes accessed | tf_op | source)
XLA Modules:
  0.0 132.2 jit_solution(13002321879608161147)
XLA Ops:
  1.1 4.9 %collective-permute-start = (bf16[80,4096]{1,0:T(8,128)(2,1)S(1)}, bf16[80,4096]{1,0:T(8,128)(2,1)S(1)}, u32[]{:S(2)}, u32[]{:S(2)}) collective-permute-start(bf16[80,4096]{1,0:T(8,128)(2,1)S(1)} %bundle.1), channel_id=1, source_target_pairs={{0,2},{1,3},{2,4},{3,5},{4,6},{5,7},{6,8},{7,9},{8,10},{9,11},{10,... | collective-permute-start | bytes 1966088 | tf_op jit(solution)/shard_map/ppermute | solution.py:391
  6.0 3.4 %collective-permute-start.1 = (bf16[64,4096]{1,0:T(8,128)(2,1)}, bf16[64,4096]{1,0:T(8,128)(2,1)S(1)}, u32[]{:S(2)}, u32[]{:S(2)}) collective-permute-start(bf16[64,4096]{1,0:T(8,128)(2,1)} %v0.1), channel_id=1, source_target_pairs={{0,2},{1,3},{2,4},{3,5},{4,6},{5,7},{6,8},{7,9},{8,10},{9,11},{10,... | collective-permute-start | bytes 1572872 | tf_op jit(solution)/shard_map/ppermute | solution.py:389
  10.8 3.5 %fetch.3.w_gate = bf16[4096,1024]{1,0:T(8,128)(2,1)S(1)} custom-call(bf16[4096,1024]{1,0:T(8,128)(2,1)} %source.3), custom_call_target="tpu_custom_call" | custom-call | bytes 16777216 | tf_op jit(solution)/shard_map/fetch/pallas_call | solution.py:221
  14.3 3.2 %copy-done = bf16[4096,1024]{1,0:T(8,128)(2,1)} copy-done((bf16[4096,1024]{1,0:T(8,128)(2,1)}, bf16[4096,1024]{1,0:T(8,128)(2,1)S(1)}, u32[]{:S(2)}) %copy-start) | copy-done | bytes 8388632
  17.5 3.5 %fetch.4.w_up = bf16[4096,1024]{1,0:T(8,128)(2,1)S(1)} custom-call(bf16[4096,1024]{1,0:T(8,128)(2,1)} %source.4), custom_call_target="tpu_custom_call" | custom-call | bytes 16777216 | tf_op jit(solution)/shard_map/fetch/pallas_call | solution.py:221
  21.0 3.3 %copy-done.2 = bf16[4096,1024]{1,0:T(8,128)(2,1)} copy-done((bf16[4096,1024]{1,0:T(8,128)(2,1)}, bf16[4096,1024]{1,0:T(8,128)(2,1)S(1)}, u32[]{:S(2)}) %copy-start.2) | copy-done | bytes 8388632
  24.3 2.2 %collective-permute-start.4 = (bf16[80,4096]{1,0:T(8,128)(2,1)S(1)}, bf16[80,4096]{1,0:T(8,128)(2,1)S(1)}, u32[]{:S(2)}, u32[]{:S(2)}) collective-permute-start(bf16[80,4096]{1,0:T(8,128)(2,1)S(1)} %collective-permute-done.k1.seg1), channel_id=1, source_target_pairs={{0,1},{1,0},{2,3},{3,2},{4,5},{5,4},{6,7},{7,6},{8,9},{9,8},{10,11... | collective-permute-start | bytes 1966088 | tf_op jit(solution)/shard_map/ppermute | solution.py:386
  26.5 2.8 %collective-permute-start.3 = (bf16[64,4096]{1,0:T(8,128)(2,1)}, bf16[64,4096]{1,0:T(8,128)(2,1)}, u32[]{:S(2)}, u32[]{:S(2)}) collective-permute-start(bf16[64,4096]{1,0:T(8,128)(2,1)} %v0.1), channel_id=1, source_target_pairs={{0,1},{2,3},{4,5},{6,7},{8,9},{10,11},{12,13},{14,15},{1,4},{3,6},... | collective-permute-start | bytes 1572872 | tf_op jit(solution)/shard_map/ppermute | solution.py:392
  29.3 3.5 %fetch.5.w_down = bf16[1024,4096]{1,0:T(8,128)(2,1)S(1)} custom-call(bf16[1024,4096]{1,0:T(8,128)(2,1)} %source.5), custom_call_target="tpu_custom_call" | custom-call | bytes 16777216 | tf_op jit(solution)/shard_map/fetch/pallas_call | solution.py:221
  32.8 3.3 %copy-done.5 = bf16[1024,4096]{1,0:T(8,128)(2,1)} copy-done((bf16[1024,4096]{1,0:T(8,128)(2,1)}, bf16[1024,4096]{1,0:T(8,128)(2,1)S(1)}, u32[]{:S(2)}) %copy-start.5) | copy-done | bytes 8388632
  38.6 5.7 %attention.1 = (f32[64,4096]{1,0:T(8,128)S(1)}, bf16[20,4096]{1,0:T(8,128)(2,1)S(1)}, bf16[20,4096]{1,0:T(8,128)(2,1)S(1)}, bf16[2,64,32]{2,1,0:T(8,128)(2,1)S(1)}) custom-call(s32[5]{0:T(128)S(1)} %stack.23.deltas, bf16[64,4096]{1,0:T(8,128)(2,1)} %q.1, bf16[64,4096]{1,0:T(8,128)(2,1)} %k0.1, bf16[64,4096]{1,0:T(8,128)(2,1)} %v0.1, ...), custom_call_target="tpu_custom_call" | custom-call | flops 268435456 | bytes 8388608 | tf_op jit(solution)/shard_map/attention/pallas_call | solution.py:166
  44.4 11.7 %collective-permute-done.6.second = bf16[20,4096]{1,0:T(8,128)(2,1)S(1)} collective-permute-done((bf16[20,4096]{1,0:T(8,128)(2,1)S(1)}, bf16[20,4096]{1,0:T(8,128)(2,1)S(1)}, u32[]{:S(2)}, u32[]{:S(2)}) %collective-permute-start.6) | collective-permute-done | bytes 163872 | tf_op jit(solution)/shard_map/ppermute | solution.py:415
  56.2 5.0 %collective-permute-start.9 = (bf16[40,4096]{1,0:T(8,128)(2,1)S(1)}, bf16[40,4096]{1,0:T(8,128)(2,1)S(1)}, u32[]{:S(2)}, u32[]{:S(2)}) collective-permute-start(bf16[40,4096]{1,0:T(8,128)(2,1)S(1)} %join.1.refs_0_), channel_id=1, source_target_pairs={{0,6},{1,7},{2,4},{3,5},{4,2},{5,3},{6,0},{7,1},{8,14},{9,15},{10,... | collective-permute-start | bytes 983048 | tf_op jit(solution)/shard_map/ppermute | solution.py:386
  61.2 3.6 %collective-permute-start.8 = (bf16[40,4096]{1,0:T(8,128)(2,1)S(1)}, bf16[40,4096]{1,0:T(8,128)(2,1)S(1)}, u32[]{:S(2)}, u32[]{:S(2)}) collective-permute-start(bf16[40,4096]{1,0:T(8,128)(2,1)S(1)} %join.1.refs_0_), channel_id=1, source_target_pairs={{0,4},{1,5},{2,6},{3,7},{4,0},{5,1},{6,2},{7,3},{8,12},{9,13},{10,... | collective-permute-start | bytes 983048 | tf_op jit(solution)/shard_map/ppermute | solution.py:386
  64.8 5.0 %collective-permute-done.9.refs_3_ = bf16[40,4096]{1,0:T(8,128)(2,1)S(1)} collective-permute-done((bf16[40,4096]{1,0:T(8,128)(2,1)S(1)}, bf16[40,4096]{1,0:T(8,128)(2,1)S(1)}, u32[]{:S(2)}, u32[]{:S(2)}) %collective-permute-start.9) | collective-permute-done | bytes 327712 | tf_op jit(solution)/shard_map/ppermute | solution.py:386
  69.8 8.5 %collective-permute-done.8.refs_2_ = bf16[40,4096]{1,0:T(8,128)(2,1)S(1)} collective-permute-done((bf16[40,4096]{1,0:T(8,128)(2,1)S(1)}, bf16[40,4096]{1,0:T(8,128)(2,1)S(1)}, u32[]{:S(2)}, u32[]{:S(2)}) %collective-permute-start.8) | collective-permute-done | bytes 327712 | tf_op jit(solution)/shard_map/ppermute | solution.py:386
  78.5 3.0 %collective-permute-done.10.x = bf16[160,4096]{1,0:T(8,128)(2,1)S(1)} collective-permute-done((bf16[160,4096]{1,0:T(8,128)(2,1)S(1)}, bf16[160,4096]{1,0:T(8,128)(2,1)S(1)}, u32[]{:S(2)}, u32[]{:S(2)}) %collective-permute-start.10) | collective-permute-done | bytes 1310752 | tf_op jit(solution)/shard_map/ppermute | solution.py:386
  81.5 3.4 %copy-done.3 = bf16[4096,1024]{1,0:T(8,128)(2,1)S(1)} copy-done((bf16[4096,1024]{1,0:T(8,128)(2,1)S(1)}, bf16[4096,1024]{1,0:T(8,128)(2,1)}, u32[]{:S(2)}) %copy-start.3) | copy-done | bytes 8388632
  84.9 3.4 %copy-done.6 = bf16[1024,4096]{1,0:T(8,128)(2,1)S(1)} copy-done((bf16[1024,4096]{1,0:T(8,128)(2,1)S(1)}, bf16[1024,4096]{1,0:T(8,128)(2,1)}, u32[]{:S(2)}) %copy-start.6) | copy-done | bytes 8388632
  88.3 6.4 %experts.3 = bf16[160,4096]{1,0:T(8,128)(2,1)S(1)} custom-call(bf16[160,4096]{1,0:T(8,128)(2,1)S(1)} %collective-permute-done.10.x, bf16[4096,1024]{1,0:T(8,128)(2,1)S(1)} %copy-done.1, bf16[4096,1024]{1,0:T(8,128)(2,1)S(1)} %copy-done.3, bf16[1024,4096]{1,0:T(8,128)(2,1)S(1)} %copy-done.6), custom_call_target="tpu_custom_call" | custom-call | flops 4026531840 | bytes 2621440 | tf_op jit(solution)/shard_map/experts/pallas_call | solution.py:257
  94.9 6.4 %experts.2.first = bf16[160,4096]{1,0:T(8,128)(2,1)S(1)} custom-call(bf16[160,4096]{1,0:T(8,128)(2,1)S(1)} %pile.1.x, bf16[4096,1024]{1,0:T(8,128)(2,1)S(1)} %copy-done.1, bf16[4096,1024]{1,0:T(8,128)(2,1)S(1)} %copy-done.4, bf16[1024,4096]{1,0:T(8,128)(2,1)S(1)} %copy-done.6), custom_call_target="tpu_custom_call" | custom-call | flops 4026531840 | bytes 2621440 | tf_op jit(solution)/shard_map/experts/pallas_call | solution.py:257
  105.1 6.5 %collective-permute-done.12.refs_1_ = bf16[40,4096]{1,0:T(8,128)(2,1)S(1)} collective-permute-done((bf16[40,4096]{1,0:T(8,128)(2,1)S(1)}, bf16[40,4096]{1,0:T(8,128)(2,1)S(1)}, u32[]{:S(2)}, u32[]{:S(2)}) %collective-permute-start.12) | collective-permute-done | bytes 327712 | tf_op jit(solution)/shard_map/ppermute | solution.py:386
  113.6 6.2 %collective-permute-done.14.refs_3_ = bf16[40,4096]{1,0:T(8,128)(2,1)S(1)} collective-permute-done((bf16[40,4096]{1,0:T(8,128)(2,1)S(1)}, bf16[40,4096]{1,0:T(8,128)(2,1)S(1)}, u32[]{:S(2)}, u32[]{:S(2)}) %collective-permute-start.14) | collective-permute-done | bytes 327712 | tf_op jit(solution)/shard_map/ppermute | solution.py:386
  120.1 10.9 %collective-permute-done.15.other = bf16[20,4096]{1,0:T(8,128)(2,1)S(1)} collective-permute-done((bf16[20,4096]{1,0:T(8,128)(2,1)S(1)}, bf16[20,4096]{1,0:T(8,128)(2,1)S(1)}, u32[]{:S(2)}, u32[]{:S(2)}) %collective-permute-start.15) | collective-permute-done | bytes 163872 | tf_op jit(solution)/shard_map/ppermute | solution.py:424
  (35 shorter events, 12.8 us)
Async XLA Ops:
  1.1 23.2 %collective-permute-start = (bf16[80,4096]{1,0:T(8,128)(2,1)S(1)}, bf16[80,4096]{1,0:T(8,128)(2,1)S(1)}, u32[]{:S(2)}, u32[]{:S(2)}) collective-permute-start(bf16[80,4096]{1,0:T(8,128)(2,1)S(1)} %bundle.1), channel_id=1, source_target_pairs={{0,2},{1,3},{2,4},{3,5},{4,6},{5,7},{6,8},{7,9},{8,10},{9,11},{10,... | collective-permute-start | bytes 1966088 | tf_op jit(solution)/shard_map/ppermute | solution.py:391
  6.0 30.1 %collective-permute-start.1 = (bf16[64,4096]{1,0:T(8,128)(2,1)}, bf16[64,4096]{1,0:T(8,128)(2,1)S(1)}, u32[]{:S(2)}, u32[]{:S(2)}) collective-permute-start(bf16[64,4096]{1,0:T(8,128)(2,1)} %v0.1), channel_id=1, source_target_pairs={{0,2},{1,3},{2,4},{3,5},{4,6},{5,7},{6,8},{7,9},{8,10},{9,11},{10,... | collective-permute-start | bytes 1572872 | tf_op jit(solution)/shard_map/ppermute | solution.py:389
  9.4 27.6 %collective-permute-start.2 = (bf16[80,4096]{1,0:T(8,128)(2,1)S(1)}, bf16[80,4096]{1,0:T(8,128)(2,1)S(1)}, u32[]{:S(2)}, u32[]{:S(2)}) collective-permute-start(bf16[80,4096]{1,0:T(8,128)(2,1)S(1)} %bundle.1), channel_id=1, source_target_pairs={{0,1},{2,3},{4,5},{6,7},{8,9},{10,11},{12,13},{14,15},{1,4},{3,6},... | collective-permute-start | bytes 1966088 | tf_op jit(solution)/shard_map/ppermute | solution.py:393
  14.3 3.2 %copy-start = (bf16[4096,1024]{1,0:T(8,128)(2,1)}, bf16[4096,1024]{1,0:T(8,128)(2,1)S(1)}, u32[]{:S(2)}) copy-start(bf16[4096,1024]{1,0:T(8,128)(2,1)S(1)} %fetch.3.w_gate) | copy-start | bytes 25165828
  21.0 3.3 %copy-start.2 = (bf16[4096,1024]{1,0:T(8,128)(2,1)}, bf16[4096,1024]{1,0:T(8,128)(2,1)S(1)}, u32[]{:S(2)}) copy-start(bf16[4096,1024]{1,0:T(8,128)(2,1)S(1)} %fetch.4.w_up) | copy-start | bytes 25165828
  24.3 14.3 %collective-permute-start.4 = (bf16[80,4096]{1,0:T(8,128)(2,1)S(1)}, bf16[80,4096]{1,0:T(8,128)(2,1)S(1)}, u32[]{:S(2)}, u32[]{:S(2)}) collective-permute-start(bf16[80,4096]{1,0:T(8,128)(2,1)S(1)} %collective-permute-done.k1.seg1), channel_id=1, source_target_pairs={{0,1},{1,0},{2,3},{3,2},{4,5},{5,4},{6,7},{7,6},{8,9},{9,8},{10,11... | collective-permute-start | bytes 1966088 | tf_op jit(solution)/shard_map/ppermute | solution.py:386
  26.5 10.5 %collective-permute-start.3 = (bf16[64,4096]{1,0:T(8,128)(2,1)}, bf16[64,4096]{1,0:T(8,128)(2,1)}, u32[]{:S(2)}, u32[]{:S(2)}) collective-permute-start(bf16[64,4096]{1,0:T(8,128)(2,1)} %v0.1), channel_id=1, source_target_pairs={{0,1},{2,3},{4,5},{6,7},{8,9},{10,11},{12,13},{14,15},{1,4},{3,6},... | collective-permute-start | bytes 1572872 | tf_op jit(solution)/shard_map/ppermute | solution.py:392
  32.8 3.3 %copy-start.5 = (bf16[1024,4096]{1,0:T(8,128)(2,1)}, bf16[1024,4096]{1,0:T(8,128)(2,1)S(1)}, u32[]{:S(2)}) copy-start(bf16[1024,4096]{1,0:T(8,128)(2,1)S(1)} %fetch.5.w_down) | copy-start | bytes 25165828
  36.1 2.5 %collective-permute-start.5 = (bf16[64,4096]{1,0:T(8,128)(2,1)S(1)}, bf16[64,4096]{1,0:T(8,128)(2,1)}, u32[]{:S(2)}, u32[]{:S(2)}) collective-permute-start(bf16[64,4096]{1,0:T(8,128)(2,1)S(1)} %collective-permute-done.1.v1), channel_id=1, source_target_pairs={{0,1},{1,0},{2,3},{3,2},{4,5},{5,4},{6,7},{7,6},{8,9},{9,8},{10,11... | collective-permute-start | bytes 1572872 | tf_op jit(solution)/shard_map/ppermute | solution.py:386
  37.0 44.5 %copy-start.1 = (bf16[4096,1024]{1,0:T(8,128)(2,1)S(1)}, bf16[4096,1024]{1,0:T(8,128)(2,1)}, u32[]{:S(2)}) copy-start(bf16[4096,1024]{1,0:T(8,128)(2,1)} %copy-done) | copy-start | bytes 25165828
  44.3 11.8 %collective-permute-start.6 = (bf16[20,4096]{1,0:T(8,128)(2,1)S(1)}, bf16[20,4096]{1,0:T(8,128)(2,1)S(1)}, u32[]{:S(2)}, u32[]{:S(2)}) collective-permute-start(bf16[20,4096]{1,0:T(8,128)(2,1)S(1)} %get-tuple-element.25), channel_id=1, source_target_pairs={{0,8},{1,9},{2,10},{3,11},{4,12},{5,13},{6,14},{7,15},{8,0},{9,1},... | collective-permute-start | bytes 491528 | tf_op jit(solution)/shard_map/ppermute | solution.py:415
  56.2 13.6 %collective-permute-start.9 = (bf16[40,4096]{1,0:T(8,128)(2,1)S(1)}, bf16[40,4096]{1,0:T(8,128)(2,1)S(1)}, u32[]{:S(2)}, u32[]{:S(2)}) collective-permute-start(bf16[40,4096]{1,0:T(8,128)(2,1)S(1)} %join.1.refs_0_), channel_id=1, source_target_pairs={{0,6},{1,7},{2,4},{3,5},{4,2},{5,3},{6,0},{7,1},{8,14},{9,15},{10,... | collective-permute-start | bytes 983048 | tf_op jit(solution)/shard_map/ppermute | solution.py:386
  61.2 17.1 %collective-permute-start.8 = (bf16[40,4096]{1,0:T(8,128)(2,1)S(1)}, bf16[40,4096]{1,0:T(8,128)(2,1)S(1)}, u32[]{:S(2)}, u32[]{:S(2)}) collective-permute-start(bf16[40,4096]{1,0:T(8,128)(2,1)S(1)} %join.1.refs_0_), channel_id=1, source_target_pairs={{0,4},{1,5},{2,6},{3,7},{4,0},{5,1},{6,2},{7,3},{8,12},{9,13},{10,... | collective-permute-start | bytes 983048 | tf_op jit(solution)/shard_map/ppermute | solution.py:386
  64.8 13.5 %collective-permute-start.7 = (bf16[40,4096]{1,0:T(8,128)(2,1)S(1)}, bf16[40,4096]{1,0:T(8,128)(2,1)S(1)}, u32[]{:S(2)}, u32[]{:S(2)}) collective-permute-start(bf16[40,4096]{1,0:T(8,128)(2,1)S(1)} %join.1.refs_0_), channel_id=1, source_target_pairs={{0,2},{1,3},{2,0},{3,1},{4,6},{5,7},{6,4},{7,5},{8,10},{9,11},{10,... | collective-permute-start | bytes 983048 | tf_op jit(solution)/shard_map/ppermute | solution.py:386
  78.4 3.1 %collective-permute-start.10 = (bf16[160,4096]{1,0:T(8,128)(2,1)S(1)}, bf16[160,4096]{1,0:T(8,128)(2,1)S(1)}, u32[]{:S(2)}, u32[]{:S(2)}) collective-permute-start(bf16[160,4096]{1,0:T(8,128)(2,1)S(1)} %pile.1.x), channel_id=1, source_target_pairs={{0,1},{1,0},{2,3},{3,2},{4,5},{5,4},{6,7},{7,6},{8,9},{9,8},{10,11... | collective-permute-start | bytes 3932168 | tf_op jit(solution)/shard_map/ppermute | solution.py:386
  81.5 3.4 %copy-start.3 = (bf16[4096,1024]{1,0:T(8,128)(2,1)S(1)}, bf16[4096,1024]{1,0:T(8,128)(2,1)}, u32[]{:S(2)}) copy-start(bf16[4096,1024]{1,0:T(8,128)(2,1)} %copy-done.2) | copy-start | bytes 25165828
  84.9 3.4 %copy-start.6 = (bf16[1024,4096]{1,0:T(8,128)(2,1)S(1)}, bf16[1024,4096]{1,0:T(8,128)(2,1)}, u32[]{:S(2)}) copy-start(bf16[1024,4096]{1,0:T(8,128)(2,1)} %copy-done.5) | copy-start | bytes 25165828
  88.3 6.6 %copy-start.4 = (bf16[4096,1024]{1,0:T(8,128)(2,1)S(1)}, bf16[4096,1024]{1,0:T(8,128)(2,1)}, u32[]{:S(2)}) copy-start(bf16[4096,1024]{1,0:T(8,128)(2,1)} %copy-done.2) | copy-start | bytes 25165828
  94.7 6.6 %collective-permute-start.11 = (bf16[160,4096]{1,0:T(8,128)(2,1)S(1)}, bf16[160,4096]{1,0:T(8,128)(2,1)S(1)}, u32[]{:S(2)}, u32[]{:S(2)}) collective-permute-start(bf16[160,4096]{1,0:T(8,128)(2,1)S(1)} %experts.3), channel_id=1, source_target_pairs={{0,1},{1,0},{2,3},{3,2},{4,5},{5,4},{6,7},{7,6},{8,9},{9,8},{10,11... | collective-permute-start | bytes 3932168 | tf_op jit(solution)/shard_map/ppermute | solution.py:386
  101.6 10.0 %collective-permute-start.12 = (bf16[40,4096]{1,0:T(8,128)(2,1)S(1)}, bf16[40,4096]{1,0:T(8,128)(2,1)S(1)}, u32[]{:S(2)}, u32[]{:S(2)}) collective-permute-start(bf16[40,4096]{1,0:T(8,128)(2,1)S(1)} %get-tuple-element.30), channel_id=1, source_target_pairs={{0,2},{1,3},{2,0},{3,1},{4,6},{5,7},{6,4},{7,5},{8,10},{9,11},{10,... | collective-permute-start | bytes 983048 | tf_op jit(solution)/shard_map/ppermute | solution.py:386
  103.1 10.6 %collective-permute-start.13 = (bf16[40,4096]{1,0:T(8,128)(2,1)S(1)}, bf16[40,4096]{1,0:T(8,128)(2,1)S(1)}, u32[]{:S(2)}, u32[]{:S(2)}) collective-permute-start(bf16[40,4096]{1,0:T(8,128)(2,1)S(1)} %get-tuple-element.31), channel_id=1, source_target_pairs={{0,4},{1,5},{2,6},{3,7},{4,0},{5,1},{6,2},{7,3},{8,12},{9,13},{10,... | collective-permute-start | bytes 983048 | tf_op jit(solution)/shard_map/ppermute | solution.py:386
  103.1 16.7 %collective-permute-start.14 = (bf16[40,4096]{1,0:T(8,128)(2,1)S(1)}, bf16[40,4096]{1,0:T(8,128)(2,1)S(1)}, u32[]{:S(2)}, u32[]{:S(2)}) collective-permute-start(bf16[40,4096]{1,0:T(8,128)(2,1)S(1)} %get-tuple-element.32), channel_id=1, source_target_pairs={{0,6},{1,7},{2,4},{3,5},{4,2},{5,3},{6,0},{7,1},{8,14},{9,15},{10,... | collective-permute-start | bytes 983048 | tf_op jit(solution)/shard_map/ppermute | solution.py:386
  120.0 11.0 %collective-permute-start.15 = (bf16[20,4096]{1,0:T(8,128)(2,1)S(1)}, bf16[20,4096]{1,0:T(8,128)(2,1)S(1)}, u32[]{:S(2)}, u32[]{:S(2)}) collective-permute-start(bf16[20,4096]{1,0:T(8,128)(2,1)S(1)} %get-tuple-element.34), channel_id=1, source_target_pairs={{0,8},{1,9},{2,10},{3,11},{4,12},{5,13},{6,14},{7,15},{8,0},{9,1},... | collective-permute-start | bytes 491528 | tf_op jit(solution)/shard_map/ppermute | solution.py:424

commit v6 on v4

--- a/solution.py
+++ b/solution.py
@@ -11,6 +11,7 @@
 E_WIN = 2
 WIN_DEV = 3
 CAP = 20
+EARLY = 16
 SPARE = 16
 HEADS_STEP = 8
 MASKED = -1e30
@@ -48,13 +49,14 @@
         cost_estimate=pl.CostEstimate(
             flops=0, bytes_accessed=4 * rows * width, transcendentals=0
         ),
+        compiler_params=pltpu.CompilerParams(vmem_limit_bytes=6 * MIB),
         name="bundle",
     )(far(keys), far(segs))
 
 
 def attention_kernel(
     deltas, q, k0, v0, k1, v1, k2, v2, k3, v3, seg0, seg1, seg2, seg3, resid, gain, routes, gates,
-    mixed_out, keep_out, send_out, weight_out, bias,
+    mixed_out, early_out, rest_out, send_out, weight_out, bias,
 ):
     step = pl.program_id(0)
     steps = pl.num_programs(0)
@@ -125,8 +127,8 @@
         upper = jnp.where(down < across, 1.0, 0.0).astype(jnp.bfloat16)
         eye = jnp.where(down == across, 1.0, 0.0).astype(jnp.bfloat16)
         slot = lax.broadcasted_iota(jnp.int32, (32, rows), 0)
-        for place, out in ((0, keep_out), (1, send_out)):
-            expert = deltas[4] if place == 0 else 1 - deltas[4]
+
+        def picks(expert):
             hit = routes[...] == expert
             member = jnp.max(jnp.where(hit, 1.0, 0.0), axis=0, keepdims=True)
             weight = jnp.sum(
@@ -137,18 +139,34 @@
                 upper,
                 preferred_element_type=jnp.float32,
             )[0:1].astype(jnp.int32)
-            pick = (slot == rank) & (member > 0.5)
-            out[...] = jnp.dot(
-                jnp.where(pick, 1.0, 0.0).astype(jnp.bfloat16),
-                normed,
-                preferred_element_type=jnp.float32,
-            )[:CAP].astype(jnp.bfloat16)
-            weight_out[place] = lax.dot_general(
+            return member > 0.5, weight, rank
+
+        def spread(pick, weight):
+            return lax.dot_general(
                 eye,
                 jnp.where(pick, weight, 0.0).astype(jnp.bfloat16),
                 (((1,), (1,)), ((), ())),
                 preferred_element_type=jnp.float32,
             ).astype(jnp.bfloat16)
+
+        def packed(pick):
+            return jnp.dot(
+                jnp.where(pick, 1.0, 0.0).astype(jnp.bfloat16),
+                normed,
+                preferred_element_type=jnp.float32,
+            ).astype(jnp.bfloat16)
+
+        member, weight, rank = picks(deltas[4])
+        pick = (slot == rank) & member
+        mine = packed(pick)
+        early_out[...] = mine[:EARLY]
+        rest_out[...] = mine[EARLY:CAP]
+        weight_out[0] = spread(pick & (slot < EARLY), weight)
+        weight_out[1] = spread((slot - CAP + EARLY == rank) & (slot >= CAP) & member, weight)
+        member, weight, rank = picks(1 - deltas[4])
+        pick = (slot == rank) & member
+        send_out[...] = packed(pick)[:CAP]
+        weight_out[2] = spread(pick, weight)
 
 
 def attention(deltas, q, pairs, seg_own, resid, gain, routes, gates):
@@ -178,17 +196,19 @@
             ],
             out_specs=[
                 whole((rows, width)),
+                whole((EARLY, width)),
+                whole((CAP - EARLY, width)),
                 whole((CAP, width)),
-                whole((CAP, width)),
-                whole((E_WIN, rows, 32)),
+                whole((3, rows, 32)),
             ],
             scratch_shapes=[pltpu.VMEM((rows, (WIN_DEV + 1) * rows), jnp.float32)],
         ),
         out_shape=[
             pltpu.VMEM((rows, width), jnp.float32),
+            jax.ShapeDtypeStruct((EARLY, width), jnp.bfloat16),
+            jax.ShapeDtypeStruct((CAP - EARLY, width), jnp.bfloat16),
             jax.ShapeDtypeStruct((CAP, width), jnp.bfloat16),
-            jax.ShapeDtypeStruct((CAP, width), jnp.bfloat16),
-            jax.ShapeDtypeStruct((E_WIN, rows, 32), jnp.bfloat16),
+            jax.ShapeDtypeStruct((3, rows, 32), jnp.bfloat16),
         ],
         compiler_params=pltpu.CompilerParams(vmem_limit_bytes=14 * MIB),
         cost_estimate=pl.CostEstimate(
@@ -231,9 +251,12 @@
     )(far(weights), after)
 
 
-def experts_kernel(x, w_gate, w_up, w_down, out, hidden):
+def experts_kernel(local, remote, w_gate, w_up, w_down, local_out, remote_out, x, hidden):
     width, units = w_gate.shape
     tile = min(256, units)
+    rows = local.shape[0]
+    x[:rows] = local[...]
+    x[rows:] = remote[...]
 
     @pl.loop(0, units // tile)
     def _(part):
@@ -245,28 +268,31 @@
     @pl.loop(0, width // 512)
     def _(part):
         at = pl.ds(pl.multiple_of(part * 512, 512), 512)
-        out[:, at] = jnp.dot(
-            hidden[...], w_down[:, at], preferred_element_type=jnp.float32
-        ).astype(jnp.bfloat16)
-
-
-def experts(x, w_gate, w_up, w_down):
-    rows, width = x.shape
+        out = jnp.dot(hidden[...], w_down[:, at], preferred_element_type=jnp.float32)
+        local_out[:, at] = out[:rows].astype(jnp.bfloat16)
+        remote_out[:, at] = out[rows:].astype(jnp.bfloat16)
+
+
+def experts(local, remote, w_gate, w_up, w_down):
+    rows, width = local.shape
     units = w_gate.shape[1]
     return pl.pallas_call(
         experts_kernel,
-        in_specs=[NEAR] * 4,
-        out_specs=NEAR,
-        out_shape=jax.ShapeDtypeStruct((rows, width), jnp.bfloat16),
-        scratch_shapes=[pltpu.VMEM((rows, units), jnp.bfloat16)],
+        in_specs=[NEAR] * 5,
+        out_specs=[NEAR] * 2,
+        out_shape=[jax.ShapeDtypeStruct((rows, width), jnp.bfloat16)] * 2,
+        scratch_shapes=[
+            pltpu.VMEM((2 * rows, width), jnp.bfloat16),
+            pltpu.VMEM((2 * rows, units), jnp.bfloat16),
+        ],
         compiler_params=pltpu.CompilerParams(vmem_limit_bytes=20 * MIB),
         cost_estimate=pl.CostEstimate(
-            flops=6 * rows * width * units,
-            bytes_accessed=4 * rows * width,
-            transcendentals=rows * units,
+            flops=12 * rows * width * units,
+            bytes_accessed=8 * rows * width,
+            transcendentals=2 * rows * units,
         ),
         name="experts",
-    )(x, close(w_gate), close(w_up), close(w_down))
+    )(local, remote, close(w_gate), close(w_up), close(w_down))
 
 
 def join_kernel(first, second, out):
@@ -282,6 +308,7 @@
         in_specs=[NEAR, NEAR],
         out_specs=NEAR,
         out_shape=jax.ShapeDtypeStruct((first.shape[0] + second.shape[0], width), first.dtype),
+        compiler_params=pltpu.CompilerParams(vmem_limit_bytes=8 * MIB),
         name="join",
     )(first, second)
 
@@ -300,7 +327,7 @@
         in_specs=[NEAR] * len(blocks),
         out_specs=NEAR,
         out_shape=jax.ShapeDtypeStruct((len(blocks) * rows, width), blocks[0].dtype),
-        compiler_params=pltpu.CompilerParams(vmem_limit_bytes=24 * MIB),
+        compiler_params=pltpu.CompilerParams(vmem_limit_bytes=(4 + len(blocks)) * MIB),
         name="pile",
     )(*blocks)
 
@@ -322,48 +349,58 @@
         in_specs=[NEAR, NEAR],
         out_specs=[NEAR] * blocks,
         out_shape=[jax.ShapeDtypeStruct((each, width), first.dtype)] * blocks,
-        compiler_params=pltpu.CompilerParams(vmem_limit_bytes=24 * MIB),
+        compiler_params=pltpu.CompilerParams(vmem_limit_bytes=(6 + blocks) * MIB),
         name="add_split",
     )(first, second)
 
 
 def total_kernel(*refs):
-    blocks, own_out, back_out = refs[:-2], refs[-2], refs[-1]
+    blocks, all_out, back_out = refs[:-2], refs[-2], refs[-1]
     total = blocks[0][...].astype(jnp.float32)
     for block in blocks[1:]:
         total = total + block[...].astype(jnp.float32)
-    own_out[...] = total[:CAP].astype(own_out.dtype)
-    back_out[...] = total[CAP:].astype(back_out.dtype)
+    total = total.astype(all_out.dtype)
+    all_out[...] = total
+    back_out[...] = total[:CAP]
 
 
 def total_of(blocks):
-    width = blocks[0].shape[1]
+    rows, width = blocks[0].shape
     return pl.pallas_call(
         total_kernel,
         in_specs=[NEAR] * len(blocks),
         out_specs=[NEAR] * 2,
-        out_shape=[jax.ShapeDtypeStruct((CAP, width), blocks[0].dtype)] * 2,
+        out_shape=[
+            jax.ShapeDtypeStruct((rows, width), blocks[0].dtype),
+            jax.ShapeDtypeStruct((CAP, width), blocks[0].dtype),
+        ],
+        compiler_params=pltpu.CompilerParams(vmem_limit_bytes=(4 + len(blocks)) * MIB),
         name="total",
     )(*blocks)
 
 
-def combine_kernel(mixed, weight, own, other, out):
+def combine_kernel(mixed, weight, late, other, *refs):
+    blocks, out = refs[:-1], refs[-1]
+    early = blocks[0][...].astype(jnp.float32)
+    for block in blocks[1:]:
+        early = early + block[...].astype(jnp.float32)
     total = mixed[...]
-    for place, part in enumerate((own, other)):
+    for place, part in enumerate((early.astype(jnp.bfloat16), late[...], other[...])):
         total = total + jnp.dot(
-            weight[place][:, : part.shape[0]], part[...], preferred_element_type=jnp.float32
+            weight[place][:, : part.shape[0]], part, preferred_element_type=jnp.float32
         )
     out[...] = total.astype(jnp.bfloat16)
 
 
-def combine(mixed, weight, own, other):
+def combine(mixed, weight, blocks, late, other):
     return pl.pallas_call(
         combine_kernel,
-        in_specs=[NEAR] * 4,
+        in_specs=[NEAR] * (4 + len(blocks)),
         out_specs=NEAR,
         out_shape=jax.ShapeDtypeStruct(mixed.shape, jnp.bfloat16),
+        compiler_params=pltpu.CompilerParams(vmem_limit_bytes=(8 + len(blocks)) * MIB),
         name="combine",
-    )(close(mixed), weight, own, other)
+    )(close(mixed), weight, late, other, *blocks)
 
 
 def shards(
@@ -387,19 +424,19 @@
     key_two = lax.ppermute(key_block, "expert", next_chip)
     value_cross = lax.ppermute(values, "expert", crossing)
     key_cross = lax.ppermute(key_block, "expert", crossing)
-    value_mirror = swapped(value_two, 1)
-    key_mirror = swapped(key_two, 1)
-    held = [fetch(w, value_two) for w in (w_gate, w_up, w_down)]
-    key_cross, *held = lax.optimization_barrier((key_cross, *held))
-
     beyond = 2 * WIN_DEV + 2
     delta_list = [0 * own, 0 * own + 2, 3 - 2 * odd, 1 + 2 * odd]
     my_expert = own // shard_count
     scalars = jnp.stack(
         [jnp.where(own >= delta, delta, beyond) for delta in delta_list] + [my_expert]
     ).astype(jnp.int32)
-
-    mixed, keep, send, weight = attention(
+    held = [fetch(w, scalars) for w in (w_gate, w_up, w_down)]
+    key_two, held[0], held[1] = lax.optimization_barrier((key_two, held[0], held[1]))
+    key_mirror = swapped(key_two, 1)
+    value_two, held[2] = lax.optimization_barrier((value_two, held[2]))
+    value_mirror = swapped(value_two, 1)
+
+    mixed, early, rest, send, weight = attention(
         scalars,
         queries,
         [keys, values, key_two, value_two, key_cross, value_cross, key_mirror, value_mirror],
@@ -407,16 +444,33 @@
     )
     partner = [(i, (i + shard_count) % count) for i in range(count)]
     masks = range(2, shard_count, 2)
-    pair = join(keep, lax.ppermute(send, "expert", partner))
-    local = pile([pair] + [swapped(pair, mask) for mask in masks])
-    remote = swapped(local, 1)
-    local_part = experts(local, *held)
-    remote_part = experts(remote, *held)
-    blocks = add_split(local_part, swapped(remote_part, 1), 1 + len(masks))
-    own_sum, back = total_of(
-        [blocks[0]] + [swapped(block, mask) for block, mask in zip(blocks[1:], masks)]
-    )
-    return combine(mixed, weight, own_sum, lax.ppermute(back, "expert", partner))
+    got = lax.ppermute(send, "expert", partner)
+
+    def spread(block):
+        return [block] + [swapped(block, mask) for mask in masks]
+
+    def both_cores(blocks):
+        local = pile(blocks)
+        return local, swapped(local, 1)
+
+    def summed(parts):
+        return add_split(parts[0], swapped(parts[1], 1), 1 + len(masks))
+
+    def scattered(blocks):
+        return [blocks[0]] + [swapped(block, mask) for block, mask in zip(blocks[1:], masks)]
+
+    early_blocks = spread(early)
+    got, early_blocks = lax.optimization_barrier((got, early_blocks))
+    early_parts = experts(*both_cores(early_blocks), *held)
+    late_blocks = spread(join(got, rest))
+    late_blocks, early_parts = lax.optimization_barrier((late_blocks, early_parts))
+    late_rows = both_cores(late_blocks)
+    late_blocks = summed(experts(*late_rows, *held))
+    early_blocks = summed(early_parts)
+    late_blocks, early_blocks = lax.optimization_barrier((late_blocks, early_blocks))
+    late, back = total_of(scattered(late_blocks))
+    other = lax.ppermute(back, "expert", partner)
+    return combine(mixed, weight, scattered(early_blocks), late, other)
 
 
 def solution(mesh):

time: 167 us -> 116 us (0.69)
  local copies, waits for them, and re-layouts: 33.1 us -> 0.09 us
  waiting for transfers between devices: 69 us -> 39.6 us
  starting transfers between devices: 27.3 us -> 44.1 us
  Pallas kernels: 37.1 us -> 32 us
    unnamed x44 -> x2, local copies, waits for them, and re-layouts: 33 us -> 0.01 us
    ppermute x2, waiting for transfers between devices: 18.8 us -> 0.01 us  [the longest x1 0.01 us: shards(): got = lax.ppermute(send, 'expert', partner)]
    ppermute x10 -> x18, starting transfers between devices: 7.28 us -> 24.7 us  [swapped(): return lax.ppermute(block, 'expert', [(i, i ^ mask) for i in range(count)])]
    ppermute x1, waiting for transfers between devices: 10.6 us -> 3.11 us  [shards(): key_two = lax.ppermute(key_block, 'expert', next_chip)]
    ppermute x1, waiting for transfers between devices: 7.64 us -> 4.23 us  [shards(): value_two = lax.ppermute(values, 'expert', next_chip)]
    pallas_call x1, Pallas kernels: 2.14 us -> 0.1 us  [total_of(): pl.pallas_call(total_kernel, in_specs=[NEAR] * len(blocks), out_specs=[NE...]
    pallas_call x1, Pallas kernels: 1.8 us -> 0.03 us  [join(): pl.pallas_call(join_kernel, in_specs=[NEAR, NEAR], out_specs=NEAR, out_sh...]
    ppermute x10 -> x18, waiting for transfers between devices: 31.9 us -> 32.2 us  [swapped(): return lax.ppermute(block, 'expert', [(i, i ^ mask) for i in range(count)])]
  transfers between devices with their start and end apart: 16 -> 24, of which waited for: 11 -> 16; matrix products, arithmetic and copies ran while one was open for 0% -> 0% of each run, Pallas kernels for 10% -> 14%
where the time goes in v6:
time: 116 us
  starting transfers between devices  44.1 us (38%)
  waiting for transfers between devices  39.6 us (34%)
  Pallas kernels  32 us (28%)
    ppermute x18, waiting for transfers between devices, swapped(): return lax.ppermute(block, 'expert', [(i, i ^ mask) for i in range(count)])  32.2 us
    ppermute x18, starting transfers between devices, swapped(): return lax.ppermute(block, 'expert', [(i, i ^ mask) for i in range(count)])  24.7 us
    pallas_call x2, Pallas kernels, experts(): pl.pallas_call(experts_kernel, in_specs=[NEAR] * 5, out_specs=[NEAR] * 2,...  13.1 us
    pallas_call x3, Pallas kernels, fetch(): pl.pallas_call(functools.partial(fetch_kernel, parts), in_specs=[anywhere...  10.6 us
    ppermute x1, starting transfers between devices, shards(): got = lax.ppermute(send, 'expert', partner)  5.56 us
    pallas_call x1, Pallas kernels, attention(): pl.pallas_call(attention_kernel, grid_spec=pltpu.PrefetchScalarGridSpec(n...  5.3 us
    ppermute x1, starting transfers between devices, shards(): key_two = lax.ppermute(key_block, 'expert', next_chip)  4.91 us
    ppermute x1, waiting for transfers between devices, shards(): value_two = lax.ppermute(values, 'expert', next_chip)  4.23 us
  transfers between devices with their start and end apart: 24, of which 16 were waited for; matrix products, arithmetic and copies ran while one was open for 0% of the time, Pallas kernels for 14%

profile of v6, /device:TPU:0, one launch (start us, length us, event | category | flops | bytes accessed | tf_op | source)
XLA Modules:
  0.0 115.9 jit_solution(11040359086282552935)
XLA Ops:
  1.1 4.9 %collective-permute-start = (bf16[80,4096]{1,0:T(8,128)(2,1)S(1)}, bf16[80,4096]{1,0:T(8,128)(2,1)S(1)}, u32[]{:S(2)}, u32[]{:S(2)}) collective-permute-start(bf16[80,4096]{1,0:T(8,128)(2,1)S(1)} %bundle.1), channel_id=1, source_target_pairs={{0,2},{1,3},{2,4},{3,5},{4,6},{5,7},{6,8},{7,9},{8,10},{9,11},{10,... | collective-permute-start | bytes 1966088 | tf_op jit(solution)/shard_map/ppermute | solution.py:424
  6.0 3.4 %collective-permute-start.1 = (bf16[64,4096]{1,0:T(8,128)(2,1)}, bf16[64,4096]{1,0:T(8,128)(2,1)S(1)}, u32[]{:S(2)}, u32[]{:S(2)}) collective-permute-start(bf16[64,4096]{1,0:T(8,128)(2,1)} %v0.1), channel_id=1, source_target_pairs={{0,2},{1,3},{2,4},{3,5},{4,6},{5,7},{6,8},{7,9},{8,10},{9,11},{10,... | collective-permute-start | bytes 1572872 | tf_op jit(solution)/shard_map/ppermute | solution.py:422
  10.9 3.5 %fetch.3.w_gate = bf16[4096,1024]{1,0:T(8,128)(2,1)S(1)} custom-call(bf16[4096,1024]{1,0:T(8,128)(2,1)} %source.3, s32[5]{0:T(128)S(1)} %stack.23.after.deltas), custom_call_target="tpu_custom_call" | custom-call | bytes 16777216 | tf_op jit(solution)/shard_map/fetch/pallas_call | solution.py:240
  14.4 3.6 %fetch.4.w_up = bf16[4096,1024]{1,0:T(8,128)(2,1)S(1)} custom-call(bf16[4096,1024]{1,0:T(8,128)(2,1)} %source.4, s32[5]{0:T(128)S(1)} %stack.23.after.deltas), custom_call_target="tpu_custom_call" | custom-call | bytes 16777216 | tf_op jit(solution)/shard_map/fetch/pallas_call | solution.py:240
  18.0 3.1 %collective-permute-done.k1.seg1 = bf16[80,4096]{1,0:T(8,128)(2,1)S(1)} collective-permute-done((bf16[80,4096]{1,0:T(8,128)(2,1)S(1)}, bf16[80,4096]{1,0:T(8,128)(2,1)S(1)}, u32[]{:S(2)}, u32[]{:S(2)}) %collective-permute-start) | collective-permute-done | bytes 655392 | tf_op jit(solution)/shard_map/ppermute | solution.py:424
  21.1 2.4 %collective-permute-start.3 = (bf16[64,4096]{1,0:T(8,128)(2,1)S(1)}, bf16[64,4096]{1,0:T(8,128)(2,1)S(1)}, u32[]{:S(2)}, u32[]{:S(2)}) collective-permute-start(bf16[64,4096]{1,0:T(8,128)(2,1)S(1)} %copy-done), channel_id=1, source_target_pairs={{0,1},{2,3},{4,5},{6,7},{8,9},{10,11},{12,13},{14,15},{1,4},{3,6},... | collective-permute-start | bytes 1572872 | tf_op jit(solution)/shard_map/ppermute | solution.py:425
  23.5 3.5 %fetch.5.w_down = bf16[1024,4096]{1,0:T(8,128)(2,1)S(1)} custom-call(bf16[1024,4096]{1,0:T(8,128)(2,1)} %source.5, s32[5]{0:T(128)S(1)} %stack.23.after.deltas), custom_call_target="tpu_custom_call" | custom-call | bytes 16777216 | tf_op jit(solution)/shard_map/fetch/pallas_call | solution.py:240
  27.0 4.2 %collective-permute-done.1.v1 = bf16[64,4096]{1,0:T(8,128)(2,1)S(1)} collective-permute-done((bf16[64,4096]{1,0:T(8,128)(2,1)}, bf16[64,4096]{1,0:T(8,128)(2,1)S(1)}, u32[]{:S(2)}, u32[]{:S(2)}) %collective-permute-start.1) | collective-permute-done | bytes 524320 | tf_op jit(solution)/shard_map/ppermute | solution.py:422
  33.2 5.3 %attention.1 = (f32[64,4096]{1,0:T(8,128)S(1)}, bf16[16,4096]{1,0:T(8,128)(2,1)S(1)}, bf16[4,4096]{1,0:T(4,128)(2,1)S(1)}, bf16[20,4096]{1,0:T(8,128)(2,1)S(1)}, bf16[3,64,32]{2,1,0:T(8,128)(2,1)S(1)}) custom-call(s32[5]{0:T(128)S(1)} %stack.23.after.deltas, bf16[64,4096]{1,0:T(8,128)(2,1)} %q.1, bf16[64,4096]{1,0:T(8,128)(2,1)} %k0.1, bf16[64,4096]{1,0:T(8,128)(2,1)} %v0.1, ...), custom_call_target="tpu_custom_call" | custom-call | flops 268435456 | bytes 8388608 | tf_op jit(solution)/shard_map/attention/pallas_call | solution.py:183
  38.5 5.6 %collective-permute-start.6 = (bf16[20,4096]{1,0:T(8,128)(2,1)S(1)}, bf16[20,4096]{1,0:T(8,128)(2,1)S(1)}, u32[]{:S(2)}, u32[]{:S(2)}) collective-permute-start(bf16[20,4096]{1,0:T(8,128)(2,1)S(1)} %get-tuple-element.52), channel_id=1, source_target_pairs={{0,8},{1,9},{2,10},{3,11},{4,12},{5,13},{6,14},{7,15},{8,0},{9,1},... | collective-permute-start | bytes 491528 | tf_op jit(solution)/shard_map/ppermute | solution.py:447
  44.1 11.2 %collective-permute-start.9 = (bf16[16,4096]{1,0:T(8,128)(2,1)S(1)}, bf16[16,4096]{1,0:T(8,128)(2,1)S(1)}, u32[]{:S(2)}, u32[]{:S(2)}) collective-permute-start(bf16[16,4096]{1,0:T(8,128)(2,1)S(1)} %get-tuple-element.56.refs_0_), channel_id=1, source_target_pairs={{0,6},{1,7},{2,4},{3,5},{4,2},{5,3},{6,0},{7,1},{8,14},{9,15},{10,... | collective-permute-start | bytes 393224 | tf_op jit(solution)/shard_map/ppermute | solution.py:419
  55.8 3.2 %collective-permute-done.9.refs_3_ = bf16[16,4096]{1,0:T(8,128)(2,1)S(1)} collective-permute-done((bf16[16,4096]{1,0:T(8,128)(2,1)S(1)}, bf16[16,4096]{1,0:T(8,128)(2,1)S(1)}, u32[]{:S(2)}, u32[]{:S(2)}) %collective-permute-start.9) | collective-permute-done | bytes 131104 | tf_op jit(solution)/shard_map/ppermute | solution.py:419
  61.0 4.5 %collective-permute-start.12 = (bf16[24,4096]{1,0:T(8,128)(2,1)S(1)}, bf16[24,4096]{1,0:T(8,128)(2,1)S(1)}, u32[]{:S(2)}, u32[]{:S(2)}) collective-permute-start(bf16[24,4096]{1,0:T(8,128)(2,1)S(1)} %join.1.refs_0_), channel_id=1, source_target_pairs={{0,6},{1,7},{2,4},{3,5},{4,2},{5,3},{6,0},{7,1},{8,14},{9,15},{10,... | collective-permute-start | bytes 589832 | tf_op jit(solution)/shard_map/ppermute | solution.py:419
  66.2 5.8 %experts.2 = (bf16[64,4096]{1,0:T(8,128)(2,1)S(1)}, bf16[64,4096]{1,0:T(8,128)(2,1)S(1)}) custom-call(bf16[64,4096]{1,0:T(8,128)(2,1)S(1)} %pile.2.local, bf16[64,4096]{1,0:T(8,128)(2,1)S(1)} %collective-permute-done.13.remote, bf16[4096,1024]{1,0:T(8,128)(2,1)S(1)} %fetch.3.w_gate, bf16[4096,1024]{1,0:T(8,128)(2,1)S(1)} %fetch.4.w_up, ...), custom_call_target="tpu_custom_call" | custom-call | flops 3221225472 | bytes 2097152 | tf_op jit(solution)/shard_map/experts/pallas_call | solution.py:279
  72.0 2.6 %collective-permute-done.11.refs_2_ = bf16[24,4096]{1,0:T(8,128)(2,1)S(1)} collective-permute-done((bf16[24,4096]{1,0:T(8,128)(2,1)S(1)}, bf16[24,4096]{1,0:T(8,128)(2,1)S(1)}, u32[]{:S(2)}, u32[]{:S(2)}) %collective-permute-start.11) | collective-permute-done | bytes 196640 | tf_op jit(solution)/shard_map/ppermute | solution.py:419
  75.5 2.2 %collective-permute-done.14.remote = bf16[96,4096]{1,0:T(8,128)(2,1)S(1)} collective-permute-done((bf16[96,4096]{1,0:T(8,128)(2,1)S(1)}, bf16[96,4096]{1,0:T(8,128)(2,1)S(1)}, u32[]{:S(2)}, u32[]{:S(2)}) %collective-permute-start.14) | collective-permute-done | bytes 786464 | tf_op jit(solution)/shard_map/ppermute | solution.py:419
  77.7 7.3 %experts.3 = (bf16[96,4096]{1,0:T(8,128)(2,1)S(1)}, bf16[96,4096]{1,0:T(8,128)(2,1)S(1)}) custom-call(bf16[96,4096]{1,0:T(8,128)(2,1)S(1)} %pile.3.local, bf16[96,4096]{1,0:T(8,128)(2,1)S(1)} %collective-permute-done.14.remote, bf16[4096,1024]{1,0:T(8,128)(2,1)S(1)} %fetch.3.w_gate, bf16[4096,1024]{1,0:T(8,128)(2,1)S(1)} %fetch.4.w_up, ...), custom_call_target="tpu_custom_call" | custom-call | flops 4831838208 | bytes 3145728 | tf_op jit(solution)/shard_map/experts/pallas_call | solution.py:279
  85.6 2.5 %collective-permute-done.16.second = bf16[64,4096]{1,0:T(8,128)(2,1)S(1)} collective-permute-done((bf16[64,4096]{1,0:T(8,128)(2,1)S(1)}, bf16[64,4096]{1,0:T(8,128)(2,1)S(1)}, u32[]{:S(2)}, u32[]{:S(2)}) %collective-permute-start.16) | collective-permute-done | bytes 524320 | tf_op jit(solution)/shard_map/ppermute | solution.py:419
  89.2 2.5 %collective-permute-start.18 = (bf16[24,4096]{1,0:T(8,128)(2,1)S(1)}, bf16[24,4096]{1,0:T(8,128)(2,1)S(1)}, u32[]{:S(2)}, u32[]{:S(2)}) collective-permute-start(bf16[24,4096]{1,0:T(8,128)(2,1)S(1)} %get-tuple-element.83), channel_id=1, source_target_pairs={{0,4},{1,5},{2,6},{3,7},{4,0},{5,1},{6,2},{7,3},{8,12},{9,13},{10,... | collective-permute-start | bytes 589832 | tf_op jit(solution)/shard_map/ppermute | solution.py:419
  92.0 3.5 %collective-permute-done.17.refs_1_ = bf16[24,4096]{1,0:T(8,128)(2,1)S(1)} collective-permute-done((bf16[24,4096]{1,0:T(8,128)(2,1)S(1)}, bf16[24,4096]{1,0:T(8,128)(2,1)S(1)}, u32[]{:S(2)}, u32[]{:S(2)}) %collective-permute-start.17) | collective-permute-done | bytes 196640 | tf_op jit(solution)/shard_map/ppermute | solution.py:419
  97.5 3.5 %collective-permute-done.19.refs_3_ = bf16[24,4096]{1,0:T(8,128)(2,1)S(1)} collective-permute-done((bf16[24,4096]{1,0:T(8,128)(2,1)S(1)}, bf16[24,4096]{1,0:T(8,128)(2,1)S(1)}, u32[]{:S(2)}, u32[]{:S(2)}) %collective-permute-start.19) | collective-permute-done | bytes 196640 | tf_op jit(solution)/shard_map/ppermute | solution.py:419
  106.2 2.5 %collective-permute-done.21.refs_1_ = bf16[16,4096]{1,0:T(8,128)(2,1)S(1)} collective-permute-done((bf16[16,4096]{1,0:T(8,128)(2,1)S(1)}, bf16[16,4096]{1,0:T(8,128)(2,1)S(1)}, u32[]{:S(2)}, u32[]{:S(2)}) %collective-permute-start.21) | collective-permute-done | bytes 131104 | tf_op jit(solution)/shard_map/ppermute | solution.py:419
  108.7 3.7 %collective-permute-done.22.refs_2_ = bf16[16,4096]{1,0:T(8,128)(2,1)S(1)} collective-permute-done((bf16[16,4096]{1,0:T(8,128)(2,1)S(1)}, bf16[16,4096]{1,0:T(8,128)(2,1)S(1)}, u32[]{:S(2)}, u32[]{:S(2)}) %collective-permute-start.22) | collective-permute-done | bytes 131104 | tf_op jit(solution)/shard_map/ppermute | solution.py:419
  112.4 2.2 %collective-permute-done.23.refs_3_ = bf16[16,4096]{1,0:T(8,128)(2,1)S(1)} collective-permute-done((bf16[16,4096]{1,0:T(8,128)(2,1)S(1)}, bf16[16,4096]{1,0:T(8,128)(2,1)S(1)}, u32[]{:S(2)}, u32[]{:S(2)}) %collective-permute-start.23) | collective-permute-done | bytes 131104 | tf_op jit(solution)/shard_map/ppermute | solution.py:419
  (41 shorter events, 19.1 us)
Async XLA Ops:
  1.1 20.0 %collective-permute-start = (bf16[80,4096]{1,0:T(8,128)(2,1)S(1)}, bf16[80,4096]{1,0:T(8,128)(2,1)S(1)}, u32[]{:S(2)}, u32[]{:S(2)}) collective-permute-start(bf16[80,4096]{1,0:T(8,128)(2,1)S(1)} %bundle.1), channel_id=1, source_target_pairs={{0,2},{1,3},{2,4},{3,5},{4,6},{5,7},{6,8},{7,9},{8,10},{9,11},{10,... | collective-permute-start | bytes 1966088 | tf_op jit(solution)/shard_map/ppermute | solution.py:424
  6.0 25.3 %collective-permute-start.1 = (bf16[64,4096]{1,0:T(8,128)(2,1)}, bf16[64,4096]{1,0:T(8,128)(2,1)S(1)}, u32[]{:S(2)}, u32[]{:S(2)}) collective-permute-start(bf16[64,4096]{1,0:T(8,128)(2,1)} %v0.1), channel_id=1, source_target_pairs={{0,2},{1,3},{2,4},{3,5},{4,6},{5,7},{6,8},{7,9},{8,10},{9,11},{10,... | collective-permute-start | bytes 1572872 | tf_op jit(solution)/shard_map/ppermute | solution.py:422
  9.4 21.9 %collective-permute-start.2 = (bf16[80,4096]{1,0:T(8,128)(2,1)S(1)}, bf16[80,4096]{1,0:T(8,128)(2,1)S(1)}, u32[]{:S(2)}, u32[]{:S(2)}) collective-permute-start(bf16[80,4096]{1,0:T(8,128)(2,1)S(1)} %bundle.1), channel_id=1, source_target_pairs={{0,1},{2,3},{4,5},{6,7},{8,9},{10,11},{12,13},{14,15},{1,4},{3,6},... | collective-permute-start | bytes 1966088 | tf_op jit(solution)/shard_map/ppermute | solution.py:426
  21.1 12.1 %collective-permute-start.4 = (bf16[80,4096]{1,0:T(8,128)(2,1)S(1)}, bf16[80,4096]{1,0:T(8,128)(2,1)S(1)}, u32[]{:S(2)}, u32[]{:S(2)}) collective-permute-start(bf16[80,4096]{1,0:T(8,128)(2,1)S(1)} %collective-permute-done.k1.seg1), channel_id=1, source_target_pairs={{0,1},{1,0},{2,3},{3,2},{4,5},{5,4},{6,7},{7,6},{8,9},{9,8},{10,11... | collective-permute-start | bytes 1966088 | tf_op jit(solution)/shard_map/ppermute | solution.py:419
  21.1 10.2 %collective-permute-start.3 = (bf16[64,4096]{1,0:T(8,128)(2,1)S(1)}, bf16[64,4096]{1,0:T(8,128)(2,1)S(1)}, u32[]{:S(2)}, u32[]{:S(2)}) collective-permute-start(bf16[64,4096]{1,0:T(8,128)(2,1)S(1)} %copy-done), channel_id=1, source_target_pairs={{0,1},{2,3},{4,5},{6,7},{8,9},{10,11},{12,13},{14,15},{1,4},{3,6},... | collective-permute-start | bytes 1572872 | tf_op jit(solution)/shard_map/ppermute | solution.py:425
  31.3 1.9 %collective-permute-start.5 = (bf16[64,4096]{1,0:T(8,128)(2,1)S(1)}, bf16[64,4096]{1,0:T(8,128)(2,1)S(1)}, u32[]{:S(2)}, u32[]{:S(2)}) collective-permute-start(bf16[64,4096]{1,0:T(8,128)(2,1)S(1)} %collective-permute-done.1.v1), channel_id=1, source_target_pairs={{0,1},{1,0},{2,3},{3,2},{4,5},{5,4},{6,7},{7,6},{8,9},{9,8},{10,11... | collective-permute-start | bytes 1572872 | tf_op jit(solution)/shard_map/ppermute | solution.py:419
  38.5 22.4 %collective-permute-start.6 = (bf16[20,4096]{1,0:T(8,128)(2,1)S(1)}, bf16[20,4096]{1,0:T(8,128)(2,1)S(1)}, u32[]{:S(2)}, u32[]{:S(2)}) collective-permute-start(bf16[20,4096]{1,0:T(8,128)(2,1)S(1)} %get-tuple-element.52), channel_id=1, source_target_pairs={{0,8},{1,9},{2,10},{3,11},{4,12},{5,13},{6,14},{7,15},{8,0},{9,1},... | collective-permute-start | bytes 491528 | tf_op jit(solution)/shard_map/ppermute | solution.py:447
  44.1 14.9 %collective-permute-start.9 = (bf16[16,4096]{1,0:T(8,128)(2,1)S(1)}, bf16[16,4096]{1,0:T(8,128)(2,1)S(1)}, u32[]{:S(2)}, u32[]{:S(2)}) collective-permute-start(bf16[16,4096]{1,0:T(8,128)(2,1)S(1)} %get-tuple-element.56.refs_0_), channel_id=1, source_target_pairs={{0,6},{1,7},{2,4},{3,5},{4,2},{5,3},{6,0},{7,1},{8,14},{9,15},{10,... | collective-permute-start | bytes 393224 | tf_op jit(solution)/shard_map/ppermute | solution.py:419
  55.3 5.6 %collective-permute-start.8 = (bf16[16,4096]{1,0:T(8,128)(2,1)S(1)}, bf16[16,4096]{1,0:T(8,128)(2,1)S(1)}, u32[]{:S(2)}, u32[]{:S(2)}) collective-permute-start(bf16[16,4096]{1,0:T(8,128)(2,1)S(1)} %get-tuple-element.56.refs_0_), channel_id=1, source_target_pairs={{0,4},{1,5},{2,6},{3,7},{4,0},{5,1},{6,2},{7,3},{8,12},{9,13},{10,... | collective-permute-start | bytes 393224 | tf_op jit(solution)/shard_map/ppermute | solution.py:419
  55.7 5.2 %collective-permute-start.7 = (bf16[16,4096]{1,0:T(8,128)(2,1)S(1)}, bf16[16,4096]{1,0:T(8,128)(2,1)S(1)}, u32[]{:S(2)}, u32[]{:S(2)}) collective-permute-start(bf16[16,4096]{1,0:T(8,128)(2,1)S(1)} %get-tuple-element.56.refs_0_), channel_id=1, source_target_pairs={{0,2},{1,3},{2,0},{3,1},{4,6},{5,7},{6,4},{7,5},{8,10},{9,11},{10,... | collective-permute-start | bytes 393224 | tf_op jit(solution)/shard_map/ppermute | solution.py:419
  60.9 5.3 %collective-permute-start.13 = (bf16[64,4096]{1,0:T(8,128)(2,1)S(1)}, bf16[64,4096]{1,0:T(8,128)(2,1)S(1)}, u32[]{:S(2)}, u32[]{:S(2)}) collective-permute-start(bf16[64,4096]{1,0:T(8,128)(2,1)S(1)} %pile.2.local), channel_id=1, source_target_pairs={{0,1},{1,0},{2,3},{3,2},{4,5},{5,4},{6,7},{7,6},{8,9},{9,8},{10,11... | collective-permute-start | bytes 1572872 | tf_op jit(solution)/shard_map/ppermute | solution.py:419
  61.0 11.0 %collective-permute-start.12 = (bf16[24,4096]{1,0:T(8,128)(2,1)S(1)}, bf16[24,4096]{1,0:T(8,128)(2,1)S(1)}, u32[]{:S(2)}, u32[]{:S(2)}) collective-permute-start(bf16[24,4096]{1,0:T(8,128)(2,1)S(1)} %join.1.refs_0_), channel_id=1, source_target_pairs={{0,6},{1,7},{2,4},{3,5},{4,2},{5,3},{6,0},{7,1},{8,14},{9,15},{10,... | collective-permute-start | bytes 589832 | tf_op jit(solution)/shard_map/ppermute | solution.py:419
  65.5 9.1 %collective-permute-start.11 = (bf16[24,4096]{1,0:T(8,128)(2,1)S(1)}, bf16[24,4096]{1,0:T(8,128)(2,1)S(1)}, u32[]{:S(2)}, u32[]{:S(2)}) collective-permute-start(bf16[24,4096]{1,0:T(8,128)(2,1)S(1)} %join.1.refs_0_), channel_id=1, source_target_pairs={{0,4},{1,5},{2,6},{3,7},{4,0},{5,1},{6,2},{7,3},{8,12},{9,13},{10,... | collective-permute-start | bytes 589832 | tf_op jit(solution)/shard_map/ppermute | solution.py:419
  65.5 9.8 %collective-permute-start.10 = (bf16[24,4096]{1,0:T(8,128)(2,1)S(1)}, bf16[24,4096]{1,0:T(8,128)(2,1)S(1)}, u32[]{:S(2)}, u32[]{:S(2)}) collective-permute-start(bf16[24,4096]{1,0:T(8,128)(2,1)S(1)} %join.1.refs_0_), channel_id=1, source_target_pairs={{0,2},{1,3},{2,0},{3,1},{4,6},{5,7},{6,4},{7,5},{8,10},{9,11},{10,... | collective-permute-start | bytes 589832 | tf_op jit(solution)/shard_map/ppermute | solution.py:419
  75.4 2.4 %collective-permute-start.14 = (bf16[96,4096]{1,0:T(8,128)(2,1)S(1)}, bf16[96,4096]{1,0:T(8,128)(2,1)S(1)}, u32[]{:S(2)}, u32[]{:S(2)}) collective-permute-start(bf16[96,4096]{1,0:T(8,128)(2,1)S(1)} %pile.3.local), channel_id=1, source_target_pairs={{0,1},{1,0},{2,3},{3,2},{4,5},{5,4},{6,7},{7,6},{8,9},{9,8},{10,11... | collective-permute-start | bytes 2359304 | tf_op jit(solution)/shard_map/ppermute | solution.py:419
  85.0 3.2 %collective-permute-start.15 = (bf16[96,4096]{1,0:T(8,128)(2,1)S(1)}, bf16[96,4096]{1,0:T(8,128)(2,1)S(1)}, u32[]{:S(2)}, u32[]{:S(2)}) collective-permute-start(bf16[96,4096]{1,0:T(8,128)(2,1)S(1)} %get-tuple-element.70), channel_id=1, source_target_pairs={{0,1},{1,0},{2,3},{3,2},{4,5},{5,4},{6,7},{7,6},{8,9},{9,8},{10,11... | collective-permute-start | bytes 2359304 | tf_op jit(solution)/shard_map/ppermute | solution.py:419
  85.2 2.9 %collective-permute-start.16 = (bf16[64,4096]{1,0:T(8,128)(2,1)S(1)}, bf16[64,4096]{1,0:T(8,128)(2,1)S(1)}, u32[]{:S(2)}, u32[]{:S(2)}) collective-permute-start(bf16[64,4096]{1,0:T(8,128)(2,1)S(1)} %get-tuple-element.76), channel_id=1, source_target_pairs={{0,1},{1,0},{2,3},{3,2},{4,5},{5,4},{6,7},{7,6},{8,9},{9,8},{10,11... | collective-permute-start | bytes 1572872 | tf_op jit(solution)/shard_map/ppermute | solution.py:419
  88.5 7.0 %collective-permute-start.17 = (bf16[24,4096]{1,0:T(8,128)(2,1)S(1)}, bf16[24,4096]{1,0:T(8,128)(2,1)S(1)}, u32[]{:S(2)}, u32[]{:S(2)}) collective-permute-start(bf16[24,4096]{1,0:T(8,128)(2,1)S(1)} %get-tuple-element.82), channel_id=1, source_target_pairs={{0,2},{1,3},{2,0},{3,1},{4,6},{5,7},{6,4},{7,5},{8,10},{9,11},{10,... | collective-permute-start | bytes 589832 | tf_op jit(solution)/shard_map/ppermute | solution.py:419
  89.2 8.2 %collective-permute-start.18 = (bf16[24,4096]{1,0:T(8,128)(2,1)S(1)}, bf16[24,4096]{1,0:T(8,128)(2,1)S(1)}, u32[]{:S(2)}, u32[]{:S(2)}) collective-permute-start(bf16[24,4096]{1,0:T(8,128)(2,1)S(1)} %get-tuple-element.83), channel_id=1, source_target_pairs={{0,4},{1,5},{2,6},{3,7},{4,0},{5,1},{6,2},{7,3},{8,12},{9,13},{10,... | collective-permute-start | bytes 589832 | tf_op jit(solution)/shard_map/ppermute | solution.py:419
  91.7 9.2 %collective-permute-start.19 = (bf16[24,4096]{1,0:T(8,128)(2,1)S(1)}, bf16[24,4096]{1,0:T(8,128)(2,1)S(1)}, u32[]{:S(2)}, u32[]{:S(2)}) collective-permute-start(bf16[24,4096]{1,0:T(8,128)(2,1)S(1)} %get-tuple-element.84), channel_id=1, source_target_pairs={{0,6},{1,7},{2,4},{3,5},{4,2},{5,3},{6,0},{7,1},{8,14},{9,15},{10,... | collective-permute-start | bytes 589832 | tf_op jit(solution)/shard_map/ppermute | solution.py:419
  101.0 13.6 %collective-permute-start.20 = (bf16[20,4096]{1,0:T(8,128)(2,1)S(1)}, bf16[20,4096]{1,0:T(8,128)(2,1)S(1)}, u32[]{:S(2)}, u32[]{:S(2)}) collective-permute-start(bf16[20,4096]{1,0:T(8,128)(2,1)S(1)} %get-tuple-element.86), channel_id=1, source_target_pairs={{0,8},{1,9},{2,10},{3,11},{4,12},{5,13},{6,14},{7,15},{8,0},{9,1},... | collective-permute-start | bytes 491528 | tf_op jit(solution)/shard_map/ppermute | solution.py:472
  102.8 6.0 %collective-permute-start.21 = (bf16[16,4096]{1,0:T(8,128)(2,1)S(1)}, bf16[16,4096]{1,0:T(8,128)(2,1)S(1)}, u32[]{:S(2)}, u32[]{:S(2)}) collective-permute-start(bf16[16,4096]{1,0:T(8,128)(2,1)S(1)} %get-tuple-element.88), channel_id=1, source_target_pairs={{0,2},{1,3},{2,0},{3,1},{4,6},{5,7},{6,4},{7,5},{8,10},{9,11},{10,... | collective-permute-start | bytes 393224 | tf_op jit(solution)/shard_map/ppermute | solution.py:419
  104.2 8.2 %collective-permute-start.22 = (bf16[16,4096]{1,0:T(8,128)(2,1)S(1)}, bf16[16,4096]{1,0:T(8,128)(2,1)S(1)}, u32[]{:S(2)}, u32[]{:S(2)}) collective-permute-start(bf16[16,4096]{1,0:T(8,128)(2,1)S(1)} %get-tuple-element.89), channel_id=1, source_target_pairs={{0,4},{1,5},{2,6},{3,7},{4,0},{5,1},{6,2},{7,3},{8,12},{9,13},{10,... | collective-permute-start | bytes 393224 | tf_op jit(solution)/shard_map/ppermute | solution.py:419
  104.5 10.1 %collective-permute-start.23 = (bf16[16,4096]{1,0:T(8,128)(2,1)S(1)}, bf16[16,4096]{1,0:T(8,128)(2,1)S(1)}, u32[]{:S(2)}, u32[]{:S(2)}) collective-permute-start(bf16[16,4096]{1,0:T(8,128)(2,1)S(1)} %get-tuple-element.90), channel_id=1, source_target_pairs={{0,6},{1,7},{2,4},{3,5},{4,2},{5,3},{6,0},{7,1},{8,14},{9,15},{10,... | collective-permute-start | bytes 393224 | tf_op jit(solution)/shard_map/ppermute | solution.py:419
  (1 other events, 6.7 us)

commit v7 on v6

--- a/solution.py
+++ b/solution.py
@@ -30,12 +30,11 @@
 
 
 def bundle_kernel(keys, segs, out):
-    rows = keys.shape[0]
-    spare = out.shape[0] - rows
-    out[:rows] = keys[...]
-    out[rows:] = jnp.zeros((spare, keys.shape[1]), keys.dtype)
-    out[rows:, : segs.shape[1]] = jnp.broadcast_to(
-        segs[...].astype(jnp.float32), (spare, segs.shape[1])
+    rows, width = keys.shape
+    out[:, :width] = keys[...]
+    out[:, width:] = jnp.zeros((rows, HEAD_DIM), keys.dtype)
+    out[:SPARE, width : width + rows] = jnp.broadcast_to(
+        segs[...].astype(jnp.float32), (SPARE, rows)
     ).astype(keys.dtype)
 
 
@@ -45,7 +44,7 @@
         bundle_kernel,
         in_specs=[NEAR, NEAR],
         out_specs=NEAR,
-        out_shape=jax.ShapeDtypeStruct((rows + SPARE, width), keys.dtype),
+        out_shape=jax.ShapeDtypeStruct((rows, width + HEAD_DIM), keys.dtype),
         cost_estimate=pl.CostEstimate(
             flops=0, bytes_accessed=4 * rows * width, transcendentals=0
         ),
@@ -174,7 +173,7 @@
     cols = HEADS_STEP * HEAD_DIM
     top = routes.shape[0]
     piece = pl.BlockSpec((rows, cols), lambda j, *_: (0, j))
-    tail = pl.BlockSpec((SPARE, HEAD_DIM), lambda j, *_: (rows // SPARE, 0))
+    tail = pl.BlockSpec((SPARE, HEAD_DIM), lambda j, *_: (0, width // HEAD_DIM))
 
     def whole(shape):
         return pl.BlockSpec(shape, lambda j, *_: (0,) * len(shape))
@@ -253,7 +252,7 @@
 
 def experts_kernel(local, remote, w_gate, w_up, w_down, local_out, remote_out, x, hidden):
     width, units = w_gate.shape
-    tile = min(256, units)
+    tile = min(512, units)
     rows = local.shape[0]
     x[:rows] = local[...]
     x[rows:] = remote[...]
@@ -265,9 +264,9 @@
         up = jnp.dot(x[...], w_up[:, at], preferred_element_type=jnp.float32)
         hidden[:, at] = (jax.nn.silu(gate) * up).astype(jnp.bfloat16)
 
-    @pl.loop(0, width // 512)
+    @pl.loop(0, width // 1024)
     def _(part):
-        at = pl.ds(pl.multiple_of(part * 512, 512), 512)
+        at = pl.ds(pl.multiple_of(part * 1024, 1024), 1024)
         out = jnp.dot(hidden[...], w_down[:, at], preferred_element_type=jnp.float32)
         local_out[:, at] = out[:rows].astype(jnp.bfloat16)
         remote_out[:, at] = out[rows:].astype(jnp.bfloat16)
@@ -443,7 +442,7 @@
         seg_own, resid, norm_gain.reshape(1, -1), routes.T, route_gates.T,
     )
     partner = [(i, (i + shard_count) % count) for i in range(count)]
-    masks = range(2, shard_count, 2)
+    masks = list(range(2, shard_count, 2))[::-1]
     got = lax.ppermute(send, "expert", partner)
 
     def spread(block):
@@ -457,7 +456,8 @@
         return add_split(parts[0], swapped(parts[1], 1), 1 + len(masks))
 
     def scattered(blocks):
-        return [blocks[0]] + [swapped(block, mask) for block, mask in zip(blocks[1:], masks)]
+        moved = [swapped(block, mask) for block, mask in zip(blocks[1:], masks)]
+        return [blocks[0]] + moved[::-1]
 
     early_blocks = spread(early)
     got, early_blocks = lax.optimization_barrier((got, early_blocks))
@@ -465,12 +465,15 @@
     late_blocks = spread(join(got, rest))
     late_blocks, early_parts = lax.optimization_barrier((late_blocks, early_parts))
     late_rows = both_cores(late_blocks)
-    late_blocks = summed(experts(*late_rows, *held))
     early_blocks = summed(early_parts)
-    late_blocks, early_blocks = lax.optimization_barrier((late_blocks, early_blocks))
+    late_rows, early_blocks = lax.optimization_barrier((late_rows, early_blocks))
+    early_blocks = scattered(early_blocks)
+    late_parts = experts(*late_rows, *held)
+    late_parts, early_blocks = lax.optimization_barrier((late_parts, early_blocks))
+    late_blocks = summed(late_parts)
     late, back = total_of(scattered(late_blocks))
     other = lax.ppermute(back, "expert", partner)
-    return combine(mixed, weight, scattered(early_blocks), late, other)
+    return combine(mixed, weight, early_blocks, late, other)
 
 
 def solution(mesh):

time: 116 us -> 114 us (0.983)
  Pallas kernels: 32 us -> 29.6 us
  waiting for transfers between devices: 39.6 us -> 41.7 us
  starting transfers between devices: 44.1 us -> 42.1 us
    ppermute x1, waiting for transfers between devices: 0.01 us -> 9.59 us  [shards(): other = lax.ppermute(back, 'expert', partner)]
    ppermute x18, waiting for transfers between devices: 32.2 us -> 28.4 us  [swapped(): return lax.ppermute(block, 'expert', [(i, i ^ mask) for i in range(count)])]
    pallas_call x2, Pallas kernels: 13.1 us -> 10.6 us  [experts(): pl.pallas_call(experts_kernel, in_specs=[NEAR] * 5, out_specs=[NEAR] * 2,...]
    ppermute x1, waiting for transfers between devices: 3.11 us -> 0.66 us  [shards(): key_two = lax.ppermute(key_block, 'expert', next_chip)]
    ppermute x1, waiting for transfers between devices: 4.23 us -> 3.05 us  [shards(): value_two = lax.ppermute(values, 'expert', next_chip)]
  transfers between devices with their start and end apart: 24 -> 24, of which waited for: 16 -> 13; matrix products, arithmetic and copies ran while one was open for 0% -> 0% of each run, Pallas kernels for 14% -> 19%
where the time goes in v7:
time: 114 us
  starting transfers between devices  42.1 us (37%)
  waiting for transfers between devices  41.7 us (37%)
  Pallas kernels  29.6 us (26%)
    ppermute x18, waiting for transfers between devices, swapped(): return lax.ppermute(block, 'expert', [(i, i ^ mask) for i in range(count)])  28.4 us
    ppermute x18, starting transfers between devices, swapped(): return lax.ppermute(block, 'expert', [(i, i ^ mask) for i in range(count)])  23.5 us
    pallas_call x2, Pallas kernels, experts(): pl.pallas_call(experts_kernel, in_specs=[NEAR] * 5, out_specs=[NEAR] * 2,...  10.6 us
    pallas_call x3, Pallas kernels, fetch(): pl.pallas_call(functools.partial(fetch_kernel, parts), in_specs=[anywhere...  10.6 us
    ppermute x1, waiting for transfers between devices, shards(): other = lax.ppermute(back, 'expert', partner)  9.59 us
    ppermute x1, starting transfers between devices, shards(): got = lax.ppermute(send, 'expert', partner)  5.56 us
    pallas_call x1, Pallas kernels, attention(): pl.pallas_call(attention_kernel, grid_spec=pltpu.PrefetchScalarGridSpec(n...  5.49 us
    ppermute x1, starting transfers between devices, shards(): key_two = lax.ppermute(key_block, 'expert', next_chip)  4.9 us
  transfers between devices with their start and end apart: 24, of which 13 were waited for; matrix products, arithmetic and copies ran while one was open for 0% of the time, Pallas kernels for 19%

profile of v7, /device:TPU:0, one launch (start us, length us, event | category | flops | bytes accessed | tf_op | source)
XLA Modules:
  0.0 113.7 jit_solution(18150525747564263175)
XLA Ops:
  1.1 4.9 %collective-permute-start = (bf16[64,4224]{1,0:T(8,128)(2,1)S(1)}, bf16[64,4224]{1,0:T(8,128)(2,1)S(1)}, u32[]{:S(2)}, u32[]{:S(2)}) collective-permute-start(bf16[64,4224]{1,0:T(8,128)(2,1)S(1)} %bundle.1), channel_id=1, source_target_pairs={{0,2},{1,3},{2,4},{3,5},{4,6},{5,7},{6,8},{7,9},{8,10},{9,11},{10,... | collective-permute-start | bytes 1622024 | tf_op jit(solution)/shard_map/ppermute | solution.py:423
  6.0 3.4 %collective-permute-start.1 = (bf16[64,4096]{1,0:T(8,128)(2,1)}, bf16[64,4096]{1,0:T(8,128)(2,1)S(1)}, u32[]{:S(2)}, u32[]{:S(2)}) collective-permute-start(bf16[64,4096]{1,0:T(8,128)(2,1)} %v0.1), channel_id=1, source_target_pairs={{0,2},{1,3},{2,4},{3,5},{4,6},{5,7},{6,8},{7,9},{8,10},{9,11},{10,... | collective-permute-start | bytes 1572872 | tf_op jit(solution)/shard_map/ppermute | solution.py:421
  10.9 3.5 %fetch.3.w_gate = bf16[4096,1024]{1,0:T(8,128)(2,1)S(1)} custom-call(bf16[4096,1024]{1,0:T(8,128)(2,1)} %source.3, s32[5]{0:T(128)S(1)} %stack.23.after.deltas), custom_call_target="tpu_custom_call" | custom-call | bytes 16777216 | tf_op jit(solution)/shard_map/fetch/pallas_call | solution.py:239
  14.4 3.6 %fetch.4.w_up = bf16[4096,1024]{1,0:T(8,128)(2,1)S(1)} custom-call(bf16[4096,1024]{1,0:T(8,128)(2,1)} %source.4, s32[5]{0:T(128)S(1)} %stack.23.after.deltas), custom_call_target="tpu_custom_call" | custom-call | bytes 16777216 | tf_op jit(solution)/shard_map/fetch/pallas_call | solution.py:239
  20.3 2.0 %collective-permute-start.3 = (bf16[64,4096]{1,0:T(8,128)(2,1)S(1)}, bf16[64,4096]{1,0:T(8,128)(2,1)S(1)}, u32[]{:S(2)}, u32[]{:S(2)}) collective-permute-start(bf16[64,4096]{1,0:T(8,128)(2,1)S(1)} %copy-done), channel_id=1, source_target_pairs={{0,1},{2,3},{4,5},{6,7},{8,9},{10,11},{12,13},{14,15},{1,4},{3,6},... | collective-permute-start | bytes 1572872 | tf_op jit(solution)/shard_map/ppermute | solution.py:424
  22.3 3.5 %fetch.5.w_down = bf16[1024,4096]{1,0:T(8,128)(2,1)S(1)} custom-call(bf16[1024,4096]{1,0:T(8,128)(2,1)} %source.5, s32[5]{0:T(128)S(1)} %stack.23.after.deltas), custom_call_target="tpu_custom_call" | custom-call | bytes 16777216 | tf_op jit(solution)/shard_map/fetch/pallas_call | solution.py:239
  25.8 3.0 %collective-permute-done.1.v1 = bf16[64,4096]{1,0:T(8,128)(2,1)S(1)} collective-permute-done((bf16[64,4096]{1,0:T(8,128)(2,1)}, bf16[64,4096]{1,0:T(8,128)(2,1)S(1)}, u32[]{:S(2)}, u32[]{:S(2)}) %collective-permute-start.1) | collective-permute-done | bytes 524320 | tf_op jit(solution)/shard_map/ppermute | solution.py:421
  28.8 1.9 %collective-permute-done.5.v3 = bf16[64,4096]{1,0:T(8,128)(2,1)S(1)} collective-permute-done((bf16[64,4096]{1,0:T(8,128)(2,1)S(1)}, bf16[64,4096]{1,0:T(8,128)(2,1)S(1)}, u32[]{:S(2)}, u32[]{:S(2)}) %collective-permute-start.5) | collective-permute-done | bytes 524320 | tf_op jit(solution)/shard_map/ppermute | solution.py:418
  30.7 5.5 %attention.1 = (f32[64,4096]{1,0:T(8,128)S(1)}, bf16[16,4096]{1,0:T(8,128)(2,1)S(1)}, bf16[4,4096]{1,0:T(4,128)(2,1)S(1)}, bf16[20,4096]{1,0:T(8,128)(2,1)S(1)}, bf16[3,64,32]{2,1,0:T(8,128)(2,1)S(1)}) custom-call(s32[5]{0:T(128)S(1)} %stack.23.after.deltas, bf16[64,4096]{1,0:T(8,128)(2,1)} %q.1, bf16[64,4096]{1,0:T(8,128)(2,1)} %k0.1, bf16[64,4096]{1,0:T(8,128)(2,1)} %v0.1, ...), custom_call_target="tpu_custom_call" | custom-call | flops 268435456 | bytes 8388608 | tf_op jit(solution)/shard_map/attention/pallas_call | solution.py:182
  36.2 5.6 %collective-permute-start.6 = (bf16[20,4096]{1,0:T(8,128)(2,1)S(1)}, bf16[20,4096]{1,0:T(8,128)(2,1)S(1)}, u32[]{:S(2)}, u32[]{:S(2)}) collective-permute-start(bf16[20,4096]{1,0:T(8,128)(2,1)S(1)} %get-tuple-element.56), channel_id=1, source_target_pairs={{0,8},{1,9},{2,10},{3,11},{4,12},{5,13},{6,14},{7,15},{8,0},{9,1},... | collective-permute-start | bytes 491528 | tf_op jit(solution)/shard_map/ppermute | solution.py:446
  41.8 8.9 %collective-permute-start.9 = (bf16[16,4096]{1,0:T(8,128)(2,1)S(1)}, bf16[16,4096]{1,0:T(8,128)(2,1)S(1)}, u32[]{:S(2)}, u32[]{:S(2)}) collective-permute-start(bf16[16,4096]{1,0:T(8,128)(2,1)S(1)} %get-tuple-element.60.refs_0_), channel_id=1, source_target_pairs={{0,2},{1,3},{2,0},{3,1},{4,6},{5,7},{6,4},{7,5},{8,10},{9,11},{10,... | collective-permute-start | bytes 393224 | tf_op jit(solution)/shard_map/ppermute | solution.py:418
  52.3 2.3 %collective-permute-done.9.refs_3_ = bf16[16,4096]{1,0:T(8,128)(2,1)S(1)} collective-permute-done((bf16[16,4096]{1,0:T(8,128)(2,1)S(1)}, bf16[16,4096]{1,0:T(8,128)(2,1)S(1)}, u32[]{:S(2)}, u32[]{:S(2)}) %collective-permute-start.9) | collective-permute-done | bytes 131104 | tf_op jit(solution)/shard_map/ppermute | solution.py:418
  56.2 4.2 %collective-permute-done.7.refs_1_ = bf16[16,4096]{1,0:T(8,128)(2,1)S(1)} collective-permute-done((bf16[16,4096]{1,0:T(8,128)(2,1)S(1)}, bf16[16,4096]{1,0:T(8,128)(2,1)S(1)}, u32[]{:S(2)}, u32[]{:S(2)}) %collective-permute-start.7) | collective-permute-done | bytes 131104 | tf_op jit(solution)/shard_map/ppermute | solution.py:418
  62.1 2.0 %collective-permute-start.10 = (bf16[24,4096]{1,0:T(8,128)(2,1)S(1)}, bf16[24,4096]{1,0:T(8,128)(2,1)S(1)}, u32[]{:S(2)}, u32[]{:S(2)}) collective-permute-start(bf16[24,4096]{1,0:T(8,128)(2,1)S(1)} %join.1.refs_0_), channel_id=1, source_target_pairs={{0,6},{1,7},{2,4},{3,5},{4,2},{5,3},{6,0},{7,1},{8,14},{9,15},{10,... | collective-permute-start | bytes 589832 | tf_op jit(solution)/shard_map/ppermute | solution.py:418
  64.1 4.5 %experts.2 = (bf16[64,4096]{1,0:T(8,128)(2,1)S(1)}, bf16[64,4096]{1,0:T(8,128)(2,1)S(1)}) custom-call(bf16[64,4096]{1,0:T(8,128)(2,1)S(1)} %pile.2.local, bf16[64,4096]{1,0:T(8,128)(2,1)S(1)} %collective-permute-done.13.remote, bf16[4096,1024]{1,0:T(8,128)(2,1)S(1)} %fetch.3.w_gate, bf16[4096,1024]{1,0:T(8,128)(2,1)S(1)} %fetch.4.w_up, ...), custom_call_target="tpu_custom_call" | custom-call | flops 3221225472 | bytes 2097152 | tf_op jit(solution)/shard_map/experts/pallas_call | solution.py:278
  68.6 4.7 %collective-permute-done.10.refs_1_ = bf16[24,4096]{1,0:T(8,128)(2,1)S(1)} collective-permute-done((bf16[24,4096]{1,0:T(8,128)(2,1)S(1)}, bf16[24,4096]{1,0:T(8,128)(2,1)S(1)}, u32[]{:S(2)}, u32[]{:S(2)}) %collective-permute-start.10) | collective-permute-done | bytes 196640 | tf_op jit(solution)/shard_map/ppermute | solution.py:418
  74.0 2.5 %collective-permute-done.15.second = bf16[64,4096]{1,0:T(8,128)(2,1)S(1)} collective-permute-done((bf16[64,4096]{1,0:T(8,128)(2,1)S(1)}, bf16[64,4096]{1,0:T(8,128)(2,1)S(1)}, u32[]{:S(2)}, u32[]{:S(2)}) %collective-permute-start.15) | collective-permute-done | bytes 524320 | tf_op jit(solution)/shard_map/ppermute | solution.py:418
  78.4 1.7 %collective-permute-start.18 = (bf16[16,4096]{1,0:T(8,128)(2,1)S(1)}, bf16[16,4096]{1,0:T(8,128)(2,1)S(1)}, u32[]{:S(2)}, u32[]{:S(2)}) collective-permute-start(bf16[16,4096]{1,0:T(8,128)(2,1)S(1)} %get-tuple-element.86), channel_id=1, source_target_pairs={{0,6},{1,7},{2,4},{3,5},{4,2},{5,3},{6,0},{7,1},{8,14},{9,15},{10,... | collective-permute-start | bytes 393224 | tf_op jit(solution)/shard_map/ppermute | solution.py:418
  80.2 6.1 %experts.3 = (bf16[96,4096]{1,0:T(8,128)(2,1)S(1)}, bf16[96,4096]{1,0:T(8,128)(2,1)S(1)}) custom-call(bf16[96,4096]{1,0:T(8,128)(2,1)S(1)} %pile.3.local, bf16[96,4096]{1,0:T(8,128)(2,1)S(1)} %collective-permute-done.14.remote, bf16[4096,1024]{1,0:T(8,128)(2,1)S(1)} %fetch.3.w_gate, bf16[4096,1024]{1,0:T(8,128)(2,1)S(1)} %fetch.4.w_up, ...), custom_call_target="tpu_custom_call" | custom-call | flops 4831838208 | bytes 3145728 | tf_op jit(solution)/shard_map/experts/pallas_call | solution.py:278
  86.4 2.3 %collective-permute-done.19.second = bf16[96,4096]{1,0:T(8,128)(2,1)S(1)} collective-permute-done((bf16[96,4096]{1,0:T(8,128)(2,1)S(1)}, bf16[96,4096]{1,0:T(8,128)(2,1)S(1)}, u32[]{:S(2)}, u32[]{:S(2)}) %collective-permute-start.19) | collective-permute-done | bytes 786464 | tf_op jit(solution)/shard_map/ppermute | solution.py:418
  90.7 1.8 %collective-permute-start.22 = (bf16[24,4096]{1,0:T(8,128)(2,1)S(1)}, bf16[24,4096]{1,0:T(8,128)(2,1)S(1)}, u32[]{:S(2)}, u32[]{:S(2)}) collective-permute-start(bf16[24,4096]{1,0:T(8,128)(2,1)S(1)} %get-tuple-element.92), channel_id=1, source_target_pairs={{0,6},{1,7},{2,4},{3,5},{4,2},{5,3},{6,0},{7,1},{8,14},{9,15},{10,... | collective-permute-start | bytes 589832 | tf_op jit(solution)/shard_map/ppermute | solution.py:418
  92.4 3.5 %collective-permute-done.20.refs_1_ = bf16[24,4096]{1,0:T(8,128)(2,1)S(1)} collective-permute-done((bf16[24,4096]{1,0:T(8,128)(2,1)S(1)}, bf16[24,4096]{1,0:T(8,128)(2,1)S(1)}, u32[]{:S(2)}, u32[]{:S(2)}) %collective-permute-start.20) | collective-permute-done | bytes 196640 | tf_op jit(solution)/shard_map/ppermute | solution.py:418
  97.1 4.2 %collective-permute-done.22.refs_3_ = bf16[24,4096]{1,0:T(8,128)(2,1)S(1)} collective-permute-done((bf16[24,4096]{1,0:T(8,128)(2,1)S(1)}, bf16[24,4096]{1,0:T(8,128)(2,1)S(1)}, u32[]{:S(2)}, u32[]{:S(2)}) %collective-permute-start.22) | collective-permute-done | bytes 196640 | tf_op jit(solution)/shard_map/ppermute | solution.py:418
  102.8 9.6 %collective-permute-done.23.other = bf16[20,4096]{1,0:T(8,128)(2,1)S(1)} collective-permute-done((bf16[20,4096]{1,0:T(8,128)(2,1)S(1)}, bf16[20,4096]{1,0:T(8,128)(2,1)S(1)}, u32[]{:S(2)}, u32[]{:S(2)}) %collective-permute-start.23) | collective-permute-done | bytes 163872 | tf_op jit(solution)/shard_map/ppermute | solution.py:475
  (41 shorter events, 18.3 us)
Async XLA Ops:
  1.1 17.5 %collective-permute-start = (bf16[64,4224]{1,0:T(8,128)(2,1)S(1)}, bf16[64,4224]{1,0:T(8,128)(2,1)S(1)}, u32[]{:S(2)}, u32[]{:S(2)}) collective-permute-start(bf16[64,4224]{1,0:T(8,128)(2,1)S(1)} %bundle.1), channel_id=1, source_target_pairs={{0,2},{1,3},{2,4},{3,5},{4,6},{5,7},{6,8},{7,9},{8,10},{9,11},{10,... | collective-permute-start | bytes 1622024 | tf_op jit(solution)/shard_map/ppermute | solution.py:423
  6.0 22.8 %collective-permute-start.1 = (bf16[64,4096]{1,0:T(8,128)(2,1)}, bf16[64,4096]{1,0:T(8,128)(2,1)S(1)}, u32[]{:S(2)}, u32[]{:S(2)}) collective-permute-start(bf16[64,4096]{1,0:T(8,128)(2,1)} %v0.1), channel_id=1, source_target_pairs={{0,2},{1,3},{2,4},{3,5},{4,6},{5,7},{6,8},{7,9},{8,10},{9,11},{10,... | collective-permute-start | bytes 1572872 | tf_op jit(solution)/shard_map/ppermute | solution.py:421
  9.4 19.4 %collective-permute-start.2 = (bf16[64,4224]{1,0:T(8,128)(2,1)S(1)}, bf16[64,4224]{1,0:T(8,128)(2,1)S(1)}, u32[]{:S(2)}, u32[]{:S(2)}) collective-permute-start(bf16[64,4224]{1,0:T(8,128)(2,1)S(1)} %bundle.1), channel_id=1, source_target_pairs={{0,1},{2,3},{4,5},{6,7},{8,9},{10,11},{12,13},{14,15},{1,4},{3,6},... | collective-permute-start | bytes 1622024 | tf_op jit(solution)/shard_map/ppermute | solution.py:425
  18.6 12.1 %collective-permute-start.4 = (bf16[64,4224]{1,0:T(8,128)(2,1)S(1)}, bf16[64,4224]{1,0:T(8,128)(2,1)S(1)}, u32[]{:S(2)}, u32[]{:S(2)}) collective-permute-start(bf16[64,4224]{1,0:T(8,128)(2,1)S(1)} %collective-permute-done.k1.seg1), channel_id=1, source_target_pairs={{0,1},{1,0},{2,3},{3,2},{4,5},{5,4},{6,7},{7,6},{8,9},{9,8},{10,11... | collective-permute-start | bytes 1622024 | tf_op jit(solution)/shard_map/ppermute | solution.py:418
  20.3 8.5 %collective-permute-start.3 = (bf16[64,4096]{1,0:T(8,128)(2,1)S(1)}, bf16[64,4096]{1,0:T(8,128)(2,1)S(1)}, u32[]{:S(2)}, u32[]{:S(2)}) collective-permute-start(bf16[64,4096]{1,0:T(8,128)(2,1)S(1)} %copy-done), channel_id=1, source_target_pairs={{0,1},{2,3},{4,5},{6,7},{8,9},{10,11},{12,13},{14,15},{1,4},{3,6},... | collective-permute-start | bytes 1572872 | tf_op jit(solution)/shard_map/ppermute | solution.py:424
  28.8 1.9 %collective-permute-start.5 = (bf16[64,4096]{1,0:T(8,128)(2,1)S(1)}, bf16[64,4096]{1,0:T(8,128)(2,1)S(1)}, u32[]{:S(2)}, u32[]{:S(2)}) collective-permute-start(bf16[64,4096]{1,0:T(8,128)(2,1)S(1)} %collective-permute-done.1.v1), channel_id=1, source_target_pairs={{0,1},{1,0},{2,3},{3,2},{4,5},{5,4},{6,7},{7,6},{8,9},{9,8},{10,11... | collective-permute-start | bytes 1572872 | tf_op jit(solution)/shard_map/ppermute | solution.py:418
  36.2 24.2 %collective-permute-start.6 = (bf16[20,4096]{1,0:T(8,128)(2,1)S(1)}, bf16[20,4096]{1,0:T(8,128)(2,1)S(1)}, u32[]{:S(2)}, u32[]{:S(2)}) collective-permute-start(bf16[20,4096]{1,0:T(8,128)(2,1)S(1)} %get-tuple-element.56), channel_id=1, source_target_pairs={{0,8},{1,9},{2,10},{3,11},{4,12},{5,13},{6,14},{7,15},{8,0},{9,1},... | collective-permute-start | bytes 491528 | tf_op jit(solution)/shard_map/ppermute | solution.py:446
  41.8 12.9 %collective-permute-start.9 = (bf16[16,4096]{1,0:T(8,128)(2,1)S(1)}, bf16[16,4096]{1,0:T(8,128)(2,1)S(1)}, u32[]{:S(2)}, u32[]{:S(2)}) collective-permute-start(bf16[16,4096]{1,0:T(8,128)(2,1)S(1)} %get-tuple-element.60.refs_0_), channel_id=1, source_target_pairs={{0,2},{1,3},{2,0},{3,1},{4,6},{5,7},{6,4},{7,5},{8,10},{9,11},{10,... | collective-permute-start | bytes 393224 | tf_op jit(solution)/shard_map/ppermute | solution.py:418
  50.7 5.5 %collective-permute-start.8 = (bf16[16,4096]{1,0:T(8,128)(2,1)S(1)}, bf16[16,4096]{1,0:T(8,128)(2,1)S(1)}, u32[]{:S(2)}, u32[]{:S(2)}) collective-permute-start(bf16[16,4096]{1,0:T(8,128)(2,1)S(1)} %get-tuple-element.60.refs_0_), channel_id=1, source_target_pairs={{0,4},{1,5},{2,6},{3,7},{4,0},{5,1},{6,2},{7,3},{8,12},{9,13},{10,... | collective-permute-start | bytes 393224 | tf_op jit(solution)/shard_map/ppermute | solution.py:418
  52.3 8.1 %collective-permute-start.7 = (bf16[16,4096]{1,0:T(8,128)(2,1)S(1)}, bf16[16,4096]{1,0:T(8,128)(2,1)S(1)}, u32[]{:S(2)}, u32[]{:S(2)}) collective-permute-start(bf16[16,4096]{1,0:T(8,128)(2,1)S(1)} %get-tuple-element.60.refs_0_), channel_id=1, source_target_pairs={{0,6},{1,7},{2,4},{3,5},{4,2},{5,3},{6,0},{7,1},{8,14},{9,15},{10,... | collective-permute-start | bytes 393224 | tf_op jit(solution)/shard_map/ppermute | solution.py:418
  60.5 3.7 %collective-permute-start.13 = (bf16[64,4096]{1,0:T(8,128)(2,1)S(1)}, bf16[64,4096]{1,0:T(8,128)(2,1)S(1)}, u32[]{:S(2)}, u32[]{:S(2)}) collective-permute-start(bf16[64,4096]{1,0:T(8,128)(2,1)S(1)} %pile.2.local), channel_id=1, source_target_pairs={{0,1},{1,0},{2,3},{3,2},{4,5},{5,4},{6,7},{7,6},{8,9},{9,8},{10,11... | collective-permute-start | bytes 1572872 | tf_op jit(solution)/shard_map/ppermute | solution.py:418
  60.6 8.0 %collective-permute-start.12 = (bf16[24,4096]{1,0:T(8,128)(2,1)S(1)}, bf16[24,4096]{1,0:T(8,128)(2,1)S(1)}, u32[]{:S(2)}, u32[]{:S(2)}) collective-permute-start(bf16[24,4096]{1,0:T(8,128)(2,1)S(1)} %join.1.refs_0_), channel_id=1, source_target_pairs={{0,2},{1,3},{2,0},{3,1},{4,6},{5,7},{6,4},{7,5},{8,10},{9,11},{10,... | collective-permute-start | bytes 589832 | tf_op jit(solution)/shard_map/ppermute | solution.py:418
  60.7 8.0 %collective-permute-start.11 = (bf16[24,4096]{1,0:T(8,128)(2,1)S(1)}, bf16[24,4096]{1,0:T(8,128)(2,1)S(1)}, u32[]{:S(2)}, u32[]{:S(2)}) collective-permute-start(bf16[24,4096]{1,0:T(8,128)(2,1)S(1)} %join.1.refs_0_), channel_id=1, source_target_pairs={{0,4},{1,5},{2,6},{3,7},{4,0},{5,1},{6,2},{7,3},{8,12},{9,13},{10,... | collective-permute-start | bytes 589832 | tf_op jit(solution)/shard_map/ppermute | solution.py:418
  62.1 11.2 %collective-permute-start.10 = (bf16[24,4096]{1,0:T(8,128)(2,1)S(1)}, bf16[24,4096]{1,0:T(8,128)(2,1)S(1)}, u32[]{:S(2)}, u32[]{:S(2)}) collective-permute-start(bf16[24,4096]{1,0:T(8,128)(2,1)S(1)} %join.1.refs_0_), channel_id=1, source_target_pairs={{0,6},{1,7},{2,4},{3,5},{4,2},{5,3},{6,0},{7,1},{8,14},{9,15},{10,... | collective-permute-start | bytes 589832 | tf_op jit(solution)/shard_map/ppermute | solution.py:418
  73.4 3.2 %collective-permute-start.14 = (bf16[96,4096]{1,0:T(8,128)(2,1)S(1)}, bf16[96,4096]{1,0:T(8,128)(2,1)S(1)}, u32[]{:S(2)}, u32[]{:S(2)}) collective-permute-start(bf16[96,4096]{1,0:T(8,128)(2,1)S(1)} %pile.3.local), channel_id=1, source_target_pairs={{0,1},{1,0},{2,3},{3,2},{4,5},{5,4},{6,7},{7,6},{8,9},{9,8},{10,11... | collective-permute-start | bytes 2359304 | tf_op jit(solution)/shard_map/ppermute | solution.py:418
  73.5 3.0 %collective-permute-start.15 = (bf16[64,4096]{1,0:T(8,128)(2,1)S(1)}, bf16[64,4096]{1,0:T(8,128)(2,1)S(1)}, u32[]{:S(2)}, u32[]{:S(2)}) collective-permute-start(bf16[64,4096]{1,0:T(8,128)(2,1)S(1)} %get-tuple-element.74), channel_id=1, source_target_pairs={{0,1},{1,0},{2,3},{3,2},{4,5},{5,4},{6,7},{7,6},{8,9},{9,8},{10,11... | collective-permute-start | bytes 1572872 | tf_op jit(solution)/shard_map/ppermute | solution.py:418
  76.6 9.7 %collective-permute-start.16 = (bf16[16,4096]{1,0:T(8,128)(2,1)S(1)}, bf16[16,4096]{1,0:T(8,128)(2,1)S(1)}, u32[]{:S(2)}, u32[]{:S(2)}) collective-permute-start(bf16[16,4096]{1,0:T(8,128)(2,1)S(1)} %get-tuple-element.84), channel_id=1, source_target_pairs={{0,2},{1,3},{2,0},{3,1},{4,6},{5,7},{6,4},{7,5},{8,10},{9,11},{10,... | collective-permute-start | bytes 393224 | tf_op jit(solution)/shard_map/ppermute | solution.py:418
  77.1 9.3 %collective-permute-start.17 = (bf16[16,4096]{1,0:T(8,128)(2,1)S(1)}, bf16[16,4096]{1,0:T(8,128)(2,1)S(1)}, u32[]{:S(2)}, u32[]{:S(2)}) collective-permute-start(bf16[16,4096]{1,0:T(8,128)(2,1)S(1)} %get-tuple-element.85), channel_id=1, source_target_pairs={{0,4},{1,5},{2,6},{3,7},{4,0},{5,1},{6,2},{7,3},{8,12},{9,13},{10,... | collective-permute-start | bytes 393224 | tf_op jit(solution)/shard_map/ppermute | solution.py:418
  78.4 7.9 %collective-permute-start.18 = (bf16[16,4096]{1,0:T(8,128)(2,1)S(1)}, bf16[16,4096]{1,0:T(8,128)(2,1)S(1)}, u32[]{:S(2)}, u32[]{:S(2)}) collective-permute-start(bf16[16,4096]{1,0:T(8,128)(2,1)S(1)} %get-tuple-element.86), channel_id=1, source_target_pairs={{0,6},{1,7},{2,4},{3,5},{4,2},{5,3},{6,0},{7,1},{8,14},{9,15},{10,... | collective-permute-start | bytes 393224 | tf_op jit(solution)/shard_map/ppermute | solution.py:418
  86.4 2.4 %collective-permute-start.19 = (bf16[96,4096]{1,0:T(8,128)(2,1)S(1)}, bf16[96,4096]{1,0:T(8,128)(2,1)S(1)}, u32[]{:S(2)}, u32[]{:S(2)}) collective-permute-start(bf16[96,4096]{1,0:T(8,128)(2,1)S(1)} %get-tuple-element.88), channel_id=1, source_target_pairs={{0,1},{1,0},{2,3},{3,2},{4,5},{5,4},{6,7},{7,6},{8,9},{9,8},{10,11... | collective-permute-start | bytes 2359304 | tf_op jit(solution)/shard_map/ppermute | solution.py:418
  88.9 7.0 %collective-permute-start.20 = (bf16[24,4096]{1,0:T(8,128)(2,1)S(1)}, bf16[24,4096]{1,0:T(8,128)(2,1)S(1)}, u32[]{:S(2)}, u32[]{:S(2)}) collective-permute-start(bf16[24,4096]{1,0:T(8,128)(2,1)S(1)} %get-tuple-element.90), channel_id=1, source_target_pairs={{0,2},{1,3},{2,0},{3,1},{4,6},{5,7},{6,4},{7,5},{8,10},{9,11},{10,... | collective-permute-start | bytes 589832 | tf_op jit(solution)/shard_map/ppermute | solution.py:418
  89.3 7.8 %collective-permute-start.21 = (bf16[24,4096]{1,0:T(8,128)(2,1)S(1)}, bf16[24,4096]{1,0:T(8,128)(2,1)S(1)}, u32[]{:S(2)}, u32[]{:S(2)}) collective-permute-start(bf16[24,4096]{1,0:T(8,128)(2,1)S(1)} %get-tuple-element.91), channel_id=1, source_target_pairs={{0,4},{1,5},{2,6},{3,7},{4,0},{5,1},{6,2},{7,3},{8,12},{9,13},{10,... | collective-permute-start | bytes 589832 | tf_op jit(solution)/shard_map/ppermute | solution.py:418
  90.7 10.6 %collective-permute-start.22 = (bf16[24,4096]{1,0:T(8,128)(2,1)S(1)}, bf16[24,4096]{1,0:T(8,128)(2,1)S(1)}, u32[]{:S(2)}, u32[]{:S(2)}) collective-permute-start(bf16[24,4096]{1,0:T(8,128)(2,1)S(1)} %get-tuple-element.92), channel_id=1, source_target_pairs={{0,6},{1,7},{2,4},{3,5},{4,2},{5,3},{6,0},{7,1},{8,14},{9,15},{10,... | collective-permute-start | bytes 589832 | tf_op jit(solution)/shard_map/ppermute | solution.py:418
  101.4 11.0 %collective-permute-start.23 = (bf16[20,4096]{1,0:T(8,128)(2,1)S(1)}, bf16[20,4096]{1,0:T(8,128)(2,1)S(1)}, u32[]{:S(2)}, u32[]{:S(2)}) collective-permute-start(bf16[20,4096]{1,0:T(8,128)(2,1)S(1)} %get-tuple-element.94), channel_id=1, source_target_pairs={{0,8},{1,9},{2,10},{3,11},{4,12},{5,13},{6,14},{7,15},{8,0},{9,1},... | collective-permute-start | bytes 491528 | tf_op jit(solution)/shard_map/ppermute | solution.py:475
  (1 other events, 5.9 us)

commit v8 on v7

--- a/solution.py
+++ b/solution.py
@@ -53,155 +53,142 @@
     )(far(keys), far(segs))
 
 
+def choose_kernel(flags, first, second, out):
+    @pl.when(flags[5] == 1)
+    def _():
+        out[...] = first[...]
+
+    @pl.when(flags[5] != 1)
+    def _():
+        out[...] = second[...]
+
+
+def choose(flags, first, second):
+    return pl.pallas_call(
+        choose_kernel,
+        in_specs=[pl.BlockSpec(memory_space=pltpu.SMEM), NEAR, NEAR],
+        out_specs=NEAR,
+        out_shape=jax.ShapeDtypeStruct(first.shape, first.dtype),
+        compiler_params=pltpu.CompilerParams(vmem_limit_bytes=6 * MIB),
+        name="choose",
+    )(flags, first, second)
+
+
 def attention_kernel(
-    deltas, q, k0, v0, k1, v1, k2, v2, k3, v3, seg0, seg1, seg2, seg3, resid, gain, routes, gates,
-    mixed_out, early_out, rest_out, send_out, weight_out, bias,
+    deltas, q, k0, v0, k1, v1, k2, v2, k3, v3, seg0, resid, gain, routes, gates,
+    mixed_out, early_out, rest_out, send_out, weight_out,
 ):
-    step = pl.program_id(0)
-    steps = pl.num_programs(0)
-    rows = q.shape[0]
+    rows, model = q.shape
     keys = (WIN_DEV + 1) * rows
-
-    @pl.when(step == 0)
-    def _():
-        seg_own = seg0[...].astype(jnp.float32)
-        seg_row = jnp.concatenate(
-            [seg_own] + [seg[0:1, :rows].astype(jnp.float32) for seg in (seg1, seg2, seg3)],
-            axis=1,
-        )
-        eye = lax.broadcasted_iota(jnp.int32, (rows, rows), 0) == lax.broadcasted_iota(
-            jnp.int32, (rows, rows), 1
-        )
-        seg_col = jnp.sum(jnp.where(eye, seg_own, 0.0), axis=1, keepdims=True)
-        lane = lax.broadcasted_iota(jnp.int32, (rows, keys), 1)
-        sub = lax.broadcasted_iota(jnp.int32, (rows, keys), 0)
-        block = lane // rows
-        back = jnp.where(
-            block == 0,
-            deltas[0],
-            jnp.where(block == 1, deltas[1], jnp.where(block == 2, deltas[2], deltas[3])),
-        )
-        distance = sub - (lane - block * rows) + back * rows
-        allowed = (distance >= 0) & (distance <= WIN_DEV * rows) & (seg_col == seg_row)
-        bias[...] = jnp.where(allowed, 0.0, MASKED)
-
+    width = HEADS_STEP * HEAD_DIM
+
+    seg_own = seg0[...].astype(jnp.float32)
+    seg_row = jnp.concatenate(
+        [seg_own]
+        + [block[:SPARE, model:][0:1, :rows].astype(jnp.float32) for block in (k1, k2, k3)],
+        axis=1,
+    )
+    eye = lax.broadcasted_iota(jnp.int32, (rows, rows), 0) == lax.broadcasted_iota(
+        jnp.int32, (rows, rows), 1
+    )
+    seg_col = jnp.sum(jnp.where(eye, seg_own, 0.0), axis=1, keepdims=True)
+    lane = lax.broadcasted_iota(jnp.int32, (rows, keys), 1)
+    sub = lax.broadcasted_iota(jnp.int32, (rows, keys), 0)
+    block = lane // rows
+    back = jnp.where(
+        block == 0,
+        deltas[0],
+        jnp.where(block == 1, deltas[1], jnp.where(block == 2, deltas[2], deltas[3])),
+    )
+    distance = sub - (lane - block * rows) + back * rows
+    allowed = (distance >= 0) & (distance <= WIN_DEV * rows) & (seg_col == seg_row)
+    bias = jnp.where(allowed, 0.0, MASKED)
     scale = 1.0 / HEAD_DIM**0.5
     heads = [slice(head * HEAD_DIM, (head + 1) * HEAD_DIM) for head in range(HEADS_STEP)]
-    scores = jnp.stack(
-        [
-            lax.dot_general(
-                q[:, cols],
-                jnp.concatenate([k0[:, cols], k1[:, cols], k2[:, cols], k3[:, cols]], axis=0),
-                (((1,), (1,)), ((), ())),
-                preferred_element_type=jnp.float32,
-            )
-            for cols in heads
+
+    @pl.loop(0, model // width)
+    def _(step):
+        at = pl.ds(pl.multiple_of(step * width, width), width)
+        query = q[:, at]
+        key = jnp.concatenate([k0[:, at], k1[:, at], k2[:, at], k3[:, at]], axis=0)
+        value = jnp.concatenate([v0[:, at], v1[:, at], v2[:, at], v3[:, at]], axis=0)
+        scores = jnp.stack(
+            [
+                lax.dot_general(
+                    query[:, cols], key[:, cols], (((1,), (1,)), ((), ())),
+                    preferred_element_type=jnp.float32,
+                )
+                for cols in heads
+            ]
+        )
+        scores = scores * scale + bias[None]
+        expo = jnp.exp(scores - jnp.max(scores, axis=2, keepdims=True))
+        denom = jnp.sum(expo, axis=2, keepdims=True)
+        probs = expo.astype(jnp.bfloat16)
+        outs = [
+            jnp.dot(probs[head], value[:, cols], preferred_element_type=jnp.float32)
+            / denom[head]
+            for head, cols in enumerate(heads)
         ]
-    )
-    scores = scores * scale + bias[...][None]
-    expo = jnp.exp(scores - jnp.max(scores, axis=2, keepdims=True))
-    denom = jnp.sum(expo, axis=2, keepdims=True)
-    probs = expo.astype(jnp.bfloat16)
-    outs = [
-        jnp.dot(
-            probs[head],
-            jnp.concatenate([v0[:, cols], v1[:, cols], v2[:, cols], v3[:, cols]], axis=0),
+        mixed_out[:, at] = resid[:, at].astype(jnp.float32) + jnp.concatenate(outs, axis=1)
+
+    mixed = mixed_out[...]
+    normed = (
+        mixed * lax.rsqrt(jnp.mean(mixed * mixed, axis=1, keepdims=True) + 1e-05) * gain[...]
+    ).astype(jnp.bfloat16)
+    across = lax.broadcasted_iota(jnp.int32, (rows, rows), 1)
+    down = lax.broadcasted_iota(jnp.int32, (rows, rows), 0)
+    upper = jnp.where(down < across, 1.0, 0.0).astype(jnp.bfloat16)
+    eye = jnp.where(down == across, 1.0, 0.0).astype(jnp.bfloat16)
+    slot = lax.broadcasted_iota(jnp.int32, (32, rows), 0)
+
+    def picks(expert):
+        hit = routes[...] == expert
+        member = jnp.max(jnp.where(hit, 1.0, 0.0), axis=0, keepdims=True)
+        weight = jnp.sum(
+            jnp.where(hit, gates[...].astype(jnp.float32), 0.0), axis=0, keepdims=True
+        )
+        rank = jnp.dot(
+            jnp.broadcast_to(member, (8, rows)).astype(jnp.bfloat16),
+            upper,
             preferred_element_type=jnp.float32,
-        )
-        / denom[head]
-        for head, cols in enumerate(heads)
-    ]
-    width = HEADS_STEP * HEAD_DIM
-    at = pl.ds(pl.multiple_of(step * width, width), width)
-    mixed_out[:, at] = resid[...].astype(jnp.float32) + jnp.concatenate(outs, axis=1)
-
-    @pl.when(step == steps - 1)
-    def _():
-        mixed = mixed_out[...]
-        normed = (
-            mixed * lax.rsqrt(jnp.mean(mixed * mixed, axis=1, keepdims=True) + 1e-05) * gain[...]
+        )[0:1].astype(jnp.int32)
+        return member > 0.5, weight, rank
+
+    def spread(pick, weight):
+        return lax.dot_general(
+            eye,
+            jnp.where(pick, weight, 0.0).astype(jnp.bfloat16),
+            (((1,), (1,)), ((), ())),
+            preferred_element_type=jnp.float32,
         ).astype(jnp.bfloat16)
-        across = lax.broadcasted_iota(jnp.int32, (rows, rows), 1)
-        down = lax.broadcasted_iota(jnp.int32, (rows, rows), 0)
-        upper = jnp.where(down < across, 1.0, 0.0).astype(jnp.bfloat16)
-        eye = jnp.where(down == across, 1.0, 0.0).astype(jnp.bfloat16)
-        slot = lax.broadcasted_iota(jnp.int32, (32, rows), 0)
-
-        def picks(expert):
-            hit = routes[...] == expert
-            member = jnp.max(jnp.where(hit, 1.0, 0.0), axis=0, keepdims=True)
-            weight = jnp.sum(
-                jnp.where(hit, gates[...].astype(jnp.float32), 0.0), axis=0, keepdims=True
-            )
-            rank = jnp.dot(
-                jnp.broadcast_to(member, (8, rows)).astype(jnp.bfloat16),
-                upper,
-                preferred_element_type=jnp.float32,
-            )[0:1].astype(jnp.int32)
-            return member > 0.5, weight, rank
-
-        def spread(pick, weight):
-            return lax.dot_general(
-                eye,
-                jnp.where(pick, weight, 0.0).astype(jnp.bfloat16),
-                (((1,), (1,)), ((), ())),
-                preferred_element_type=jnp.float32,
-            ).astype(jnp.bfloat16)
-
-        def packed(pick):
-            return jnp.dot(
-                jnp.where(pick, 1.0, 0.0).astype(jnp.bfloat16),
-                normed,
-                preferred_element_type=jnp.float32,
-            ).astype(jnp.bfloat16)
-
-        member, weight, rank = picks(deltas[4])
-        pick = (slot == rank) & member
-        mine = packed(pick)
-        early_out[...] = mine[:EARLY]
-        rest_out[...] = mine[EARLY:CAP]
-        weight_out[0] = spread(pick & (slot < EARLY), weight)
-        weight_out[1] = spread((slot - CAP + EARLY == rank) & (slot >= CAP) & member, weight)
-        member, weight, rank = picks(1 - deltas[4])
-        pick = (slot == rank) & member
-        send_out[...] = packed(pick)[:CAP]
-        weight_out[2] = spread(pick, weight)
+
+    def packed(pick):
+        return jnp.dot(
+            jnp.where(pick, 1.0, 0.0).astype(jnp.bfloat16),
+            normed,
+            preferred_element_type=jnp.float32,
+        ).astype(jnp.bfloat16)
+
+    member, weight, rank = picks(deltas[4])
+    pick = (slot == rank) & member
+    mine = packed(pick)
+    early_out[...] = mine[:EARLY]
+    rest_out[...] = mine[EARLY:CAP]
+    weight_out[0] = spread(pick & (slot < EARLY), weight)
+    weight_out[1] = spread((slot - CAP + EARLY == rank) & (slot >= CAP) & member, weight)
+    member, weight, rank = picks(1 - deltas[4])
+    pick = (slot == rank) & member
+    send_out[...] = packed(pick)[:CAP]
+    weight_out[2] = spread(pick, weight)
 
 
 def attention(deltas, q, pairs, seg_own, resid, gain, routes, gates):
     rows, width = q.shape
-    cols = HEADS_STEP * HEAD_DIM
-    top = routes.shape[0]
-    piece = pl.BlockSpec((rows, cols), lambda j, *_: (0, j))
-    tail = pl.BlockSpec((SPARE, HEAD_DIM), lambda j, *_: (0, width // HEAD_DIM))
-
-    def whole(shape):
-        return pl.BlockSpec(shape, lambda j, *_: (0,) * len(shape))
-
-    bundles = pairs[2::2]
     return pl.pallas_call(
         attention_kernel,
-        grid_spec=pltpu.PrefetchScalarGridSpec(
-            num_scalar_prefetch=1,
-            grid=(width // cols,),
-            in_specs=[piece] * (1 + len(pairs))
-            + [whole((1, rows))]
-            + [tail] * len(bundles)
-            + [
-                piece,
-                whole((1, width)),
-                whole((top, rows)),
-                whole((top, rows)),
-            ],
-            out_specs=[
-                whole((rows, width)),
-                whole((EARLY, width)),
-                whole((CAP - EARLY, width)),
-                whole((CAP, width)),
-                whole((3, rows, 32)),
-            ],
-            scratch_shapes=[pltpu.VMEM((rows, (WIN_DEV + 1) * rows), jnp.float32)],
-        ),
+        in_specs=[pl.BlockSpec(memory_space=pltpu.SMEM)] + [NEAR] * (6 + len(pairs)),
+        out_specs=[NEAR] * 5,
         out_shape=[
             pltpu.VMEM((rows, width), jnp.float32),
             jax.ShapeDtypeStruct((EARLY, width), jnp.bfloat16),
@@ -216,9 +203,38 @@
         ),
         name="attention",
     )(
-        deltas, far(q), far(pairs[0]), far(pairs[1]), *pairs[2:], far(seg_own), *bundles,
-        far(resid), far(gain), far(routes), far(gates),
-    )
+        deltas, close(q), close(pairs[0]), close(pairs[1]), *pairs[2:], close(seg_own),
+        close(resid), close(gain), close(routes), close(gates),
+    )
+
+
+def bring_kernel(count, *refs):
+    sources, held, sems = refs[:count], refs[count + 1 : 2 * count + 1], refs[-1]
+    copies = [
+        pltpu.make_async_copy(source, target, sems.at[at])
+        for at, (source, target) in enumerate(zip(sources, held))
+    ]
+    for copy in copies:
+        copy.start()
+    for copy in copies:
+        copy.wait()
+
+
+def bring(arrays, after):
+    count = len(arrays)
+    anywhere = pl.BlockSpec(memory_space=pl.ANY)
+    return pl.pallas_call(
+        functools.partial(bring_kernel, count),
+        in_specs=[anywhere] * (count + 1),
+        out_specs=[NEAR] * count,
+        out_shape=[pltpu.VMEM(x.shape, x.dtype) for x in arrays],
+        scratch_shapes=[pltpu.SemaphoreType.DMA((count,))],
+        compiler_params=pltpu.CompilerParams(vmem_limit_bytes=2 * MIB),
+        cost_estimate=pl.CostEstimate(
+            flops=0, bytes_accessed=4 * sum(x.size for x in arrays), transcendentals=0
+        ),
+        name="bring",
+    )(*[far(x) for x in arrays], after)
 
 
 def fetch_kernel(parts, source, after, held, sems):
@@ -410,37 +426,52 @@
     shard_count = count // E_WIN
     odd = own % 2
 
-    next_chip = [(i, i + 2) for i in range(count - 2)]
+    next_chip = [(i, i + 2) for i in range(count - 2) if i % 4 != 3]
     crossing = [(i, i + 1) for i in range(0, count, 2)]
     crossing += [(i, i + 3) for i in range(1, count - 3, 2)]
+    passing = [(i, i - 1) for i in range(2, count, 4)]
 
     def swapped(block, mask):
         return lax.ppermute(block, "expert", [(i, i ^ mask) for i in range(count)])
 
     seg_own = segment_ids.reshape(1, -1)
-    value_two = lax.ppermute(values, "expert", next_chip)
-    key_block = bundle(keys, seg_own)
-    key_two = lax.ppermute(key_block, "expert", next_chip)
-    value_cross = lax.ppermute(values, "expert", crossing)
-    key_cross = lax.ppermute(key_block, "expert", crossing)
     beyond = 2 * WIN_DEV + 2
     delta_list = [0 * own, 0 * own + 2, 3 - 2 * odd, 1 + 2 * odd]
     my_expert = own // shard_count
+    relayed = (own % 4 == 1).astype(jnp.int32)
     scalars = jnp.stack(
-        [jnp.where(own >= delta, delta, beyond) for delta in delta_list] + [my_expert]
+        [jnp.where(own >= delta, delta, beyond) for delta in delta_list] + [my_expert, relayed]
     ).astype(jnp.int32)
-    held = [fetch(w, scalars) for w in (w_gate, w_up, w_down)]
-    key_two, held[0], held[1] = lax.optimization_barrier((key_two, held[0], held[1]))
+
+    key_block = bundle(keys, seg_own)
+    key_cross = lax.ppermute(key_block, "expert", crossing)
+    value_cross = lax.ppermute(values, "expert", crossing)
+    key_next = lax.ppermute(key_block, "expert", next_chip)
+    value_next = lax.ppermute(values, "expert", next_chip)
+    key_passed = lax.ppermute(key_cross, "expert", passing)
+    value_passed = lax.ppermute(value_cross, "expert", passing)
+    mine = bring(
+        [
+            queries, keys, values, seg_own, resid, norm_gain.reshape(1, -1), routes.T,
+            route_gates.T,
+        ],
+        scalars,
+    )
+    gate_held = fetch(w_gate, scalars)
+    key_two = choose(scalars, key_passed, key_next)
+    key_two, gate_held, mine = lax.optimization_barrier((key_two, gate_held, mine))
     key_mirror = swapped(key_two, 1)
-    value_two, held[2] = lax.optimization_barrier((value_two, held[2]))
+    value_two = choose(scalars, value_passed, value_next)
     value_mirror = swapped(value_two, 1)
 
+    queries, keys, values, seg_own, resid, gain, routes_held, gates_held = mine
     mixed, early, rest, send, weight = attention(
         scalars,
         queries,
         [keys, values, key_two, value_two, key_cross, value_cross, key_mirror, value_mirror],
-        seg_own, resid, norm_gain.reshape(1, -1), routes.T, route_gates.T,
-    )
+        seg_own, resid, gain, routes_held, gates_held,
+    )
+    up_held, down_held = fetch(w_up, weight), fetch(w_down, weight)
     partner = [(i, (i + shard_count) % count) for i in range(count)]
     masks = list(range(2, shard_count, 2))[::-1]
     got = lax.ppermute(send, "expert", partner)
@@ -460,7 +491,10 @@
         return [blocks[0]] + moved[::-1]
 
     early_blocks = spread(early)
-    got, early_blocks = lax.optimization_barrier((got, early_blocks))
+    got, early_blocks, up_held, down_held = lax.optimization_barrier(
+        (got, early_blocks, up_held, down_held)
+    )
+    held = [gate_held, up_held, down_held]
     early_parts = experts(*both_cores(early_blocks), *held)
     late_blocks = spread(join(got, rest))
     late_blocks, early_parts = lax.optimization_barrier((late_blocks, early_parts))

time: 114 us -> 113 us (level)
  Pallas kernels: 29.6 us -> 30.8 us
    ppermute x18, starting transfers between devices: 23.5 us -> 15 us  [swapped(): return lax.ppermute(block, 'expert', [(i, i ^ mask) for i in range(count)])]
    ppermute x18, waiting for transfers between devices: 28.4 us -> 22.3 us  [swapped(): return lax.ppermute(block, 'expert', [(i, i ^ mask) for i in range(count)])]
    ppermute x2 -> x4, waiting for transfers between devices: 3.71 us -> 9.15 us  [the longest x1 9.14 us: shards(): value_next = lax.ppermute(values, 'expert', next_chip)]
    ppermute x2 -> x4, starting transfers between devices: 8.33 us -> 11.3 us  [the longest x1 5.66 us: shards(): value_next = lax.ppermute(values, 'expert', next_chip)]
    ppermute x1, starting transfers between devices: 1.96 us -> 4.6 us  [shards(): value_cross = lax.ppermute(values, 'expert', crossing)]
    pallas_call x1 -> x4, Pallas kernels: 5.49 us -> 6.79 us  [the longest x1 3.49 us: attention(): pl.pallas_call(attention_kernel, in_specs=[pl.BlockSpec(memory_space=pltp...]
  transfers between devices with their start and end apart: 24 -> 26, of which waited for: 13 -> 10; matrix products, arithmetic and copies ran while one was open for 0% -> 0% of each run, Pallas kernels for 19% -> 22%
where the time goes in v8:
time: 113 us
  starting transfers between devices  41.1 us (36%)
  waiting for transfers between devices  40.9 us (36%)
  Pallas kernels  30.8 us (27%)
    ppermute x18, waiting for transfers between devices, swapped(): return lax.ppermute(block, 'expert', [(i, i ^ mask) for i in range(count)])  22.3 us
    ppermute x18, starting transfers between devices, swapped(): return lax.ppermute(block, 'expert', [(i, i ^ mask) for i in range(count)])  15 us
    pallas_call x2, Pallas kernels, experts(): pl.pallas_call(experts_kernel, in_specs=[NEAR] * 5, out_specs=[NEAR] * 2,...  10.6 us
    pallas_call x3, Pallas kernels, fetch(): pl.pallas_call(functools.partial(fetch_kernel, parts), in_specs=[anywhere...  10.5 us
    ppermute x1, waiting for transfers between devices, shards(): other = lax.ppermute(back, 'expert', partner)  9.45 us
    ppermute x1, waiting for transfers between devices, shards(): value_next = lax.ppermute(values, 'expert', next_chip)  9.14 us
    ppermute x1, starting transfers between devices, shards(): got = lax.ppermute(send, 'expert', partner)  6.52 us
    ppermute x1, starting transfers between devices, shards(): value_next = lax.ppermute(values, 'expert', next_chip)  5.66 us
  transfers between devices with their start and end apart: 26, of which 10 were waited for; matrix products, arithmetic and copies ran while one was open for 0% of the time, Pallas kernels for 22%

profile of v8, /device:TPU:0, one launch (start us, length us, event | category | flops | bytes accessed | tf_op | source)
XLA Modules:
  0.0 113.2 jit_solution(13740919646012378933)
XLA Ops:
  1.1 2.4 %collective-permute-start = (bf16[64,4224]{1,0:T(8,128)(2,1)S(1)}, bf16[64,4224]{1,0:T(8,128)(2,1)S(1)}, u32[]{:S(2)}, u32[]{:S(2)}) collective-permute-start(bf16[64,4224]{1,0:T(8,128)(2,1)S(1)} %bundle.1), channel_id=1, source_target_pairs={{0,1},{2,3},{4,5},{6,7},{8,9},{10,11},{12,13},{14,15},{1,4},{3,6},... | collective-permute-start | bytes 1622024 | tf_op jit(solution)/shard_map/ppermute | solution.py:447
  3.5 4.6 %collective-permute-start.3 = (bf16[64,4096]{1,0:T(8,128)(2,1)}, bf16[64,4096]{1,0:T(8,128)(2,1)S(1)}, u32[]{:S(2)}, u32[]{:S(2)}) collective-permute-start(bf16[64,4096]{1,0:T(8,128)(2,1)} %refs_2_.1), channel_id=1, source_target_pairs={{0,1},{2,3},{4,5},{6,7},{8,9},{10,11},{12,13},{14,15},{1,4},{3,6},... | collective-permute-start | bytes 1572872 | tf_op jit(solution)/shard_map/ppermute | solution.py:448
  8.1 3.5 %collective-permute-start.2 = (bf16[64,4224]{1,0:T(8,128)(2,1)S(1)}, bf16[64,4224]{1,0:T(8,128)(2,1)S(1)}, u32[]{:S(2)}, u32[]{:S(2)}) collective-permute-start(bf16[64,4224]{1,0:T(8,128)(2,1)S(1)} %bundle.1), channel_id=1, source_target_pairs={{0,2},{1,3},{2,4},{4,6},{5,7},{6,8},{8,10},{9,11},{10,12},{12,14},... | collective-permute-start | bytes 1622024 | tf_op jit(solution)/shard_map/ppermute | solution.py:449
  12.3 5.7 %collective-permute-start.5 = (bf16[64,4096]{1,0:T(8,128)(2,1)}, bf16[64,4096]{1,0:T(8,128)(2,1)S(1)}, u32[]{:S(2)}, u32[]{:S(2)}) collective-permute-start(bf16[64,4096]{1,0:T(8,128)(2,1)} %refs_2_.1), channel_id=1, source_target_pairs={{0,2},{1,3},{2,4},{4,6},{5,7},{6,8},{8,10},{9,11},{10,12},{12,14},... | collective-permute-start | bytes 1572872 | tf_op jit(solution)/shard_map/ppermute | solution.py:450
  19.5 3.5 %fetch.3.w_gate = bf16[4096,1024]{1,0:T(8,128)(2,1)S(1)} custom-call(bf16[4096,1024]{1,0:T(8,128)(2,1)} %source.3, s32[6]{0:T(128)S(1)} %stack.31.flags.after.refs_8_.deltas), custom_call_target="tpu_custom_call" | custom-call | bytes 16777216 | tf_op jit(solution)/shard_map/fetch/pallas_call | solution.py:255
  25.4 9.1 %collective-permute-done.5.second = bf16[64,4096]{1,0:T(8,128)(2,1)S(1)} collective-permute-done((bf16[64,4096]{1,0:T(8,128)(2,1)}, bf16[64,4096]{1,0:T(8,128)(2,1)S(1)}, u32[]{:S(2)}, u32[]{:S(2)}) %collective-permute-start.5) | collective-permute-done | bytes 524320 | tf_op jit(solution)/shard_map/ppermute | solution.py:450
  35.7 1.9 %collective-permute-done.7.v3 = bf16[64,4096]{1,0:T(8,128)(2,1)S(1)} collective-permute-done((bf16[64,4096]{1,0:T(8,128)(2,1)S(1)}, bf16[64,4096]{1,0:T(8,128)(2,1)S(1)}, u32[]{:S(2)}, u32[]{:S(2)}) %collective-permute-start.7) | collective-permute-done | bytes 524320 | tf_op jit(solution)/shard_map/ppermute | solution.py:435
  37.6 3.5 %attention.1 = (f32[64,4096]{1,0:T(8,128)S(1)}, bf16[16,4096]{1,0:T(8,128)(2,1)S(1)}, bf16[4,4096]{1,0:T(4,128)(2,1)S(1)}, bf16[20,4096]{1,0:T(8,128)(2,1)S(1)}, bf16[3,64,32]{2,1,0:T(8,128)(2,1)S(1)}) custom-call(s32[6]{0:T(128)S(1)} %stack.31.flags.after.refs_8_.deltas, bf16[64,4096]{1,0:T(8,128)(2,1)S(1)} %get-tuple-element.75.q, ...), custom_call_target="tpu_custom_call" | custom-call | flops 268435456 | bytes 8388608 | tf_op jit(solution)/shard_map/attention/pallas_call | solution.py:188
  41.1 6.5 %collective-permute-start.8 = (bf16[20,4096]{1,0:T(8,128)(2,1)S(1)}, bf16[20,4096]{1,0:T(8,128)(2,1)S(1)}, u32[]{:S(2)}, u32[]{:S(2)}) collective-permute-start(bf16[20,4096]{1,0:T(8,128)(2,1)S(1)} %get-tuple-element.86), channel_id=1, source_target_pairs={{0,8},{1,9},{2,10},{3,11},{4,12},{5,13},{6,14},{7,15},{8,0},{9,1},... | collective-permute-start | bytes 491528 | tf_op jit(solution)/shard_map/ppermute | solution.py:477
  49.0 2.1 %collective-permute-start.9 = (bf16[16,4096]{1,0:T(8,128)(2,1)S(1)}, bf16[16,4096]{1,0:T(8,128)(2,1)S(1)}, u32[]{:S(2)}, u32[]{:S(2)}) collective-permute-start(bf16[16,4096]{1,0:T(8,128)(2,1)S(1)} %get-tuple-element.90.refs_0_), channel_id=1, source_target_pairs={{0,6},{1,7},{2,4},{3,5},{4,2},{5,3},{6,0},{7,1},{8,14},{9,15},{10,... | collective-permute-start | bytes 393224 | tf_op jit(solution)/shard_map/ppermute | solution.py:435
  51.1 3.5 %fetch.5.w_down = bf16[1024,4096]{1,0:T(8,128)(2,1)S(1)} custom-call(bf16[1024,4096]{1,0:T(8,128)(2,1)} %source.5, bf16[3,64,32]{2,1,0:T(8,128)(2,1)S(1)} %get-tuple-element.85.after.weight), custom_call_target="tpu_custom_call" | custom-call | bytes 16777216 | tf_op jit(solution)/shard_map/fetch/pallas_call | solution.py:255
  54.6 3.5 %fetch.4.w_up = bf16[4096,1024]{1,0:T(8,128)(2,1)S(1)} custom-call(bf16[4096,1024]{1,0:T(8,128)(2,1)} %source.4, bf16[3,64,32]{2,1,0:T(8,128)(2,1)S(1)} %get-tuple-element.85.after.weight), custom_call_target="tpu_custom_call" | custom-call | bytes 16777216 | tf_op jit(solution)/shard_map/fetch/pallas_call | solution.py:255
  58.2 2.0 %collective-permute-done.9.refs_1_ = bf16[16,4096]{1,0:T(8,128)(2,1)S(1)} collective-permute-done((bf16[16,4096]{1,0:T(8,128)(2,1)S(1)}, bf16[16,4096]{1,0:T(8,128)(2,1)S(1)}, u32[]{:S(2)}, u32[]{:S(2)}) %collective-permute-start.9) | collective-permute-done | bytes 131104 | tf_op jit(solution)/shard_map/ppermute | solution.py:435
  62.1 1.7 %collective-permute-start.12 = (bf16[24,4096]{1,0:T(8,128)(2,1)S(1)}, bf16[24,4096]{1,0:T(8,128)(2,1)S(1)}, u32[]{:S(2)}, u32[]{:S(2)}) collective-permute-start(bf16[24,4096]{1,0:T(8,128)(2,1)S(1)} %join.1.refs_0_), channel_id=1, source_target_pairs={{0,6},{1,7},{2,4},{3,5},{4,2},{5,3},{6,0},{7,1},{8,14},{9,15},{10,... | collective-permute-start | bytes 589832 | tf_op jit(solution)/shard_map/ppermute | solution.py:435
  63.9 4.5 %experts.2 = (bf16[64,4096]{1,0:T(8,128)(2,1)S(1)}, bf16[64,4096]{1,0:T(8,128)(2,1)S(1)}) custom-call(bf16[64,4096]{1,0:T(8,128)(2,1)S(1)} %pile.2.local, bf16[64,4096]{1,0:T(8,128)(2,1)S(1)} %collective-permute-done.15.remote, bf16[4096,1024]{1,0:T(8,128)(2,1)S(1)} %fetch.3.w_gate, bf16[4096,1024]{1,0:T(8,128)(2,1)S(1)} %fetch.4.w_up, ...), custom_call_target="tpu_custom_call" | custom-call | flops 3221225472 | bytes 2097152 | tf_op jit(solution)/shard_map/experts/pallas_call | solution.py:294
  68.4 4.7 %collective-permute-done.12.refs_1_ = bf16[24,4096]{1,0:T(8,128)(2,1)S(1)} collective-permute-done((bf16[24,4096]{1,0:T(8,128)(2,1)S(1)}, bf16[24,4096]{1,0:T(8,128)(2,1)S(1)}, u32[]{:S(2)}, u32[]{:S(2)}) %collective-permute-start.12) | collective-permute-done | bytes 196640 | tf_op jit(solution)/shard_map/ppermute | solution.py:435
  73.7 2.5 %collective-permute-done.17.second = bf16[64,4096]{1,0:T(8,128)(2,1)S(1)} collective-permute-done((bf16[64,4096]{1,0:T(8,128)(2,1)S(1)}, bf16[64,4096]{1,0:T(8,128)(2,1)S(1)}, u32[]{:S(2)}, u32[]{:S(2)}) %collective-permute-start.17) | collective-permute-done | bytes 524320 | tf_op jit(solution)/shard_map/ppermute | solution.py:435
  78.2 1.7 %collective-permute-start.20 = (bf16[16,4096]{1,0:T(8,128)(2,1)S(1)}, bf16[16,4096]{1,0:T(8,128)(2,1)S(1)}, u32[]{:S(2)}, u32[]{:S(2)}) collective-permute-start(bf16[16,4096]{1,0:T(8,128)(2,1)S(1)} %get-tuple-element.116), channel_id=1, source_target_pairs={{0,6},{1,7},{2,4},{3,5},{4,2},{5,3},{6,0},{7,1},{8,14},{9,15},{10,... | collective-permute-start | bytes 393224 | tf_op jit(solution)/shard_map/ppermute | solution.py:435
  79.9 6.1 %experts.3 = (bf16[96,4096]{1,0:T(8,128)(2,1)S(1)}, bf16[96,4096]{1,0:T(8,128)(2,1)S(1)}) custom-call(bf16[96,4096]{1,0:T(8,128)(2,1)S(1)} %pile.3.local, bf16[96,4096]{1,0:T(8,128)(2,1)S(1)} %collective-permute-done.16.remote, bf16[4096,1024]{1,0:T(8,128)(2,1)S(1)} %fetch.3.w_gate, bf16[4096,1024]{1,0:T(8,128)(2,1)S(1)} %fetch.4.w_up, ...), custom_call_target="tpu_custom_call" | custom-call | flops 4831838208 | bytes 3145728 | tf_op jit(solution)/shard_map/experts/pallas_call | solution.py:294
  86.2 2.3 %collective-permute-done.21.second = bf16[96,4096]{1,0:T(8,128)(2,1)S(1)} collective-permute-done((bf16[96,4096]{1,0:T(8,128)(2,1)S(1)}, bf16[96,4096]{1,0:T(8,128)(2,1)S(1)}, u32[]{:S(2)}, u32[]{:S(2)}) %collective-permute-start.21) | collective-permute-done | bytes 786464 | tf_op jit(solution)/shard_map/ppermute | solution.py:435
  90.5 1.7 %collective-permute-start.24 = (bf16[24,4096]{1,0:T(8,128)(2,1)S(1)}, bf16[24,4096]{1,0:T(8,128)(2,1)S(1)}, u32[]{:S(2)}, u32[]{:S(2)}) collective-permute-start(bf16[24,4096]{1,0:T(8,128)(2,1)S(1)} %get-tuple-element.122), channel_id=1, source_target_pairs={{0,6},{1,7},{2,4},{3,5},{4,2},{5,3},{6,0},{7,1},{8,14},{9,15},{10,... | collective-permute-start | bytes 589832 | tf_op jit(solution)/shard_map/ppermute | solution.py:435
  92.2 3.5 %collective-permute-done.22.refs_1_ = bf16[24,4096]{1,0:T(8,128)(2,1)S(1)} collective-permute-done((bf16[24,4096]{1,0:T(8,128)(2,1)S(1)}, bf16[24,4096]{1,0:T(8,128)(2,1)S(1)}, u32[]{:S(2)}, u32[]{:S(2)}) %collective-permute-start.22) | collective-permute-done | bytes 196640 | tf_op jit(solution)/shard_map/ppermute | solution.py:435
  96.8 4.2 %collective-permute-done.24.refs_3_ = bf16[24,4096]{1,0:T(8,128)(2,1)S(1)} collective-permute-done((bf16[24,4096]{1,0:T(8,128)(2,1)S(1)}, bf16[24,4096]{1,0:T(8,128)(2,1)S(1)}, u32[]{:S(2)}, u32[]{:S(2)}) %collective-permute-start.24) | collective-permute-done | bytes 196640 | tf_op jit(solution)/shard_map/ppermute | solution.py:435
  102.4 9.4 %collective-permute-done.25.other = bf16[20,4096]{1,0:T(8,128)(2,1)S(1)} collective-permute-done((bf16[20,4096]{1,0:T(8,128)(2,1)S(1)}, bf16[20,4096]{1,0:T(8,128)(2,1)S(1)}, u32[]{:S(2)}, u32[]{:S(2)}) %collective-permute-start.25) | collective-permute-done | bytes 163872 | tf_op jit(solution)/shard_map/ppermute | solution.py:509
  (46 shorter events, 18.8 us)
Async XLA Ops:
  1.1 10.5 %collective-permute-start = (bf16[64,4224]{1,0:T(8,128)(2,1)S(1)}, bf16[64,4224]{1,0:T(8,128)(2,1)S(1)}, u32[]{:S(2)}, u32[]{:S(2)}) collective-permute-start(bf16[64,4224]{1,0:T(8,128)(2,1)S(1)} %bundle.1), channel_id=1, source_target_pairs={{0,1},{2,3},{4,5},{6,7},{8,9},{10,11},{12,13},{14,15},{1,4},{3,6},... | collective-permute-start | bytes 1622024 | tf_op jit(solution)/shard_map/ppermute | solution.py:447
  3.5 14.5 %collective-permute-start.3 = (bf16[64,4096]{1,0:T(8,128)(2,1)}, bf16[64,4096]{1,0:T(8,128)(2,1)S(1)}, u32[]{:S(2)}, u32[]{:S(2)}) collective-permute-start(bf16[64,4096]{1,0:T(8,128)(2,1)} %refs_2_.1), channel_id=1, source_target_pairs={{0,1},{2,3},{4,5},{6,7},{8,9},{10,11},{12,13},{14,15},{1,4},{3,6},... | collective-permute-start | bytes 1572872 | tf_op jit(solution)/shard_map/ppermute | solution.py:448
  8.1 16.6 %collective-permute-start.2 = (bf16[64,4224]{1,0:T(8,128)(2,1)S(1)}, bf16[64,4224]{1,0:T(8,128)(2,1)S(1)}, u32[]{:S(2)}, u32[]{:S(2)}) collective-permute-start(bf16[64,4224]{1,0:T(8,128)(2,1)S(1)} %bundle.1), channel_id=1, source_target_pairs={{0,2},{1,3},{2,4},{4,6},{5,7},{6,8},{8,10},{9,11},{10,12},{12,14},... | collective-permute-start | bytes 1622024 | tf_op jit(solution)/shard_map/ppermute | solution.py:449
  11.6 13.1 %collective-permute-start.1 = (bf16[64,4224]{1,0:T(8,128)(2,1)S(1)}, bf16[64,4224]{1,0:T(8,128)(2,1)S(1)}, u32[]{:S(2)}, u32[]{:S(2)}) collective-permute-start(bf16[64,4224]{1,0:T(8,128)(2,1)S(1)} %collective-permute-done.k2), channel_id=1, source_target_pairs={{2,1},{6,5},{10,9},{14,13},{18,17},{22,21},{26,25},{30,29}} | collective-permute-start | bytes 1622024 | tf_op jit(solution)/shard_map/ppermute | solution.py:451
  12.3 22.3 %collective-permute-start.5 = (bf16[64,4096]{1,0:T(8,128)(2,1)}, bf16[64,4096]{1,0:T(8,128)(2,1)S(1)}, u32[]{:S(2)}, u32[]{:S(2)}) collective-permute-start(bf16[64,4096]{1,0:T(8,128)(2,1)} %refs_2_.1), channel_id=1, source_target_pairs={{0,2},{1,3},{2,4},{4,6},{5,7},{6,8},{8,10},{9,11},{10,12},{12,14},... | collective-permute-start | bytes 1572872 | tf_op jit(solution)/shard_map/ppermute | solution.py:450
  17.9 16.6 %collective-permute-start.4 = (bf16[64,4096]{1,0:T(8,128)(2,1)S(1)}, bf16[64,4096]{1,0:T(8,128)(2,1)}, u32[]{:S(2)}, u32[]{:S(2)}) collective-permute-start(bf16[64,4096]{1,0:T(8,128)(2,1)S(1)} %collective-permute-done.3.v2), channel_id=1, source_target_pairs={{2,1},{6,5},{10,9},{14,13},{18,17},{22,21},{26,25},{30,29}} | collective-permute-start | bytes 1572872 | tf_op jit(solution)/shard_map/ppermute | solution.py:452
  25.3 12.4 %collective-permute-start.6 = (bf16[64,4224]{1,0:T(8,128)(2,1)S(1)}, bf16[64,4224]{1,0:T(8,128)(2,1)S(1)}, u32[]{:S(2)}, u32[]{:S(2)}) collective-permute-start(bf16[64,4224]{1,0:T(8,128)(2,1)S(1)} %choose.2.k1), channel_id=1, source_target_pairs={{0,1},{1,0},{2,3},{3,2},{4,5},{5,4},{6,7},{7,6},{8,9},{9,8},{10,11... | collective-permute-start | bytes 1622024 | tf_op jit(solution)/shard_map/ppermute | solution.py:435
  41.1 19.0 %collective-permute-start.8 = (bf16[20,4096]{1,0:T(8,128)(2,1)S(1)}, bf16[20,4096]{1,0:T(8,128)(2,1)S(1)}, u32[]{:S(2)}, u32[]{:S(2)}) collective-permute-start(bf16[20,4096]{1,0:T(8,128)(2,1)S(1)} %get-tuple-element.86), channel_id=1, source_target_pairs={{0,8},{1,9},{2,10},{3,11},{4,12},{5,13},{6,14},{7,15},{8,0},{9,1},... | collective-permute-start | bytes 491528 | tf_op jit(solution)/shard_map/ppermute | solution.py:477
  47.6 10.5 %collective-permute-start.11 = (bf16[16,4096]{1,0:T(8,128)(2,1)S(1)}, bf16[16,4096]{1,0:T(8,128)(2,1)S(1)}, u32[]{:S(2)}, u32[]{:S(2)}) collective-permute-start(bf16[16,4096]{1,0:T(8,128)(2,1)S(1)} %get-tuple-element.90.refs_0_), channel_id=1, source_target_pairs={{0,2},{1,3},{2,0},{3,1},{4,6},{5,7},{6,4},{7,5},{8,10},{9,11},{10,... | collective-permute-start | bytes 393224 | tf_op jit(solution)/shard_map/ppermute | solution.py:435
  47.6 10.5 %collective-permute-start.10 = (bf16[16,4096]{1,0:T(8,128)(2,1)S(1)}, bf16[16,4096]{1,0:T(8,128)(2,1)S(1)}, u32[]{:S(2)}, u32[]{:S(2)}) collective-permute-start(bf16[16,4096]{1,0:T(8,128)(2,1)S(1)} %get-tuple-element.90.refs_0_), channel_id=1, source_target_pairs={{0,4},{1,5},{2,6},{3,7},{4,0},{5,1},{6,2},{7,3},{8,12},{9,13},{10,... | collective-permute-start | bytes 393224 | tf_op jit(solution)/shard_map/ppermute | solution.py:435
  49.0 11.1 %collective-permute-start.9 = (bf16[16,4096]{1,0:T(8,128)(2,1)S(1)}, bf16[16,4096]{1,0:T(8,128)(2,1)S(1)}, u32[]{:S(2)}, u32[]{:S(2)}) collective-permute-start(bf16[16,4096]{1,0:T(8,128)(2,1)S(1)} %get-tuple-element.90.refs_0_), channel_id=1, source_target_pairs={{0,6},{1,7},{2,4},{3,5},{4,2},{5,3},{6,0},{7,1},{8,14},{9,15},{10,... | collective-permute-start | bytes 393224 | tf_op jit(solution)/shard_map/ppermute | solution.py:435
  60.2 3.7 %collective-permute-start.15 = (bf16[64,4096]{1,0:T(8,128)(2,1)S(1)}, bf16[64,4096]{1,0:T(8,128)(2,1)S(1)}, u32[]{:S(2)}, u32[]{:S(2)}) collective-permute-start(bf16[64,4096]{1,0:T(8,128)(2,1)S(1)} %pile.2.local), channel_id=1, source_target_pairs={{0,1},{1,0},{2,3},{3,2},{4,5},{5,4},{6,7},{7,6},{8,9},{9,8},{10,11... | collective-permute-start | bytes 1572872 | tf_op jit(solution)/shard_map/ppermute | solution.py:435
  60.3 8.0 %collective-permute-start.14 = (bf16[24,4096]{1,0:T(8,128)(2,1)S(1)}, bf16[24,4096]{1,0:T(8,128)(2,1)S(1)}, u32[]{:S(2)}, u32[]{:S(2)}) collective-permute-start(bf16[24,4096]{1,0:T(8,128)(2,1)S(1)} %join.1.refs_0_), channel_id=1, source_target_pairs={{0,2},{1,3},{2,0},{3,1},{4,6},{5,7},{6,4},{7,5},{8,10},{9,11},{10,... | collective-permute-start | bytes 589832 | tf_op jit(solution)/shard_map/ppermute | solution.py:435
  60.7 7.7 %collective-permute-start.13 = (bf16[24,4096]{1,0:T(8,128)(2,1)S(1)}, bf16[24,4096]{1,0:T(8,128)(2,1)S(1)}, u32[]{:S(2)}, u32[]{:S(2)}) collective-permute-start(bf16[24,4096]{1,0:T(8,128)(2,1)S(1)} %join.1.refs_0_), channel_id=1, source_target_pairs={{0,4},{1,5},{2,6},{3,7},{4,0},{5,1},{6,2},{7,3},{8,12},{9,13},{10,... | collective-permute-start | bytes 589832 | tf_op jit(solution)/shard_map/ppermute | solution.py:435
  62.1 10.9 %collective-permute-start.12 = (bf16[24,4096]{1,0:T(8,128)(2,1)S(1)}, bf16[24,4096]{1,0:T(8,128)(2,1)S(1)}, u32[]{:S(2)}, u32[]{:S(2)}) collective-permute-start(bf16[24,4096]{1,0:T(8,128)(2,1)S(1)} %join.1.refs_0_), channel_id=1, source_target_pairs={{0,6},{1,7},{2,4},{3,5},{4,2},{5,3},{6,0},{7,1},{8,14},{9,15},{10,... | collective-permute-start | bytes 589832 | tf_op jit(solution)/shard_map/ppermute | solution.py:435
  73.1 3.2 %collective-permute-start.16 = (bf16[96,4096]{1,0:T(8,128)(2,1)S(1)}, bf16[96,4096]{1,0:T(8,128)(2,1)S(1)}, u32[]{:S(2)}, u32[]{:S(2)}) collective-permute-start(bf16[96,4096]{1,0:T(8,128)(2,1)S(1)} %pile.3.local), channel_id=1, source_target_pairs={{0,1},{1,0},{2,3},{3,2},{4,5},{5,4},{6,7},{7,6},{8,9},{9,8},{10,11... | collective-permute-start | bytes 2359304 | tf_op jit(solution)/shard_map/ppermute | solution.py:435
  73.2 3.0 %collective-permute-start.17 = (bf16[64,4096]{1,0:T(8,128)(2,1)S(1)}, bf16[64,4096]{1,0:T(8,128)(2,1)S(1)}, u32[]{:S(2)}, u32[]{:S(2)}) collective-permute-start(bf16[64,4096]{1,0:T(8,128)(2,1)S(1)} %get-tuple-element.104), channel_id=1, source_target_pairs={{0,1},{1,0},{2,3},{3,2},{4,5},{5,4},{6,7},{7,6},{8,9},{9,8},{10,11... | collective-permute-start | bytes 1572872 | tf_op jit(solution)/shard_map/ppermute | solution.py:435
  76.4 9.7 %collective-permute-start.18 = (bf16[16,4096]{1,0:T(8,128)(2,1)S(1)}, bf16[16,4096]{1,0:T(8,128)(2,1)S(1)}, u32[]{:S(2)}, u32[]{:S(2)}) collective-permute-start(bf16[16,4096]{1,0:T(8,128)(2,1)S(1)} %get-tuple-element.114), channel_id=1, source_target_pairs={{0,2},{1,3},{2,0},{3,1},{4,6},{5,7},{6,4},{7,5},{8,10},{9,11},{10,... | collective-permute-start | bytes 393224 | tf_op jit(solution)/shard_map/ppermute | solution.py:435
  76.8 9.3 %collective-permute-start.19 = (bf16[16,4096]{1,0:T(8,128)(2,1)S(1)}, bf16[16,4096]{1,0:T(8,128)(2,1)S(1)}, u32[]{:S(2)}, u32[]{:S(2)}) collective-permute-start(bf16[16,4096]{1,0:T(8,128)(2,1)S(1)} %get-tuple-element.115), channel_id=1, source_target_pairs={{0,4},{1,5},{2,6},{3,7},{4,0},{5,1},{6,2},{7,3},{8,12},{9,13},{10,... | collective-permute-start | bytes 393224 | tf_op jit(solution)/shard_map/ppermute | solution.py:435
  78.2 7.9 %collective-permute-start.20 = (bf16[16,4096]{1,0:T(8,128)(2,1)S(1)}, bf16[16,4096]{1,0:T(8,128)(2,1)S(1)}, u32[]{:S(2)}, u32[]{:S(2)}) collective-permute-start(bf16[16,4096]{1,0:T(8,128)(2,1)S(1)} %get-tuple-element.116), channel_id=1, source_target_pairs={{0,6},{1,7},{2,4},{3,5},{4,2},{5,3},{6,0},{7,1},{8,14},{9,15},{10,... | collective-permute-start | bytes 393224 | tf_op jit(solution)/shard_map/ppermute | solution.py:435
  88.6 7.0 %collective-permute-start.22 = (bf16[24,4096]{1,0:T(8,128)(2,1)S(1)}, bf16[24,4096]{1,0:T(8,128)(2,1)S(1)}, u32[]{:S(2)}, u32[]{:S(2)}) collective-permute-start(bf16[24,4096]{1,0:T(8,128)(2,1)S(1)} %get-tuple-element.120), channel_id=1, source_target_pairs={{0,2},{1,3},{2,0},{3,1},{4,6},{5,7},{6,4},{7,5},{8,10},{9,11},{10,... | collective-permute-start | bytes 589832 | tf_op jit(solution)/shard_map/ppermute | solution.py:435
  89.0 7.8 %collective-permute-start.23 = (bf16[24,4096]{1,0:T(8,128)(2,1)S(1)}, bf16[24,4096]{1,0:T(8,128)(2,1)S(1)}, u32[]{:S(2)}, u32[]{:S(2)}) collective-permute-start(bf16[24,4096]{1,0:T(8,128)(2,1)S(1)} %get-tuple-element.121), channel_id=1, source_target_pairs={{0,4},{1,5},{2,6},{3,7},{4,0},{5,1},{6,2},{7,3},{8,12},{9,13},{10,... | collective-permute-start | bytes 589832 | tf_op jit(solution)/shard_map/ppermute | solution.py:435
  90.5 10.6 %collective-permute-start.24 = (bf16[24,4096]{1,0:T(8,128)(2,1)S(1)}, bf16[24,4096]{1,0:T(8,128)(2,1)S(1)}, u32[]{:S(2)}, u32[]{:S(2)}) collective-permute-start(bf16[24,4096]{1,0:T(8,128)(2,1)S(1)} %get-tuple-element.122), channel_id=1, source_target_pairs={{0,6},{1,7},{2,4},{3,5},{4,2},{5,3},{6,0},{7,1},{8,14},{9,15},{10,... | collective-permute-start | bytes 589832 | tf_op jit(solution)/shard_map/ppermute | solution.py:435
  101.1 10.7 %collective-permute-start.25 = (bf16[20,4096]{1,0:T(8,128)(2,1)S(1)}, bf16[20,4096]{1,0:T(8,128)(2,1)S(1)}, u32[]{:S(2)}, u32[]{:S(2)}) collective-permute-start(bf16[20,4096]{1,0:T(8,128)(2,1)S(1)} %get-tuple-element.124), channel_id=1, source_target_pairs={{0,8},{1,9},{2,10},{3,11},{4,12},{5,13},{6,14},{7,15},{8,0},{9,1},... | collective-permute-start | bytes 491528 | tf_op jit(solution)/shard_map/ppermute | solution.py:509
  (2 other events, 4.3 us)

commit v9 on v8

--- a/solution.py
+++ b/solution.py
@@ -11,7 +11,6 @@
 E_WIN = 2
 WIN_DEV = 3
 CAP = 20
-EARLY = 16
 SPARE = 16
 HEADS_STEP = 8
 MASKED = -1e30
@@ -71,12 +70,12 @@
         out_shape=jax.ShapeDtypeStruct(first.shape, first.dtype),
         compiler_params=pltpu.CompilerParams(vmem_limit_bytes=6 * MIB),
         name="choose",
-    )(flags, first, second)
+    )(flags, close(first), close(second))
 
 
 def attention_kernel(
     deltas, q, k0, v0, k1, v1, k2, v2, k3, v3, seg0, resid, gain, routes, gates,
-    mixed_out, early_out, rest_out, send_out, weight_out,
+    mixed_out, keep_out, send_out, weight_out,
 ):
     rows, model = q.shape
     keys = (WIN_DEV + 1) * rows
@@ -170,17 +169,11 @@
             preferred_element_type=jnp.float32,
         ).astype(jnp.bfloat16)
 
-    member, weight, rank = picks(deltas[4])
-    pick = (slot == rank) & member
-    mine = packed(pick)
-    early_out[...] = mine[:EARLY]
-    rest_out[...] = mine[EARLY:CAP]
-    weight_out[0] = spread(pick & (slot < EARLY), weight)
-    weight_out[1] = spread((slot - CAP + EARLY == rank) & (slot >= CAP) & member, weight)
-    member, weight, rank = picks(1 - deltas[4])
-    pick = (slot == rank) & member
-    send_out[...] = packed(pick)[:CAP]
-    weight_out[2] = spread(pick, weight)
+    for place, out in ((0, keep_out), (1, send_out)):
+        member, weight, rank = picks(deltas[4] if place == 0 else 1 - deltas[4])
+        pick = (slot == rank) & member
+        out[...] = packed(pick)[:CAP]
+        weight_out[place] = spread(pick, weight)
 
 
 def attention(deltas, q, pairs, seg_own, resid, gain, routes, gates):
@@ -188,13 +181,12 @@
     return pl.pallas_call(
         attention_kernel,
         in_specs=[pl.BlockSpec(memory_space=pltpu.SMEM)] + [NEAR] * (6 + len(pairs)),
-        out_specs=[NEAR] * 5,
+        out_specs=[NEAR] * 4,
         out_shape=[
             pltpu.VMEM((rows, width), jnp.float32),
-            jax.ShapeDtypeStruct((EARLY, width), jnp.bfloat16),
-            jax.ShapeDtypeStruct((CAP - EARLY, width), jnp.bfloat16),
             jax.ShapeDtypeStruct((CAP, width), jnp.bfloat16),
-            jax.ShapeDtypeStruct((3, rows, 32), jnp.bfloat16),
+            jax.ShapeDtypeStruct((CAP, width), jnp.bfloat16),
+            jax.ShapeDtypeStruct((E_WIN, rows, 32), jnp.bfloat16),
         ],
         compiler_params=pltpu.CompilerParams(vmem_limit_bytes=14 * MIB),
         cost_estimate=pl.CostEstimate(
@@ -310,29 +302,11 @@
     )(local, remote, close(w_gate), close(w_up), close(w_down))
 
 
-def join_kernel(first, second, out):
-    out[...] = jnp.concatenate(
-        [first[...].astype(jnp.float32), second[...].astype(jnp.float32)], axis=0
-    ).astype(out.dtype)
-
-
-def join(first, second):
-    width = first.shape[1]
-    return pl.pallas_call(
-        join_kernel,
-        in_specs=[NEAR, NEAR],
-        out_specs=NEAR,
-        out_shape=jax.ShapeDtypeStruct((first.shape[0] + second.shape[0], width), first.dtype),
-        compiler_params=pltpu.CompilerParams(vmem_limit_bytes=8 * MIB),
-        name="join",
-    )(first, second)
-
-
 def pile_kernel(*refs):
     blocks, out = refs[:-1], refs[-1]
-    rows = blocks[0].shape[0]
-    for at, block in enumerate(blocks):
-        out[pl.ds(at * rows, rows)] = block[...]
+    out[...] = jnp.concatenate(
+        [block[...].astype(jnp.float32) for block in blocks], axis=0
+    ).astype(out.dtype)
 
 
 def pile(blocks):
@@ -349,11 +323,9 @@
 
 def add_kernel(first, second, *outs):
     rows = outs[0].shape[0]
+    total = first[...].astype(jnp.float32) + second[...].astype(jnp.float32)
     for at, out in enumerate(outs):
-        part = pl.ds(at * rows, rows)
-        out[...] = (
-            first[part].astype(jnp.float32) + second[part].astype(jnp.float32)
-        ).astype(out.dtype)
+        out[...] = total[at * rows : (at + 1) * rows].astype(out.dtype)
 
 
 def add_split(first, second, blocks):
@@ -369,53 +341,45 @@
     )(first, second)
 
 
+def total(blocks):
+    result = blocks[0][...].astype(jnp.float32)
+    for block in blocks[1:]:
+        result = result + block[...].astype(jnp.float32)
+    return result.astype(jnp.bfloat16)
+
+
 def total_kernel(*refs):
-    blocks, all_out, back_out = refs[:-2], refs[-2], refs[-1]
-    total = blocks[0][...].astype(jnp.float32)
-    for block in blocks[1:]:
-        total = total + block[...].astype(jnp.float32)
-    total = total.astype(all_out.dtype)
-    all_out[...] = total
-    back_out[...] = total[:CAP]
+    refs[-1][...] = total(refs[:-1])
 
 
 def total_of(blocks):
-    rows, width = blocks[0].shape
     return pl.pallas_call(
         total_kernel,
         in_specs=[NEAR] * len(blocks),
-        out_specs=[NEAR] * 2,
-        out_shape=[
-            jax.ShapeDtypeStruct((rows, width), blocks[0].dtype),
-            jax.ShapeDtypeStruct((CAP, width), blocks[0].dtype),
-        ],
+        out_specs=NEAR,
+        out_shape=jax.ShapeDtypeStruct(blocks[0].shape, blocks[0].dtype),
         compiler_params=pltpu.CompilerParams(vmem_limit_bytes=(4 + len(blocks)) * MIB),
         name="total",
     )(*blocks)
 
 
-def combine_kernel(mixed, weight, late, other, *refs):
+def combine_kernel(place, base, weight, *refs):
     blocks, out = refs[:-1], refs[-1]
-    early = blocks[0][...].astype(jnp.float32)
-    for block in blocks[1:]:
-        early = early + block[...].astype(jnp.float32)
-    total = mixed[...]
-    for place, part in enumerate((early.astype(jnp.bfloat16), late[...], other[...])):
-        total = total + jnp.dot(
-            weight[place][:, : part.shape[0]], part, preferred_element_type=jnp.float32
-        )
-    out[...] = total.astype(jnp.bfloat16)
-
-
-def combine(mixed, weight, blocks, late, other):
-    return pl.pallas_call(
-        combine_kernel,
-        in_specs=[NEAR] * (4 + len(blocks)),
-        out_specs=NEAR,
-        out_shape=jax.ShapeDtypeStruct(mixed.shape, jnp.bfloat16),
+    part = jnp.dot(
+        weight[place][:, :CAP], total(blocks), preferred_element_type=jnp.float32
+    )
+    out[...] = (base[...] + part).astype(out.dtype)
+
+
+def combine(place, base, weight, blocks, result):
+    return pl.pallas_call(
+        functools.partial(combine_kernel, place),
+        in_specs=[NEAR] * (2 + len(blocks)),
+        out_specs=NEAR,
+        out_shape=result,
         compiler_params=pltpu.CompilerParams(vmem_limit_bytes=(8 + len(blocks)) * MIB),
         name="combine",
-    )(close(mixed), weight, late, other, *blocks)
+    )(close(base), weight, *blocks)
 
 
 def shards(
@@ -465,7 +429,7 @@
     value_mirror = swapped(value_two, 1)
 
     queries, keys, values, seg_own, resid, gain, routes_held, gates_held = mine
-    mixed, early, rest, send, weight = attention(
+    mixed, keep, send, weight = attention(
         scalars,
         queries,
         [keys, values, key_two, value_two, key_cross, value_cross, key_mirror, value_mirror],
@@ -490,24 +454,26 @@
         moved = [swapped(block, mask) for block, mask in zip(blocks[1:], masks)]
         return [blocks[0]] + moved[::-1]
 
-    early_blocks = spread(early)
-    got, early_blocks, up_held, down_held = lax.optimization_barrier(
-        (got, early_blocks, up_held, down_held)
+    early_blocks = spread(keep)
+    early_blocks, got, up_held, down_held = lax.optimization_barrier(
+        (early_blocks, got, up_held, down_held)
     )
     held = [gate_held, up_held, down_held]
     early_parts = experts(*both_cores(early_blocks), *held)
-    late_blocks = spread(join(got, rest))
+    late_blocks = spread(got)
     late_blocks, early_parts = lax.optimization_barrier((late_blocks, early_parts))
-    late_rows = both_cores(late_blocks)
+    late_blocks = summed(experts(*both_cores(late_blocks), *held))
     early_blocks = summed(early_parts)
-    late_rows, early_blocks = lax.optimization_barrier((late_rows, early_blocks))
+    late_blocks, early_blocks = lax.optimization_barrier((late_blocks, early_blocks))
+    late_blocks = scattered(late_blocks)
+    late_blocks[:-1], early_blocks = lax.optimization_barrier((late_blocks[:-1], early_blocks))
     early_blocks = scattered(early_blocks)
-    late_parts = experts(*late_rows, *held)
-    late_parts, early_blocks = lax.optimization_barrier((late_parts, early_blocks))
-    late_blocks = summed(late_parts)
-    late, back = total_of(scattered(late_blocks))
+    back = total_of(late_blocks)
     other = lax.ppermute(back, "expert", partner)
-    return combine(mixed, weight, early_blocks, late, other)
+    base = combine(0, mixed, weight, early_blocks, pltpu.VMEM(mixed.shape, jnp.float32))
+    return combine(
+        1, base, weight, [other], jax.ShapeDtypeStruct(mixed.shape, jnp.bfloat16)
+    )
 
 
 def solution(mesh):

time: 113 us -> 112 us (level)
    ppermute x1, waiting for transfers between devices: 9.45 us -> 0.01 us  [shards(): other = lax.ppermute(back, 'expert', partner)]
    ppermute x18, waiting for transfers between devices: 22.3 us -> 30.6 us  [swapped(): return lax.ppermute(block, 'expert', [(i, i ^ mask) for i in range(count)])]
    ppermute x18, starting transfers between devices: 15 us -> 17.5 us  [swapped(): return lax.ppermute(block, 'expert', [(i, i ^ mask) for i in range(count)])]
    ppermute x1, starting transfers between devices: 6.52 us -> 4.16 us  [shards(): got = lax.ppermute(send, 'expert', partner)]
  transfers between devices with their start and end apart: 26 -> 26, of which waited for: 10 -> 14; matrix products, arithmetic and copies ran while one was open for 0% -> 0% of each run, Pallas kernels for 22% -> 22%
where the time goes in v9:
time: 112 us
  starting transfers between devices  40.9 us (37%)
  waiting for transfers between devices  39.8 us (36%)
  Pallas kernels  30.9 us (28%)
    ppermute x18, waiting for transfers between devices, swapped(): return lax.ppermute(block, 'expert', [(i, i ^ mask) for i in range(count)])  30.6 us
    ppermute x18, starting transfers between devices, swapped(): return lax.ppermute(block, 'expert', [(i, i ^ mask) for i in range(count)])  17.5 us
    pallas_call x3, Pallas kernels, fetch(): pl.pallas_call(functools.partial(fetch_kernel, parts), in_specs=[anywhere...  10.5 us
    pallas_call x2, Pallas kernels, experts(): pl.pallas_call(experts_kernel, in_specs=[NEAR] * 5, out_specs=[NEAR] * 2,...  10.5 us
    ppermute x1, waiting for transfers between devices, shards(): value_next = lax.ppermute(values, 'expert', next_chip)  9.14 us
    ppermute x1, starting transfers between devices, shards(): value_next = lax.ppermute(values, 'expert', next_chip)  5.66 us
    ppermute x1, starting transfers between devices, shards(): value_cross = lax.ppermute(values, 'expert', crossing)  4.6 us
    ppermute x1, starting transfers between devices, shards(): got = lax.ppermute(send, 'expert', partner)  4.16 us
  transfers between devices with their start and end apart: 26, of which 14 were waited for; matrix products, arithmetic and copies ran while one was open for 0% of the time, Pallas kernels for 22%

profile of v9, /device:TPU:0, one launch (start us, length us, event | category | flops | bytes accessed | tf_op | source)
XLA Modules:
  0.0 111.9 jit_solution(11814099934873353647)
XLA Ops:
  1.1 2.4 %collective-permute-start = (bf16[64,4224]{1,0:T(8,128)(2,1)S(1)}, bf16[64,4224]{1,0:T(8,128)(2,1)S(1)}, u32[]{:S(2)}, u32[]{:S(2)}) collective-permute-start(bf16[64,4224]{1,0:T(8,128)(2,1)S(1)} %bundle.1), channel_id=1, source_target_pairs={{0,1},{2,3},{4,5},{6,7},{8,9},{10,11},{12,13},{14,15},{1,4},{3,6},... | collective-permute-start | bytes 1622024 | tf_op jit(solution)/shard_map/ppermute | solution.py:411
  3.5 4.6 %collective-permute-start.3 = (bf16[64,4096]{1,0:T(8,128)(2,1)}, bf16[64,4096]{1,0:T(8,128)(2,1)S(1)}, u32[]{:S(2)}, u32[]{:S(2)}) collective-permute-start(bf16[64,4096]{1,0:T(8,128)(2,1)} %refs_2_.1), channel_id=1, source_target_pairs={{0,1},{2,3},{4,5},{6,7},{8,9},{10,11},{12,13},{14,15},{1,4},{3,6},... | collective-permute-start | bytes 1572872 | tf_op jit(solution)/shard_map/ppermute | solution.py:412
  8.1 3.5 %collective-permute-start.2 = (bf16[64,4224]{1,0:T(8,128)(2,1)S(1)}, bf16[64,4224]{1,0:T(8,128)(2,1)S(1)}, u32[]{:S(2)}, u32[]{:S(2)}) collective-permute-start(bf16[64,4224]{1,0:T(8,128)(2,1)S(1)} %bundle.1), channel_id=1, source_target_pairs={{0,2},{1,3},{2,4},{4,6},{5,7},{6,8},{8,10},{9,11},{10,12},{12,14},... | collective-permute-start | bytes 1622024 | tf_op jit(solution)/shard_map/ppermute | solution.py:413
  12.3 5.7 %collective-permute-start.5 = (bf16[64,4096]{1,0:T(8,128)(2,1)}, bf16[64,4096]{1,0:T(8,128)(2,1)S(1)}, u32[]{:S(2)}, u32[]{:S(2)}) collective-permute-start(bf16[64,4096]{1,0:T(8,128)(2,1)} %refs_2_.1), channel_id=1, source_target_pairs={{0,2},{1,3},{2,4},{4,6},{5,7},{6,8},{8,10},{9,11},{10,12},{12,14},... | collective-permute-start | bytes 1572872 | tf_op jit(solution)/shard_map/ppermute | solution.py:414
  19.5 3.5 %fetch.3.w_gate = bf16[4096,1024]{1,0:T(8,128)(2,1)S(1)} custom-call(bf16[4096,1024]{1,0:T(8,128)(2,1)} %source.3, s32[6]{0:T(128)S(1)} %stack.31.flags.after.refs_8_.deltas), custom_call_target="tpu_custom_call" | custom-call | bytes 16777216 | tf_op jit(solution)/shard_map/fetch/pallas_call | solution.py:247
  25.4 9.1 %collective-permute-done.5.second = bf16[64,4096]{1,0:T(8,128)(2,1)S(1)} collective-permute-done((bf16[64,4096]{1,0:T(8,128)(2,1)}, bf16[64,4096]{1,0:T(8,128)(2,1)S(1)}, u32[]{:S(2)}, u32[]{:S(2)}) %collective-permute-start.5) | collective-permute-done | bytes 524320 | tf_op jit(solution)/shard_map/ppermute | solution.py:414
  35.7 1.9 %collective-permute-done.7.v3 = bf16[64,4096]{1,0:T(8,128)(2,1)S(1)} collective-permute-done((bf16[64,4096]{1,0:T(8,128)(2,1)S(1)}, bf16[64,4096]{1,0:T(8,128)(2,1)S(1)}, u32[]{:S(2)}, u32[]{:S(2)}) %collective-permute-start.7) | collective-permute-done | bytes 524320 | tf_op jit(solution)/shard_map/ppermute | solution.py:399
  37.6 3.5 %attention.1 = (f32[64,4096]{1,0:T(8,128)S(1)}, bf16[20,4096]{1,0:T(8,128)(2,1)S(1)}, bf16[20,4096]{1,0:T(8,128)(2,1)S(1)}, bf16[2,64,32]{2,1,0:T(8,128)(2,1)S(1)}) custom-call(s32[6]{0:T(128)S(1)} %stack.31.flags.after.refs_8_.deltas, bf16[64,4096]{1,0:T(8,128)(2,1)S(1)} %get-tuple-element.75.q, bf16[64,4096]{1,0:T(8,128)(2,1)S(1)} %get-tuple-element.76.k0, ...), custom_call_target="tpu_custom_call" | custom-call | flops 268435456 | bytes 8388608 | tf_op jit(solution)/shard_map/attention/pallas_call | solution.py:181
  41.1 2.4 %collective-permute-start.10 = (bf16[20,4096]{1,0:T(8,128)(2,1)S(1)}, bf16[20,4096]{1,0:T(8,128)(2,1)S(1)}, u32[]{:S(2)}, u32[]{:S(2)}) collective-permute-start(bf16[20,4096]{1,0:T(8,128)(2,1)S(1)} %get-tuple-element.89.refs_0_), channel_id=1, source_target_pairs={{0,2},{1,3},{2,0},{3,1},{4,6},{5,7},{6,4},{7,5},{8,10},{9,11},{10,... | collective-permute-start | bytes 491528 | tf_op jit(solution)/shard_map/ppermute | solution.py:399
  43.5 4.2 %collective-permute-start.11 = (bf16[20,4096]{1,0:T(8,128)(2,1)S(1)}, bf16[20,4096]{1,0:T(8,128)(2,1)S(1)}, u32[]{:S(2)}, u32[]{:S(2)}) collective-permute-start(bf16[20,4096]{1,0:T(8,128)(2,1)S(1)} %get-tuple-element.87), channel_id=1, source_target_pairs={{0,8},{1,9},{2,10},{3,11},{4,12},{5,13},{6,14},{7,15},{8,0},{9,1},... | collective-permute-start | bytes 491528 | tf_op jit(solution)/shard_map/ppermute | solution.py:441
  47.7 2.8 %collective-permute-start.8 = (bf16[20,4096]{1,0:T(8,128)(2,1)S(1)}, bf16[20,4096]{1,0:T(8,128)(2,1)S(1)}, u32[]{:S(2)}, u32[]{:S(2)}) collective-permute-start(bf16[20,4096]{1,0:T(8,128)(2,1)S(1)} %get-tuple-element.89.refs_0_), channel_id=1, source_target_pairs={{0,6},{1,7},{2,4},{3,5},{4,2},{5,3},{6,0},{7,1},{8,14},{9,15},{10,... | collective-permute-start | bytes 491528 | tf_op jit(solution)/shard_map/ppermute | solution.py:399
  51.1 3.5 %fetch.4.w_up = bf16[4096,1024]{1,0:T(8,128)(2,1)S(1)} custom-call(bf16[4096,1024]{1,0:T(8,128)(2,1)} %source.4, bf16[2,64,32]{2,1,0:T(8,128)(2,1)S(1)} %get-tuple-element.85.after.weight), custom_call_target="tpu_custom_call" | custom-call | bytes 16777216 | tf_op jit(solution)/shard_map/fetch/pallas_call | solution.py:247
  54.6 3.5 %fetch.5.w_down = bf16[1024,4096]{1,0:T(8,128)(2,1)S(1)} custom-call(bf16[1024,4096]{1,0:T(8,128)(2,1)} %source.5, bf16[2,64,32]{2,1,0:T(8,128)(2,1)S(1)} %get-tuple-element.85.after.weight), custom_call_target="tpu_custom_call" | custom-call | bytes 16777216 | tf_op jit(solution)/shard_map/fetch/pallas_call | solution.py:247
  59.4 3.5 %collective-permute-done.9.refs_2_ = bf16[20,4096]{1,0:T(8,128)(2,1)S(1)} collective-permute-done((bf16[20,4096]{1,0:T(8,128)(2,1)S(1)}, bf16[20,4096]{1,0:T(8,128)(2,1)S(1)}, u32[]{:S(2)}, u32[]{:S(2)}) %collective-permute-start.9) | collective-permute-done | bytes 163872 | tf_op jit(solution)/shard_map/ppermute | solution.py:399
  65.0 1.7 %collective-permute-start.14 = (bf16[20,4096]{1,0:T(8,128)(2,1)S(1)}, bf16[20,4096]{1,0:T(8,128)(2,1)S(1)}, u32[]{:S(2)}, u32[]{:S(2)}) collective-permute-start(bf16[20,4096]{1,0:T(8,128)(2,1)S(1)} %collective-permute-done.11.refs_0_), channel_id=1, source_target_pairs={{0,2},{1,3},{2,0},{3,1},{4,6},{5,7},{6,4},{7,5},{8,10},{9,11},{10,... | collective-permute-start | bytes 491528 | tf_op jit(solution)/shard_map/ppermute | solution.py:399
  66.7 5.2 %experts.2 = (bf16[80,4096]{1,0:T(8,128)(2,1)S(1)}, bf16[80,4096]{1,0:T(8,128)(2,1)S(1)}) custom-call(bf16[80,4096]{1,0:T(8,128)(2,1)S(1)} %pile.2.local, bf16[80,4096]{1,0:T(8,128)(2,1)S(1)} %collective-permute-done.15.remote, bf16[4096,1024]{1,0:T(8,128)(2,1)S(1)} %fetch.3.w_gate, bf16[4096,1024]{1,0:T(8,128)(2,1)S(1)} %fetch.4.w_up, ...), custom_call_target="tpu_custom_call" | custom-call | flops 4026531840 | bytes 2621440 | tf_op jit(solution)/shard_map/experts/pallas_call | solution.py:286
  72.0 2.6 %collective-permute-done.13.refs_2_ = bf16[20,4096]{1,0:T(8,128)(2,1)S(1)} collective-permute-done((bf16[20,4096]{1,0:T(8,128)(2,1)S(1)}, bf16[20,4096]{1,0:T(8,128)(2,1)S(1)}, u32[]{:S(2)}, u32[]{:S(2)}) %collective-permute-start.13) | collective-permute-done | bytes 163872 | tf_op jit(solution)/shard_map/ppermute | solution.py:399
  77.8 5.2 %experts.3 = (bf16[80,4096]{1,0:T(8,128)(2,1)S(1)}, bf16[80,4096]{1,0:T(8,128)(2,1)S(1)}) custom-call(bf16[80,4096]{1,0:T(8,128)(2,1)S(1)} %pile.3.local, bf16[80,4096]{1,0:T(8,128)(2,1)S(1)} %collective-permute-done.16.remote, bf16[4096,1024]{1,0:T(8,128)(2,1)S(1)} %fetch.3.w_gate, bf16[4096,1024]{1,0:T(8,128)(2,1)S(1)} %fetch.4.w_up, ...), custom_call_target="tpu_custom_call" | custom-call | flops 4026531840 | bytes 2621440 | tf_op jit(solution)/shard_map/experts/pallas_call | solution.py:286
  83.5 1.8 %collective-permute-done.17.second = bf16[80,4096]{1,0:T(8,128)(2,1)S(1)} collective-permute-done((bf16[80,4096]{1,0:T(8,128)(2,1)S(1)}, bf16[80,4096]{1,0:T(8,128)(2,1)S(1)}, u32[]{:S(2)}, u32[]{:S(2)}) %collective-permute-start.17) | collective-permute-done | bytes 655392 | tf_op jit(solution)/shard_map/ppermute | solution.py:399
  89.0 3.5 %collective-permute-done.19.refs_1_ = bf16[20,4096]{1,0:T(8,128)(2,1)S(1)} collective-permute-done((bf16[20,4096]{1,0:T(8,128)(2,1)S(1)}, bf16[20,4096]{1,0:T(8,128)(2,1)S(1)}, u32[]{:S(2)}, u32[]{:S(2)}) %collective-permute-start.19) | collective-permute-done | bytes 163872 | tf_op jit(solution)/shard_map/ppermute | solution.py:399
  97.4 1.6 %collective-permute-done.24.refs_3_ = bf16[20,4096]{1,0:T(8,128)(2,1)S(1)} collective-permute-done((bf16[20,4096]{1,0:T(8,128)(2,1)S(1)}, bf16[20,4096]{1,0:T(8,128)(2,1)S(1)}, u32[]{:S(2)}, u32[]{:S(2)}) %collective-permute-start.24) | collective-permute-done | bytes 163872 | tf_op jit(solution)/shard_map/ppermute | solution.py:399
  100.1 1.8 %collective-permute-done.21.refs_1_ = bf16[20,4096]{1,0:T(8,128)(2,1)S(1)} collective-permute-done((bf16[20,4096]{1,0:T(8,128)(2,1)S(1)}, bf16[20,4096]{1,0:T(8,128)(2,1)S(1)}, u32[]{:S(2)}, u32[]{:S(2)}) %collective-permute-start.21) | collective-permute-done | bytes 163872 | tf_op jit(solution)/shard_map/ppermute | solution.py:399
  101.9 5.5 %collective-permute-done.22.refs_2_ = bf16[20,4096]{1,0:T(8,128)(2,1)S(1)} collective-permute-done((bf16[20,4096]{1,0:T(8,128)(2,1)S(1)}, bf16[20,4096]{1,0:T(8,128)(2,1)S(1)}, u32[]{:S(2)}, u32[]{:S(2)}) %collective-permute-start.22) | collective-permute-done | bytes 163872 | tf_op jit(solution)/shard_map/ppermute | solution.py:399
  107.4 3.2 %collective-permute-done.23.refs_3_ = bf16[20,4096]{1,0:T(8,128)(2,1)S(1)} collective-permute-done((bf16[20,4096]{1,0:T(8,128)(2,1)S(1)}, bf16[20,4096]{1,0:T(8,128)(2,1)S(1)}, u32[]{:S(2)}, u32[]{:S(2)}) %collective-permute-start.23) | collective-permute-done | bytes 163872 | tf_op jit(solution)/shard_map/ppermute | solution.py:399
  (46 shorter events, 25.6 us)
Async XLA Ops:
  1.1 10.5 %collective-permute-start = (bf16[64,4224]{1,0:T(8,128)(2,1)S(1)}, bf16[64,4224]{1,0:T(8,128)(2,1)S(1)}, u32[]{:S(2)}, u32[]{:S(2)}) collective-permute-start(bf16[64,4224]{1,0:T(8,128)(2,1)S(1)} %bundle.1), channel_id=1, source_target_pairs={{0,1},{2,3},{4,5},{6,7},{8,9},{10,11},{12,13},{14,15},{1,4},{3,6},... | collective-permute-start | bytes 1622024 | tf_op jit(solution)/shard_map/ppermute | solution.py:411
  3.5 14.5 %collective-permute-start.3 = (bf16[64,4096]{1,0:T(8,128)(2,1)}, bf16[64,4096]{1,0:T(8,128)(2,1)S(1)}, u32[]{:S(2)}, u32[]{:S(2)}) collective-permute-start(bf16[64,4096]{1,0:T(8,128)(2,1)} %refs_2_.1), channel_id=1, source_target_pairs={{0,1},{2,3},{4,5},{6,7},{8,9},{10,11},{12,13},{14,15},{1,4},{3,6},... | collective-permute-start | bytes 1572872 | tf_op jit(solution)/shard_map/ppermute | solution.py:412
  8.1 16.6 %collective-permute-start.2 = (bf16[64,4224]{1,0:T(8,128)(2,1)S(1)}, bf16[64,4224]{1,0:T(8,128)(2,1)S(1)}, u32[]{:S(2)}, u32[]{:S(2)}) collective-permute-start(bf16[64,4224]{1,0:T(8,128)(2,1)S(1)} %bundle.1), channel_id=1, source_target_pairs={{0,2},{1,3},{2,4},{4,6},{5,7},{6,8},{8,10},{9,11},{10,12},{12,14},... | collective-permute-start | bytes 1622024 | tf_op jit(solution)/shard_map/ppermute | solution.py:413
  11.6 13.1 %collective-permute-start.1 = (bf16[64,4224]{1,0:T(8,128)(2,1)S(1)}, bf16[64,4224]{1,0:T(8,128)(2,1)S(1)}, u32[]{:S(2)}, u32[]{:S(2)}) collective-permute-start(bf16[64,4224]{1,0:T(8,128)(2,1)S(1)} %collective-permute-done.k2), channel_id=1, source_target_pairs={{2,1},{6,5},{10,9},{14,13},{18,17},{22,21},{26,25},{30,29}} | collective-permute-start | bytes 1622024 | tf_op jit(solution)/shard_map/ppermute | solution.py:415
  12.3 22.3 %collective-permute-start.5 = (bf16[64,4096]{1,0:T(8,128)(2,1)}, bf16[64,4096]{1,0:T(8,128)(2,1)S(1)}, u32[]{:S(2)}, u32[]{:S(2)}) collective-permute-start(bf16[64,4096]{1,0:T(8,128)(2,1)} %refs_2_.1), channel_id=1, source_target_pairs={{0,2},{1,3},{2,4},{4,6},{5,7},{6,8},{8,10},{9,11},{10,12},{12,14},... | collective-permute-start | bytes 1572872 | tf_op jit(solution)/shard_map/ppermute | solution.py:414
  17.9 16.6 %collective-permute-start.4 = (bf16[64,4096]{1,0:T(8,128)(2,1)S(1)}, bf16[64,4096]{1,0:T(8,128)(2,1)}, u32[]{:S(2)}, u32[]{:S(2)}) collective-permute-start(bf16[64,4096]{1,0:T(8,128)(2,1)S(1)} %collective-permute-done.3.v2), channel_id=1, source_target_pairs={{2,1},{6,5},{10,9},{14,13},{18,17},{22,21},{26,25},{30,29}} | collective-permute-start | bytes 1572872 | tf_op jit(solution)/shard_map/ppermute | solution.py:416
  25.3 12.3 %collective-permute-start.6 = (bf16[64,4224]{1,0:T(8,128)(2,1)S(1)}, bf16[64,4224]{1,0:T(8,128)(2,1)S(1)}, u32[]{:S(2)}, u32[]{:S(2)}) collective-permute-start(bf16[64,4224]{1,0:T(8,128)(2,1)S(1)} %choose.2.k1), channel_id=1, source_target_pairs={{0,1},{1,0},{2,3},{3,2},{4,5},{5,4},{6,7},{7,6},{8,9},{9,8},{10,11... | collective-permute-start | bytes 1622024 | tf_op jit(solution)/shard_map/ppermute | solution.py:399
  41.1 17.0 %collective-permute-start.10 = (bf16[20,4096]{1,0:T(8,128)(2,1)S(1)}, bf16[20,4096]{1,0:T(8,128)(2,1)S(1)}, u32[]{:S(2)}, u32[]{:S(2)}) collective-permute-start(bf16[20,4096]{1,0:T(8,128)(2,1)S(1)} %get-tuple-element.89.refs_0_), channel_id=1, source_target_pairs={{0,2},{1,3},{2,0},{3,1},{4,6},{5,7},{6,4},{7,5},{8,10},{9,11},{10,... | collective-permute-start | bytes 491528 | tf_op jit(solution)/shard_map/ppermute | solution.py:399
  43.5 14.6 %collective-permute-start.11 = (bf16[20,4096]{1,0:T(8,128)(2,1)S(1)}, bf16[20,4096]{1,0:T(8,128)(2,1)S(1)}, u32[]{:S(2)}, u32[]{:S(2)}) collective-permute-start(bf16[20,4096]{1,0:T(8,128)(2,1)S(1)} %get-tuple-element.87), channel_id=1, source_target_pairs={{0,8},{1,9},{2,10},{3,11},{4,12},{5,13},{6,14},{7,15},{8,0},{9,1},... | collective-permute-start | bytes 491528 | tf_op jit(solution)/shard_map/ppermute | solution.py:441
  47.7 11.7 %collective-permute-start.8 = (bf16[20,4096]{1,0:T(8,128)(2,1)S(1)}, bf16[20,4096]{1,0:T(8,128)(2,1)S(1)}, u32[]{:S(2)}, u32[]{:S(2)}) collective-permute-start(bf16[20,4096]{1,0:T(8,128)(2,1)S(1)} %get-tuple-element.89.refs_0_), channel_id=1, source_target_pairs={{0,6},{1,7},{2,4},{3,5},{4,2},{5,3},{6,0},{7,1},{8,14},{9,15},{10,... | collective-permute-start | bytes 491528 | tf_op jit(solution)/shard_map/ppermute | solution.py:399
  50.5 12.4 %collective-permute-start.9 = (bf16[20,4096]{1,0:T(8,128)(2,1)S(1)}, bf16[20,4096]{1,0:T(8,128)(2,1)S(1)}, u32[]{:S(2)}, u32[]{:S(2)}) collective-permute-start(bf16[20,4096]{1,0:T(8,128)(2,1)S(1)} %get-tuple-element.89.refs_0_), channel_id=1, source_target_pairs={{0,4},{1,5},{2,6},{3,7},{4,0},{5,1},{6,2},{7,3},{8,12},{9,13},{10,... | collective-permute-start | bytes 491528 | tf_op jit(solution)/shard_map/ppermute | solution.py:399
  63.1 3.6 %collective-permute-start.15 = (bf16[80,4096]{1,0:T(8,128)(2,1)S(1)}, bf16[80,4096]{1,0:T(8,128)(2,1)S(1)}, u32[]{:S(2)}, u32[]{:S(2)}) collective-permute-start(bf16[80,4096]{1,0:T(8,128)(2,1)S(1)} %pile.2.local), channel_id=1, source_target_pairs={{0,1},{1,0},{2,3},{3,2},{4,5},{5,4},{6,7},{7,6},{8,9},{9,8},{10,11... | collective-permute-start | bytes 1966088 | tf_op jit(solution)/shard_map/ppermute | solution.py:399
  63.1 8.8 %collective-permute-start.12 = (bf16[20,4096]{1,0:T(8,128)(2,1)S(1)}, bf16[20,4096]{1,0:T(8,128)(2,1)S(1)}, u32[]{:S(2)}, u32[]{:S(2)}) collective-permute-start(bf16[20,4096]{1,0:T(8,128)(2,1)S(1)} %collective-permute-done.11.refs_0_), channel_id=1, source_target_pairs={{0,6},{1,7},{2,4},{3,5},{4,2},{5,3},{6,0},{7,1},{8,14},{9,15},{10,... | collective-permute-start | bytes 491528 | tf_op jit(solution)/shard_map/ppermute | solution.py:399
  64.7 9.8 %collective-permute-start.13 = (bf16[20,4096]{1,0:T(8,128)(2,1)S(1)}, bf16[20,4096]{1,0:T(8,128)(2,1)S(1)}, u32[]{:S(2)}, u32[]{:S(2)}) collective-permute-start(bf16[20,4096]{1,0:T(8,128)(2,1)S(1)} %collective-permute-done.11.refs_0_), channel_id=1, source_target_pairs={{0,4},{1,5},{2,6},{3,7},{4,0},{5,1},{6,2},{7,3},{8,12},{9,13},{10,... | collective-permute-start | bytes 491528 | tf_op jit(solution)/shard_map/ppermute | solution.py:399
  65.0 10.5 %collective-permute-start.14 = (bf16[20,4096]{1,0:T(8,128)(2,1)S(1)}, bf16[20,4096]{1,0:T(8,128)(2,1)S(1)}, u32[]{:S(2)}, u32[]{:S(2)}) collective-permute-start(bf16[20,4096]{1,0:T(8,128)(2,1)S(1)} %collective-permute-done.11.refs_0_), channel_id=1, source_target_pairs={{0,2},{1,3},{2,0},{3,1},{4,6},{5,7},{6,4},{7,5},{8,10},{9,11},{10,... | collective-permute-start | bytes 491528 | tf_op jit(solution)/shard_map/ppermute | solution.py:399
  75.8 7.5 %collective-permute-start.18 = (bf16[80,4096]{1,0:T(8,128)(2,1)S(1)}, bf16[80,4096]{1,0:T(8,128)(2,1)S(1)}, u32[]{:S(2)}, u32[]{:S(2)}) collective-permute-start(bf16[80,4096]{1,0:T(8,128)(2,1)S(1)} %get-tuple-element.109), channel_id=1, source_target_pairs={{0,1},{1,0},{2,3},{3,2},{4,5},{5,4},{6,7},{7,6},{8,9},{9,8},{10,11... | collective-permute-start | bytes 1966088 | tf_op jit(solution)/shard_map/ppermute | solution.py:399
  83.1 2.2 %collective-permute-start.17 = (bf16[80,4096]{1,0:T(8,128)(2,1)S(1)}, bf16[80,4096]{1,0:T(8,128)(2,1)S(1)}, u32[]{:S(2)}, u32[]{:S(2)}) collective-permute-start(bf16[80,4096]{1,0:T(8,128)(2,1)S(1)} %get-tuple-element.103), channel_id=1, source_target_pairs={{0,1},{1,0},{2,3},{3,2},{4,5},{5,4},{6,7},{7,6},{8,9},{9,8},{10,11... | collective-permute-start | bytes 1966088 | tf_op jit(solution)/shard_map/ppermute | solution.py:399
  85.5 7.0 %collective-permute-start.19 = (bf16[20,4096]{1,0:T(8,128)(2,1)S(1)}, bf16[20,4096]{1,0:T(8,128)(2,1)S(1)}, u32[]{:S(2)}, u32[]{:S(2)}) collective-permute-start(bf16[20,4096]{1,0:T(8,128)(2,1)S(1)} %get-tuple-element.115), channel_id=1, source_target_pairs={{0,2},{1,3},{2,0},{3,1},{4,6},{5,7},{6,4},{7,5},{8,10},{9,11},{10,... | collective-permute-start | bytes 491528 | tf_op jit(solution)/shard_map/ppermute | solution.py:399
  86.1 7.8 %collective-permute-start.20 = (bf16[20,4096]{1,0:T(8,128)(2,1)S(1)}, bf16[20,4096]{1,0:T(8,128)(2,1)S(1)}, u32[]{:S(2)}, u32[]{:S(2)}) collective-permute-start(bf16[20,4096]{1,0:T(8,128)(2,1)S(1)} %get-tuple-element.116), channel_id=1, source_target_pairs={{0,4},{1,5},{2,6},{3,7},{4,0},{5,1},{6,2},{7,3},{8,12},{9,13},{10,... | collective-permute-start | bytes 491528 | tf_op jit(solution)/shard_map/ppermute | solution.py:399
  87.6 11.5 %collective-permute-start.24 = (bf16[20,4096]{1,0:T(8,128)(2,1)S(1)}, bf16[20,4096]{1,0:T(8,128)(2,1)S(1)}, u32[]{:S(2)}, u32[]{:S(2)}) collective-permute-start(bf16[20,4096]{1,0:T(8,128)(2,1)S(1)} %get-tuple-element.128), channel_id=1, source_target_pairs={{0,6},{1,7},{2,4},{3,5},{4,2},{5,3},{6,0},{7,1},{8,14},{9,15},{10,... | collective-permute-start | bytes 491528 | tf_op jit(solution)/shard_map/ppermute | solution.py:399
  93.9 8.0 %collective-permute-start.21 = (bf16[20,4096]{1,0:T(8,128)(2,1)S(1)}, bf16[20,4096]{1,0:T(8,128)(2,1)S(1)}, u32[]{:S(2)}, u32[]{:S(2)}) collective-permute-start(bf16[20,4096]{1,0:T(8,128)(2,1)S(1)} %get-tuple-element.122), channel_id=1, source_target_pairs={{0,2},{1,3},{2,0},{3,1},{4,6},{5,7},{6,4},{7,5},{8,10},{9,11},{10,... | collective-permute-start | bytes 491528 | tf_op jit(solution)/shard_map/ppermute | solution.py:399
  95.3 12.1 %collective-permute-start.22 = (bf16[20,4096]{1,0:T(8,128)(2,1)S(1)}, bf16[20,4096]{1,0:T(8,128)(2,1)S(1)}, u32[]{:S(2)}, u32[]{:S(2)}) collective-permute-start(bf16[20,4096]{1,0:T(8,128)(2,1)S(1)} %get-tuple-element.123), channel_id=1, source_target_pairs={{0,4},{1,5},{2,6},{3,7},{4,0},{5,1},{6,2},{7,3},{8,12},{9,13},{10,... | collective-permute-start | bytes 491528 | tf_op jit(solution)/shard_map/ppermute | solution.py:399
  96.0 14.6 %collective-permute-start.23 = (bf16[20,4096]{1,0:T(8,128)(2,1)S(1)}, bf16[20,4096]{1,0:T(8,128)(2,1)S(1)}, u32[]{:S(2)}, u32[]{:S(2)}) collective-permute-start(bf16[20,4096]{1,0:T(8,128)(2,1)S(1)} %get-tuple-element.124), channel_id=1, source_target_pairs={{0,6},{1,7},{2,4},{3,5},{4,2},{5,3},{6,0},{7,1},{8,14},{9,15},{10,... | collective-permute-start | bytes 491528 | tf_op jit(solution)/shard_map/ppermute | solution.py:399
  99.1 11.7 %collective-permute-start.25 = (bf16[20,4096]{1,0:T(8,128)(2,1)S(1)}, bf16[20,4096]{1,0:T(8,128)(2,1)S(1)}, u32[]{:S(2)}, u32[]{:S(2)}) collective-permute-start(bf16[20,4096]{1,0:T(8,128)(2,1)S(1)} %total.1), channel_id=1, source_target_pairs={{0,8},{1,9},{2,10},{3,11},{4,12},{5,13},{6,14},{7,15},{8,0},{9,1},... | collective-permute-start | bytes 491528 | tf_op jit(solution)/shard_map/ppermute | solution.py:472
  (2 other events, 4.1 us)

commit v10 on v9

--- a/solution.py
+++ b/solution.py
@@ -390,10 +390,11 @@
     shard_count = count // E_WIN
     odd = own % 2
 
-    next_chip = [(i, i + 2) for i in range(count - 2) if i % 4 != 3]
+    next_chip = [(i, i + 2) for i in range(count - 2) if i % 4 < 2]
     crossing = [(i, i + 1) for i in range(0, count, 2)]
     crossing += [(i, i + 3) for i in range(1, count - 3, 2)]
     passing = [(i, i - 1) for i in range(2, count, 4)]
+    passing += [(i, i + 1) for i in range(3, count - 1, 4)]
 
     def swapped(block, mask):
         return lax.ppermute(block, "expert", [(i, i ^ mask) for i in range(count)])
@@ -402,15 +403,15 @@
     beyond = 2 * WIN_DEV + 2
     delta_list = [0 * own, 0 * own + 2, 3 - 2 * odd, 1 + 2 * odd]
     my_expert = own // shard_count
-    relayed = (own % 4 == 1).astype(jnp.int32)
+    relayed = (own % 4 < 2).astype(jnp.int32)
     scalars = jnp.stack(
         [jnp.where(own >= delta, delta, beyond) for delta in delta_list] + [my_expert, relayed]
     ).astype(jnp.int32)
 
     key_block = bundle(keys, seg_own)
+    key_next = lax.ppermute(key_block, "expert", next_chip)
     key_cross = lax.ppermute(key_block, "expert", crossing)
     value_cross = lax.ppermute(values, "expert", crossing)
-    key_next = lax.ppermute(key_block, "expert", next_chip)
     value_next = lax.ppermute(values, "expert", next_chip)
     key_passed = lax.ppermute(key_cross, "expert", passing)
     value_passed = lax.ppermute(value_cross, "expert", passing)

time: 112 us -> 114 us (1.018)
  starting transfers between devices: 40.9 us -> 44.3 us
  waiting for transfers between devices: 39.8 us -> 37.9 us
    ppermute x18, starting transfers between devices: 17.5 us -> 19.3 us  [swapped(): return lax.ppermute(block, 'expert', [(i, i ^ mask) for i in range(count)])]
    ppermute x1, waiting for transfers between devices: 9.14 us -> 7.3 us  [shards(): value_next = lax.ppermute(values, 'expert', next_chip)]
    ppermute x1, starting transfers between devices: 4.16 us -> 5.68 us  [shards(): got = lax.ppermute(send, 'expert', partner)]
where the time goes in v10:
time: 114 us; the launch traced here: 113 us
  starting transfers between devices  44.3 us (39%)
  waiting for transfers between devices  37.9 us (33%)
  Pallas kernels  30.9 us (27%)
    ppermute x18, waiting for transfers between devices, swapped(): return lax.ppermute(block, 'expert', [(i, i ^ mask) for i in range(count)])  30.6 us
    ppermute x18, starting transfers between devices, swapped(): return lax.ppermute(block, 'expert', [(i, i ^ mask) for i in range(count)])  19.3 us
    pallas_call x3, Pallas kernels, fetch(): pl.pallas_call(functools.partial(fetch_kernel, parts), in_specs=[anywhere...  10.5 us
    pallas_call x2, Pallas kernels, experts(): pl.pallas_call(experts_kernel, in_specs=[NEAR] * 5, out_specs=[NEAR] * 2,...  10.5 us
    ppermute x1, waiting for transfers between devices, shards(): value_next = lax.ppermute(values, 'expert', next_chip)  7.3 us
    ppermute x1, starting transfers between devices, shards(): got = lax.ppermute(send, 'expert', partner)  5.68 us
    ppermute x1, starting transfers between devices, shards(): value_next = lax.ppermute(values, 'expert', next_chip)  5.66 us
    ppermute x1, starting transfers between devices, shards(): value_cross = lax.ppermute(values, 'expert', crossing)  4.6 us
  transfers between devices with their start and end apart: 26, of which 14 were waited for; matrix products, arithmetic and copies ran while one was open for 0% of the time, Pallas kernels for 22%

profile of v10, /device:TPU:0, one launch (start us, length us, event | category | flops | bytes accessed | tf_op | source)
XLA Modules:
  0.0 113.5 jit_solution(15051814610694357482)
XLA Ops:
  1.1 2.4 %collective-permute-start = (bf16[64,4224]{1,0:T(8,128)(2,1)S(1)}, bf16[64,4224]{1,0:T(8,128)(2,1)S(1)}, u32[]{:S(2)}, u32[]{:S(2)}) collective-permute-start(bf16[64,4224]{1,0:T(8,128)(2,1)S(1)} %bundle.1), channel_id=1, source_target_pairs={{0,1},{2,3},{4,5},{6,7},{8,9},{10,11},{12,13},{14,15},{1,4},{3,6},... | collective-permute-start | bytes 1622024 | tf_op jit(solution)/shard_map/ppermute | solution.py:413
  3.5 4.6 %collective-permute-start.3 = (bf16[64,4096]{1,0:T(8,128)(2,1)}, bf16[64,4096]{1,0:T(8,128)(2,1)S(1)}, u32[]{:S(2)}, u32[]{:S(2)}) collective-permute-start(bf16[64,4096]{1,0:T(8,128)(2,1)} %refs_2_.1), channel_id=1, source_target_pairs={{0,1},{2,3},{4,5},{6,7},{8,9},{10,11},{12,13},{14,15},{1,4},{3,6},... | collective-permute-start | bytes 1572872 | tf_op jit(solution)/shard_map/ppermute | solution.py:414
  8.1 3.5 %collective-permute-start.2 = (bf16[64,4224]{1,0:T(8,128)(2,1)S(1)}, bf16[64,4224]{1,0:T(8,128)(2,1)S(1)}, u32[]{:S(2)}, u32[]{:S(2)}) collective-permute-start(bf16[64,4224]{1,0:T(8,128)(2,1)S(1)} %bundle.1), channel_id=1, source_target_pairs={{0,2},{1,3},{4,6},{5,7},{8,10},{9,11},{12,14},{13,15},{16,18},{17,... | collective-permute-start | bytes 1622024 | tf_op jit(solution)/shard_map/ppermute | solution.py:412
  12.3 5.7 %collective-permute-start.5 = (bf16[64,4096]{1,0:T(8,128)(2,1)}, bf16[64,4096]{1,0:T(8,128)(2,1)S(1)}, u32[]{:S(2)}, u32[]{:S(2)}) collective-permute-start(bf16[64,4096]{1,0:T(8,128)(2,1)} %refs_2_.1), channel_id=1, source_target_pairs={{0,2},{1,3},{4,6},{5,7},{8,10},{9,11},{12,14},{13,15},{16,18},{17,... | collective-permute-start | bytes 1572872 | tf_op jit(solution)/shard_map/ppermute | solution.py:415
  19.5 3.5 %fetch.3.w_gate = bf16[4096,1024]{1,0:T(8,128)(2,1)S(1)} custom-call(bf16[4096,1024]{1,0:T(8,128)(2,1)} %source.3, s32[6]{0:T(128)S(1)} %stack.31.flags.after.refs_8_.deltas), custom_call_target="tpu_custom_call" | custom-call | bytes 16777216 | tf_op jit(solution)/shard_map/fetch/pallas_call | solution.py:247
  25.3 2.0 %collective-permute-start.6 = (bf16[64,4224]{1,0:T(8,128)(2,1)S(1)}, bf16[64,4224]{1,0:T(8,128)(2,1)S(1)}, u32[]{:S(2)}, u32[]{:S(2)}) collective-permute-start(bf16[64,4224]{1,0:T(8,128)(2,1)S(1)} %choose.2.k1), channel_id=1, source_target_pairs={{0,1},{1,0},{2,3},{3,2},{4,5},{5,4},{6,7},{7,6},{8,9},{9,8},{10,11... | collective-permute-start | bytes 1622024 | tf_op jit(solution)/shard_map/ppermute | solution.py:400
  27.2 7.3 %collective-permute-done.5.second = bf16[64,4096]{1,0:T(8,128)(2,1)S(1)} collective-permute-done((bf16[64,4096]{1,0:T(8,128)(2,1)}, bf16[64,4096]{1,0:T(8,128)(2,1)S(1)}, u32[]{:S(2)}, u32[]{:S(2)}) %collective-permute-start.5) | collective-permute-done | bytes 524320 | tf_op jit(solution)/shard_map/ppermute | solution.py:415
  35.7 1.9 %collective-permute-done.7.v3 = bf16[64,4096]{1,0:T(8,128)(2,1)S(1)} collective-permute-done((bf16[64,4096]{1,0:T(8,128)(2,1)S(1)}, bf16[64,4096]{1,0:T(8,128)(2,1)S(1)}, u32[]{:S(2)}, u32[]{:S(2)}) %collective-permute-start.7) | collective-permute-done | bytes 524320 | tf_op jit(solution)/shard_map/ppermute | solution.py:400
  37.6 3.5 %attention.1 = (f32[64,4096]{1,0:T(8,128)S(1)}, bf16[20,4096]{1,0:T(8,128)(2,1)S(1)}, bf16[20,4096]{1,0:T(8,128)(2,1)S(1)}, bf16[2,64,32]{2,1,0:T(8,128)(2,1)S(1)}) custom-call(s32[6]{0:T(128)S(1)} %stack.31.flags.after.refs_8_.deltas, bf16[64,4096]{1,0:T(8,128)(2,1)S(1)} %get-tuple-element.75.q, bf16[64,4096]{1,0:T(8,128)(2,1)S(1)} %get-tuple-element.76.k0, ...), custom_call_target="tpu_custom_call" | custom-call | flops 268435456 | bytes 8388608 | tf_op jit(solution)/shard_map/attention/pallas_call | solution.py:181
  41.1 2.4 %collective-permute-start.10 = (bf16[20,4096]{1,0:T(8,128)(2,1)S(1)}, bf16[20,4096]{1,0:T(8,128)(2,1)S(1)}, u32[]{:S(2)}, u32[]{:S(2)}) collective-permute-start(bf16[20,4096]{1,0:T(8,128)(2,1)S(1)} %get-tuple-element.89.refs_0_), channel_id=1, source_target_pairs={{0,2},{1,3},{2,0},{3,1},{4,6},{5,7},{6,4},{7,5},{8,10},{9,11},{10,... | collective-permute-start | bytes 491528 | tf_op jit(solution)/shard_map/ppermute | solution.py:400
  43.5 5.7 %collective-permute-start.11 = (bf16[20,4096]{1,0:T(8,128)(2,1)S(1)}, bf16[20,4096]{1,0:T(8,128)(2,1)S(1)}, u32[]{:S(2)}, u32[]{:S(2)}) collective-permute-start(bf16[20,4096]{1,0:T(8,128)(2,1)S(1)} %get-tuple-element.87), channel_id=1, source_target_pairs={{0,8},{1,9},{2,10},{3,11},{4,12},{5,13},{6,14},{7,15},{8,0},{9,1},... | collective-permute-start | bytes 491528 | tf_op jit(solution)/shard_map/ppermute | solution.py:442
  49.2 3.0 %collective-permute-start.8 = (bf16[20,4096]{1,0:T(8,128)(2,1)S(1)}, bf16[20,4096]{1,0:T(8,128)(2,1)S(1)}, u32[]{:S(2)}, u32[]{:S(2)}) collective-permute-start(bf16[20,4096]{1,0:T(8,128)(2,1)S(1)} %get-tuple-element.89.refs_0_), channel_id=1, source_target_pairs={{0,6},{1,7},{2,4},{3,5},{4,2},{5,3},{6,0},{7,1},{8,14},{9,15},{10,... | collective-permute-start | bytes 491528 | tf_op jit(solution)/shard_map/ppermute | solution.py:400
  52.6 3.5 %fetch.4.w_up = bf16[4096,1024]{1,0:T(8,128)(2,1)S(1)} custom-call(bf16[4096,1024]{1,0:T(8,128)(2,1)} %source.4, bf16[2,64,32]{2,1,0:T(8,128)(2,1)S(1)} %get-tuple-element.85.after.weight), custom_call_target="tpu_custom_call" | custom-call | bytes 16777216 | tf_op jit(solution)/shard_map/fetch/pallas_call | solution.py:247
  56.1 3.5 %fetch.5.w_down = bf16[1024,4096]{1,0:T(8,128)(2,1)S(1)} custom-call(bf16[1024,4096]{1,0:T(8,128)(2,1)} %source.5, bf16[2,64,32]{2,1,0:T(8,128)(2,1)S(1)} %get-tuple-element.85.after.weight), custom_call_target="tpu_custom_call" | custom-call | bytes 16777216 | tf_op jit(solution)/shard_map/fetch/pallas_call | solution.py:247
  61.0 3.5 %collective-permute-done.9.refs_2_ = bf16[20,4096]{1,0:T(8,128)(2,1)S(1)} collective-permute-done((bf16[20,4096]{1,0:T(8,128)(2,1)S(1)}, bf16[20,4096]{1,0:T(8,128)(2,1)S(1)}, u32[]{:S(2)}, u32[]{:S(2)}) %collective-permute-start.9) | collective-permute-done | bytes 163872 | tf_op jit(solution)/shard_map/ppermute | solution.py:400
  66.6 1.6 %collective-permute-start.14 = (bf16[20,4096]{1,0:T(8,128)(2,1)S(1)}, bf16[20,4096]{1,0:T(8,128)(2,1)S(1)}, u32[]{:S(2)}, u32[]{:S(2)}) collective-permute-start(bf16[20,4096]{1,0:T(8,128)(2,1)S(1)} %collective-permute-done.11.refs_0_), channel_id=1, source_target_pairs={{0,2},{1,3},{2,0},{3,1},{4,6},{5,7},{6,4},{7,5},{8,10},{9,11},{10,... | collective-permute-start | bytes 491528 | tf_op jit(solution)/shard_map/ppermute | solution.py:400
  68.2 5.2 %experts.2 = (bf16[80,4096]{1,0:T(8,128)(2,1)S(1)}, bf16[80,4096]{1,0:T(8,128)(2,1)S(1)}) custom-call(bf16[80,4096]{1,0:T(8,128)(2,1)S(1)} %pile.2.local, bf16[80,4096]{1,0:T(8,128)(2,1)S(1)} %collective-permute-done.15.remote, bf16[4096,1024]{1,0:T(8,128)(2,1)S(1)} %fetch.3.w_gate, bf16[4096,1024]{1,0:T(8,128)(2,1)S(1)} %fetch.4.w_up, ...), custom_call_target="tpu_custom_call" | custom-call | flops 4026531840 | bytes 2621440 | tf_op jit(solution)/shard_map/experts/pallas_call | solution.py:286
  73.5 2.6 %collective-permute-done.13.refs_2_ = bf16[20,4096]{1,0:T(8,128)(2,1)S(1)} collective-permute-done((bf16[20,4096]{1,0:T(8,128)(2,1)S(1)}, bf16[20,4096]{1,0:T(8,128)(2,1)S(1)}, u32[]{:S(2)}, u32[]{:S(2)}) %collective-permute-start.13) | collective-permute-done | bytes 163872 | tf_op jit(solution)/shard_map/ppermute | solution.py:400
  79.4 5.2 %experts.3 = (bf16[80,4096]{1,0:T(8,128)(2,1)S(1)}, bf16[80,4096]{1,0:T(8,128)(2,1)S(1)}) custom-call(bf16[80,4096]{1,0:T(8,128)(2,1)S(1)} %pile.3.local, bf16[80,4096]{1,0:T(8,128)(2,1)S(1)} %collective-permute-done.16.remote, bf16[4096,1024]{1,0:T(8,128)(2,1)S(1)} %fetch.3.w_gate, bf16[4096,1024]{1,0:T(8,128)(2,1)S(1)} %fetch.4.w_up, ...), custom_call_target="tpu_custom_call" | custom-call | flops 4026531840 | bytes 2621440 | tf_op jit(solution)/shard_map/experts/pallas_call | solution.py:286
  85.0 1.8 %collective-permute-done.17.second = bf16[80,4096]{1,0:T(8,128)(2,1)S(1)} collective-permute-done((bf16[80,4096]{1,0:T(8,128)(2,1)S(1)}, bf16[80,4096]{1,0:T(8,128)(2,1)S(1)}, u32[]{:S(2)}, u32[]{:S(2)}) %collective-permute-start.17) | collective-permute-done | bytes 655392 | tf_op jit(solution)/shard_map/ppermute | solution.py:400
  90.5 3.5 %collective-permute-done.19.refs_1_ = bf16[20,4096]{1,0:T(8,128)(2,1)S(1)} collective-permute-done((bf16[20,4096]{1,0:T(8,128)(2,1)S(1)}, bf16[20,4096]{1,0:T(8,128)(2,1)S(1)}, u32[]{:S(2)}, u32[]{:S(2)}) %collective-permute-start.19) | collective-permute-done | bytes 163872 | tf_op jit(solution)/shard_map/ppermute | solution.py:400
  101.7 1.7 %collective-permute-done.21.refs_1_ = bf16[20,4096]{1,0:T(8,128)(2,1)S(1)} collective-permute-done((bf16[20,4096]{1,0:T(8,128)(2,1)S(1)}, bf16[20,4096]{1,0:T(8,128)(2,1)S(1)}, u32[]{:S(2)}, u32[]{:S(2)}) %collective-permute-start.21) | collective-permute-done | bytes 163872 | tf_op jit(solution)/shard_map/ppermute | solution.py:400
  103.4 5.5 %collective-permute-done.22.refs_2_ = bf16[20,4096]{1,0:T(8,128)(2,1)S(1)} collective-permute-done((bf16[20,4096]{1,0:T(8,128)(2,1)S(1)}, bf16[20,4096]{1,0:T(8,128)(2,1)S(1)}, u32[]{:S(2)}, u32[]{:S(2)}) %collective-permute-start.22) | collective-permute-done | bytes 163872 | tf_op jit(solution)/shard_map/ppermute | solution.py:400
  108.9 3.2 %collective-permute-done.23.refs_3_ = bf16[20,4096]{1,0:T(8,128)(2,1)S(1)} collective-permute-done((bf16[20,4096]{1,0:T(8,128)(2,1)S(1)}, bf16[20,4096]{1,0:T(8,128)(2,1)S(1)}, u32[]{:S(2)}, u32[]{:S(2)}) %collective-permute-start.23) | collective-permute-done | bytes 163872 | tf_op jit(solution)/shard_map/ppermute | solution.py:400
  (46 shorter events, 27.1 us)
Async XLA Ops:
  1.1 10.5 %collective-permute-start = (bf16[64,4224]{1,0:T(8,128)(2,1)S(1)}, bf16[64,4224]{1,0:T(8,128)(2,1)S(1)}, u32[]{:S(2)}, u32[]{:S(2)}) collective-permute-start(bf16[64,4224]{1,0:T(8,128)(2,1)S(1)} %bundle.1), channel_id=1, source_target_pairs={{0,1},{2,3},{4,5},{6,7},{8,9},{10,11},{12,13},{14,15},{1,4},{3,6},... | collective-permute-start | bytes 1622024 | tf_op jit(solution)/shard_map/ppermute | solution.py:413
  3.5 14.5 %collective-permute-start.3 = (bf16[64,4096]{1,0:T(8,128)(2,1)}, bf16[64,4096]{1,0:T(8,128)(2,1)S(1)}, u32[]{:S(2)}, u32[]{:S(2)}) collective-permute-start(bf16[64,4096]{1,0:T(8,128)(2,1)} %refs_2_.1), channel_id=1, source_target_pairs={{0,1},{2,3},{4,5},{6,7},{8,9},{10,11},{12,13},{14,15},{1,4},{3,6},... | collective-permute-start | bytes 1572872 | tf_op jit(solution)/shard_map/ppermute | solution.py:414
  8.1 16.6 %collective-permute-start.2 = (bf16[64,4224]{1,0:T(8,128)(2,1)S(1)}, bf16[64,4224]{1,0:T(8,128)(2,1)S(1)}, u32[]{:S(2)}, u32[]{:S(2)}) collective-permute-start(bf16[64,4224]{1,0:T(8,128)(2,1)S(1)} %bundle.1), channel_id=1, source_target_pairs={{0,2},{1,3},{4,6},{5,7},{8,10},{9,11},{12,14},{13,15},{16,18},{17,... | collective-permute-start | bytes 1622024 | tf_op jit(solution)/shard_map/ppermute | solution.py:412
  11.6 13.1 %collective-permute-start.1 = (bf16[64,4224]{1,0:T(8,128)(2,1)S(1)}, bf16[64,4224]{1,0:T(8,128)(2,1)S(1)}, u32[]{:S(2)}, u32[]{:S(2)}) collective-permute-start(bf16[64,4224]{1,0:T(8,128)(2,1)S(1)} %collective-permute-done.k2), channel_id=1, source_target_pairs={{2,1},{6,5},{10,9},{14,13},{3,4},{7,8},{11,12},{18,17},{22,21},{26... | collective-permute-start | bytes 1622024 | tf_op jit(solution)/shard_map/ppermute | solution.py:416
  12.3 22.3 %collective-permute-start.5 = (bf16[64,4096]{1,0:T(8,128)(2,1)}, bf16[64,4096]{1,0:T(8,128)(2,1)S(1)}, u32[]{:S(2)}, u32[]{:S(2)}) collective-permute-start(bf16[64,4096]{1,0:T(8,128)(2,1)} %refs_2_.1), channel_id=1, source_target_pairs={{0,2},{1,3},{4,6},{5,7},{8,10},{9,11},{12,14},{13,15},{16,18},{17,... | collective-permute-start | bytes 1572872 | tf_op jit(solution)/shard_map/ppermute | solution.py:415
  17.9 16.6 %collective-permute-start.4 = (bf16[64,4096]{1,0:T(8,128)(2,1)S(1)}, bf16[64,4096]{1,0:T(8,128)(2,1)}, u32[]{:S(2)}, u32[]{:S(2)}) collective-permute-start(bf16[64,4096]{1,0:T(8,128)(2,1)S(1)} %collective-permute-done.3.v2), channel_id=1, source_target_pairs={{2,1},{6,5},{10,9},{14,13},{3,4},{7,8},{11,12},{18,17},{22,21},{26... | collective-permute-start | bytes 1572872 | tf_op jit(solution)/shard_map/ppermute | solution.py:417
  25.3 12.3 %collective-permute-start.6 = (bf16[64,4224]{1,0:T(8,128)(2,1)S(1)}, bf16[64,4224]{1,0:T(8,128)(2,1)S(1)}, u32[]{:S(2)}, u32[]{:S(2)}) collective-permute-start(bf16[64,4224]{1,0:T(8,128)(2,1)S(1)} %choose.2.k1), channel_id=1, source_target_pairs={{0,1},{1,0},{2,3},{3,2},{4,5},{5,4},{6,7},{7,6},{8,9},{9,8},{10,11... | collective-permute-start | bytes 1622024 | tf_op jit(solution)/shard_map/ppermute | solution.py:400
  41.1 18.6 %collective-permute-start.10 = (bf16[20,4096]{1,0:T(8,128)(2,1)S(1)}, bf16[20,4096]{1,0:T(8,128)(2,1)S(1)}, u32[]{:S(2)}, u32[]{:S(2)}) collective-permute-start(bf16[20,4096]{1,0:T(8,128)(2,1)S(1)} %get-tuple-element.89.refs_0_), channel_id=1, source_target_pairs={{0,2},{1,3},{2,0},{3,1},{4,6},{5,7},{6,4},{7,5},{8,10},{9,11},{10,... | collective-permute-start | bytes 491528 | tf_op jit(solution)/shard_map/ppermute | solution.py:400
  43.5 16.1 %collective-permute-start.11 = (bf16[20,4096]{1,0:T(8,128)(2,1)S(1)}, bf16[20,4096]{1,0:T(8,128)(2,1)S(1)}, u32[]{:S(2)}, u32[]{:S(2)}) collective-permute-start(bf16[20,4096]{1,0:T(8,128)(2,1)S(1)} %get-tuple-element.87), channel_id=1, source_target_pairs={{0,8},{1,9},{2,10},{3,11},{4,12},{5,13},{6,14},{7,15},{8,0},{9,1},... | collective-permute-start | bytes 491528 | tf_op jit(solution)/shard_map/ppermute | solution.py:442
  49.2 11.7 %collective-permute-start.8 = (bf16[20,4096]{1,0:T(8,128)(2,1)S(1)}, bf16[20,4096]{1,0:T(8,128)(2,1)S(1)}, u32[]{:S(2)}, u32[]{:S(2)}) collective-permute-start(bf16[20,4096]{1,0:T(8,128)(2,1)S(1)} %get-tuple-element.89.refs_0_), channel_id=1, source_target_pairs={{0,6},{1,7},{2,4},{3,5},{4,2},{5,3},{6,0},{7,1},{8,14},{9,15},{10,... | collective-permute-start | bytes 491528 | tf_op jit(solution)/shard_map/ppermute | solution.py:400
  52.2 12.3 %collective-permute-start.9 = (bf16[20,4096]{1,0:T(8,128)(2,1)S(1)}, bf16[20,4096]{1,0:T(8,128)(2,1)S(1)}, u32[]{:S(2)}, u32[]{:S(2)}) collective-permute-start(bf16[20,4096]{1,0:T(8,128)(2,1)S(1)} %get-tuple-element.89.refs_0_), channel_id=1, source_target_pairs={{0,4},{1,5},{2,6},{3,7},{4,0},{5,1},{6,2},{7,3},{8,12},{9,13},{10,... | collective-permute-start | bytes 491528 | tf_op jit(solution)/shard_map/ppermute | solution.py:400
  64.6 3.6 %collective-permute-start.15 = (bf16[80,4096]{1,0:T(8,128)(2,1)S(1)}, bf16[80,4096]{1,0:T(8,128)(2,1)S(1)}, u32[]{:S(2)}, u32[]{:S(2)}) collective-permute-start(bf16[80,4096]{1,0:T(8,128)(2,1)S(1)} %pile.2.local), channel_id=1, source_target_pairs={{0,1},{1,0},{2,3},{3,2},{4,5},{5,4},{6,7},{7,6},{8,9},{9,8},{10,11... | collective-permute-start | bytes 1966088 | tf_op jit(solution)/shard_map/ppermute | solution.py:400
  64.7 8.8 %collective-permute-start.12 = (bf16[20,4096]{1,0:T(8,128)(2,1)S(1)}, bf16[20,4096]{1,0:T(8,128)(2,1)S(1)}, u32[]{:S(2)}, u32[]{:S(2)}) collective-permute-start(bf16[20,4096]{1,0:T(8,128)(2,1)S(1)} %collective-permute-done.11.refs_0_), channel_id=1, source_target_pairs={{0,6},{1,7},{2,4},{3,5},{4,2},{5,3},{6,0},{7,1},{8,14},{9,15},{10,... | collective-permute-start | bytes 491528 | tf_op jit(solution)/shard_map/ppermute | solution.py:400
  66.2 9.9 %collective-permute-start.13 = (bf16[20,4096]{1,0:T(8,128)(2,1)S(1)}, bf16[20,4096]{1,0:T(8,128)(2,1)S(1)}, u32[]{:S(2)}, u32[]{:S(2)}) collective-permute-start(bf16[20,4096]{1,0:T(8,128)(2,1)S(1)} %collective-permute-done.11.refs_0_), channel_id=1, source_target_pairs={{0,4},{1,5},{2,6},{3,7},{4,0},{5,1},{6,2},{7,3},{8,12},{9,13},{10,... | collective-permute-start | bytes 491528 | tf_op jit(solution)/shard_map/ppermute | solution.py:400
  66.6 10.5 %collective-permute-start.14 = (bf16[20,4096]{1,0:T(8,128)(2,1)S(1)}, bf16[20,4096]{1,0:T(8,128)(2,1)S(1)}, u32[]{:S(2)}, u32[]{:S(2)}) collective-permute-start(bf16[20,4096]{1,0:T(8,128)(2,1)S(1)} %collective-permute-done.11.refs_0_), channel_id=1, source_target_pairs={{0,2},{1,3},{2,0},{3,1},{4,6},{5,7},{6,4},{7,5},{8,10},{9,11},{10,... | collective-permute-start | bytes 491528 | tf_op jit(solution)/shard_map/ppermute | solution.py:400
  77.2 2.2 %collective-permute-start.16 = (bf16[80,4096]{1,0:T(8,128)(2,1)S(1)}, bf16[80,4096]{1,0:T(8,128)(2,1)S(1)}, u32[]{:S(2)}, u32[]{:S(2)}) collective-permute-start(bf16[80,4096]{1,0:T(8,128)(2,1)S(1)} %pile.3.local), channel_id=1, source_target_pairs={{0,1},{1,0},{2,3},{3,2},{4,5},{5,4},{6,7},{7,6},{8,9},{9,8},{10,11... | collective-permute-start | bytes 1966088 | tf_op jit(solution)/shard_map/ppermute | solution.py:400
  77.3 7.5 %collective-permute-start.18 = (bf16[80,4096]{1,0:T(8,128)(2,1)S(1)}, bf16[80,4096]{1,0:T(8,128)(2,1)S(1)}, u32[]{:S(2)}, u32[]{:S(2)}) collective-permute-start(bf16[80,4096]{1,0:T(8,128)(2,1)S(1)} %get-tuple-element.109), channel_id=1, source_target_pairs={{0,1},{1,0},{2,3},{3,2},{4,5},{5,4},{6,7},{7,6},{8,9},{9,8},{10,11... | collective-permute-start | bytes 1966088 | tf_op jit(solution)/shard_map/ppermute | solution.py:400
  87.0 7.0 %collective-permute-start.19 = (bf16[20,4096]{1,0:T(8,128)(2,1)S(1)}, bf16[20,4096]{1,0:T(8,128)(2,1)S(1)}, u32[]{:S(2)}, u32[]{:S(2)}) collective-permute-start(bf16[20,4096]{1,0:T(8,128)(2,1)S(1)} %get-tuple-element.115), channel_id=1, source_target_pairs={{0,2},{1,3},{2,0},{3,1},{4,6},{5,7},{6,4},{7,5},{8,10},{9,11},{10,... | collective-permute-start | bytes 491528 | tf_op jit(solution)/shard_map/ppermute | solution.py:400
  87.7 7.8 %collective-permute-start.20 = (bf16[20,4096]{1,0:T(8,128)(2,1)S(1)}, bf16[20,4096]{1,0:T(8,128)(2,1)S(1)}, u32[]{:S(2)}, u32[]{:S(2)}) collective-permute-start(bf16[20,4096]{1,0:T(8,128)(2,1)S(1)} %get-tuple-element.116), channel_id=1, source_target_pairs={{0,4},{1,5},{2,6},{3,7},{4,0},{5,1},{6,2},{7,3},{8,12},{9,13},{10,... | collective-permute-start | bytes 491528 | tf_op jit(solution)/shard_map/ppermute | solution.py:400
  89.1 11.5 %collective-permute-start.24 = (bf16[20,4096]{1,0:T(8,128)(2,1)S(1)}, bf16[20,4096]{1,0:T(8,128)(2,1)S(1)}, u32[]{:S(2)}, u32[]{:S(2)}) collective-permute-start(bf16[20,4096]{1,0:T(8,128)(2,1)S(1)} %get-tuple-element.128), channel_id=1, source_target_pairs={{0,6},{1,7},{2,4},{3,5},{4,2},{5,3},{6,0},{7,1},{8,14},{9,15},{10,... | collective-permute-start | bytes 491528 | tf_op jit(solution)/shard_map/ppermute | solution.py:400
  95.5 8.0 %collective-permute-start.21 = (bf16[20,4096]{1,0:T(8,128)(2,1)S(1)}, bf16[20,4096]{1,0:T(8,128)(2,1)S(1)}, u32[]{:S(2)}, u32[]{:S(2)}) collective-permute-start(bf16[20,4096]{1,0:T(8,128)(2,1)S(1)} %get-tuple-element.122), channel_id=1, source_target_pairs={{0,2},{1,3},{2,0},{3,1},{4,6},{5,7},{6,4},{7,5},{8,10},{9,11},{10,... | collective-permute-start | bytes 491528 | tf_op jit(solution)/shard_map/ppermute | solution.py:400
  96.9 12.1 %collective-permute-start.22 = (bf16[20,4096]{1,0:T(8,128)(2,1)S(1)}, bf16[20,4096]{1,0:T(8,128)(2,1)S(1)}, u32[]{:S(2)}, u32[]{:S(2)}) collective-permute-start(bf16[20,4096]{1,0:T(8,128)(2,1)S(1)} %get-tuple-element.123), channel_id=1, source_target_pairs={{0,4},{1,5},{2,6},{3,7},{4,0},{5,1},{6,2},{7,3},{8,12},{9,13},{10,... | collective-permute-start | bytes 491528 | tf_op jit(solution)/shard_map/ppermute | solution.py:400
  97.5 14.6 %collective-permute-start.23 = (bf16[20,4096]{1,0:T(8,128)(2,1)S(1)}, bf16[20,4096]{1,0:T(8,128)(2,1)S(1)}, u32[]{:S(2)}, u32[]{:S(2)}) collective-permute-start(bf16[20,4096]{1,0:T(8,128)(2,1)S(1)} %get-tuple-element.124), channel_id=1, source_target_pairs={{0,6},{1,7},{2,4},{3,5},{4,2},{5,3},{6,0},{7,1},{8,14},{9,15},{10,... | collective-permute-start | bytes 491528 | tf_op jit(solution)/shard_map/ppermute | solution.py:400
  100.7 11.7 %collective-permute-start.25 = (bf16[20,4096]{1,0:T(8,128)(2,1)S(1)}, bf16[20,4096]{1,0:T(8,128)(2,1)S(1)}, u32[]{:S(2)}, u32[]{:S(2)}) collective-permute-start(bf16[20,4096]{1,0:T(8,128)(2,1)S(1)} %total.1), channel_id=1, source_target_pairs={{0,8},{1,9},{2,10},{3,11},{4,12},{5,13},{6,14},{7,15},{8,0},{9,1},... | collective-permute-start | bytes 491528 | tf_op jit(solution)/shard_map/ppermute | solution.py:473
  (2 other events, 4.1 us)

commit v11 on v9

--- a/solution.py
+++ b/solution.py
@@ -10,6 +10,7 @@
 HEAD_DIM = 128
 E_WIN = 2
 WIN_DEV = 3
+BLOCKS = 5
 CAP = 20
 SPARE = 16
 HEADS_STEP = 8
@@ -52,39 +53,37 @@
     )(far(keys), far(segs))
 
 
-def choose_kernel(flags, first, second, out):
-    @pl.when(flags[5] == 1)
-    def _():
-        out[...] = first[...]
-
-    @pl.when(flags[5] != 1)
-    def _():
-        out[...] = second[...]
-
-
-def choose(flags, first, second):
+def choose_kernel(flags, first, second, third, out):
+    for value, block in enumerate((first, second, third)):
+
+        @pl.when(flags[6] == value)
+        def _():
+            out[...] = block[...]
+
+
+def choose(flags, blocks):
     return pl.pallas_call(
         choose_kernel,
-        in_specs=[pl.BlockSpec(memory_space=pltpu.SMEM), NEAR, NEAR],
+        in_specs=[pl.BlockSpec(memory_space=pltpu.SMEM)] + [NEAR] * 3,
         out_specs=NEAR,
-        out_shape=jax.ShapeDtypeStruct(first.shape, first.dtype),
+        out_shape=jax.ShapeDtypeStruct(blocks[0].shape, blocks[0].dtype),
         compiler_params=pltpu.CompilerParams(vmem_limit_bytes=6 * MIB),
         name="choose",
-    )(flags, close(first), close(second))
+    )(flags, *[close(block) for block in blocks])
 
 
 def attention_kernel(
-    deltas, q, k0, v0, k1, v1, k2, v2, k3, v3, seg0, resid, gain, routes, gates,
+    deltas, q, k0, v0, k1, v1, k2, v2, k3, v3, k4, v4, seg0, resid, gain, routes, gates,
     mixed_out, keep_out, send_out, weight_out,
 ):
     rows, model = q.shape
-    keys = (WIN_DEV + 1) * rows
+    keys = BLOCKS * rows
     width = HEADS_STEP * HEAD_DIM
 
     seg_own = seg0[...].astype(jnp.float32)
     seg_row = jnp.concatenate(
         [seg_own]
-        + [block[:SPARE, model:][0:1, :rows].astype(jnp.float32) for block in (k1, k2, k3)],
+        + [block[:SPARE, model:][0:1, :rows].astype(jnp.float32) for block in (k1, k2, k3, k4)],
         axis=1,
     )
     eye = lax.broadcasted_iota(jnp.int32, (rows, rows), 0) == lax.broadcasted_iota(
@@ -94,11 +93,9 @@
     lane = lax.broadcasted_iota(jnp.int32, (rows, keys), 1)
     sub = lax.broadcasted_iota(jnp.int32, (rows, keys), 0)
     block = lane // rows
-    back = jnp.where(
-        block == 0,
-        deltas[0],
-        jnp.where(block == 1, deltas[1], jnp.where(block == 2, deltas[2], deltas[3])),
-    )
+    back = jnp.zeros_like(block)
+    for at in range(1, BLOCKS):
+        back = jnp.where(block == at, deltas[at], back)
     distance = sub - (lane - block * rows) + back * rows
     allowed = (distance >= 0) & (distance <= WIN_DEV * rows) & (seg_col == seg_row)
     bias = jnp.where(allowed, 0.0, MASKED)
@@ -109,8 +106,8 @@
     def _(step):
         at = pl.ds(pl.multiple_of(step * width, width), width)
         query = q[:, at]
-        key = jnp.concatenate([k0[:, at], k1[:, at], k2[:, at], k3[:, at]], axis=0)
-        value = jnp.concatenate([v0[:, at], v1[:, at], v2[:, at], v3[:, at]], axis=0)
+        key = jnp.concatenate([k0[:, at], k1[:, at], k2[:, at], k3[:, at], k4[:, at]], axis=0)
+        value = jnp.concatenate([v0[:, at], v1[:, at], v2[:, at], v3[:, at], v4[:, at]], axis=0)
         scores = jnp.stack(
             [
                 lax.dot_general(
@@ -170,7 +167,7 @@
         ).astype(jnp.bfloat16)
 
     for place, out in ((0, keep_out), (1, send_out)):
-        member, weight, rank = picks(deltas[4] if place == 0 else 1 - deltas[4])
+        member, weight, rank = picks(deltas[5] if place == 0 else 1 - deltas[5])
         pick = (slot == rank) & member
         out[...] = packed(pick)[:CAP]
         weight_out[place] = spread(pick, weight)
@@ -190,8 +187,8 @@
         ],
         compiler_params=pltpu.CompilerParams(vmem_limit_bytes=14 * MIB),
         cost_estimate=pl.CostEstimate(
-            flops=4 * rows * 4 * rows * width, bytes_accessed=8 * rows * width * 4,
-            transcendentals=rows * 4 * rows * (width // HEAD_DIM),
+            flops=4 * rows * BLOCKS * rows * width, bytes_accessed=8 * rows * width * 4,
+            transcendentals=rows * BLOCKS * rows * (width // HEAD_DIM),
         ),
         name="attention",
     )(
@@ -388,32 +385,39 @@
     count = lax.axis_size("expert")
     own = lax.axis_index("expert")
     shard_count = count // E_WIN
-    odd = own % 2
-
-    next_chip = [(i, i + 2) for i in range(count - 2) if i % 4 != 3]
-    crossing = [(i, i + 1) for i in range(0, count, 2)]
-    crossing += [(i, i + 3) for i in range(1, count - 3, 2)]
-    passing = [(i, i - 1) for i in range(2, count, 4)]
+
+    place = own % 4
+
+    def moved(block, steps):
+        pairs = [(i, i + steps[i % 4]) for i in range(count) if i % 4 in steps]
+        return lax.ppermute(block, "expert", [pair for pair in pairs if pair[1] < count])
+
+    across = {0: 3, 1: 3, 2: -1, 3: 3}
+    passed = {1: 4, 2: -2}
+    beside = {0: 1, 1: 1, 2: 1}
 
     def swapped(block, mask):
         return lax.ppermute(block, "expert", [(i, i ^ mask) for i in range(count)])
 
     seg_own = segment_ids.reshape(1, -1)
     beyond = 2 * WIN_DEV + 2
-    delta_list = [0 * own, 0 * own + 2, 3 - 2 * odd, 1 + 2 * odd]
+    delta_list = [
+        0 * own,
+        jnp.where(place == 1, beyond, 3),
+        jnp.where(place == 0, 1, jnp.where(place == 1, 3, beyond)),
+        jnp.where(place == 0, beyond, 1),
+        0 * own + 2,
+    ]
     my_expert = own // shard_count
-    relayed = (own % 4 == 1).astype(jnp.int32)
+    source = jnp.where(place < 2, 0, jnp.where(place == 2, 1, 2))
     scalars = jnp.stack(
-        [jnp.where(own >= delta, delta, beyond) for delta in delta_list] + [my_expert, relayed]
+        [jnp.where(own >= delta, delta, beyond) for delta in delta_list] + [my_expert, source]
     ).astype(jnp.int32)
 
     key_block = bundle(keys, seg_own)
-    key_cross = lax.ppermute(key_block, "expert", crossing)
-    value_cross = lax.ppermute(values, "expert", crossing)
-    key_next = lax.ppermute(key_block, "expert", next_chip)
-    value_next = lax.ppermute(values, "expert", next_chip)
-    key_passed = lax.ppermute(key_cross, "expert", passing)
-    value_passed = lax.ppermute(value_cross, "expert", passing)
+    key_one, value_one = moved(key_block, across), moved(values, across)
+    key_three, value_three = moved(key_block, beside), moved(values, beside)
+    key_two, value_two = moved(key_one, passed), moved(value_one, passed)
     mine = bring(
         [
             queries, keys, values, seg_own, resid, norm_gain.reshape(1, -1), routes.T,
@@ -422,17 +426,19 @@
         scalars,
     )
     gate_held = fetch(w_gate, scalars)
-    key_two = choose(scalars, key_passed, key_next)
-    key_two, gate_held, mine = lax.optimization_barrier((key_two, gate_held, mine))
-    key_mirror = swapped(key_two, 1)
-    value_two = choose(scalars, value_passed, value_next)
-    value_mirror = swapped(value_two, 1)
+    key_four = choose(scalars, [key_two, key_three, key_one])
+    key_four, gate_held, mine = lax.optimization_barrier((key_four, gate_held, mine))
+    key_four = swapped(key_four, 1)
+    value_four = swapped(choose(scalars, [value_two, value_three, value_one]), 1)
 
     queries, keys, values, seg_own, resid, gain, routes_held, gates_held = mine
     mixed, keep, send, weight = attention(
         scalars,
         queries,
-        [keys, values, key_two, value_two, key_cross, value_cross, key_mirror, value_mirror],
+        [
+            keys, values, key_one, value_one, key_two, value_two, key_three, value_three,
+            key_four, value_four,
+        ],
         seg_own, resid, gain, routes_held, gates_held,
     )
     up_held, down_held = fetch(w_up, weight), fetch(w_down, weight)

time: 112 us -> 108 us (0.964)
  waiting for transfers between devices: 39.8 us -> 35.9 us
    ppermute x18, waiting for transfers between devices: 30.6 us -> 25.3 us  [swapped(): return lax.ppermute(block, 'expert', [(i, i ^ mask) for i in range(count)])]
    ppermute x1, starting transfers between devices: 0.97 us -> 3.77 us  [shards(): other = lax.ppermute(back, 'expert', partner)]
    ppermute x1, starting transfers between devices: 4.16 us -> 2.69 us  [shards(): got = lax.ppermute(send, 'expert', partner)]
    ppermute x6, waiting for transfers between devices: 9.16 us -> 10.6 us  [moved(): lax.ppermute(block, 'expert', [pair for pair in pairs if pair[1] < count])]
  transfers between devices with their start and end apart: 26 -> 26, of which waited for: 14 -> 15; matrix products, arithmetic and copies ran while one was open for 0% -> 0% of each run, Pallas kernels for 22% -> 23%
where the time goes in v11:
time: 108 us
  starting transfers between devices  40.1 us (37%)
  waiting for transfers between devices  35.9 us (33%)
  Pallas kernels  31.6 us (29%)
    ppermute x18, waiting for transfers between devices, swapped(): return lax.ppermute(block, 'expert', [(i, i ^ mask) for i in range(count)])  25.3 us
    ppermute x6, starting transfers between devices, moved(): lax.ppermute(block, 'expert', [pair for pair in pairs if pair[1] < count])  17.2 us
    ppermute x18, starting transfers between devices, swapped(): return lax.ppermute(block, 'expert', [(i, i ^ mask) for i in range(count)])  16.4 us
    ppermute x6, waiting for transfers between devices, moved(): lax.ppermute(block, 'expert', [pair for pair in pairs if pair[1] < count])  10.6 us
    pallas_call x3, Pallas kernels, fetch(): pl.pallas_call(functools.partial(fetch_kernel, parts), in_specs=[anywhere...  10.5 us
    pallas_call x2, Pallas kernels, experts(): pl.pallas_call(experts_kernel, in_specs=[NEAR] * 5, out_specs=[NEAR] * 2,...  10.5 us
    pallas_call x1, Pallas kernels, attention(): pl.pallas_call(attention_kernel, in_specs=[pl.BlockSpec(memory_space=pltp...  3.83 us
    ppermute x1, starting transfers between devices, shards(): other = lax.ppermute(back, 'expert', partner)  3.77 us
  transfers between devices with their start and end apart: 26, of which 15 were waited for; matrix products, arithmetic and copies ran while one was open for 0% of the time, Pallas kernels for 23%

profile of v11, /device:TPU:0, one launch (start us, length us, event | category | flops | bytes accessed | tf_op | source)
XLA Modules:
  0.0 107.9 jit_solution(3524769686221358371)
XLA Ops:
  0.0 1.9 %bundle.1 = bf16[64,4224]{1,0:T(8,128)(2,1)} custom-call(bf16[64,4096]{1,0:T(8,128)(2,1)} %refs_1_.1, s32[1,64]{1,0:T(1,128)} %bitcast.12), custom_call_target="tpu_custom_call" | custom-call | bytes 1048576 | tf_op jit(solution)/shard_map/bundle/pallas_call | solution.py:43
  1.9 4.3 %collective-permute-start = (bf16[64,4224]{1,0:T(8,128)(2,1)}, bf16[64,4224]{1,0:T(8,128)(2,1)S(1)}, u32[]{:S(2)}, u32[]{:S(2)}) collective-permute-start(bf16[64,4224]{1,0:T(8,128)(2,1)} %bundle.1), channel_id=1, source_target_pairs={{0,3},{1,4},{2,1},{3,6},{4,7},{5,8},{6,5},{7,10},{8,11},{9,12},{10... | collective-permute-start | bytes 1622024 | tf_op jit(solution)/shard_map/ppermute | solution.py:393
  6.2 3.8 %collective-permute-start.3 = (bf16[64,4096]{1,0:T(8,128)(2,1)}, bf16[64,4096]{1,0:T(8,128)(2,1)S(1)}, u32[]{:S(2)}, u32[]{:S(2)}) collective-permute-start(bf16[64,4096]{1,0:T(8,128)(2,1)} %refs_2_.1), channel_id=1, source_target_pairs={{0,3},{1,4},{2,1},{3,6},{4,7},{5,8},{6,5},{7,10},{8,11},{9,12},{10... | collective-permute-start | bytes 1572872 | tf_op jit(solution)/shard_map/ppermute | solution.py:393
  14.7 4.8 %collective-permute-start.5 = (bf16[64,4096]{1,0:T(8,128)(2,1)}, bf16[64,4096]{1,0:T(8,128)(2,1)S(1)}, u32[]{:S(2)}, u32[]{:S(2)}) collective-permute-start(bf16[64,4096]{1,0:T(8,128)(2,1)} %refs_2_.1), channel_id=1, source_target_pairs={{0,1},{1,2},{2,3},{4,5},{5,6},{6,7},{8,9},{9,10},{10,11},{12,13},{... | collective-permute-start | bytes 1572872 | tf_op jit(solution)/shard_map/ppermute | solution.py:393
  19.6 5.1 %collective-permute-done.3.third.v1 = bf16[64,4096]{1,0:T(8,128)(2,1)S(1)} collective-permute-done((bf16[64,4096]{1,0:T(8,128)(2,1)}, bf16[64,4096]{1,0:T(8,128)(2,1)S(1)}, u32[]{:S(2)}, u32[]{:S(2)}) %collective-permute-start.3) | collective-permute-done | bytes 524320 | tf_op jit(solution)/shard_map/ppermute | solution.py:393
  26.1 3.5 %fetch.3.w_gate = bf16[4096,1024]{1,0:T(8,128)(2,1)S(1)} custom-call(bf16[4096,1024]{1,0:T(8,128)(2,1)} %source.3, s32[7]{0:T(128)S(1)} %stack.31.flags.after.refs_8_.deltas), custom_call_target="tpu_custom_call" | custom-call | bytes 16777216 | tf_op jit(solution)/shard_map/fetch/pallas_call | solution.py:244
  32.0 3.8 %collective-permute-done.4.first.v2 = bf16[64,4096]{1,0:T(8,128)(2,1)S(1)} collective-permute-done((bf16[64,4096]{1,0:T(8,128)(2,1)S(1)}, bf16[64,4096]{1,0:T(8,128)(2,1)S(1)}, u32[]{:S(2)}, u32[]{:S(2)}) %collective-permute-start.4) | collective-permute-done | bytes 524320 | tf_op jit(solution)/shard_map/ppermute | solution.py:393
  36.4 1.9 %collective-permute-done.7.v4 = bf16[64,4096]{1,0:T(8,128)(2,1)S(1)} collective-permute-done((bf16[64,4096]{1,0:T(8,128)(2,1)S(1)}, bf16[64,4096]{1,0:T(8,128)(2,1)S(1)}, u32[]{:S(2)}, u32[]{:S(2)}) %collective-permute-start.7) | collective-permute-done | bytes 524320 | tf_op jit(solution)/shard_map/ppermute | solution.py:400
  38.3 3.8 %attention.1 = (f32[64,4096]{1,0:T(8,128)S(1)}, bf16[20,4096]{1,0:T(8,128)(2,1)S(1)}, bf16[20,4096]{1,0:T(8,128)(2,1)S(1)}, bf16[2,64,32]{2,1,0:T(8,128)(2,1)S(1)}) custom-call(s32[7]{0:T(128)S(1)} %stack.31.flags.after.refs_8_.deltas, bf16[64,4096]{1,0:T(8,128)(2,1)S(1)} %get-tuple-element.75.q, bf16[64,4096]{1,0:T(8,128)(2,1)S(1)} %get-tuple-element.76.k0, ...), custom_call_target="tpu_custom_call" | custom-call | flops 335544320 | bytes 8388608 | tf_op jit(solution)/shard_map/attention/pallas_call | solution.py:178
  42.2 2.7 %collective-permute-start.11 = (bf16[20,4096]{1,0:T(8,128)(2,1)S(1)}, bf16[20,4096]{1,0:T(8,128)(2,1)S(1)}, u32[]{:S(2)}, u32[]{:S(2)}) collective-permute-start(bf16[20,4096]{1,0:T(8,128)(2,1)S(1)} %get-tuple-element.87), channel_id=1, source_target_pairs={{0,8},{1,9},{2,10},{3,11},{4,12},{5,13},{6,14},{7,15},{8,0},{9,1},... | collective-permute-start | bytes 491528 | tf_op jit(solution)/shard_map/ppermute | solution.py:447
  44.9 4.7 %collective-permute-start.8 = (bf16[20,4096]{1,0:T(8,128)(2,1)S(1)}, bf16[20,4096]{1,0:T(8,128)(2,1)S(1)}, u32[]{:S(2)}, u32[]{:S(2)}) collective-permute-start(bf16[20,4096]{1,0:T(8,128)(2,1)S(1)} %get-tuple-element.89.refs_0_), channel_id=1, source_target_pairs={{0,6},{1,7},{2,4},{3,5},{4,2},{5,3},{6,0},{7,1},{8,14},{9,15},{10,... | collective-permute-start | bytes 491528 | tf_op jit(solution)/shard_map/ppermute | solution.py:400
  49.7 3.5 %fetch.4.w_up = bf16[4096,1024]{1,0:T(8,128)(2,1)S(1)} custom-call(bf16[4096,1024]{1,0:T(8,128)(2,1)} %source.4, bf16[2,64,32]{2,1,0:T(8,128)(2,1)S(1)} %get-tuple-element.85.after.weight), custom_call_target="tpu_custom_call" | custom-call | bytes 16777216 | tf_op jit(solution)/shard_map/fetch/pallas_call | solution.py:244
  53.2 3.5 %fetch.5.w_down = bf16[1024,4096]{1,0:T(8,128)(2,1)S(1)} custom-call(bf16[1024,4096]{1,0:T(8,128)(2,1)} %source.5, bf16[2,64,32]{2,1,0:T(8,128)(2,1)S(1)} %get-tuple-element.85.after.weight), custom_call_target="tpu_custom_call" | custom-call | bytes 16777216 | tf_op jit(solution)/shard_map/fetch/pallas_call | solution.py:244
  56.8 2.0 %collective-permute-done.9.refs_2_ = bf16[20,4096]{1,0:T(8,128)(2,1)S(1)} collective-permute-done((bf16[20,4096]{1,0:T(8,128)(2,1)S(1)}, bf16[20,4096]{1,0:T(8,128)(2,1)S(1)}, u32[]{:S(2)}, u32[]{:S(2)}) %collective-permute-start.9) | collective-permute-done | bytes 163872 | tf_op jit(solution)/shard_map/ppermute | solution.py:400
  58.9 2.7 %collective-permute-start.12 = (bf16[20,4096]{1,0:T(8,128)(2,1)S(1)}, bf16[20,4096]{1,0:T(8,128)(2,1)S(1)}, u32[]{:S(2)}, u32[]{:S(2)}) collective-permute-start(bf16[20,4096]{1,0:T(8,128)(2,1)S(1)} %collective-permute-done.11.refs_0_), channel_id=1, source_target_pairs={{0,6},{1,7},{2,4},{3,5},{4,2},{5,3},{6,0},{7,1},{8,14},{9,15},{10,... | collective-permute-start | bytes 491528 | tf_op jit(solution)/shard_map/ppermute | solution.py:400
  62.5 5.2 %experts.2 = (bf16[80,4096]{1,0:T(8,128)(2,1)S(1)}, bf16[80,4096]{1,0:T(8,128)(2,1)S(1)}) custom-call(bf16[80,4096]{1,0:T(8,128)(2,1)S(1)} %pile.2.local, bf16[80,4096]{1,0:T(8,128)(2,1)S(1)} %collective-permute-done.15.remote, bf16[4096,1024]{1,0:T(8,128)(2,1)S(1)} %fetch.3.w_gate, bf16[4096,1024]{1,0:T(8,128)(2,1)S(1)} %fetch.4.w_up, ...), custom_call_target="tpu_custom_call" | custom-call | flops 4026531840 | bytes 2621440 | tf_op jit(solution)/shard_map/experts/pallas_call | solution.py:283
  67.8 3.9 %collective-permute-done.13.refs_2_ = bf16[20,4096]{1,0:T(8,128)(2,1)S(1)} collective-permute-done((bf16[20,4096]{1,0:T(8,128)(2,1)S(1)}, bf16[20,4096]{1,0:T(8,128)(2,1)S(1)}, u32[]{:S(2)}, u32[]{:S(2)}) %collective-permute-start.13) | collective-permute-done | bytes 163872 | tf_op jit(solution)/shard_map/ppermute | solution.py:400
  73.9 5.2 %experts.3 = (bf16[80,4096]{1,0:T(8,128)(2,1)S(1)}, bf16[80,4096]{1,0:T(8,128)(2,1)S(1)}) custom-call(bf16[80,4096]{1,0:T(8,128)(2,1)S(1)} %pile.3.local, bf16[80,4096]{1,0:T(8,128)(2,1)S(1)} %collective-permute-done.16.remote, bf16[4096,1024]{1,0:T(8,128)(2,1)S(1)} %fetch.3.w_gate, bf16[4096,1024]{1,0:T(8,128)(2,1)S(1)} %fetch.4.w_up, ...), custom_call_target="tpu_custom_call" | custom-call | flops 4026531840 | bytes 2621440 | tf_op jit(solution)/shard_map/experts/pallas_call | solution.py:283
  79.6 1.8 %collective-permute-done.17.second = bf16[80,4096]{1,0:T(8,128)(2,1)S(1)} collective-permute-done((bf16[80,4096]{1,0:T(8,128)(2,1)S(1)}, bf16[80,4096]{1,0:T(8,128)(2,1)S(1)}, u32[]{:S(2)}, u32[]{:S(2)}) %collective-permute-start.17) | collective-permute-done | bytes 655392 | tf_op jit(solution)/shard_map/ppermute | solution.py:400
  85.1 3.5 %collective-permute-done.19.refs_1_ = bf16[20,4096]{1,0:T(8,128)(2,1)S(1)} collective-permute-done((bf16[20,4096]{1,0:T(8,128)(2,1)S(1)}, bf16[20,4096]{1,0:T(8,128)(2,1)S(1)}, u32[]{:S(2)}, u32[]{:S(2)}) %collective-permute-start.19) | collective-permute-done | bytes 163872 | tf_op jit(solution)/shard_map/ppermute | solution.py:400
  88.5 2.3 %collective-permute-done.20.refs_2_ = bf16[20,4096]{1,0:T(8,128)(2,1)S(1)} collective-permute-done((bf16[20,4096]{1,0:T(8,128)(2,1)S(1)}, bf16[20,4096]{1,0:T(8,128)(2,1)S(1)}, u32[]{:S(2)}, u32[]{:S(2)}) %collective-permute-start.20) | collective-permute-done | bytes 163872 | tf_op jit(solution)/shard_map/ppermute | solution.py:400
  95.2 3.8 %collective-permute-start.25 = (bf16[20,4096]{1,0:T(8,128)(2,1)S(1)}, bf16[20,4096]{1,0:T(8,128)(2,1)S(1)}, u32[]{:S(2)}, u32[]{:S(2)}) collective-permute-start(bf16[20,4096]{1,0:T(8,128)(2,1)S(1)} %total.1), channel_id=1, source_target_pairs={{0,8},{1,9},{2,10},{3,11},{4,12},{5,13},{6,14},{7,15},{8,0},{9,1},... | collective-permute-start | bytes 491528 | tf_op jit(solution)/shard_map/ppermute | solution.py:478
  99.1 4.4 %collective-permute-done.22.refs_2_ = bf16[20,4096]{1,0:T(8,128)(2,1)S(1)} collective-permute-done((bf16[20,4096]{1,0:T(8,128)(2,1)S(1)}, bf16[20,4096]{1,0:T(8,128)(2,1)S(1)}, u32[]{:S(2)}, u32[]{:S(2)}) %collective-permute-start.22) | collective-permute-done | bytes 163872 | tf_op jit(solution)/shard_map/ppermute | solution.py:400
  103.5 3.1 %collective-permute-done.23.refs_3_ = bf16[20,4096]{1,0:T(8,128)(2,1)S(1)} collective-permute-done((bf16[20,4096]{1,0:T(8,128)(2,1)S(1)}, bf16[20,4096]{1,0:T(8,128)(2,1)S(1)}, u32[]{:S(2)}, u32[]{:S(2)}) %collective-permute-start.23) | collective-permute-done | bytes 163872 | tf_op jit(solution)/shard_map/ppermute | solution.py:400
  (46 shorter events, 22.5 us)
Async XLA Ops:
  1.9 11.6 %collective-permute-start = (bf16[64,4224]{1,0:T(8,128)(2,1)}, bf16[64,4224]{1,0:T(8,128)(2,1)S(1)}, u32[]{:S(2)}, u32[]{:S(2)}) collective-permute-start(bf16[64,4224]{1,0:T(8,128)(2,1)} %bundle.1), channel_id=1, source_target_pairs={{0,3},{1,4},{2,1},{3,6},{4,7},{5,8},{6,5},{7,10},{8,11},{9,12},{10... | collective-permute-start | bytes 1622024 | tf_op jit(solution)/shard_map/ppermute | solution.py:393
  6.2 18.4 %collective-permute-start.3 = (bf16[64,4096]{1,0:T(8,128)(2,1)}, bf16[64,4096]{1,0:T(8,128)(2,1)S(1)}, u32[]{:S(2)}, u32[]{:S(2)}) collective-permute-start(bf16[64,4096]{1,0:T(8,128)(2,1)} %refs_2_.1), channel_id=1, source_target_pairs={{0,3},{1,4},{2,1},{3,6},{4,7},{5,8},{6,5},{7,10},{8,11},{9,12},{10... | collective-permute-start | bytes 1572872 | tf_op jit(solution)/shard_map/ppermute | solution.py:393
  10.0 21.2 %collective-permute-start.2 = (bf16[64,4224]{1,0:T(8,128)(2,1)}, bf16[64,4224]{1,0:T(8,128)(2,1)S(1)}, u32[]{:S(2)}, u32[]{:S(2)}) collective-permute-start(bf16[64,4224]{1,0:T(8,128)(2,1)} %bundle.1), channel_id=1, source_target_pairs={{0,1},{1,2},{2,3},{4,5},{5,6},{6,7},{8,9},{9,10},{10,11},{12,13},{... | collective-permute-start | bytes 1622024 | tf_op jit(solution)/shard_map/ppermute | solution.py:393
  13.4 17.8 %collective-permute-start.1 = (bf16[64,4224]{1,0:T(8,128)(2,1)S(1)}, bf16[64,4224]{1,0:T(8,128)(2,1)S(1)}, u32[]{:S(2)}, u32[]{:S(2)}) collective-permute-start(bf16[64,4224]{1,0:T(8,128)(2,1)S(1)} %collective-permute-done.third.k1), channel_id=1, source_target_pairs={{1,5},{2,0},{5,9},{6,4},{9,13},{10,8},{14,12},{17,21},{18,16},{21,... | collective-permute-start | bytes 1622024 | tf_op jit(solution)/shard_map/ppermute | solution.py:393
  14.7 17.2 %collective-permute-start.5 = (bf16[64,4096]{1,0:T(8,128)(2,1)}, bf16[64,4096]{1,0:T(8,128)(2,1)S(1)}, u32[]{:S(2)}, u32[]{:S(2)}) collective-permute-start(bf16[64,4096]{1,0:T(8,128)(2,1)} %refs_2_.1), channel_id=1, source_target_pairs={{0,1},{1,2},{2,3},{4,5},{5,6},{6,7},{8,9},{9,10},{10,11},{12,13},{... | collective-permute-start | bytes 1572872 | tf_op jit(solution)/shard_map/ppermute | solution.py:393
  24.7 11.1 %collective-permute-start.4 = (bf16[64,4096]{1,0:T(8,128)(2,1)S(1)}, bf16[64,4096]{1,0:T(8,128)(2,1)S(1)}, u32[]{:S(2)}, u32[]{:S(2)}) collective-permute-start(bf16[64,4096]{1,0:T(8,128)(2,1)S(1)} %collective-permute-done.3.third.v1), channel_id=1, source_target_pairs={{1,5},{2,0},{5,9},{6,4},{9,13},{10,8},{14,12},{17,21},{18,16},{21,... | collective-permute-start | bytes 1572872 | tf_op jit(solution)/shard_map/ppermute | solution.py:393
  31.9 6.5 %collective-permute-start.6 = (bf16[64,4224]{1,0:T(8,128)(2,1)S(1)}, bf16[64,4224]{1,0:T(8,128)(2,1)S(1)}, u32[]{:S(2)}, u32[]{:S(2)}) collective-permute-start(bf16[64,4224]{1,0:T(8,128)(2,1)S(1)} %choose.2), channel_id=1, source_target_pairs={{0,1},{1,0},{2,3},{3,2},{4,5},{5,4},{6,7},{7,6},{8,9},{9,8},{10,11... | collective-permute-start | bytes 1622024 | tf_op jit(solution)/shard_map/ppermute | solution.py:400
  42.2 14.5 %collective-permute-start.10 = (bf16[20,4096]{1,0:T(8,128)(2,1)S(1)}, bf16[20,4096]{1,0:T(8,128)(2,1)S(1)}, u32[]{:S(2)}, u32[]{:S(2)}) collective-permute-start(bf16[20,4096]{1,0:T(8,128)(2,1)S(1)} %get-tuple-element.89.refs_0_), channel_id=1, source_target_pairs={{0,2},{1,3},{2,0},{3,1},{4,6},{5,7},{6,4},{7,5},{8,10},{9,11},{10,... | collective-permute-start | bytes 491528 | tf_op jit(solution)/shard_map/ppermute | solution.py:400
  42.2 14.5 %collective-permute-start.11 = (bf16[20,4096]{1,0:T(8,128)(2,1)S(1)}, bf16[20,4096]{1,0:T(8,128)(2,1)S(1)}, u32[]{:S(2)}, u32[]{:S(2)}) collective-permute-start(bf16[20,4096]{1,0:T(8,128)(2,1)S(1)} %get-tuple-element.87), channel_id=1, source_target_pairs={{0,8},{1,9},{2,10},{3,11},{4,12},{5,13},{6,14},{7,15},{8,0},{9,1},... | collective-permute-start | bytes 491528 | tf_op jit(solution)/shard_map/ppermute | solution.py:447
  44.9 11.8 %collective-permute-start.8 = (bf16[20,4096]{1,0:T(8,128)(2,1)S(1)}, bf16[20,4096]{1,0:T(8,128)(2,1)S(1)}, u32[]{:S(2)}, u32[]{:S(2)}) collective-permute-start(bf16[20,4096]{1,0:T(8,128)(2,1)S(1)} %get-tuple-element.89.refs_0_), channel_id=1, source_target_pairs={{0,6},{1,7},{2,4},{3,5},{4,2},{5,3},{6,0},{7,1},{8,14},{9,15},{10,... | collective-permute-start | bytes 491528 | tf_op jit(solution)/shard_map/ppermute | solution.py:400
  49.7 9.1 %collective-permute-start.9 = (bf16[20,4096]{1,0:T(8,128)(2,1)S(1)}, bf16[20,4096]{1,0:T(8,128)(2,1)S(1)}, u32[]{:S(2)}, u32[]{:S(2)}) collective-permute-start(bf16[20,4096]{1,0:T(8,128)(2,1)S(1)} %get-tuple-element.89.refs_0_), channel_id=1, source_target_pairs={{0,4},{1,5},{2,6},{3,7},{4,0},{5,1},{6,2},{7,3},{8,12},{9,13},{10,... | collective-permute-start | bytes 491528 | tf_op jit(solution)/shard_map/ppermute | solution.py:400
  58.9 3.6 %collective-permute-start.15 = (bf16[80,4096]{1,0:T(8,128)(2,1)S(1)}, bf16[80,4096]{1,0:T(8,128)(2,1)S(1)}, u32[]{:S(2)}, u32[]{:S(2)}) collective-permute-start(bf16[80,4096]{1,0:T(8,128)(2,1)S(1)} %pile.2.local), channel_id=1, source_target_pairs={{0,1},{1,0},{2,3},{3,2},{4,5},{5,4},{6,7},{7,6},{8,9},{9,8},{10,11... | collective-permute-start | bytes 1966088 | tf_op jit(solution)/shard_map/ppermute | solution.py:400
  58.9 8.8 %collective-permute-start.12 = (bf16[20,4096]{1,0:T(8,128)(2,1)S(1)}, bf16[20,4096]{1,0:T(8,128)(2,1)S(1)}, u32[]{:S(2)}, u32[]{:S(2)}) collective-permute-start(bf16[20,4096]{1,0:T(8,128)(2,1)S(1)} %collective-permute-done.11.refs_0_), channel_id=1, source_target_pairs={{0,6},{1,7},{2,4},{3,5},{4,2},{5,3},{6,0},{7,1},{8,14},{9,15},{10,... | collective-permute-start | bytes 491528 | tf_op jit(solution)/shard_map/ppermute | solution.py:400
  61.7 10.0 %collective-permute-start.13 = (bf16[20,4096]{1,0:T(8,128)(2,1)S(1)}, bf16[20,4096]{1,0:T(8,128)(2,1)S(1)}, u32[]{:S(2)}, u32[]{:S(2)}) collective-permute-start(bf16[20,4096]{1,0:T(8,128)(2,1)S(1)} %collective-permute-done.11.refs_0_), channel_id=1, source_target_pairs={{0,4},{1,5},{2,6},{3,7},{4,0},{5,1},{6,2},{7,3},{8,12},{9,13},{10,... | collective-permute-start | bytes 491528 | tf_op jit(solution)/shard_map/ppermute | solution.py:400
  62.1 9.5 %collective-permute-start.14 = (bf16[20,4096]{1,0:T(8,128)(2,1)S(1)}, bf16[20,4096]{1,0:T(8,128)(2,1)S(1)}, u32[]{:S(2)}, u32[]{:S(2)}) collective-permute-start(bf16[20,4096]{1,0:T(8,128)(2,1)S(1)} %collective-permute-done.11.refs_0_), channel_id=1, source_target_pairs={{0,2},{1,3},{2,0},{3,1},{4,6},{5,7},{6,4},{7,5},{8,10},{9,11},{10,... | collective-permute-start | bytes 491528 | tf_op jit(solution)/shard_map/ppermute | solution.py:400
  71.7 2.2 %collective-permute-start.16 = (bf16[80,4096]{1,0:T(8,128)(2,1)S(1)}, bf16[80,4096]{1,0:T(8,128)(2,1)S(1)}, u32[]{:S(2)}, u32[]{:S(2)}) collective-permute-start(bf16[80,4096]{1,0:T(8,128)(2,1)S(1)} %pile.3.local), channel_id=1, source_target_pairs={{0,1},{1,0},{2,3},{3,2},{4,5},{5,4},{6,7},{7,6},{8,9},{9,8},{10,11... | collective-permute-start | bytes 1966088 | tf_op jit(solution)/shard_map/ppermute | solution.py:400
  71.8 7.5 %collective-permute-start.18 = (bf16[80,4096]{1,0:T(8,128)(2,1)S(1)}, bf16[80,4096]{1,0:T(8,128)(2,1)S(1)}, u32[]{:S(2)}, u32[]{:S(2)}) collective-permute-start(bf16[80,4096]{1,0:T(8,128)(2,1)S(1)} %get-tuple-element.109), channel_id=1, source_target_pairs={{0,1},{1,0},{2,3},{3,2},{4,5},{5,4},{6,7},{7,6},{8,9},{9,8},{10,11... | collective-permute-start | bytes 1966088 | tf_op jit(solution)/shard_map/ppermute | solution.py:400
  81.5 7.0 %collective-permute-start.19 = (bf16[20,4096]{1,0:T(8,128)(2,1)S(1)}, bf16[20,4096]{1,0:T(8,128)(2,1)S(1)}, u32[]{:S(2)}, u32[]{:S(2)}) collective-permute-start(bf16[20,4096]{1,0:T(8,128)(2,1)S(1)} %get-tuple-element.115), channel_id=1, source_target_pairs={{0,2},{1,3},{2,0},{3,1},{4,6},{5,7},{6,4},{7,5},{8,10},{9,11},{10,... | collective-permute-start | bytes 491528 | tf_op jit(solution)/shard_map/ppermute | solution.py:400
  83.0 7.8 %collective-permute-start.20 = (bf16[20,4096]{1,0:T(8,128)(2,1)S(1)}, bf16[20,4096]{1,0:T(8,128)(2,1)S(1)}, u32[]{:S(2)}, u32[]{:S(2)}) collective-permute-start(bf16[20,4096]{1,0:T(8,128)(2,1)S(1)} %get-tuple-element.116), channel_id=1, source_target_pairs={{0,4},{1,5},{2,6},{3,7},{4,0},{5,1},{6,2},{7,3},{8,12},{9,13},{10,... | collective-permute-start | bytes 491528 | tf_op jit(solution)/shard_map/ppermute | solution.py:400
  84.5 10.5 %collective-permute-start.24 = (bf16[20,4096]{1,0:T(8,128)(2,1)S(1)}, bf16[20,4096]{1,0:T(8,128)(2,1)S(1)}, u32[]{:S(2)}, u32[]{:S(2)}) collective-permute-start(bf16[20,4096]{1,0:T(8,128)(2,1)S(1)} %get-tuple-element.128), channel_id=1, source_target_pairs={{0,6},{1,7},{2,4},{3,5},{4,2},{5,3},{6,0},{7,1},{8,14},{9,15},{10,... | collective-permute-start | bytes 491528 | tf_op jit(solution)/shard_map/ppermute | solution.py:400
  90.8 8.3 %collective-permute-start.21 = (bf16[20,4096]{1,0:T(8,128)(2,1)S(1)}, bf16[20,4096]{1,0:T(8,128)(2,1)S(1)}, u32[]{:S(2)}, u32[]{:S(2)}) collective-permute-start(bf16[20,4096]{1,0:T(8,128)(2,1)S(1)} %get-tuple-element.122), channel_id=1, source_target_pairs={{0,2},{1,3},{2,0},{3,1},{4,6},{5,7},{6,4},{7,5},{8,10},{9,11},{10,... | collective-permute-start | bytes 491528 | tf_op jit(solution)/shard_map/ppermute | solution.py:400
  91.4 12.1 %collective-permute-start.22 = (bf16[20,4096]{1,0:T(8,128)(2,1)S(1)}, bf16[20,4096]{1,0:T(8,128)(2,1)S(1)}, u32[]{:S(2)}, u32[]{:S(2)}) collective-permute-start(bf16[20,4096]{1,0:T(8,128)(2,1)S(1)} %get-tuple-element.123), channel_id=1, source_target_pairs={{0,4},{1,5},{2,6},{3,7},{4,0},{5,1},{6,2},{7,3},{8,12},{9,13},{10,... | collective-permute-start | bytes 491528 | tf_op jit(solution)/shard_map/ppermute | solution.py:400
  92.9 13.6 %collective-permute-start.23 = (bf16[20,4096]{1,0:T(8,128)(2,1)S(1)}, bf16[20,4096]{1,0:T(8,128)(2,1)S(1)}, u32[]{:S(2)}, u32[]{:S(2)}) collective-permute-start(bf16[20,4096]{1,0:T(8,128)(2,1)S(1)} %get-tuple-element.124), channel_id=1, source_target_pairs={{0,6},{1,7},{2,4},{3,5},{4,2},{5,3},{6,0},{7,1},{8,14},{9,15},{10,... | collective-permute-start | bytes 491528 | tf_op jit(solution)/shard_map/ppermute | solution.py:400
  95.2 11.7 %collective-permute-start.25 = (bf16[20,4096]{1,0:T(8,128)(2,1)S(1)}, bf16[20,4096]{1,0:T(8,128)(2,1)S(1)}, u32[]{:S(2)}, u32[]{:S(2)}) collective-permute-start(bf16[20,4096]{1,0:T(8,128)(2,1)S(1)} %total.1), channel_id=1, source_target_pairs={{0,8},{1,9},{2,10},{3,11},{4,12},{5,13},{6,14},{7,15},{8,0},{9,1},... | collective-permute-start | bytes 491528 | tf_op jit(solution)/shard_map/ppermute | solution.py:478
  (2 other events, 4.1 us)

commit v12 on v11

--- a/solution.py
+++ b/solution.py
@@ -44,7 +44,7 @@
         bundle_kernel,
         in_specs=[NEAR, NEAR],
         out_specs=NEAR,
-        out_shape=jax.ShapeDtypeStruct((rows, width + HEAD_DIM), keys.dtype),
+        out_shape=pltpu.VMEM((rows, width + HEAD_DIM), keys.dtype),
         cost_estimate=pl.CostEstimate(
             flops=0, bytes_accessed=4 * rows * width, transcendentals=0
         ),
@@ -417,7 +417,6 @@
     key_block = bundle(keys, seg_own)
     key_one, value_one = moved(key_block, across), moved(values, across)
     key_three, value_three = moved(key_block, beside), moved(values, beside)
-    key_two, value_two = moved(key_one, passed), moved(value_one, passed)
     mine = bring(
         [
             queries, keys, values, seg_own, resid, norm_gain.reshape(1, -1), routes.T,
@@ -426,9 +425,10 @@
         scalars,
     )
     gate_held = fetch(w_gate, scalars)
-    key_four = choose(scalars, [key_two, key_three, key_one])
-    key_four, gate_held, mine = lax.optimization_barrier((key_four, gate_held, mine))
-    key_four = swapped(key_four, 1)
+    key_two = moved(key_one, passed)
+    value_one, gate_held, mine = lax.optimization_barrier((value_one, gate_held, mine))
+    value_two = moved(value_one, passed)
+    key_four = swapped(choose(scalars, [key_two, key_three, key_one]), 1)
     value_four = swapped(choose(scalars, [value_two, value_three, value_one]), 1)
 
     queries, keys, values, seg_own, resid, gain, routes_held, gates_held = mine

time: 108 us -> 107 us (level)
  starting transfers between devices: 40.1 us -> 42.4 us
  waiting for transfers between devices: 35.9 us -> 33.6 us
    ppermute x6, waiting for transfers between devices: 10.6 us -> 7.83 us  [moved(): lax.ppermute(block, 'expert', [pair for pair in pairs if pair[1] < count])]
    ppermute x18, starting transfers between devices: 16.4 us -> 18.8 us  [swapped(): return lax.ppermute(block, 'expert', [(i, i ^ mask) for i in range(count)])]
  transfers between devices with their start and end apart: 26 -> 26, of which waited for: 15 -> 14; matrix products, arithmetic and copies ran while one was open for 0% -> 0% of each run, Pallas kernels for 23% -> 23%
where the time goes in v12:
time: 107 us
  starting transfers between devices  42.4 us (40%)
  waiting for transfers between devices  33.6 us (31%)
  Pallas kernels  30.8 us (29%)
    ppermute x18, waiting for transfers between devices, swapped(): return lax.ppermute(block, 'expert', [(i, i ^ mask) for i in range(count)])  25.7 us
    ppermute x18, starting transfers between devices, swapped(): return lax.ppermute(block, 'expert', [(i, i ^ mask) for i in range(count)])  18.8 us
    ppermute x6, starting transfers between devices, moved(): lax.ppermute(block, 'expert', [pair for pair in pairs if pair[1] < count])  17.5 us
    pallas_call x3, Pallas kernels, fetch(): pl.pallas_call(functools.partial(fetch_kernel, parts), in_specs=[anywhere...  10.5 us
    pallas_call x2, Pallas kernels, experts(): pl.pallas_call(experts_kernel, in_specs=[NEAR] * 5, out_specs=[NEAR] * 2,...  10.5 us
    ppermute x6, waiting for transfers between devices, moved(): lax.ppermute(block, 'expert', [pair for pair in pairs if pair[1] < count])  7.83 us
    pallas_call x1, Pallas kernels, attention(): pl.pallas_call(attention_kernel, in_specs=[pl.BlockSpec(memory_space=pltp...  3.84 us
    ppermute x1, starting transfers between devices, shards(): other = lax.ppermute(back, 'expert', partner)  3.56 us
  transfers between devices with their start and end apart: 26, of which 14 were waited for; matrix products, arithmetic and copies ran while one was open for 0% of the time, Pallas kernels for 23%

profile of v12, /device:TPU:0, one launch (start us, length us, event | category | flops | bytes accessed | tf_op | source)
XLA Modules:
  0.0 107.1 jit_solution(14644015351205972276)
XLA Ops:
  1.1 4.3 %collective-permute-start.1 = (bf16[64,4224]{1,0:T(8,128)(2,1)S(1)}, bf16[64,4224]{1,0:T(8,128)(2,1)S(1)}, u32[]{:S(2)}, u32[]{:S(2)}) collective-permute-start(bf16[64,4224]{1,0:T(8,128)(2,1)S(1)} %bundle.1), channel_id=1, source_target_pairs={{0,3},{1,4},{2,1},{3,6},{4,7},{5,8},{6,5},{7,10},{8,11},{9,12},{10... | collective-permute-start | bytes 1622024 | tf_op jit(solution)/shard_map/ppermute | solution.py:393
  5.4 3.8 %collective-permute-start = (bf16[64,4096]{1,0:T(8,128)(2,1)}, bf16[64,4096]{1,0:T(8,128)(2,1)S(1)}, u32[]{:S(2)}, u32[]{:S(2)}) collective-permute-start(bf16[64,4096]{1,0:T(8,128)(2,1)} %refs_2_.1), channel_id=1, source_target_pairs={{0,3},{1,4},{2,1},{3,6},{4,7},{5,8},{6,5},{7,10},{8,11},{9,12},{10... | collective-permute-start | bytes 1572872 | tf_op jit(solution)/shard_map/ppermute | solution.py:393
  9.2 1.7 %collective-permute-start.4 = (bf16[64,4224]{1,0:T(8,128)(2,1)S(1)}, bf16[64,4224]{1,0:T(8,128)(2,1)S(1)}, u32[]{:S(2)}, u32[]{:S(2)}) collective-permute-start(bf16[64,4224]{1,0:T(8,128)(2,1)S(1)} %bundle.1), channel_id=1, source_target_pairs={{0,1},{1,2},{2,3},{4,5},{5,6},{6,7},{8,9},{9,10},{10,11},{12,13},{... | collective-permute-start | bytes 1622024 | tf_op jit(solution)/shard_map/ppermute | solution.py:393
  13.5 5.0 %collective-permute-start.5 = (bf16[64,4096]{1,0:T(8,128)(2,1)}, bf16[64,4096]{1,0:T(8,128)(2,1)S(1)}, u32[]{:S(2)}, u32[]{:S(2)}) collective-permute-start(bf16[64,4096]{1,0:T(8,128)(2,1)} %refs_2_.1), channel_id=1, source_target_pairs={{0,1},{1,2},{2,3},{4,5},{5,6},{6,7},{8,9},{9,10},{10,11},{12,13},{... | collective-permute-start | bytes 1572872 | tf_op jit(solution)/shard_map/ppermute | solution.py:393
  18.7 3.5 %fetch.3.w_gate = bf16[4096,1024]{1,0:T(8,128)(2,1)S(1)} custom-call(bf16[4096,1024]{1,0:T(8,128)(2,1)} %source.3, s32[7]{0:T(128)S(1)} %stack.31.after.refs_8_.flags.deltas), custom_call_target="tpu_custom_call" | custom-call | bytes 16777216 | tf_op jit(solution)/shard_map/fetch/pallas_call | solution.py:244
  25.8 2.6 %collective-permute-start.6 = (bf16[64,4224]{1,0:T(8,128)(2,1)S(1)}, bf16[64,4224]{1,0:T(8,128)(2,1)S(1)}, u32[]{:S(2)}, u32[]{:S(2)}) collective-permute-start(bf16[64,4224]{1,0:T(8,128)(2,1)S(1)} %choose.2), channel_id=1, source_target_pairs={{0,1},{1,0},{2,3},{3,2},{4,5},{5,4},{6,7},{7,6},{8,9},{9,8},{10,11... | collective-permute-start | bytes 1622024 | tf_op jit(solution)/shard_map/ppermute | solution.py:400
  28.4 6.5 %collective-permute-done.3.first.v2 = bf16[64,4096]{1,0:T(8,128)(2,1)S(1)} collective-permute-done((bf16[64,4096]{1,0:T(8,128)(2,1)S(1)}, bf16[64,4096]{1,0:T(8,128)(2,1)S(1)}, u32[]{:S(2)}, u32[]{:S(2)}) %collective-permute-start.3) | collective-permute-done | bytes 524320 | tf_op jit(solution)/shard_map/ppermute | solution.py:393
  35.6 1.9 %collective-permute-done.7.v4 = bf16[64,4096]{1,0:T(8,128)(2,1)S(1)} collective-permute-done((bf16[64,4096]{1,0:T(8,128)(2,1)S(1)}, bf16[64,4096]{1,0:T(8,128)(2,1)S(1)}, u32[]{:S(2)}, u32[]{:S(2)}) %collective-permute-start.7) | collective-permute-done | bytes 524320 | tf_op jit(solution)/shard_map/ppermute | solution.py:400
  37.5 3.8 %attention.1 = (f32[64,4096]{1,0:T(8,128)S(1)}, bf16[20,4096]{1,0:T(8,128)(2,1)S(1)}, bf16[20,4096]{1,0:T(8,128)(2,1)S(1)}, bf16[2,64,32]{2,1,0:T(8,128)(2,1)S(1)}) custom-call(s32[7]{0:T(128)S(1)} %stack.31.after.refs_8_.flags.deltas, bf16[64,4096]{1,0:T(8,128)(2,1)S(1)} %get-tuple-element.75.q, bf16[64,4096]{1,0:T(8,128)(2,1)S(1)} %get-tuple-element.76.k0, ...), custom_call_target="tpu_custom_call" | custom-call | flops 335544320 | bytes 8388608 | tf_op jit(solution)/shard_map/attention/pallas_call | solution.py:178
  41.5 2.6 %collective-permute-start.11 = (bf16[20,4096]{1,0:T(8,128)(2,1)S(1)}, bf16[20,4096]{1,0:T(8,128)(2,1)S(1)}, u32[]{:S(2)}, u32[]{:S(2)}) collective-permute-start(bf16[20,4096]{1,0:T(8,128)(2,1)S(1)} %get-tuple-element.87), channel_id=1, source_target_pairs={{0,8},{1,9},{2,10},{3,11},{4,12},{5,13},{6,14},{7,15},{8,0},{9,1},... | collective-permute-start | bytes 491528 | tf_op jit(solution)/shard_map/ppermute | solution.py:447
  44.1 4.6 %collective-permute-start.8 = (bf16[20,4096]{1,0:T(8,128)(2,1)S(1)}, bf16[20,4096]{1,0:T(8,128)(2,1)S(1)}, u32[]{:S(2)}, u32[]{:S(2)}) collective-permute-start(bf16[20,4096]{1,0:T(8,128)(2,1)S(1)} %get-tuple-element.89.refs_0_), channel_id=1, source_target_pairs={{0,6},{1,7},{2,4},{3,5},{4,2},{5,3},{6,0},{7,1},{8,14},{9,15},{10,... | collective-permute-start | bytes 491528 | tf_op jit(solution)/shard_map/ppermute | solution.py:400
  48.7 3.5 %fetch.4.w_up = bf16[4096,1024]{1,0:T(8,128)(2,1)S(1)} custom-call(bf16[4096,1024]{1,0:T(8,128)(2,1)} %source.4, bf16[2,64,32]{2,1,0:T(8,128)(2,1)S(1)} %get-tuple-element.85.after.weight), custom_call_target="tpu_custom_call" | custom-call | bytes 16777216 | tf_op jit(solution)/shard_map/fetch/pallas_call | solution.py:244
  52.2 3.5 %fetch.5.w_down = bf16[1024,4096]{1,0:T(8,128)(2,1)S(1)} custom-call(bf16[1024,4096]{1,0:T(8,128)(2,1)} %source.5, bf16[2,64,32]{2,1,0:T(8,128)(2,1)S(1)} %get-tuple-element.85.after.weight), custom_call_target="tpu_custom_call" | custom-call | bytes 16777216 | tf_op jit(solution)/shard_map/fetch/pallas_call | solution.py:244
  56.0 2.0 %collective-permute-done.9.refs_2_ = bf16[20,4096]{1,0:T(8,128)(2,1)S(1)} collective-permute-done((bf16[20,4096]{1,0:T(8,128)(2,1)S(1)}, bf16[20,4096]{1,0:T(8,128)(2,1)S(1)}, u32[]{:S(2)}, u32[]{:S(2)}) %collective-permute-start.9) | collective-permute-done | bytes 163872 | tf_op jit(solution)/shard_map/ppermute | solution.py:400
  58.2 2.6 %collective-permute-start.12 = (bf16[20,4096]{1,0:T(8,128)(2,1)S(1)}, bf16[20,4096]{1,0:T(8,128)(2,1)S(1)}, u32[]{:S(2)}, u32[]{:S(2)}) collective-permute-start(bf16[20,4096]{1,0:T(8,128)(2,1)S(1)} %collective-permute-done.11.refs_0_), channel_id=1, source_target_pairs={{0,6},{1,7},{2,4},{3,5},{4,2},{5,3},{6,0},{7,1},{8,14},{9,15},{10,... | collective-permute-start | bytes 491528 | tf_op jit(solution)/shard_map/ppermute | solution.py:400
  61.7 5.2 %experts.2 = (bf16[80,4096]{1,0:T(8,128)(2,1)S(1)}, bf16[80,4096]{1,0:T(8,128)(2,1)S(1)}) custom-call(bf16[80,4096]{1,0:T(8,128)(2,1)S(1)} %pile.2.local, bf16[80,4096]{1,0:T(8,128)(2,1)S(1)} %collective-permute-done.15.remote, bf16[4096,1024]{1,0:T(8,128)(2,1)S(1)} %fetch.3.w_gate, bf16[4096,1024]{1,0:T(8,128)(2,1)S(1)} %fetch.4.w_up, ...), custom_call_target="tpu_custom_call" | custom-call | flops 4026531840 | bytes 2621440 | tf_op jit(solution)/shard_map/experts/pallas_call | solution.py:283
  67.0 3.9 %collective-permute-done.13.refs_2_ = bf16[20,4096]{1,0:T(8,128)(2,1)S(1)} collective-permute-done((bf16[20,4096]{1,0:T(8,128)(2,1)S(1)}, bf16[20,4096]{1,0:T(8,128)(2,1)S(1)}, u32[]{:S(2)}, u32[]{:S(2)}) %collective-permute-start.13) | collective-permute-done | bytes 163872 | tf_op jit(solution)/shard_map/ppermute | solution.py:400
  73.1 5.2 %experts.3 = (bf16[80,4096]{1,0:T(8,128)(2,1)S(1)}, bf16[80,4096]{1,0:T(8,128)(2,1)S(1)}) custom-call(bf16[80,4096]{1,0:T(8,128)(2,1)S(1)} %pile.3.local, bf16[80,4096]{1,0:T(8,128)(2,1)S(1)} %collective-permute-done.16.remote, bf16[4096,1024]{1,0:T(8,128)(2,1)S(1)} %fetch.3.w_gate, bf16[4096,1024]{1,0:T(8,128)(2,1)S(1)} %fetch.4.w_up, ...), custom_call_target="tpu_custom_call" | custom-call | flops 4026531840 | bytes 2621440 | tf_op jit(solution)/shard_map/experts/pallas_call | solution.py:283
  78.8 1.8 %collective-permute-done.17.second = bf16[80,4096]{1,0:T(8,128)(2,1)S(1)} collective-permute-done((bf16[80,4096]{1,0:T(8,128)(2,1)S(1)}, bf16[80,4096]{1,0:T(8,128)(2,1)S(1)}, u32[]{:S(2)}, u32[]{:S(2)}) %collective-permute-start.17) | collective-permute-done | bytes 655392 | tf_op jit(solution)/shard_map/ppermute | solution.py:400
  84.3 3.5 %collective-permute-done.19.refs_1_ = bf16[20,4096]{1,0:T(8,128)(2,1)S(1)} collective-permute-done((bf16[20,4096]{1,0:T(8,128)(2,1)S(1)}, bf16[20,4096]{1,0:T(8,128)(2,1)S(1)}, u32[]{:S(2)}, u32[]{:S(2)}) %collective-permute-start.19) | collective-permute-done | bytes 163872 | tf_op jit(solution)/shard_map/ppermute | solution.py:400
  87.7 2.3 %collective-permute-done.20.refs_2_ = bf16[20,4096]{1,0:T(8,128)(2,1)S(1)} collective-permute-done((bf16[20,4096]{1,0:T(8,128)(2,1)S(1)}, bf16[20,4096]{1,0:T(8,128)(2,1)S(1)}, u32[]{:S(2)}, u32[]{:S(2)}) %collective-permute-start.20) | collective-permute-done | bytes 163872 | tf_op jit(solution)/shard_map/ppermute | solution.py:400
  94.4 3.6 %collective-permute-start.25 = (bf16[20,4096]{1,0:T(8,128)(2,1)S(1)}, bf16[20,4096]{1,0:T(8,128)(2,1)S(1)}, u32[]{:S(2)}, u32[]{:S(2)}) collective-permute-start(bf16[20,4096]{1,0:T(8,128)(2,1)S(1)} %total.1), channel_id=1, source_target_pairs={{0,8},{1,9},{2,10},{3,11},{4,12},{5,13},{6,14},{7,15},{8,0},{9,1},... | collective-permute-start | bytes 491528 | tf_op jit(solution)/shard_map/ppermute | solution.py:478
  98.2 4.5 %collective-permute-done.22.refs_2_ = bf16[20,4096]{1,0:T(8,128)(2,1)S(1)} collective-permute-done((bf16[20,4096]{1,0:T(8,128)(2,1)S(1)}, bf16[20,4096]{1,0:T(8,128)(2,1)S(1)}, u32[]{:S(2)}, u32[]{:S(2)}) %collective-permute-start.22) | collective-permute-done | bytes 163872 | tf_op jit(solution)/shard_map/ppermute | solution.py:400
  102.7 3.1 %collective-permute-done.23.refs_3_ = bf16[20,4096]{1,0:T(8,128)(2,1)S(1)} collective-permute-done((bf16[20,4096]{1,0:T(8,128)(2,1)S(1)}, bf16[20,4096]{1,0:T(8,128)(2,1)S(1)}, u32[]{:S(2)}, u32[]{:S(2)}) %collective-permute-start.23) | collective-permute-done | bytes 163872 | tf_op jit(solution)/shard_map/ppermute | solution.py:400
  (46 shorter events, 21.8 us)
Async XLA Ops:
  1.1 11.2 %collective-permute-start.1 = (bf16[64,4224]{1,0:T(8,128)(2,1)S(1)}, bf16[64,4224]{1,0:T(8,128)(2,1)S(1)}, u32[]{:S(2)}, u32[]{:S(2)}) collective-permute-start(bf16[64,4224]{1,0:T(8,128)(2,1)S(1)} %bundle.1), channel_id=1, source_target_pairs={{0,3},{1,4},{2,1},{3,6},{4,7},{5,8},{6,5},{7,10},{8,11},{9,12},{10... | collective-permute-start | bytes 1622024 | tf_op jit(solution)/shard_map/ppermute | solution.py:393
  5.4 18.4 %collective-permute-start = (bf16[64,4096]{1,0:T(8,128)(2,1)}, bf16[64,4096]{1,0:T(8,128)(2,1)S(1)}, u32[]{:S(2)}, u32[]{:S(2)}) collective-permute-start(bf16[64,4096]{1,0:T(8,128)(2,1)} %refs_2_.1), channel_id=1, source_target_pairs={{0,3},{1,4},{2,1},{3,6},{4,7},{5,8},{6,5},{7,10},{8,11},{9,12},{10... | collective-permute-start | bytes 1572872 | tf_op jit(solution)/shard_map/ppermute | solution.py:393
  9.2 16.0 %collective-permute-start.4 = (bf16[64,4224]{1,0:T(8,128)(2,1)S(1)}, bf16[64,4224]{1,0:T(8,128)(2,1)S(1)}, u32[]{:S(2)}, u32[]{:S(2)}) collective-permute-start(bf16[64,4224]{1,0:T(8,128)(2,1)S(1)} %bundle.1), channel_id=1, source_target_pairs={{0,1},{1,2},{2,3},{4,5},{5,6},{6,7},{8,9},{9,10},{10,11},{12,13},{... | collective-permute-start | bytes 1622024 | tf_op jit(solution)/shard_map/ppermute | solution.py:393
  12.3 12.9 %collective-permute-start.2 = (bf16[64,4224]{1,0:T(8,128)(2,1)S(1)}, bf16[64,4224]{1,0:T(8,128)(2,1)S(1)}, u32[]{:S(2)}, u32[]{:S(2)}) collective-permute-start(bf16[64,4224]{1,0:T(8,128)(2,1)S(1)} %collective-permute-done.1.third.k1), channel_id=1, source_target_pairs={{1,5},{2,0},{5,9},{6,4},{9,13},{10,8},{14,12},{17,21},{18,16},{21,... | collective-permute-start | bytes 1622024 | tf_op jit(solution)/shard_map/ppermute | solution.py:393
  13.5 14.9 %collective-permute-start.5 = (bf16[64,4096]{1,0:T(8,128)(2,1)}, bf16[64,4096]{1,0:T(8,128)(2,1)S(1)}, u32[]{:S(2)}, u32[]{:S(2)}) collective-permute-start(bf16[64,4096]{1,0:T(8,128)(2,1)} %refs_2_.1), channel_id=1, source_target_pairs={{0,1},{1,2},{2,3},{4,5},{5,6},{6,7},{8,9},{9,10},{10,11},{12,13},{... | collective-permute-start | bytes 1572872 | tf_op jit(solution)/shard_map/ppermute | solution.py:393
  23.9 11.1 %collective-permute-start.3 = (bf16[64,4096]{1,0:T(8,128)(2,1)S(1)}, bf16[64,4096]{1,0:T(8,128)(2,1)S(1)}, u32[]{:S(2)}, u32[]{:S(2)}) collective-permute-start(bf16[64,4096]{1,0:T(8,128)(2,1)S(1)} %collective-permute-done.third.v1), channel_id=1, source_target_pairs={{1,5},{2,0},{5,9},{6,4},{9,13},{10,8},{14,12},{17,21},{18,16},{21,... | collective-permute-start | bytes 1572872 | tf_op jit(solution)/shard_map/ppermute | solution.py:393
  25.8 11.7 %collective-permute-start.6 = (bf16[64,4224]{1,0:T(8,128)(2,1)S(1)}, bf16[64,4224]{1,0:T(8,128)(2,1)S(1)}, u32[]{:S(2)}, u32[]{:S(2)}) collective-permute-start(bf16[64,4224]{1,0:T(8,128)(2,1)S(1)} %choose.2), channel_id=1, source_target_pairs={{0,1},{1,0},{2,3},{3,2},{4,5},{5,4},{6,7},{7,6},{8,9},{9,8},{10,11... | collective-permute-start | bytes 1622024 | tf_op jit(solution)/shard_map/ppermute | solution.py:400
  41.4 14.3 %collective-permute-start.10 = (bf16[20,4096]{1,0:T(8,128)(2,1)S(1)}, bf16[20,4096]{1,0:T(8,128)(2,1)S(1)}, u32[]{:S(2)}, u32[]{:S(2)}) collective-permute-start(bf16[20,4096]{1,0:T(8,128)(2,1)S(1)} %get-tuple-element.89.refs_0_), channel_id=1, source_target_pairs={{0,2},{1,3},{2,0},{3,1},{4,6},{5,7},{6,4},{7,5},{8,10},{9,11},{10,... | collective-permute-start | bytes 491528 | tf_op jit(solution)/shard_map/ppermute | solution.py:400
  41.5 14.3 %collective-permute-start.11 = (bf16[20,4096]{1,0:T(8,128)(2,1)S(1)}, bf16[20,4096]{1,0:T(8,128)(2,1)S(1)}, u32[]{:S(2)}, u32[]{:S(2)}) collective-permute-start(bf16[20,4096]{1,0:T(8,128)(2,1)S(1)} %get-tuple-element.87), channel_id=1, source_target_pairs={{0,8},{1,9},{2,10},{3,11},{4,12},{5,13},{6,14},{7,15},{8,0},{9,1},... | collective-permute-start | bytes 491528 | tf_op jit(solution)/shard_map/ppermute | solution.py:447
  44.1 11.9 %collective-permute-start.8 = (bf16[20,4096]{1,0:T(8,128)(2,1)S(1)}, bf16[20,4096]{1,0:T(8,128)(2,1)S(1)}, u32[]{:S(2)}, u32[]{:S(2)}) collective-permute-start(bf16[20,4096]{1,0:T(8,128)(2,1)S(1)} %get-tuple-element.89.refs_0_), channel_id=1, source_target_pairs={{0,6},{1,7},{2,4},{3,5},{4,2},{5,3},{6,0},{7,1},{8,14},{9,15},{10,... | collective-permute-start | bytes 491528 | tf_op jit(solution)/shard_map/ppermute | solution.py:400
  48.7 9.3 %collective-permute-start.9 = (bf16[20,4096]{1,0:T(8,128)(2,1)S(1)}, bf16[20,4096]{1,0:T(8,128)(2,1)S(1)}, u32[]{:S(2)}, u32[]{:S(2)}) collective-permute-start(bf16[20,4096]{1,0:T(8,128)(2,1)S(1)} %get-tuple-element.89.refs_0_), channel_id=1, source_target_pairs={{0,4},{1,5},{2,6},{3,7},{4,0},{5,1},{6,2},{7,3},{8,12},{9,13},{10,... | collective-permute-start | bytes 491528 | tf_op jit(solution)/shard_map/ppermute | solution.py:400
  58.1 3.6 %collective-permute-start.15 = (bf16[80,4096]{1,0:T(8,128)(2,1)S(1)}, bf16[80,4096]{1,0:T(8,128)(2,1)S(1)}, u32[]{:S(2)}, u32[]{:S(2)}) collective-permute-start(bf16[80,4096]{1,0:T(8,128)(2,1)S(1)} %pile.2.local), channel_id=1, source_target_pairs={{0,1},{1,0},{2,3},{3,2},{4,5},{5,4},{6,7},{7,6},{8,9},{9,8},{10,11... | collective-permute-start | bytes 1966088 | tf_op jit(solution)/shard_map/ppermute | solution.py:400
  58.2 8.8 %collective-permute-start.12 = (bf16[20,4096]{1,0:T(8,128)(2,1)S(1)}, bf16[20,4096]{1,0:T(8,128)(2,1)S(1)}, u32[]{:S(2)}, u32[]{:S(2)}) collective-permute-start(bf16[20,4096]{1,0:T(8,128)(2,1)S(1)} %collective-permute-done.11.refs_0_), channel_id=1, source_target_pairs={{0,6},{1,7},{2,4},{3,5},{4,2},{5,3},{6,0},{7,1},{8,14},{9,15},{10,... | collective-permute-start | bytes 491528 | tf_op jit(solution)/shard_map/ppermute | solution.py:400
  60.8 10.0 %collective-permute-start.13 = (bf16[20,4096]{1,0:T(8,128)(2,1)S(1)}, bf16[20,4096]{1,0:T(8,128)(2,1)S(1)}, u32[]{:S(2)}, u32[]{:S(2)}) collective-permute-start(bf16[20,4096]{1,0:T(8,128)(2,1)S(1)} %collective-permute-done.11.refs_0_), channel_id=1, source_target_pairs={{0,4},{1,5},{2,6},{3,7},{4,0},{5,1},{6,2},{7,3},{8,12},{9,13},{10,... | collective-permute-start | bytes 491528 | tf_op jit(solution)/shard_map/ppermute | solution.py:400
  61.4 9.5 %collective-permute-start.14 = (bf16[20,4096]{1,0:T(8,128)(2,1)S(1)}, bf16[20,4096]{1,0:T(8,128)(2,1)S(1)}, u32[]{:S(2)}, u32[]{:S(2)}) collective-permute-start(bf16[20,4096]{1,0:T(8,128)(2,1)S(1)} %collective-permute-done.11.refs_0_), channel_id=1, source_target_pairs={{0,2},{1,3},{2,0},{3,1},{4,6},{5,7},{6,4},{7,5},{8,10},{9,11},{10,... | collective-permute-start | bytes 491528 | tf_op jit(solution)/shard_map/ppermute | solution.py:400
  71.0 2.2 %collective-permute-start.16 = (bf16[80,4096]{1,0:T(8,128)(2,1)S(1)}, bf16[80,4096]{1,0:T(8,128)(2,1)S(1)}, u32[]{:S(2)}, u32[]{:S(2)}) collective-permute-start(bf16[80,4096]{1,0:T(8,128)(2,1)S(1)} %pile.3.local), channel_id=1, source_target_pairs={{0,1},{1,0},{2,3},{3,2},{4,5},{5,4},{6,7},{7,6},{8,9},{9,8},{10,11... | collective-permute-start | bytes 1966088 | tf_op jit(solution)/shard_map/ppermute | solution.py:400
  71.0 7.5 %collective-permute-start.18 = (bf16[80,4096]{1,0:T(8,128)(2,1)S(1)}, bf16[80,4096]{1,0:T(8,128)(2,1)S(1)}, u32[]{:S(2)}, u32[]{:S(2)}) collective-permute-start(bf16[80,4096]{1,0:T(8,128)(2,1)S(1)} %get-tuple-element.109), channel_id=1, source_target_pairs={{0,1},{1,0},{2,3},{3,2},{4,5},{5,4},{6,7},{7,6},{8,9},{9,8},{10,11... | collective-permute-start | bytes 1966088 | tf_op jit(solution)/shard_map/ppermute | solution.py:400
  80.7 7.0 %collective-permute-start.19 = (bf16[20,4096]{1,0:T(8,128)(2,1)S(1)}, bf16[20,4096]{1,0:T(8,128)(2,1)S(1)}, u32[]{:S(2)}, u32[]{:S(2)}) collective-permute-start(bf16[20,4096]{1,0:T(8,128)(2,1)S(1)} %get-tuple-element.115), channel_id=1, source_target_pairs={{0,2},{1,3},{2,0},{3,1},{4,6},{5,7},{6,4},{7,5},{8,10},{9,11},{10,... | collective-permute-start | bytes 491528 | tf_op jit(solution)/shard_map/ppermute | solution.py:400
  82.2 7.8 %collective-permute-start.20 = (bf16[20,4096]{1,0:T(8,128)(2,1)S(1)}, bf16[20,4096]{1,0:T(8,128)(2,1)S(1)}, u32[]{:S(2)}, u32[]{:S(2)}) collective-permute-start(bf16[20,4096]{1,0:T(8,128)(2,1)S(1)} %get-tuple-element.116), channel_id=1, source_target_pairs={{0,4},{1,5},{2,6},{3,7},{4,0},{5,1},{6,2},{7,3},{8,12},{9,13},{10,... | collective-permute-start | bytes 491528 | tf_op jit(solution)/shard_map/ppermute | solution.py:400
  83.7 10.6 %collective-permute-start.24 = (bf16[20,4096]{1,0:T(8,128)(2,1)S(1)}, bf16[20,4096]{1,0:T(8,128)(2,1)S(1)}, u32[]{:S(2)}, u32[]{:S(2)}) collective-permute-start(bf16[20,4096]{1,0:T(8,128)(2,1)S(1)} %get-tuple-element.128), channel_id=1, source_target_pairs={{0,6},{1,7},{2,4},{3,5},{4,2},{5,3},{6,0},{7,1},{8,14},{9,15},{10,... | collective-permute-start | bytes 491528 | tf_op jit(solution)/shard_map/ppermute | solution.py:400
  90.0 8.2 %collective-permute-start.21 = (bf16[20,4096]{1,0:T(8,128)(2,1)S(1)}, bf16[20,4096]{1,0:T(8,128)(2,1)S(1)}, u32[]{:S(2)}, u32[]{:S(2)}) collective-permute-start(bf16[20,4096]{1,0:T(8,128)(2,1)S(1)} %get-tuple-element.122), channel_id=1, source_target_pairs={{0,2},{1,3},{2,0},{3,1},{4,6},{5,7},{6,4},{7,5},{8,10},{9,11},{10,... | collective-permute-start | bytes 491528 | tf_op jit(solution)/shard_map/ppermute | solution.py:400
  90.6 12.1 %collective-permute-start.22 = (bf16[20,4096]{1,0:T(8,128)(2,1)S(1)}, bf16[20,4096]{1,0:T(8,128)(2,1)S(1)}, u32[]{:S(2)}, u32[]{:S(2)}) collective-permute-start(bf16[20,4096]{1,0:T(8,128)(2,1)S(1)} %get-tuple-element.123), channel_id=1, source_target_pairs={{0,4},{1,5},{2,6},{3,7},{4,0},{5,1},{6,2},{7,3},{8,12},{9,13},{10,... | collective-permute-start | bytes 491528 | tf_op jit(solution)/shard_map/ppermute | solution.py:400
  92.1 13.7 %collective-permute-start.23 = (bf16[20,4096]{1,0:T(8,128)(2,1)S(1)}, bf16[20,4096]{1,0:T(8,128)(2,1)S(1)}, u32[]{:S(2)}, u32[]{:S(2)}) collective-permute-start(bf16[20,4096]{1,0:T(8,128)(2,1)S(1)} %get-tuple-element.124), channel_id=1, source_target_pairs={{0,6},{1,7},{2,4},{3,5},{4,2},{5,3},{6,0},{7,1},{8,14},{9,15},{10,... | collective-permute-start | bytes 491528 | tf_op jit(solution)/shard_map/ppermute | solution.py:400
  94.4 11.7 %collective-permute-start.25 = (bf16[20,4096]{1,0:T(8,128)(2,1)S(1)}, bf16[20,4096]{1,0:T(8,128)(2,1)S(1)}, u32[]{:S(2)}, u32[]{:S(2)}) collective-permute-start(bf16[20,4096]{1,0:T(8,128)(2,1)S(1)} %total.1), channel_id=1, source_target_pairs={{0,8},{1,9},{2,10},{3,11},{4,12},{5,13},{6,14},{7,15},{8,0},{9,1},... | collective-permute-start | bytes 491528 | tf_op jit(solution)/shard_map/ppermute | solution.py:478
  (2 other events, 4.1 us)

commit v13 on v12

--- a/solution.py
+++ b/solution.py
@@ -467,14 +467,12 @@
     held = [gate_held, up_held, down_held]
     early_parts = experts(*both_cores(early_blocks), *held)
     late_blocks = spread(got)
-    late_blocks, early_parts = lax.optimization_barrier((late_blocks, early_parts))
-    late_blocks = summed(experts(*both_cores(late_blocks), *held))
-    early_blocks = summed(early_parts)
-    late_blocks, early_blocks = lax.optimization_barrier((late_blocks, early_blocks))
-    late_blocks = scattered(late_blocks)
-    late_blocks[:-1], early_blocks = lax.optimization_barrier((late_blocks[:-1], early_blocks))
-    early_blocks = scattered(early_blocks)
-    back = total_of(late_blocks)
+    late_blocks, _ = lax.optimization_barrier((late_blocks, early_parts))
+    late_local = pile(late_blocks)
+    early_blocks = scattered(summed(early_parts))
+    late_parts = experts(late_local, swapped(late_local, 1), *held)
+    late_parts, early_blocks = lax.optimization_barrier((late_parts, early_blocks))
+    back = total_of(scattered(summed(late_parts)))
     other = lax.ppermute(back, "expert", partner)
     base = combine(0, mixed, weight, early_blocks, pltpu.VMEM(mixed.shape, jnp.float32))
     return combine(

time: 107 us -> 112 us (1.047)
  waiting for transfers between devices: 33.6 us -> 38.6 us
    ppermute x1, waiting for transfers between devices: 0.01 us -> 7.97 us  [shards(): other = lax.ppermute(back, 'expert', partner)]
    ppermute x18, waiting for transfers between devices: 25.7 us -> 22.8 us  [swapped(): return lax.ppermute(block, 'expert', [(i, i ^ mask) for i in range(count)])]
  transfers between devices with their start and end apart: 26 -> 26, of which waited for: 14 -> 13; matrix products, arithmetic and copies ran while one was open for 0% -> 0% of each run, Pallas kernels for 23% -> 22%
where the time goes in v13:
time: 112 us
  starting transfers between devices  42.2 us (38%)
  waiting for transfers between devices  38.6 us (34%)
  Pallas kernels  30.8 us (28%)
    ppermute x18, waiting for transfers between devices, swapped(): return lax.ppermute(block, 'expert', [(i, i ^ mask) for i in range(count)])  22.8 us
    ppermute x18, starting transfers between devices, swapped(): return lax.ppermute(block, 'expert', [(i, i ^ mask) for i in range(count)])  18.2 us
    ppermute x6, starting transfers between devices, moved(): lax.ppermute(block, 'expert', [pair for pair in pairs if pair[1] < count])  17.5 us
    pallas_call x3, Pallas kernels, fetch(): pl.pallas_call(functools.partial(fetch_kernel, parts), in_specs=[anywhere...  10.5 us
    pallas_call x2, Pallas kernels, experts(): pl.pallas_call(experts_kernel, in_specs=[NEAR] * 5, out_specs=[NEAR] * 2,...  10.5 us
    ppermute x1, waiting for transfers between devices, shards(): other = lax.ppermute(back, 'expert', partner)  7.97 us
    ppermute x6, waiting for transfers between devices, moved(): lax.ppermute(block, 'expert', [pair for pair in pairs if pair[1] < count])  7.83 us
    ppermute x1, starting transfers between devices, shards(): other = lax.ppermute(back, 'expert', partner)  3.84 us
  transfers between devices with their start and end apart: 26, of which 13 were waited for; matrix products, arithmetic and copies ran while one was open for 0% of the time, Pallas kernels for 22%

profile of v13, /device:TPU:0, one launch (start us, length us, event | category | flops | bytes accessed | tf_op | source)
XLA Modules:
  0.0 112.0 jit_solution(8354701964245577997)
XLA Ops:
  1.1 4.3 %collective-permute-start.1 = (bf16[64,4224]{1,0:T(8,128)(2,1)S(1)}, bf16[64,4224]{1,0:T(8,128)(2,1)S(1)}, u32[]{:S(2)}, u32[]{:S(2)}) collective-permute-start(bf16[64,4224]{1,0:T(8,128)(2,1)S(1)} %bundle.1), channel_id=1, source_target_pairs={{0,3},{1,4},{2,1},{3,6},{4,7},{5,8},{6,5},{7,10},{8,11},{9,12},{10... | collective-permute-start | bytes 1622024 | tf_op jit(solution)/shard_map/ppermute | solution.py:393
  5.4 3.8 %collective-permute-start = (bf16[64,4096]{1,0:T(8,128)(2,1)}, bf16[64,4096]{1,0:T(8,128)(2,1)S(1)}, u32[]{:S(2)}, u32[]{:S(2)}) collective-permute-start(bf16[64,4096]{1,0:T(8,128)(2,1)} %refs_2_.1), channel_id=1, source_target_pairs={{0,3},{1,4},{2,1},{3,6},{4,7},{5,8},{6,5},{7,10},{8,11},{9,12},{10... | collective-permute-start | bytes 1572872 | tf_op jit(solution)/shard_map/ppermute | solution.py:393
  13.5 5.0 %collective-permute-start.5 = (bf16[64,4096]{1,0:T(8,128)(2,1)}, bf16[64,4096]{1,0:T(8,128)(2,1)S(1)}, u32[]{:S(2)}, u32[]{:S(2)}) collective-permute-start(bf16[64,4096]{1,0:T(8,128)(2,1)} %refs_2_.1), channel_id=1, source_target_pairs={{0,1},{1,2},{2,3},{4,5},{5,6},{6,7},{8,9},{9,10},{10,11},{12,13},{... | collective-permute-start | bytes 1572872 | tf_op jit(solution)/shard_map/ppermute | solution.py:393
  18.7 3.5 %fetch.3.w_gate = bf16[4096,1024]{1,0:T(8,128)(2,1)S(1)} custom-call(bf16[4096,1024]{1,0:T(8,128)(2,1)} %source.3, s32[7]{0:T(128)S(1)} %stack.31.after.refs_8_.flags.deltas), custom_call_target="tpu_custom_call" | custom-call | bytes 16777216 | tf_op jit(solution)/shard_map/fetch/pallas_call | solution.py:244
  25.8 2.6 %collective-permute-start.6 = (bf16[64,4224]{1,0:T(8,128)(2,1)S(1)}, bf16[64,4224]{1,0:T(8,128)(2,1)S(1)}, u32[]{:S(2)}, u32[]{:S(2)}) collective-permute-start(bf16[64,4224]{1,0:T(8,128)(2,1)S(1)} %choose.2), channel_id=1, source_target_pairs={{0,1},{1,0},{2,3},{3,2},{4,5},{5,4},{6,7},{7,6},{8,9},{9,8},{10,11... | collective-permute-start | bytes 1622024 | tf_op jit(solution)/shard_map/ppermute | solution.py:400
  28.4 6.5 %collective-permute-done.3.first.v2 = bf16[64,4096]{1,0:T(8,128)(2,1)S(1)} collective-permute-done((bf16[64,4096]{1,0:T(8,128)(2,1)S(1)}, bf16[64,4096]{1,0:T(8,128)(2,1)S(1)}, u32[]{:S(2)}, u32[]{:S(2)}) %collective-permute-start.3) | collective-permute-done | bytes 524320 | tf_op jit(solution)/shard_map/ppermute | solution.py:393
  35.6 1.9 %collective-permute-done.7.v4 = bf16[64,4096]{1,0:T(8,128)(2,1)S(1)} collective-permute-done((bf16[64,4096]{1,0:T(8,128)(2,1)S(1)}, bf16[64,4096]{1,0:T(8,128)(2,1)S(1)}, u32[]{:S(2)}, u32[]{:S(2)}) %collective-permute-start.7) | collective-permute-done | bytes 524320 | tf_op jit(solution)/shard_map/ppermute | solution.py:400
  37.5 3.8 %attention.1 = (f32[64,4096]{1,0:T(8,128)S(1)}, bf16[20,4096]{1,0:T(8,128)(2,1)S(1)}, bf16[20,4096]{1,0:T(8,128)(2,1)S(1)}, bf16[2,64,32]{2,1,0:T(8,128)(2,1)S(1)}) custom-call(s32[7]{0:T(128)S(1)} %stack.31.after.refs_8_.flags.deltas, bf16[64,4096]{1,0:T(8,128)(2,1)S(1)} %get-tuple-element.64.q, bf16[64,4096]{1,0:T(8,128)(2,1)S(1)} %get-tuple-element.65.k0, ...), custom_call_target="tpu_custom_call" | custom-call | flops 335544320 | bytes 8388608 | tf_op jit(solution)/shard_map/attention/pallas_call | solution.py:178
  41.5 2.6 %collective-permute-start.11 = (bf16[20,4096]{1,0:T(8,128)(2,1)S(1)}, bf16[20,4096]{1,0:T(8,128)(2,1)S(1)}, u32[]{:S(2)}, u32[]{:S(2)}) collective-permute-start(bf16[20,4096]{1,0:T(8,128)(2,1)S(1)} %get-tuple-element.76), channel_id=1, source_target_pairs={{0,8},{1,9},{2,10},{3,11},{4,12},{5,13},{6,14},{7,15},{8,0},{9,1},... | collective-permute-start | bytes 491528 | tf_op jit(solution)/shard_map/ppermute | solution.py:447
  44.1 4.6 %collective-permute-start.8 = (bf16[20,4096]{1,0:T(8,128)(2,1)S(1)}, bf16[20,4096]{1,0:T(8,128)(2,1)S(1)}, u32[]{:S(2)}, u32[]{:S(2)}) collective-permute-start(bf16[20,4096]{1,0:T(8,128)(2,1)S(1)} %get-tuple-element.78.refs_0_), channel_id=1, source_target_pairs={{0,6},{1,7},{2,4},{3,5},{4,2},{5,3},{6,0},{7,1},{8,14},{9,15},{10,... | collective-permute-start | bytes 491528 | tf_op jit(solution)/shard_map/ppermute | solution.py:400
  48.7 3.5 %fetch.4.w_up = bf16[4096,1024]{1,0:T(8,128)(2,1)S(1)} custom-call(bf16[4096,1024]{1,0:T(8,128)(2,1)} %source.4, bf16[2,64,32]{2,1,0:T(8,128)(2,1)S(1)} %get-tuple-element.74.after.weight), custom_call_target="tpu_custom_call" | custom-call | bytes 16777216 | tf_op jit(solution)/shard_map/fetch/pallas_call | solution.py:244
  52.2 3.5 %fetch.5.w_down = bf16[1024,4096]{1,0:T(8,128)(2,1)S(1)} custom-call(bf16[1024,4096]{1,0:T(8,128)(2,1)} %source.5, bf16[2,64,32]{2,1,0:T(8,128)(2,1)S(1)} %get-tuple-element.74.after.weight), custom_call_target="tpu_custom_call" | custom-call | bytes 16777216 | tf_op jit(solution)/shard_map/fetch/pallas_call | solution.py:244
  56.0 2.0 %collective-permute-done.9.refs_2_ = bf16[20,4096]{1,0:T(8,128)(2,1)S(1)} collective-permute-done((bf16[20,4096]{1,0:T(8,128)(2,1)S(1)}, bf16[20,4096]{1,0:T(8,128)(2,1)S(1)}, u32[]{:S(2)}, u32[]{:S(2)}) %collective-permute-start.9) | collective-permute-done | bytes 163872 | tf_op jit(solution)/shard_map/ppermute | solution.py:400
  58.2 2.6 %collective-permute-start.12 = (bf16[20,4096]{1,0:T(8,128)(2,1)S(1)}, bf16[20,4096]{1,0:T(8,128)(2,1)S(1)}, u32[]{:S(2)}, u32[]{:S(2)}) collective-permute-start(bf16[20,4096]{1,0:T(8,128)(2,1)S(1)} %collective-permute-done.11.refs_0_), channel_id=1, source_target_pairs={{0,6},{1,7},{2,4},{3,5},{4,2},{5,3},{6,0},{7,1},{8,14},{9,15},{10,... | collective-permute-start | bytes 491528 | tf_op jit(solution)/shard_map/ppermute | solution.py:400
  61.7 5.2 %experts.2 = (bf16[80,4096]{1,0:T(8,128)(2,1)S(1)}, bf16[80,4096]{1,0:T(8,128)(2,1)S(1)}) custom-call(bf16[80,4096]{1,0:T(8,128)(2,1)S(1)} %pile.2.local, bf16[80,4096]{1,0:T(8,128)(2,1)S(1)} %collective-permute-done.15.remote, bf16[4096,1024]{1,0:T(8,128)(2,1)S(1)} %fetch.3.w_gate, bf16[4096,1024]{1,0:T(8,128)(2,1)S(1)} %fetch.4.w_up, ...), custom_call_target="tpu_custom_call" | custom-call | flops 4026531840 | bytes 2621440 | tf_op jit(solution)/shard_map/experts/pallas_call | solution.py:283
  67.1 3.8 %collective-permute-done.13.refs_2_ = bf16[20,4096]{1,0:T(8,128)(2,1)S(1)} collective-permute-done((bf16[20,4096]{1,0:T(8,128)(2,1)S(1)}, bf16[20,4096]{1,0:T(8,128)(2,1)S(1)}, u32[]{:S(2)}, u32[]{:S(2)}) %collective-permute-start.13) | collective-permute-done | bytes 163872 | tf_op jit(solution)/shard_map/ppermute | solution.py:400
  74.8 5.2 %experts.3 = (bf16[80,4096]{1,0:T(8,128)(2,1)S(1)}, bf16[80,4096]{1,0:T(8,128)(2,1)S(1)}) custom-call(bf16[80,4096]{1,0:T(8,128)(2,1)S(1)} %pile.3.local, bf16[80,4096]{1,0:T(8,128)(2,1)S(1)} %collective-permute-done.16.remote, bf16[4096,1024]{1,0:T(8,128)(2,1)S(1)} %fetch.3.w_gate, bf16[4096,1024]{1,0:T(8,128)(2,1)S(1)} %fetch.4.w_up, ...), custom_call_target="tpu_custom_call" | custom-call | flops 4026531840 | bytes 2621440 | tf_op jit(solution)/shard_map/experts/pallas_call | solution.py:283
  80.5 3.5 %collective-permute-done.20.refs_3_ = bf16[20,4096]{1,0:T(8,128)(2,1)S(1)} collective-permute-done((bf16[20,4096]{1,0:T(8,128)(2,1)S(1)}, bf16[20,4096]{1,0:T(8,128)(2,1)S(1)}, u32[]{:S(2)}, u32[]{:S(2)}) %collective-permute-start.20) | collective-permute-done | bytes 163872 | tf_op jit(solution)/shard_map/ppermute | solution.py:400
  84.0 2.1 %collective-permute-done.21.second = bf16[80,4096]{1,0:T(8,128)(2,1)S(1)} collective-permute-done((bf16[80,4096]{1,0:T(8,128)(2,1)S(1)}, bf16[80,4096]{1,0:T(8,128)(2,1)S(1)}, u32[]{:S(2)}, u32[]{:S(2)}) %collective-permute-start.21) | collective-permute-done | bytes 655392 | tf_op jit(solution)/shard_map/ppermute | solution.py:400
  89.9 3.5 %collective-permute-done.22.refs_1_ = bf16[20,4096]{1,0:T(8,128)(2,1)S(1)} collective-permute-done((bf16[20,4096]{1,0:T(8,128)(2,1)S(1)}, bf16[20,4096]{1,0:T(8,128)(2,1)S(1)}, u32[]{:S(2)}, u32[]{:S(2)}) %collective-permute-start.22) | collective-permute-done | bytes 163872 | tf_op jit(solution)/shard_map/ppermute | solution.py:400
  93.3 2.3 %collective-permute-done.23.refs_2_ = bf16[20,4096]{1,0:T(8,128)(2,1)S(1)} collective-permute-done((bf16[20,4096]{1,0:T(8,128)(2,1)S(1)}, bf16[20,4096]{1,0:T(8,128)(2,1)S(1)}, u32[]{:S(2)}, u32[]{:S(2)}) %collective-permute-start.23) | collective-permute-done | bytes 163872 | tf_op jit(solution)/shard_map/ppermute | solution.py:400
  95.6 3.1 %collective-permute-done.24.refs_3_ = bf16[20,4096]{1,0:T(8,128)(2,1)S(1)} collective-permute-done((bf16[20,4096]{1,0:T(8,128)(2,1)S(1)}, bf16[20,4096]{1,0:T(8,128)(2,1)S(1)}, u32[]{:S(2)}, u32[]{:S(2)}) %collective-permute-start.24) | collective-permute-done | bytes 163872 | tf_op jit(solution)/shard_map/ppermute | solution.py:400
  98.8 3.8 %collective-permute-start.25 = (bf16[20,4096]{1,0:T(8,128)(2,1)S(1)}, bf16[20,4096]{1,0:T(8,128)(2,1)S(1)}, u32[]{:S(2)}, u32[]{:S(2)}) collective-permute-start(bf16[20,4096]{1,0:T(8,128)(2,1)S(1)} %total.1), channel_id=1, source_target_pairs={{0,8},{1,9},{2,10},{3,11},{4,12},{5,13},{6,14},{7,15},{8,0},{9,1},... | collective-permute-start | bytes 491528 | tf_op jit(solution)/shard_map/ppermute | solution.py:476
  102.9 8.0 %collective-permute-done.25.refs_0_ = bf16[20,4096]{1,0:T(8,128)(2,1)S(1)} collective-permute-done((bf16[20,4096]{1,0:T(8,128)(2,1)S(1)}, bf16[20,4096]{1,0:T(8,128)(2,1)S(1)}, u32[]{:S(2)}, u32[]{:S(2)}) %collective-permute-start.25) | collective-permute-done | bytes 163872 | tf_op jit(solution)/shard_map/ppermute | solution.py:476
  (46 shorter events, 20.7 us)
Async XLA Ops:
  1.1 11.2 %collective-permute-start.1 = (bf16[64,4224]{1,0:T(8,128)(2,1)S(1)}, bf16[64,4224]{1,0:T(8,128)(2,1)S(1)}, u32[]{:S(2)}, u32[]{:S(2)}) collective-permute-start(bf16[64,4224]{1,0:T(8,128)(2,1)S(1)} %bundle.1), channel_id=1, source_target_pairs={{0,3},{1,4},{2,1},{3,6},{4,7},{5,8},{6,5},{7,10},{8,11},{9,12},{10... | collective-permute-start | bytes 1622024 | tf_op jit(solution)/shard_map/ppermute | solution.py:393
  5.4 18.4 %collective-permute-start = (bf16[64,4096]{1,0:T(8,128)(2,1)}, bf16[64,4096]{1,0:T(8,128)(2,1)S(1)}, u32[]{:S(2)}, u32[]{:S(2)}) collective-permute-start(bf16[64,4096]{1,0:T(8,128)(2,1)} %refs_2_.1), channel_id=1, source_target_pairs={{0,3},{1,4},{2,1},{3,6},{4,7},{5,8},{6,5},{7,10},{8,11},{9,12},{10... | collective-permute-start | bytes 1572872 | tf_op jit(solution)/shard_map/ppermute | solution.py:393
  9.2 16.0 %collective-permute-start.4 = (bf16[64,4224]{1,0:T(8,128)(2,1)S(1)}, bf16[64,4224]{1,0:T(8,128)(2,1)S(1)}, u32[]{:S(2)}, u32[]{:S(2)}) collective-permute-start(bf16[64,4224]{1,0:T(8,128)(2,1)S(1)} %bundle.1), channel_id=1, source_target_pairs={{0,1},{1,2},{2,3},{4,5},{5,6},{6,7},{8,9},{9,10},{10,11},{12,13},{... | collective-permute-start | bytes 1622024 | tf_op jit(solution)/shard_map/ppermute | solution.py:393
  12.3 12.9 %collective-permute-start.2 = (bf16[64,4224]{1,0:T(8,128)(2,1)S(1)}, bf16[64,4224]{1,0:T(8,128)(2,1)S(1)}, u32[]{:S(2)}, u32[]{:S(2)}) collective-permute-start(bf16[64,4224]{1,0:T(8,128)(2,1)S(1)} %collective-permute-done.1.third.k1), channel_id=1, source_target_pairs={{1,5},{2,0},{5,9},{6,4},{9,13},{10,8},{14,12},{17,21},{18,16},{21,... | collective-permute-start | bytes 1622024 | tf_op jit(solution)/shard_map/ppermute | solution.py:393
  13.5 14.9 %collective-permute-start.5 = (bf16[64,4096]{1,0:T(8,128)(2,1)}, bf16[64,4096]{1,0:T(8,128)(2,1)S(1)}, u32[]{:S(2)}, u32[]{:S(2)}) collective-permute-start(bf16[64,4096]{1,0:T(8,128)(2,1)} %refs_2_.1), channel_id=1, source_target_pairs={{0,1},{1,2},{2,3},{4,5},{5,6},{6,7},{8,9},{9,10},{10,11},{12,13},{... | collective-permute-start | bytes 1572872 | tf_op jit(solution)/shard_map/ppermute | solution.py:393
  23.9 11.1 %collective-permute-start.3 = (bf16[64,4096]{1,0:T(8,128)(2,1)S(1)}, bf16[64,4096]{1,0:T(8,128)(2,1)S(1)}, u32[]{:S(2)}, u32[]{:S(2)}) collective-permute-start(bf16[64,4096]{1,0:T(8,128)(2,1)S(1)} %collective-permute-done.third.v1), channel_id=1, source_target_pairs={{1,5},{2,0},{5,9},{6,4},{9,13},{10,8},{14,12},{17,21},{18,16},{21,... | collective-permute-start | bytes 1572872 | tf_op jit(solution)/shard_map/ppermute | solution.py:393
  25.8 11.7 %collective-permute-start.6 = (bf16[64,4224]{1,0:T(8,128)(2,1)S(1)}, bf16[64,4224]{1,0:T(8,128)(2,1)S(1)}, u32[]{:S(2)}, u32[]{:S(2)}) collective-permute-start(bf16[64,4224]{1,0:T(8,128)(2,1)S(1)} %choose.2), channel_id=1, source_target_pairs={{0,1},{1,0},{2,3},{3,2},{4,5},{5,4},{6,7},{7,6},{8,9},{9,8},{10,11... | collective-permute-start | bytes 1622024 | tf_op jit(solution)/shard_map/ppermute | solution.py:400
  41.4 14.3 %collective-permute-start.10 = (bf16[20,4096]{1,0:T(8,128)(2,1)S(1)}, bf16[20,4096]{1,0:T(8,128)(2,1)S(1)}, u32[]{:S(2)}, u32[]{:S(2)}) collective-permute-start(bf16[20,4096]{1,0:T(8,128)(2,1)S(1)} %get-tuple-element.78.refs_0_), channel_id=1, source_target_pairs={{0,2},{1,3},{2,0},{3,1},{4,6},{5,7},{6,4},{7,5},{8,10},{9,11},{10,... | collective-permute-start | bytes 491528 | tf_op jit(solution)/shard_map/ppermute | solution.py:400
  41.5 14.3 %collective-permute-start.11 = (bf16[20,4096]{1,0:T(8,128)(2,1)S(1)}, bf16[20,4096]{1,0:T(8,128)(2,1)S(1)}, u32[]{:S(2)}, u32[]{:S(2)}) collective-permute-start(bf16[20,4096]{1,0:T(8,128)(2,1)S(1)} %get-tuple-element.76), channel_id=1, source_target_pairs={{0,8},{1,9},{2,10},{3,11},{4,12},{5,13},{6,14},{7,15},{8,0},{9,1},... | collective-permute-start | bytes 491528 | tf_op jit(solution)/shard_map/ppermute | solution.py:447
  44.1 11.9 %collective-permute-start.8 = (bf16[20,4096]{1,0:T(8,128)(2,1)S(1)}, bf16[20,4096]{1,0:T(8,128)(2,1)S(1)}, u32[]{:S(2)}, u32[]{:S(2)}) collective-permute-start(bf16[20,4096]{1,0:T(8,128)(2,1)S(1)} %get-tuple-element.78.refs_0_), channel_id=1, source_target_pairs={{0,6},{1,7},{2,4},{3,5},{4,2},{5,3},{6,0},{7,1},{8,14},{9,15},{10,... | collective-permute-start | bytes 491528 | tf_op jit(solution)/shard_map/ppermute | solution.py:400
  48.7 9.3 %collective-permute-start.9 = (bf16[20,4096]{1,0:T(8,128)(2,1)S(1)}, bf16[20,4096]{1,0:T(8,128)(2,1)S(1)}, u32[]{:S(2)}, u32[]{:S(2)}) collective-permute-start(bf16[20,4096]{1,0:T(8,128)(2,1)S(1)} %get-tuple-element.78.refs_0_), channel_id=1, source_target_pairs={{0,4},{1,5},{2,6},{3,7},{4,0},{5,1},{6,2},{7,3},{8,12},{9,13},{10,... | collective-permute-start | bytes 491528 | tf_op jit(solution)/shard_map/ppermute | solution.py:400
  58.1 3.6 %collective-permute-start.15 = (bf16[80,4096]{1,0:T(8,128)(2,1)S(1)}, bf16[80,4096]{1,0:T(8,128)(2,1)S(1)}, u32[]{:S(2)}, u32[]{:S(2)}) collective-permute-start(bf16[80,4096]{1,0:T(8,128)(2,1)S(1)} %pile.2.local), channel_id=1, source_target_pairs={{0,1},{1,0},{2,3},{3,2},{4,5},{5,4},{6,7},{7,6},{8,9},{9,8},{10,11... | collective-permute-start | bytes 1966088 | tf_op jit(solution)/shard_map/ppermute | solution.py:400
  58.2 8.9 %collective-permute-start.12 = (bf16[20,4096]{1,0:T(8,128)(2,1)S(1)}, bf16[20,4096]{1,0:T(8,128)(2,1)S(1)}, u32[]{:S(2)}, u32[]{:S(2)}) collective-permute-start(bf16[20,4096]{1,0:T(8,128)(2,1)S(1)} %collective-permute-done.11.refs_0_), channel_id=1, source_target_pairs={{0,6},{1,7},{2,4},{3,5},{4,2},{5,3},{6,0},{7,1},{8,14},{9,15},{10,... | collective-permute-start | bytes 491528 | tf_op jit(solution)/shard_map/ppermute | solution.py:400
  60.8 10.0 %collective-permute-start.13 = (bf16[20,4096]{1,0:T(8,128)(2,1)S(1)}, bf16[20,4096]{1,0:T(8,128)(2,1)S(1)}, u32[]{:S(2)}, u32[]{:S(2)}) collective-permute-start(bf16[20,4096]{1,0:T(8,128)(2,1)S(1)} %collective-permute-done.11.refs_0_), channel_id=1, source_target_pairs={{0,4},{1,5},{2,6},{3,7},{4,0},{5,1},{6,2},{7,3},{8,12},{9,13},{10,... | collective-permute-start | bytes 491528 | tf_op jit(solution)/shard_map/ppermute | solution.py:400
  61.4 9.5 %collective-permute-start.14 = (bf16[20,4096]{1,0:T(8,128)(2,1)S(1)}, bf16[20,4096]{1,0:T(8,128)(2,1)S(1)}, u32[]{:S(2)}, u32[]{:S(2)}) collective-permute-start(bf16[20,4096]{1,0:T(8,128)(2,1)S(1)} %collective-permute-done.11.refs_0_), channel_id=1, source_target_pairs={{0,2},{1,3},{2,0},{3,1},{4,6},{5,7},{6,4},{7,5},{8,10},{9,11},{10,... | collective-permute-start | bytes 491528 | tf_op jit(solution)/shard_map/ppermute | solution.py:400
  67.0 4.1 %collective-permute-start.17 = (bf16[80,4096]{1,0:T(8,128)(2,1)S(1)}, bf16[80,4096]{1,0:T(8,128)(2,1)S(1)}, u32[]{:S(2)}, u32[]{:S(2)}) collective-permute-start(bf16[80,4096]{1,0:T(8,128)(2,1)S(1)} %get-tuple-element.86), channel_id=1, source_target_pairs={{0,1},{1,0},{2,3},{3,2},{4,5},{5,4},{6,7},{7,6},{8,9},{9,8},{10,11... | collective-permute-start | bytes 1966088 | tf_op jit(solution)/shard_map/ppermute | solution.py:400
  71.0 3.9 %collective-permute-start.16 = (bf16[80,4096]{1,0:T(8,128)(2,1)S(1)}, bf16[80,4096]{1,0:T(8,128)(2,1)S(1)}, u32[]{:S(2)}, u32[]{:S(2)}) collective-permute-start(bf16[80,4096]{1,0:T(8,128)(2,1)S(1)} %pile.3.local), channel_id=1, source_target_pairs={{0,1},{1,0},{2,3},{3,2},{4,5},{5,4},{6,7},{7,6},{8,9},{9,8},{10,11... | collective-permute-start | bytes 1966088 | tf_op jit(solution)/shard_map/ppermute | solution.py:400
  71.3 8.8 %collective-permute-start.18 = (bf16[20,4096]{1,0:T(8,128)(2,1)S(1)}, bf16[20,4096]{1,0:T(8,128)(2,1)S(1)}, u32[]{:S(2)}, u32[]{:S(2)}) collective-permute-start(bf16[20,4096]{1,0:T(8,128)(2,1)S(1)} %get-tuple-element.94), channel_id=1, source_target_pairs={{0,2},{1,3},{2,0},{3,1},{4,6},{5,7},{6,4},{7,5},{8,10},{9,11},{10,... | collective-permute-start | bytes 491528 | tf_op jit(solution)/shard_map/ppermute | solution.py:400
  72.7 7.7 %collective-permute-start.19 = (bf16[20,4096]{1,0:T(8,128)(2,1)S(1)}, bf16[20,4096]{1,0:T(8,128)(2,1)S(1)}, u32[]{:S(2)}, u32[]{:S(2)}) collective-permute-start(bf16[20,4096]{1,0:T(8,128)(2,1)S(1)} %get-tuple-element.95), channel_id=1, source_target_pairs={{0,4},{1,5},{2,6},{3,7},{4,0},{5,1},{6,2},{7,3},{8,12},{9,13},{10,... | collective-permute-start | bytes 491528 | tf_op jit(solution)/shard_map/ppermute | solution.py:400
  74.2 9.8 %collective-permute-start.20 = (bf16[20,4096]{1,0:T(8,128)(2,1)S(1)}, bf16[20,4096]{1,0:T(8,128)(2,1)S(1)}, u32[]{:S(2)}, u32[]{:S(2)}) collective-permute-start(bf16[20,4096]{1,0:T(8,128)(2,1)S(1)} %get-tuple-element.96), channel_id=1, source_target_pairs={{0,6},{1,7},{2,4},{3,5},{4,2},{5,3},{6,0},{7,1},{8,14},{9,15},{10,... | collective-permute-start | bytes 491528 | tf_op jit(solution)/shard_map/ppermute | solution.py:400
  86.3 7.0 %collective-permute-start.22 = (bf16[20,4096]{1,0:T(8,128)(2,1)S(1)}, bf16[20,4096]{1,0:T(8,128)(2,1)S(1)}, u32[]{:S(2)}, u32[]{:S(2)}) collective-permute-start(bf16[20,4096]{1,0:T(8,128)(2,1)S(1)} %get-tuple-element.104), channel_id=1, source_target_pairs={{0,2},{1,3},{2,0},{3,1},{4,6},{5,7},{6,4},{7,5},{8,10},{9,11},{10,... | collective-permute-start | bytes 491528 | tf_op jit(solution)/shard_map/ppermute | solution.py:400
  87.8 7.8 %collective-permute-start.23 = (bf16[20,4096]{1,0:T(8,128)(2,1)S(1)}, bf16[20,4096]{1,0:T(8,128)(2,1)S(1)}, u32[]{:S(2)}, u32[]{:S(2)}) collective-permute-start(bf16[20,4096]{1,0:T(8,128)(2,1)S(1)} %get-tuple-element.105), channel_id=1, source_target_pairs={{0,4},{1,5},{2,6},{3,7},{4,0},{5,1},{6,2},{7,3},{8,12},{9,13},{10,... | collective-permute-start | bytes 491528 | tf_op jit(solution)/shard_map/ppermute | solution.py:400
  89.3 9.4 %collective-permute-start.24 = (bf16[20,4096]{1,0:T(8,128)(2,1)S(1)}, bf16[20,4096]{1,0:T(8,128)(2,1)S(1)}, u32[]{:S(2)}, u32[]{:S(2)}) collective-permute-start(bf16[20,4096]{1,0:T(8,128)(2,1)S(1)} %get-tuple-element.106), channel_id=1, source_target_pairs={{0,6},{1,7},{2,4},{3,5},{4,2},{5,3},{6,0},{7,1},{8,14},{9,15},{10,... | collective-permute-start | bytes 491528 | tf_op jit(solution)/shard_map/ppermute | solution.py:400
  98.8 12.1 %collective-permute-start.25 = (bf16[20,4096]{1,0:T(8,128)(2,1)S(1)}, bf16[20,4096]{1,0:T(8,128)(2,1)S(1)}, u32[]{:S(2)}, u32[]{:S(2)}) collective-permute-start(bf16[20,4096]{1,0:T(8,128)(2,1)S(1)} %total.1), channel_id=1, source_target_pairs={{0,8},{1,9},{2,10},{3,11},{4,12},{5,13},{6,14},{7,15},{8,0},{9,1},... | collective-permute-start | bytes 491528 | tf_op jit(solution)/shard_map/ppermute | solution.py:476
  (2 other events, 4.1 us)

commit v14 on v12

--- a/solution.py
+++ b/solution.py
@@ -13,7 +13,7 @@
 BLOCKS = 5
 CAP = 20
 SPARE = 16
-HEADS_STEP = 8
+HEADS_STEP = 16
 MASKED = -1e30
 MIB = 1024 * 1024
 
@@ -185,7 +185,7 @@
             jax.ShapeDtypeStruct((CAP, width), jnp.bfloat16),
             jax.ShapeDtypeStruct((E_WIN, rows, 32), jnp.bfloat16),
         ],
-        compiler_params=pltpu.CompilerParams(vmem_limit_bytes=14 * MIB),
+        compiler_params=pltpu.CompilerParams(vmem_limit_bytes=18 * MIB),
         cost_estimate=pl.CostEstimate(
             flops=4 * rows * BLOCKS * rows * width, bytes_accessed=8 * rows * width * 4,
             transcendentals=rows * BLOCKS * rows * (width // HEAD_DIM),
@@ -257,7 +257,7 @@
 
 def experts_kernel(local, remote, w_gate, w_up, w_down, local_out, remote_out, x, hidden):
     width, units = w_gate.shape
-    tile = min(512, units)
+    tile = min(1024, units)
     rows = local.shape[0]
     x[:rows] = local[...]
     x[rows:] = remote[...]
@@ -269,9 +269,9 @@
         up = jnp.dot(x[...], w_up[:, at], preferred_element_type=jnp.float32)
         hidden[:, at] = (jax.nn.silu(gate) * up).astype(jnp.bfloat16)
 
-    @pl.loop(0, width // 1024)
+    @pl.loop(0, width // 2048)
     def _(part):
-        at = pl.ds(pl.multiple_of(part * 1024, 1024), 1024)
+        at = pl.ds(pl.multiple_of(part * 2048, 2048), 2048)
         out = jnp.dot(hidden[...], w_down[:, at], preferred_element_type=jnp.float32)
         local_out[:, at] = out[:rows].astype(jnp.bfloat16)
         remote_out[:, at] = out[rows:].astype(jnp.bfloat16)

time: 107 us -> 106 us (level)
  Pallas kernels: 30.8 us -> 28.9 us
    pallas_call x2, Pallas kernels: 10.5 us -> 9.18 us  [experts(): pl.pallas_call(experts_kernel, in_specs=[NEAR] * 5, out_specs=[NEAR] * 2,...]
  transfers between devices with their start and end apart: 26 -> 26, of which waited for: 14 -> 15; matrix products, arithmetic and copies ran while one was open for 0% -> 0% of each run, Pallas kernels for 23% -> 22%
where the time goes in v14:
time: 106 us
  starting transfers between devices  42.4 us (40%)
  waiting for transfers between devices  34.2 us (32%)
  Pallas kernels  28.9 us (27%)
    ppermute x18, waiting for transfers between devices, swapped(): return lax.ppermute(block, 'expert', [(i, i ^ mask) for i in range(count)])  26.4 us
    ppermute x18, starting transfers between devices, swapped(): return lax.ppermute(block, 'expert', [(i, i ^ mask) for i in range(count)])  18.8 us
    ppermute x6, starting transfers between devices, moved(): lax.ppermute(block, 'expert', [pair for pair in pairs if pair[1] < count])  17.5 us
    pallas_call x3, Pallas kernels, fetch(): pl.pallas_call(functools.partial(fetch_kernel, parts), in_specs=[anywhere...  10.5 us
    pallas_call x2, Pallas kernels, experts(): pl.pallas_call(experts_kernel, in_specs=[NEAR] * 5, out_specs=[NEAR] * 2,...  9.18 us
    ppermute x6, waiting for transfers between devices, moved(): lax.ppermute(block, 'expert', [pair for pair in pairs if pair[1] < count])  7.83 us
    ppermute x1, starting transfers between devices, shards(): other = lax.ppermute(back, 'expert', partner)  3.56 us
    pallas_call x1, Pallas kernels, attention(): pl.pallas_call(attention_kernel, in_specs=[pl.BlockSpec(memory_space=pltp...  3.32 us
  transfers between devices with their start and end apart: 26, of which 15 were waited for; matrix products, arithmetic and copies ran while one was open for 0% of the time, Pallas kernels for 22%

profile of v14, /device:TPU:0, one launch (start us, length us, event | category | flops | bytes accessed | tf_op | source)
XLA Modules:
  0.0 106.0 jit_solution(11848697624384324148)
XLA Ops:
  1.1 4.3 %collective-permute-start.1 = (bf16[64,4224]{1,0:T(8,128)(2,1)S(1)}, bf16[64,4224]{1,0:T(8,128)(2,1)S(1)}, u32[]{:S(2)}, u32[]{:S(2)}) collective-permute-start(bf16[64,4224]{1,0:T(8,128)(2,1)S(1)} %bundle.1), channel_id=1, source_target_pairs={{0,3},{1,4},{2,1},{3,6},{4,7},{5,8},{6,5},{7,10},{8,11},{9,12},{10... | collective-permute-start | bytes 1622024 | tf_op jit(solution)/shard_map/ppermute | solution.py:393
  5.4 3.8 %collective-permute-start = (bf16[64,4096]{1,0:T(8,128)(2,1)}, bf16[64,4096]{1,0:T(8,128)(2,1)S(1)}, u32[]{:S(2)}, u32[]{:S(2)}) collective-permute-start(bf16[64,4096]{1,0:T(8,128)(2,1)} %refs_2_.1), channel_id=1, source_target_pairs={{0,3},{1,4},{2,1},{3,6},{4,7},{5,8},{6,5},{7,10},{8,11},{9,12},{10... | collective-permute-start | bytes 1572872 | tf_op jit(solution)/shard_map/ppermute | solution.py:393
  9.2 1.7 %collective-permute-start.4 = (bf16[64,4224]{1,0:T(8,128)(2,1)S(1)}, bf16[64,4224]{1,0:T(8,128)(2,1)S(1)}, u32[]{:S(2)}, u32[]{:S(2)}) collective-permute-start(bf16[64,4224]{1,0:T(8,128)(2,1)S(1)} %bundle.1), channel_id=1, source_target_pairs={{0,1},{1,2},{2,3},{4,5},{5,6},{6,7},{8,9},{9,10},{10,11},{12,13},{... | collective-permute-start | bytes 1622024 | tf_op jit(solution)/shard_map/ppermute | solution.py:393
  13.5 5.0 %collective-permute-start.5 = (bf16[64,4096]{1,0:T(8,128)(2,1)}, bf16[64,4096]{1,0:T(8,128)(2,1)S(1)}, u32[]{:S(2)}, u32[]{:S(2)}) collective-permute-start(bf16[64,4096]{1,0:T(8,128)(2,1)} %refs_2_.1), channel_id=1, source_target_pairs={{0,1},{1,2},{2,3},{4,5},{5,6},{6,7},{8,9},{9,10},{10,11},{12,13},{... | collective-permute-start | bytes 1572872 | tf_op jit(solution)/shard_map/ppermute | solution.py:393
  18.7 3.5 %fetch.3.w_gate = bf16[4096,1024]{1,0:T(8,128)(2,1)S(1)} custom-call(bf16[4096,1024]{1,0:T(8,128)(2,1)} %source.3, s32[7]{0:T(128)S(1)} %stack.31.after.refs_8_.flags.deltas), custom_call_target="tpu_custom_call" | custom-call | bytes 16777216 | tf_op jit(solution)/shard_map/fetch/pallas_call | solution.py:244
  25.8 2.6 %collective-permute-start.6 = (bf16[64,4224]{1,0:T(8,128)(2,1)S(1)}, bf16[64,4224]{1,0:T(8,128)(2,1)S(1)}, u32[]{:S(2)}, u32[]{:S(2)}) collective-permute-start(bf16[64,4224]{1,0:T(8,128)(2,1)S(1)} %choose.2), channel_id=1, source_target_pairs={{0,1},{1,0},{2,3},{3,2},{4,5},{5,4},{6,7},{7,6},{8,9},{9,8},{10,11... | collective-permute-start | bytes 1622024 | tf_op jit(solution)/shard_map/ppermute | solution.py:400
  28.4 6.5 %collective-permute-done.3.first.v2 = bf16[64,4096]{1,0:T(8,128)(2,1)S(1)} collective-permute-done((bf16[64,4096]{1,0:T(8,128)(2,1)S(1)}, bf16[64,4096]{1,0:T(8,128)(2,1)S(1)}, u32[]{:S(2)}, u32[]{:S(2)}) %collective-permute-start.3) | collective-permute-done | bytes 524320 | tf_op jit(solution)/shard_map/ppermute | solution.py:393
  35.6 1.9 %collective-permute-done.7.v4 = bf16[64,4096]{1,0:T(8,128)(2,1)S(1)} collective-permute-done((bf16[64,4096]{1,0:T(8,128)(2,1)S(1)}, bf16[64,4096]{1,0:T(8,128)(2,1)S(1)}, u32[]{:S(2)}, u32[]{:S(2)}) %collective-permute-start.7) | collective-permute-done | bytes 524320 | tf_op jit(solution)/shard_map/ppermute | solution.py:400
  37.5 3.3 %attention.1 = (f32[64,4096]{1,0:T(8,128)S(1)}, bf16[20,4096]{1,0:T(8,128)(2,1)S(1)}, bf16[20,4096]{1,0:T(8,128)(2,1)S(1)}, bf16[2,64,32]{2,1,0:T(8,128)(2,1)S(1)}) custom-call(s32[7]{0:T(128)S(1)} %stack.31.after.refs_8_.flags.deltas, bf16[64,4096]{1,0:T(8,128)(2,1)S(1)} %get-tuple-element.75.q, bf16[64,4096]{1,0:T(8,128)(2,1)S(1)} %get-tuple-element.76.k0, ...), custom_call_target="tpu_custom_call" | custom-call | flops 335544320 | bytes 8388608 | tf_op jit(solution)/shard_map/attention/pallas_call | solution.py:178
  40.9 2.6 %collective-permute-start.11 = (bf16[20,4096]{1,0:T(8,128)(2,1)S(1)}, bf16[20,4096]{1,0:T(8,128)(2,1)S(1)}, u32[]{:S(2)}, u32[]{:S(2)}) collective-permute-start(bf16[20,4096]{1,0:T(8,128)(2,1)S(1)} %get-tuple-element.87), channel_id=1, source_target_pairs={{0,8},{1,9},{2,10},{3,11},{4,12},{5,13},{6,14},{7,15},{8,0},{9,1},... | collective-permute-start | bytes 491528 | tf_op jit(solution)/shard_map/ppermute | solution.py:447
  43.6 4.6 %collective-permute-start.8 = (bf16[20,4096]{1,0:T(8,128)(2,1)S(1)}, bf16[20,4096]{1,0:T(8,128)(2,1)S(1)}, u32[]{:S(2)}, u32[]{:S(2)}) collective-permute-start(bf16[20,4096]{1,0:T(8,128)(2,1)S(1)} %get-tuple-element.89.refs_0_), channel_id=1, source_target_pairs={{0,6},{1,7},{2,4},{3,5},{4,2},{5,3},{6,0},{7,1},{8,14},{9,15},{10,... | collective-permute-start | bytes 491528 | tf_op jit(solution)/shard_map/ppermute | solution.py:400
  48.1 3.5 %fetch.4.w_up = bf16[4096,1024]{1,0:T(8,128)(2,1)S(1)} custom-call(bf16[4096,1024]{1,0:T(8,128)(2,1)} %source.4, bf16[2,64,32]{2,1,0:T(8,128)(2,1)S(1)} %get-tuple-element.85.after.weight), custom_call_target="tpu_custom_call" | custom-call | bytes 16777216 | tf_op jit(solution)/shard_map/fetch/pallas_call | solution.py:244
  51.7 3.5 %fetch.5.w_down = bf16[1024,4096]{1,0:T(8,128)(2,1)S(1)} custom-call(bf16[1024,4096]{1,0:T(8,128)(2,1)} %source.5, bf16[2,64,32]{2,1,0:T(8,128)(2,1)S(1)} %get-tuple-element.85.after.weight), custom_call_target="tpu_custom_call" | custom-call | bytes 16777216 | tf_op jit(solution)/shard_map/fetch/pallas_call | solution.py:244
  55.5 2.0 %collective-permute-done.9.refs_2_ = bf16[20,4096]{1,0:T(8,128)(2,1)S(1)} collective-permute-done((bf16[20,4096]{1,0:T(8,128)(2,1)S(1)}, bf16[20,4096]{1,0:T(8,128)(2,1)S(1)}, u32[]{:S(2)}, u32[]{:S(2)}) %collective-permute-start.9) | collective-permute-done | bytes 163872 | tf_op jit(solution)/shard_map/ppermute | solution.py:400
  57.6 2.6 %collective-permute-start.12 = (bf16[20,4096]{1,0:T(8,128)(2,1)S(1)}, bf16[20,4096]{1,0:T(8,128)(2,1)S(1)}, u32[]{:S(2)}, u32[]{:S(2)}) collective-permute-start(bf16[20,4096]{1,0:T(8,128)(2,1)S(1)} %collective-permute-done.11.refs_0_), channel_id=1, source_target_pairs={{0,6},{1,7},{2,4},{3,5},{4,2},{5,3},{6,0},{7,1},{8,14},{9,15},{10,... | collective-permute-start | bytes 491528 | tf_op jit(solution)/shard_map/ppermute | solution.py:400
  61.2 4.6 %experts.2 = (bf16[80,4096]{1,0:T(8,128)(2,1)S(1)}, bf16[80,4096]{1,0:T(8,128)(2,1)S(1)}) custom-call(bf16[80,4096]{1,0:T(8,128)(2,1)S(1)} %pile.2.local, bf16[80,4096]{1,0:T(8,128)(2,1)S(1)} %collective-permute-done.15.remote, bf16[4096,1024]{1,0:T(8,128)(2,1)S(1)} %fetch.3.w_gate, bf16[4096,1024]{1,0:T(8,128)(2,1)S(1)} %fetch.4.w_up, ...), custom_call_target="tpu_custom_call" | custom-call | flops 4026531840 | bytes 2621440 | tf_op jit(solution)/shard_map/experts/pallas_call | solution.py:283
  66.3 4.0 %collective-permute-done.13.refs_2_ = bf16[20,4096]{1,0:T(8,128)(2,1)S(1)} collective-permute-done((bf16[20,4096]{1,0:T(8,128)(2,1)S(1)}, bf16[20,4096]{1,0:T(8,128)(2,1)S(1)}, u32[]{:S(2)}, u32[]{:S(2)}) %collective-permute-start.13) | collective-permute-done | bytes 163872 | tf_op jit(solution)/shard_map/ppermute | solution.py:400
  72.6 4.6 %experts.3 = (bf16[80,4096]{1,0:T(8,128)(2,1)S(1)}, bf16[80,4096]{1,0:T(8,128)(2,1)S(1)}) custom-call(bf16[80,4096]{1,0:T(8,128)(2,1)S(1)} %pile.3.local, bf16[80,4096]{1,0:T(8,128)(2,1)S(1)} %collective-permute-done.16.remote, bf16[4096,1024]{1,0:T(8,128)(2,1)S(1)} %fetch.3.w_gate, bf16[4096,1024]{1,0:T(8,128)(2,1)S(1)} %fetch.4.w_up, ...), custom_call_target="tpu_custom_call" | custom-call | flops 4026531840 | bytes 2621440 | tf_op jit(solution)/shard_map/experts/pallas_call | solution.py:283
  77.6 1.8 %collective-permute-done.17.second = bf16[80,4096]{1,0:T(8,128)(2,1)S(1)} collective-permute-done((bf16[80,4096]{1,0:T(8,128)(2,1)S(1)}, bf16[80,4096]{1,0:T(8,128)(2,1)S(1)}, u32[]{:S(2)}, u32[]{:S(2)}) %collective-permute-start.17) | collective-permute-done | bytes 655392 | tf_op jit(solution)/shard_map/ppermute | solution.py:400
  83.1 3.5 %collective-permute-done.19.refs_1_ = bf16[20,4096]{1,0:T(8,128)(2,1)S(1)} collective-permute-done((bf16[20,4096]{1,0:T(8,128)(2,1)S(1)}, bf16[20,4096]{1,0:T(8,128)(2,1)S(1)}, u32[]{:S(2)}, u32[]{:S(2)}) %collective-permute-start.19) | collective-permute-done | bytes 163872 | tf_op jit(solution)/shard_map/ppermute | solution.py:400
  86.6 2.3 %collective-permute-done.20.refs_2_ = bf16[20,4096]{1,0:T(8,128)(2,1)S(1)} collective-permute-done((bf16[20,4096]{1,0:T(8,128)(2,1)S(1)}, bf16[20,4096]{1,0:T(8,128)(2,1)S(1)}, u32[]{:S(2)}, u32[]{:S(2)}) %collective-permute-start.20) | collective-permute-done | bytes 163872 | tf_op jit(solution)/shard_map/ppermute | solution.py:400
  93.2 3.6 %collective-permute-start.25 = (bf16[20,4096]{1,0:T(8,128)(2,1)S(1)}, bf16[20,4096]{1,0:T(8,128)(2,1)S(1)}, u32[]{:S(2)}, u32[]{:S(2)}) collective-permute-start(bf16[20,4096]{1,0:T(8,128)(2,1)S(1)} %total.1), channel_id=1, source_target_pairs={{0,8},{1,9},{2,10},{3,11},{4,12},{5,13},{6,14},{7,15},{8,0},{9,1},... | collective-permute-start | bytes 491528 | tf_op jit(solution)/shard_map/ppermute | solution.py:478
  97.0 4.5 %collective-permute-done.22.refs_2_ = bf16[20,4096]{1,0:T(8,128)(2,1)S(1)} collective-permute-done((bf16[20,4096]{1,0:T(8,128)(2,1)S(1)}, bf16[20,4096]{1,0:T(8,128)(2,1)S(1)}, u32[]{:S(2)}, u32[]{:S(2)}) %collective-permute-start.22) | collective-permute-done | bytes 163872 | tf_op jit(solution)/shard_map/ppermute | solution.py:400
  101.5 3.1 %collective-permute-done.23.refs_3_ = bf16[20,4096]{1,0:T(8,128)(2,1)S(1)} collective-permute-done((bf16[20,4096]{1,0:T(8,128)(2,1)S(1)}, bf16[20,4096]{1,0:T(8,128)(2,1)S(1)}, u32[]{:S(2)}, u32[]{:S(2)}) %collective-permute-start.23) | collective-permute-done | bytes 163872 | tf_op jit(solution)/shard_map/ppermute | solution.py:400
  (46 shorter events, 22.3 us)
Async XLA Ops:
  1.1 11.2 %collective-permute-start.1 = (bf16[64,4224]{1,0:T(8,128)(2,1)S(1)}, bf16[64,4224]{1,0:T(8,128)(2,1)S(1)}, u32[]{:S(2)}, u32[]{:S(2)}) collective-permute-start(bf16[64,4224]{1,0:T(8,128)(2,1)S(1)} %bundle.1), channel_id=1, source_target_pairs={{0,3},{1,4},{2,1},{3,6},{4,7},{5,8},{6,5},{7,10},{8,11},{9,12},{10... | collective-permute-start | bytes 1622024 | tf_op jit(solution)/shard_map/ppermute | solution.py:393
  5.4 18.4 %collective-permute-start = (bf16[64,4096]{1,0:T(8,128)(2,1)}, bf16[64,4096]{1,0:T(8,128)(2,1)S(1)}, u32[]{:S(2)}, u32[]{:S(2)}) collective-permute-start(bf16[64,4096]{1,0:T(8,128)(2,1)} %refs_2_.1), channel_id=1, source_target_pairs={{0,3},{1,4},{2,1},{3,6},{4,7},{5,8},{6,5},{7,10},{8,11},{9,12},{10... | collective-permute-start | bytes 1572872 | tf_op jit(solution)/shard_map/ppermute | solution.py:393
  9.2 16.0 %collective-permute-start.4 = (bf16[64,4224]{1,0:T(8,128)(2,1)S(1)}, bf16[64,4224]{1,0:T(8,128)(2,1)S(1)}, u32[]{:S(2)}, u32[]{:S(2)}) collective-permute-start(bf16[64,4224]{1,0:T(8,128)(2,1)S(1)} %bundle.1), channel_id=1, source_target_pairs={{0,1},{1,2},{2,3},{4,5},{5,6},{6,7},{8,9},{9,10},{10,11},{12,13},{... | collective-permute-start | bytes 1622024 | tf_op jit(solution)/shard_map/ppermute | solution.py:393
  12.3 12.9 %collective-permute-start.2 = (bf16[64,4224]{1,0:T(8,128)(2,1)S(1)}, bf16[64,4224]{1,0:T(8,128)(2,1)S(1)}, u32[]{:S(2)}, u32[]{:S(2)}) collective-permute-start(bf16[64,4224]{1,0:T(8,128)(2,1)S(1)} %collective-permute-done.1.third.k1), channel_id=1, source_target_pairs={{1,5},{2,0},{5,9},{6,4},{9,13},{10,8},{14,12},{17,21},{18,16},{21,... | collective-permute-start | bytes 1622024 | tf_op jit(solution)/shard_map/ppermute | solution.py:393
  13.5 14.9 %collective-permute-start.5 = (bf16[64,4096]{1,0:T(8,128)(2,1)}, bf16[64,4096]{1,0:T(8,128)(2,1)S(1)}, u32[]{:S(2)}, u32[]{:S(2)}) collective-permute-start(bf16[64,4096]{1,0:T(8,128)(2,1)} %refs_2_.1), channel_id=1, source_target_pairs={{0,1},{1,2},{2,3},{4,5},{5,6},{6,7},{8,9},{9,10},{10,11},{12,13},{... | collective-permute-start | bytes 1572872 | tf_op jit(solution)/shard_map/ppermute | solution.py:393
  23.9 11.1 %collective-permute-start.3 = (bf16[64,4096]{1,0:T(8,128)(2,1)S(1)}, bf16[64,4096]{1,0:T(8,128)(2,1)S(1)}, u32[]{:S(2)}, u32[]{:S(2)}) collective-permute-start(bf16[64,4096]{1,0:T(8,128)(2,1)S(1)} %collective-permute-done.third.v1), channel_id=1, source_target_pairs={{1,5},{2,0},{5,9},{6,4},{9,13},{10,8},{14,12},{17,21},{18,16},{21,... | collective-permute-start | bytes 1572872 | tf_op jit(solution)/shard_map/ppermute | solution.py:393
  25.8 11.7 %collective-permute-start.6 = (bf16[64,4224]{1,0:T(8,128)(2,1)S(1)}, bf16[64,4224]{1,0:T(8,128)(2,1)S(1)}, u32[]{:S(2)}, u32[]{:S(2)}) collective-permute-start(bf16[64,4224]{1,0:T(8,128)(2,1)S(1)} %choose.2), channel_id=1, source_target_pairs={{0,1},{1,0},{2,3},{3,2},{4,5},{5,4},{6,7},{7,6},{8,9},{9,8},{10,11... | collective-permute-start | bytes 1622024 | tf_op jit(solution)/shard_map/ppermute | solution.py:400
  40.9 14.3 %collective-permute-start.10 = (bf16[20,4096]{1,0:T(8,128)(2,1)S(1)}, bf16[20,4096]{1,0:T(8,128)(2,1)S(1)}, u32[]{:S(2)}, u32[]{:S(2)}) collective-permute-start(bf16[20,4096]{1,0:T(8,128)(2,1)S(1)} %get-tuple-element.89.refs_0_), channel_id=1, source_target_pairs={{0,2},{1,3},{2,0},{3,1},{4,6},{5,7},{6,4},{7,5},{8,10},{9,11},{10,... | collective-permute-start | bytes 491528 | tf_op jit(solution)/shard_map/ppermute | solution.py:400
  40.9 14.3 %collective-permute-start.11 = (bf16[20,4096]{1,0:T(8,128)(2,1)S(1)}, bf16[20,4096]{1,0:T(8,128)(2,1)S(1)}, u32[]{:S(2)}, u32[]{:S(2)}) collective-permute-start(bf16[20,4096]{1,0:T(8,128)(2,1)S(1)} %get-tuple-element.87), channel_id=1, source_target_pairs={{0,8},{1,9},{2,10},{3,11},{4,12},{5,13},{6,14},{7,15},{8,0},{9,1},... | collective-permute-start | bytes 491528 | tf_op jit(solution)/shard_map/ppermute | solution.py:447
  43.6 11.9 %collective-permute-start.8 = (bf16[20,4096]{1,0:T(8,128)(2,1)S(1)}, bf16[20,4096]{1,0:T(8,128)(2,1)S(1)}, u32[]{:S(2)}, u32[]{:S(2)}) collective-permute-start(bf16[20,4096]{1,0:T(8,128)(2,1)S(1)} %get-tuple-element.89.refs_0_), channel_id=1, source_target_pairs={{0,6},{1,7},{2,4},{3,5},{4,2},{5,3},{6,0},{7,1},{8,14},{9,15},{10,... | collective-permute-start | bytes 491528 | tf_op jit(solution)/shard_map/ppermute | solution.py:400
  48.1 9.3 %collective-permute-start.9 = (bf16[20,4096]{1,0:T(8,128)(2,1)S(1)}, bf16[20,4096]{1,0:T(8,128)(2,1)S(1)}, u32[]{:S(2)}, u32[]{:S(2)}) collective-permute-start(bf16[20,4096]{1,0:T(8,128)(2,1)S(1)} %get-tuple-element.89.refs_0_), channel_id=1, source_target_pairs={{0,4},{1,5},{2,6},{3,7},{4,0},{5,1},{6,2},{7,3},{8,12},{9,13},{10,... | collective-permute-start | bytes 491528 | tf_op jit(solution)/shard_map/ppermute | solution.py:400
  57.6 3.6 %collective-permute-start.15 = (bf16[80,4096]{1,0:T(8,128)(2,1)S(1)}, bf16[80,4096]{1,0:T(8,128)(2,1)S(1)}, u32[]{:S(2)}, u32[]{:S(2)}) collective-permute-start(bf16[80,4096]{1,0:T(8,128)(2,1)S(1)} %pile.2.local), channel_id=1, source_target_pairs={{0,1},{1,0},{2,3},{3,2},{4,5},{5,4},{6,7},{7,6},{8,9},{9,8},{10,11... | collective-permute-start | bytes 1966088 | tf_op jit(solution)/shard_map/ppermute | solution.py:400
  57.6 8.7 %collective-permute-start.12 = (bf16[20,4096]{1,0:T(8,128)(2,1)S(1)}, bf16[20,4096]{1,0:T(8,128)(2,1)S(1)}, u32[]{:S(2)}, u32[]{:S(2)}) collective-permute-start(bf16[20,4096]{1,0:T(8,128)(2,1)S(1)} %collective-permute-done.11.refs_0_), channel_id=1, source_target_pairs={{0,6},{1,7},{2,4},{3,5},{4,2},{5,3},{6,0},{7,1},{8,14},{9,15},{10,... | collective-permute-start | bytes 491528 | tf_op jit(solution)/shard_map/ppermute | solution.py:400
  60.3 10.0 %collective-permute-start.13 = (bf16[20,4096]{1,0:T(8,128)(2,1)S(1)}, bf16[20,4096]{1,0:T(8,128)(2,1)S(1)}, u32[]{:S(2)}, u32[]{:S(2)}) collective-permute-start(bf16[20,4096]{1,0:T(8,128)(2,1)S(1)} %collective-permute-done.11.refs_0_), channel_id=1, source_target_pairs={{0,4},{1,5},{2,6},{3,7},{4,0},{5,1},{6,2},{7,3},{8,12},{9,13},{10,... | collective-permute-start | bytes 491528 | tf_op jit(solution)/shard_map/ppermute | solution.py:400
  60.8 9.5 %collective-permute-start.14 = (bf16[20,4096]{1,0:T(8,128)(2,1)S(1)}, bf16[20,4096]{1,0:T(8,128)(2,1)S(1)}, u32[]{:S(2)}, u32[]{:S(2)}) collective-permute-start(bf16[20,4096]{1,0:T(8,128)(2,1)S(1)} %collective-permute-done.11.refs_0_), channel_id=1, source_target_pairs={{0,2},{1,3},{2,0},{3,1},{4,6},{5,7},{6,4},{7,5},{8,10},{9,11},{10,... | collective-permute-start | bytes 491528 | tf_op jit(solution)/shard_map/ppermute | solution.py:400
  70.4 2.2 %collective-permute-start.16 = (bf16[80,4096]{1,0:T(8,128)(2,1)S(1)}, bf16[80,4096]{1,0:T(8,128)(2,1)S(1)}, u32[]{:S(2)}, u32[]{:S(2)}) collective-permute-start(bf16[80,4096]{1,0:T(8,128)(2,1)S(1)} %pile.3.local), channel_id=1, source_target_pairs={{0,1},{1,0},{2,3},{3,2},{4,5},{5,4},{6,7},{7,6},{8,9},{9,8},{10,11... | collective-permute-start | bytes 1966088 | tf_op jit(solution)/shard_map/ppermute | solution.py:400
  70.5 6.9 %collective-permute-start.18 = (bf16[80,4096]{1,0:T(8,128)(2,1)S(1)}, bf16[80,4096]{1,0:T(8,128)(2,1)S(1)}, u32[]{:S(2)}, u32[]{:S(2)}) collective-permute-start(bf16[80,4096]{1,0:T(8,128)(2,1)S(1)} %get-tuple-element.109), channel_id=1, source_target_pairs={{0,1},{1,0},{2,3},{3,2},{4,5},{5,4},{6,7},{7,6},{8,9},{9,8},{10,11... | collective-permute-start | bytes 1966088 | tf_op jit(solution)/shard_map/ppermute | solution.py:400
  79.6 7.0 %collective-permute-start.19 = (bf16[20,4096]{1,0:T(8,128)(2,1)S(1)}, bf16[20,4096]{1,0:T(8,128)(2,1)S(1)}, u32[]{:S(2)}, u32[]{:S(2)}) collective-permute-start(bf16[20,4096]{1,0:T(8,128)(2,1)S(1)} %get-tuple-element.115), channel_id=1, source_target_pairs={{0,2},{1,3},{2,0},{3,1},{4,6},{5,7},{6,4},{7,5},{8,10},{9,11},{10,... | collective-permute-start | bytes 491528 | tf_op jit(solution)/shard_map/ppermute | solution.py:400
  81.0 7.8 %collective-permute-start.20 = (bf16[20,4096]{1,0:T(8,128)(2,1)S(1)}, bf16[20,4096]{1,0:T(8,128)(2,1)S(1)}, u32[]{:S(2)}, u32[]{:S(2)}) collective-permute-start(bf16[20,4096]{1,0:T(8,128)(2,1)S(1)} %get-tuple-element.116), channel_id=1, source_target_pairs={{0,4},{1,5},{2,6},{3,7},{4,0},{5,1},{6,2},{7,3},{8,12},{9,13},{10,... | collective-permute-start | bytes 491528 | tf_op jit(solution)/shard_map/ppermute | solution.py:400
  82.5 10.6 %collective-permute-start.24 = (bf16[20,4096]{1,0:T(8,128)(2,1)S(1)}, bf16[20,4096]{1,0:T(8,128)(2,1)S(1)}, u32[]{:S(2)}, u32[]{:S(2)}) collective-permute-start(bf16[20,4096]{1,0:T(8,128)(2,1)S(1)} %get-tuple-element.128), channel_id=1, source_target_pairs={{0,6},{1,7},{2,4},{3,5},{4,2},{5,3},{6,0},{7,1},{8,14},{9,15},{10,... | collective-permute-start | bytes 491528 | tf_op jit(solution)/shard_map/ppermute | solution.py:400
  88.8 8.2 %collective-permute-start.21 = (bf16[20,4096]{1,0:T(8,128)(2,1)S(1)}, bf16[20,4096]{1,0:T(8,128)(2,1)S(1)}, u32[]{:S(2)}, u32[]{:S(2)}) collective-permute-start(bf16[20,4096]{1,0:T(8,128)(2,1)S(1)} %get-tuple-element.122), channel_id=1, source_target_pairs={{0,2},{1,3},{2,0},{3,1},{4,6},{5,7},{6,4},{7,5},{8,10},{9,11},{10,... | collective-permute-start | bytes 491528 | tf_op jit(solution)/shard_map/ppermute | solution.py:400
  89.4 12.1 %collective-permute-start.22 = (bf16[20,4096]{1,0:T(8,128)(2,1)S(1)}, bf16[20,4096]{1,0:T(8,128)(2,1)S(1)}, u32[]{:S(2)}, u32[]{:S(2)}) collective-permute-start(bf16[20,4096]{1,0:T(8,128)(2,1)S(1)} %get-tuple-element.123), channel_id=1, source_target_pairs={{0,4},{1,5},{2,6},{3,7},{4,0},{5,1},{6,2},{7,3},{8,12},{9,13},{10,... | collective-permute-start | bytes 491528 | tf_op jit(solution)/shard_map/ppermute | solution.py:400
  90.9 13.7 %collective-permute-start.23 = (bf16[20,4096]{1,0:T(8,128)(2,1)S(1)}, bf16[20,4096]{1,0:T(8,128)(2,1)S(1)}, u32[]{:S(2)}, u32[]{:S(2)}) collective-permute-start(bf16[20,4096]{1,0:T(8,128)(2,1)S(1)} %get-tuple-element.124), channel_id=1, source_target_pairs={{0,6},{1,7},{2,4},{3,5},{4,2},{5,3},{6,0},{7,1},{8,14},{9,15},{10,... | collective-permute-start | bytes 491528 | tf_op jit(solution)/shard_map/ppermute | solution.py:400
  93.2 11.7 %collective-permute-start.25 = (bf16[20,4096]{1,0:T(8,128)(2,1)S(1)}, bf16[20,4096]{1,0:T(8,128)(2,1)S(1)}, u32[]{:S(2)}, u32[]{:S(2)}) collective-permute-start(bf16[20,4096]{1,0:T(8,128)(2,1)S(1)} %total.1), channel_id=1, source_target_pairs={{0,8},{1,9},{2,10},{3,11},{4,12},{5,13},{6,14},{7,15},{8,0},{9,1},... | collective-permute-start | bytes 491528 | tf_op jit(solution)/shard_map/ppermute | solution.py:478
  (2 other events, 4.1 us)

commit v15 on v14

--- a/solution.py
+++ b/solution.py
@@ -13,7 +13,7 @@
 BLOCKS = 5
 CAP = 20
 SPARE = 16
-HEADS_STEP = 16
+HEADS_STEP = 32
 MASKED = -1e30
 MIB = 1024 * 1024
 
@@ -269,12 +269,9 @@
         up = jnp.dot(x[...], w_up[:, at], preferred_element_type=jnp.float32)
         hidden[:, at] = (jax.nn.silu(gate) * up).astype(jnp.bfloat16)
 
-    @pl.loop(0, width // 2048)
-    def _(part):
-        at = pl.ds(pl.multiple_of(part * 2048, 2048), 2048)
-        out = jnp.dot(hidden[...], w_down[:, at], preferred_element_type=jnp.float32)
-        local_out[:, at] = out[:rows].astype(jnp.bfloat16)
-        remote_out[:, at] = out[rows:].astype(jnp.bfloat16)
+    out = jnp.dot(hidden[...], w_down[...], preferred_element_type=jnp.float32)
+    local_out[...] = out[:rows].astype(jnp.bfloat16)
+    remote_out[...] = out[rows:].astype(jnp.bfloat16)
 
 
 def experts(local, remote, w_gate, w_up, w_down):
@@ -379,6 +376,37 @@
     )(close(base), weight, *blocks)
 
 
+def finish_kernel(parts, base, weight, other, out, held, sems):
+    width = base.shape[1] // parts
+    copies = []
+    for part in range(parts):
+        at = pl.ds(part * width, width)
+        held[:, at] = (
+            base[:, at]
+            + jnp.dot(weight[1][:, :CAP], other[:, at], preferred_element_type=jnp.float32)
+        ).astype(held.dtype)
+        copies.append(pltpu.make_async_copy(held.at[:, at], out.at[:, at], sems.at[part]))
+        copies[-1].start()
+    for copy in copies:
+        copy.wait()
+
+
+def finish(base, weight, other):
+    parts = 4
+    return pl.pallas_call(
+        functools.partial(finish_kernel, parts),
+        in_specs=[NEAR] * 3,
+        out_specs=pl.BlockSpec(memory_space=pl.ANY),
+        out_shape=jax.ShapeDtypeStruct(base.shape, jnp.bfloat16),
+        scratch_shapes=[
+            pltpu.VMEM(base.shape, jnp.bfloat16),
+            pltpu.SemaphoreType.DMA((parts,)),
+        ],
+        compiler_params=pltpu.CompilerParams(vmem_limit_bytes=8 * MIB),
+        name="finish",
+    )(close(base), weight, other)
+
+
 def shards(
     resid, queries, keys, values, segment_ids, norm_gain, routes, route_gates, w_gate, w_up, w_down
 ):
@@ -477,9 +505,7 @@
     back = total_of(late_blocks)
     other = lax.ppermute(back, "expert", partner)
     base = combine(0, mixed, weight, early_blocks, pltpu.VMEM(mixed.shape, jnp.float32))
-    return combine(
-        1, base, weight, [other], jax.ShapeDtypeStruct(mixed.shape, jnp.bfloat16)
-    )
+    return finish(base, weight, other)
 
 
 def solution(mesh):

time: 106 us -> 106 us (level)
  transfers between devices with their start and end apart: 26 -> 26, of which waited for: 15 -> 15; matrix products, arithmetic and copies ran while one was open for 0% -> 0% of each run, Pallas kernels for 22% -> 21%
where the time goes in v15:
time: 106 us; the launch traced here: 105 us
  starting transfers between devices  42.4 us (40%)
  waiting for transfers between devices  34.6 us (33%)
  Pallas kernels  27.9 us (26%)
    ppermute x18, waiting for transfers between devices, swapped(): return lax.ppermute(block, 'expert', [(i, i ^ mask) for i in range(count)])  26.7 us
    ppermute x18, starting transfers between devices, swapped(): return lax.ppermute(block, 'expert', [(i, i ^ mask) for i in range(count)])  18.8 us
    ppermute x6, starting transfers between devices, moved(): lax.ppermute(block, 'expert', [pair for pair in pairs if pair[1] < count])  17.5 us
    pallas_call x3, Pallas kernels, fetch(): pl.pallas_call(functools.partial(fetch_kernel, parts), in_specs=[anywhere...  10.5 us
    pallas_call x2, Pallas kernels, experts(): pl.pallas_call(experts_kernel, in_specs=[NEAR] * 5, out_specs=[NEAR] * 2,...  8.47 us
    ppermute x6, waiting for transfers between devices, moved(): lax.ppermute(block, 'expert', [pair for pair in pairs if pair[1] < count])  7.83 us
    ppermute x1, starting transfers between devices, shards(): other = lax.ppermute(back, 'expert', partner)  3.57 us
    pallas_call x1, Pallas kernels, attention(): pl.pallas_call(attention_kernel, in_specs=[pl.BlockSpec(memory_space=pltp...  3 us
  transfers between devices with their start and end apart: 26, of which 15 were waited for; matrix products, arithmetic and copies ran while one was open for 0% of the time, Pallas kernels for 21%

profile of v15, /device:TPU:0, one launch (start us, length us, event | category | flops | bytes accessed | tf_op | source)
XLA Modules:
  0.0 105.2 jit_solution(2612758221880768963)
XLA Ops:
  1.1 4.3 %collective-permute-start.1 = (bf16[64,4224]{1,0:T(8,128)(2,1)S(1)}, bf16[64,4224]{1,0:T(8,128)(2,1)S(1)}, u32[]{:S(2)}, u32[]{:S(2)}) collective-permute-start(bf16[64,4224]{1,0:T(8,128)(2,1)S(1)} %bundle.1), channel_id=1, source_target_pairs={{0,3},{1,4},{2,1},{3,6},{4,7},{5,8},{6,5},{7,10},{8,11},{9,12},{10... | collective-permute-start | bytes 1622024 | tf_op jit(solution)/shard_map/ppermute | solution.py:421
  5.4 3.8 %collective-permute-start = (bf16[64,4096]{1,0:T(8,128)(2,1)}, bf16[64,4096]{1,0:T(8,128)(2,1)S(1)}, u32[]{:S(2)}, u32[]{:S(2)}) collective-permute-start(bf16[64,4096]{1,0:T(8,128)(2,1)} %refs_2_.1), channel_id=1, source_target_pairs={{0,3},{1,4},{2,1},{3,6},{4,7},{5,8},{6,5},{7,10},{8,11},{9,12},{10... | collective-permute-start | bytes 1572872 | tf_op jit(solution)/shard_map/ppermute | solution.py:421
  9.2 1.7 %collective-permute-start.4 = (bf16[64,4224]{1,0:T(8,128)(2,1)S(1)}, bf16[64,4224]{1,0:T(8,128)(2,1)S(1)}, u32[]{:S(2)}, u32[]{:S(2)}) collective-permute-start(bf16[64,4224]{1,0:T(8,128)(2,1)S(1)} %bundle.1), channel_id=1, source_target_pairs={{0,1},{1,2},{2,3},{4,5},{5,6},{6,7},{8,9},{9,10},{10,11},{12,13},{... | collective-permute-start | bytes 1622024 | tf_op jit(solution)/shard_map/ppermute | solution.py:421
  13.5 5.0 %collective-permute-start.5 = (bf16[64,4096]{1,0:T(8,128)(2,1)}, bf16[64,4096]{1,0:T(8,128)(2,1)S(1)}, u32[]{:S(2)}, u32[]{:S(2)}) collective-permute-start(bf16[64,4096]{1,0:T(8,128)(2,1)} %refs_2_.1), channel_id=1, source_target_pairs={{0,1},{1,2},{2,3},{4,5},{5,6},{6,7},{8,9},{9,10},{10,11},{12,13},{... | collective-permute-start | bytes 1572872 | tf_op jit(solution)/shard_map/ppermute | solution.py:421
  18.7 3.5 %fetch.3.w_gate = bf16[4096,1024]{1,0:T(8,128)(2,1)S(1)} custom-call(bf16[4096,1024]{1,0:T(8,128)(2,1)} %source.3, s32[7]{0:T(128)S(1)} %stack.31.after.refs_8_.flags.deltas), custom_call_target="tpu_custom_call" | custom-call | bytes 16777216 | tf_op jit(solution)/shard_map/fetch/pallas_call | solution.py:244
  25.8 2.6 %collective-permute-start.6 = (bf16[64,4224]{1,0:T(8,128)(2,1)S(1)}, bf16[64,4224]{1,0:T(8,128)(2,1)S(1)}, u32[]{:S(2)}, u32[]{:S(2)}) collective-permute-start(bf16[64,4224]{1,0:T(8,128)(2,1)S(1)} %choose.2), channel_id=1, source_target_pairs={{0,1},{1,0},{2,3},{3,2},{4,5},{5,4},{6,7},{7,6},{8,9},{9,8},{10,11... | collective-permute-start | bytes 1622024 | tf_op jit(solution)/shard_map/ppermute | solution.py:428
  28.4 6.5 %collective-permute-done.3.first.v2 = bf16[64,4096]{1,0:T(8,128)(2,1)S(1)} collective-permute-done((bf16[64,4096]{1,0:T(8,128)(2,1)S(1)}, bf16[64,4096]{1,0:T(8,128)(2,1)S(1)}, u32[]{:S(2)}, u32[]{:S(2)}) %collective-permute-start.3) | collective-permute-done | bytes 524320 | tf_op jit(solution)/shard_map/ppermute | solution.py:421
  35.6 1.9 %collective-permute-done.7.v4 = bf16[64,4096]{1,0:T(8,128)(2,1)S(1)} collective-permute-done((bf16[64,4096]{1,0:T(8,128)(2,1)S(1)}, bf16[64,4096]{1,0:T(8,128)(2,1)S(1)}, u32[]{:S(2)}, u32[]{:S(2)}) %collective-permute-start.7) | collective-permute-done | bytes 524320 | tf_op jit(solution)/shard_map/ppermute | solution.py:428
  37.5 3.0 %attention.1 = (f32[64,4096]{1,0:T(8,128)S(1)}, bf16[20,4096]{1,0:T(8,128)(2,1)S(1)}, bf16[20,4096]{1,0:T(8,128)(2,1)S(1)}, bf16[2,64,32]{2,1,0:T(8,128)(2,1)S(1)}) custom-call(s32[7]{0:T(128)S(1)} %stack.31.after.refs_8_.flags.deltas, bf16[64,4096]{1,0:T(8,128)(2,1)S(1)} %get-tuple-element.75.q, bf16[64,4096]{1,0:T(8,128)(2,1)S(1)} %get-tuple-element.76.k0, ...), custom_call_target="tpu_custom_call" | custom-call | flops 335544320 | bytes 8388608 | tf_op jit(solution)/shard_map/attention/pallas_call | solution.py:178
  40.6 2.6 %collective-permute-start.11 = (bf16[20,4096]{1,0:T(8,128)(2,1)S(1)}, bf16[20,4096]{1,0:T(8,128)(2,1)S(1)}, u32[]{:S(2)}, u32[]{:S(2)}) collective-permute-start(bf16[20,4096]{1,0:T(8,128)(2,1)S(1)} %get-tuple-element.87), channel_id=1, source_target_pairs={{0,8},{1,9},{2,10},{3,11},{4,12},{5,13},{6,14},{7,15},{8,0},{9,1},... | collective-permute-start | bytes 491528 | tf_op jit(solution)/shard_map/ppermute | solution.py:475
  43.2 4.6 %collective-permute-start.8 = (bf16[20,4096]{1,0:T(8,128)(2,1)S(1)}, bf16[20,4096]{1,0:T(8,128)(2,1)S(1)}, u32[]{:S(2)}, u32[]{:S(2)}) collective-permute-start(bf16[20,4096]{1,0:T(8,128)(2,1)S(1)} %get-tuple-element.89.refs_0_), channel_id=1, source_target_pairs={{0,6},{1,7},{2,4},{3,5},{4,2},{5,3},{6,0},{7,1},{8,14},{9,15},{10,... | collective-permute-start | bytes 491528 | tf_op jit(solution)/shard_map/ppermute | solution.py:428
  47.8 3.5 %fetch.4.w_up = bf16[4096,1024]{1,0:T(8,128)(2,1)S(1)} custom-call(bf16[4096,1024]{1,0:T(8,128)(2,1)} %source.4, bf16[2,64,32]{2,1,0:T(8,128)(2,1)S(1)} %get-tuple-element.85.after.weight), custom_call_target="tpu_custom_call" | custom-call | bytes 16777216 | tf_op jit(solution)/shard_map/fetch/pallas_call | solution.py:244
  51.3 3.5 %fetch.5.w_down = bf16[1024,4096]{1,0:T(8,128)(2,1)S(1)} custom-call(bf16[1024,4096]{1,0:T(8,128)(2,1)} %source.5, bf16[2,64,32]{2,1,0:T(8,128)(2,1)S(1)} %get-tuple-element.85.after.weight), custom_call_target="tpu_custom_call" | custom-call | bytes 16777216 | tf_op jit(solution)/shard_map/fetch/pallas_call | solution.py:244
  55.1 2.0 %collective-permute-done.9.refs_2_ = bf16[20,4096]{1,0:T(8,128)(2,1)S(1)} collective-permute-done((bf16[20,4096]{1,0:T(8,128)(2,1)S(1)}, bf16[20,4096]{1,0:T(8,128)(2,1)S(1)}, u32[]{:S(2)}, u32[]{:S(2)}) %collective-permute-start.9) | collective-permute-done | bytes 163872 | tf_op jit(solution)/shard_map/ppermute | solution.py:428
  57.3 2.6 %collective-permute-start.12 = (bf16[20,4096]{1,0:T(8,128)(2,1)S(1)}, bf16[20,4096]{1,0:T(8,128)(2,1)S(1)}, u32[]{:S(2)}, u32[]{:S(2)}) collective-permute-start(bf16[20,4096]{1,0:T(8,128)(2,1)S(1)} %collective-permute-done.11.refs_0_), channel_id=1, source_target_pairs={{0,6},{1,7},{2,4},{3,5},{4,2},{5,3},{6,0},{7,1},{8,14},{9,15},{10,... | collective-permute-start | bytes 491528 | tf_op jit(solution)/shard_map/ppermute | solution.py:428
  60.9 4.2 %experts.2 = (bf16[80,4096]{1,0:T(8,128)(2,1)S(1)}, bf16[80,4096]{1,0:T(8,128)(2,1)S(1)}) custom-call(bf16[80,4096]{1,0:T(8,128)(2,1)S(1)} %pile.2.local, bf16[80,4096]{1,0:T(8,128)(2,1)S(1)} %collective-permute-done.15.remote, bf16[4096,1024]{1,0:T(8,128)(2,1)S(1)} %fetch.3.w_gate, bf16[4096,1024]{1,0:T(8,128)(2,1)S(1)} %fetch.4.w_up, ...), custom_call_target="tpu_custom_call" | custom-call | flops 4026531840 | bytes 2621440 | tf_op jit(solution)/shard_map/experts/pallas_call | solution.py:280
  66.0 4.0 %collective-permute-done.13.refs_2_ = bf16[20,4096]{1,0:T(8,128)(2,1)S(1)} collective-permute-done((bf16[20,4096]{1,0:T(8,128)(2,1)S(1)}, bf16[20,4096]{1,0:T(8,128)(2,1)S(1)}, u32[]{:S(2)}, u32[]{:S(2)}) %collective-permute-start.13) | collective-permute-done | bytes 163872 | tf_op jit(solution)/shard_map/ppermute | solution.py:428
  72.3 4.2 %experts.3 = (bf16[80,4096]{1,0:T(8,128)(2,1)S(1)}, bf16[80,4096]{1,0:T(8,128)(2,1)S(1)}) custom-call(bf16[80,4096]{1,0:T(8,128)(2,1)S(1)} %pile.3.local, bf16[80,4096]{1,0:T(8,128)(2,1)S(1)} %collective-permute-done.16.remote, bf16[4096,1024]{1,0:T(8,128)(2,1)S(1)} %fetch.3.w_gate, bf16[4096,1024]{1,0:T(8,128)(2,1)S(1)} %fetch.4.w_up, ...), custom_call_target="tpu_custom_call" | custom-call | flops 4026531840 | bytes 2621440 | tf_op jit(solution)/shard_map/experts/pallas_call | solution.py:280
  76.9 1.8 %collective-permute-done.17.second = bf16[80,4096]{1,0:T(8,128)(2,1)S(1)} collective-permute-done((bf16[80,4096]{1,0:T(8,128)(2,1)S(1)}, bf16[80,4096]{1,0:T(8,128)(2,1)S(1)}, u32[]{:S(2)}, u32[]{:S(2)}) %collective-permute-start.17) | collective-permute-done | bytes 655392 | tf_op jit(solution)/shard_map/ppermute | solution.py:428
  82.4 3.5 %collective-permute-done.19.refs_1_ = bf16[20,4096]{1,0:T(8,128)(2,1)S(1)} collective-permute-done((bf16[20,4096]{1,0:T(8,128)(2,1)S(1)}, bf16[20,4096]{1,0:T(8,128)(2,1)S(1)}, u32[]{:S(2)}, u32[]{:S(2)}) %collective-permute-start.19) | collective-permute-done | bytes 163872 | tf_op jit(solution)/shard_map/ppermute | solution.py:428
  85.9 2.3 %collective-permute-done.20.refs_2_ = bf16[20,4096]{1,0:T(8,128)(2,1)S(1)} collective-permute-done((bf16[20,4096]{1,0:T(8,128)(2,1)S(1)}, bf16[20,4096]{1,0:T(8,128)(2,1)S(1)}, u32[]{:S(2)}, u32[]{:S(2)}) %collective-permute-start.20) | collective-permute-done | bytes 163872 | tf_op jit(solution)/shard_map/ppermute | solution.py:428
  92.5 3.6 %collective-permute-start.25 = (bf16[20,4096]{1,0:T(8,128)(2,1)S(1)}, bf16[20,4096]{1,0:T(8,128)(2,1)S(1)}, u32[]{:S(2)}, u32[]{:S(2)}) collective-permute-start(bf16[20,4096]{1,0:T(8,128)(2,1)S(1)} %total.1), channel_id=1, source_target_pairs={{0,8},{1,9},{2,10},{3,11},{4,12},{5,13},{6,14},{7,15},{8,0},{9,1},... | collective-permute-start | bytes 491528 | tf_op jit(solution)/shard_map/ppermute | solution.py:506
  96.3 4.5 %collective-permute-done.22.refs_2_ = bf16[20,4096]{1,0:T(8,128)(2,1)S(1)} collective-permute-done((bf16[20,4096]{1,0:T(8,128)(2,1)S(1)}, bf16[20,4096]{1,0:T(8,128)(2,1)S(1)}, u32[]{:S(2)}, u32[]{:S(2)}) %collective-permute-start.22) | collective-permute-done | bytes 163872 | tf_op jit(solution)/shard_map/ppermute | solution.py:428
  100.8 3.1 %collective-permute-done.23.refs_3_ = bf16[20,4096]{1,0:T(8,128)(2,1)S(1)} collective-permute-done((bf16[20,4096]{1,0:T(8,128)(2,1)S(1)}, bf16[20,4096]{1,0:T(8,128)(2,1)S(1)}, u32[]{:S(2)}, u32[]{:S(2)}) %collective-permute-start.23) | collective-permute-done | bytes 163872 | tf_op jit(solution)/shard_map/ppermute | solution.py:428
  (46 shorter events, 22.6 us)
Async XLA Ops:
  1.1 11.2 %collective-permute-start.1 = (bf16[64,4224]{1,0:T(8,128)(2,1)S(1)}, bf16[64,4224]{1,0:T(8,128)(2,1)S(1)}, u32[]{:S(2)}, u32[]{:S(2)}) collective-permute-start(bf16[64,4224]{1,0:T(8,128)(2,1)S(1)} %bundle.1), channel_id=1, source_target_pairs={{0,3},{1,4},{2,1},{3,6},{4,7},{5,8},{6,5},{7,10},{8,11},{9,12},{10... | collective-permute-start | bytes 1622024 | tf_op jit(solution)/shard_map/ppermute | solution.py:421
  5.4 18.4 %collective-permute-start = (bf16[64,4096]{1,0:T(8,128)(2,1)}, bf16[64,4096]{1,0:T(8,128)(2,1)S(1)}, u32[]{:S(2)}, u32[]{:S(2)}) collective-permute-start(bf16[64,4096]{1,0:T(8,128)(2,1)} %refs_2_.1), channel_id=1, source_target_pairs={{0,3},{1,4},{2,1},{3,6},{4,7},{5,8},{6,5},{7,10},{8,11},{9,12},{10... | collective-permute-start | bytes 1572872 | tf_op jit(solution)/shard_map/ppermute | solution.py:421
  9.2 16.0 %collective-permute-start.4 = (bf16[64,4224]{1,0:T(8,128)(2,1)S(1)}, bf16[64,4224]{1,0:T(8,128)(2,1)S(1)}, u32[]{:S(2)}, u32[]{:S(2)}) collective-permute-start(bf16[64,4224]{1,0:T(8,128)(2,1)S(1)} %bundle.1), channel_id=1, source_target_pairs={{0,1},{1,2},{2,3},{4,5},{5,6},{6,7},{8,9},{9,10},{10,11},{12,13},{... | collective-permute-start | bytes 1622024 | tf_op jit(solution)/shard_map/ppermute | solution.py:421
  12.3 12.9 %collective-permute-start.2 = (bf16[64,4224]{1,0:T(8,128)(2,1)S(1)}, bf16[64,4224]{1,0:T(8,128)(2,1)S(1)}, u32[]{:S(2)}, u32[]{:S(2)}) collective-permute-start(bf16[64,4224]{1,0:T(8,128)(2,1)S(1)} %collective-permute-done.1.third.k1), channel_id=1, source_target_pairs={{1,5},{2,0},{5,9},{6,4},{9,13},{10,8},{14,12},{17,21},{18,16},{21,... | collective-permute-start | bytes 1622024 | tf_op jit(solution)/shard_map/ppermute | solution.py:421
  13.5 14.9 %collective-permute-start.5 = (bf16[64,4096]{1,0:T(8,128)(2,1)}, bf16[64,4096]{1,0:T(8,128)(2,1)S(1)}, u32[]{:S(2)}, u32[]{:S(2)}) collective-permute-start(bf16[64,4096]{1,0:T(8,128)(2,1)} %refs_2_.1), channel_id=1, source_target_pairs={{0,1},{1,2},{2,3},{4,5},{5,6},{6,7},{8,9},{9,10},{10,11},{12,13},{... | collective-permute-start | bytes 1572872 | tf_op jit(solution)/shard_map/ppermute | solution.py:421
  23.9 11.1 %collective-permute-start.3 = (bf16[64,4096]{1,0:T(8,128)(2,1)S(1)}, bf16[64,4096]{1,0:T(8,128)(2,1)S(1)}, u32[]{:S(2)}, u32[]{:S(2)}) collective-permute-start(bf16[64,4096]{1,0:T(8,128)(2,1)S(1)} %collective-permute-done.third.v1), channel_id=1, source_target_pairs={{1,5},{2,0},{5,9},{6,4},{9,13},{10,8},{14,12},{17,21},{18,16},{21,... | collective-permute-start | bytes 1572872 | tf_op jit(solution)/shard_map/ppermute | solution.py:421
  25.8 11.7 %collective-permute-start.6 = (bf16[64,4224]{1,0:T(8,128)(2,1)S(1)}, bf16[64,4224]{1,0:T(8,128)(2,1)S(1)}, u32[]{:S(2)}, u32[]{:S(2)}) collective-permute-start(bf16[64,4224]{1,0:T(8,128)(2,1)S(1)} %choose.2), channel_id=1, source_target_pairs={{0,1},{1,0},{2,3},{3,2},{4,5},{5,4},{6,7},{7,6},{8,9},{9,8},{10,11... | collective-permute-start | bytes 1622024 | tf_op jit(solution)/shard_map/ppermute | solution.py:428
  40.5 14.3 %collective-permute-start.10 = (bf16[20,4096]{1,0:T(8,128)(2,1)S(1)}, bf16[20,4096]{1,0:T(8,128)(2,1)S(1)}, u32[]{:S(2)}, u32[]{:S(2)}) collective-permute-start(bf16[20,4096]{1,0:T(8,128)(2,1)S(1)} %get-tuple-element.89.refs_0_), channel_id=1, source_target_pairs={{0,2},{1,3},{2,0},{3,1},{4,6},{5,7},{6,4},{7,5},{8,10},{9,11},{10,... | collective-permute-start | bytes 491528 | tf_op jit(solution)/shard_map/ppermute | solution.py:428
  40.6 14.3 %collective-permute-start.11 = (bf16[20,4096]{1,0:T(8,128)(2,1)S(1)}, bf16[20,4096]{1,0:T(8,128)(2,1)S(1)}, u32[]{:S(2)}, u32[]{:S(2)}) collective-permute-start(bf16[20,4096]{1,0:T(8,128)(2,1)S(1)} %get-tuple-element.87), channel_id=1, source_target_pairs={{0,8},{1,9},{2,10},{3,11},{4,12},{5,13},{6,14},{7,15},{8,0},{9,1},... | collective-permute-start | bytes 491528 | tf_op jit(solution)/shard_map/ppermute | solution.py:475
  43.2 11.9 %collective-permute-start.8 = (bf16[20,4096]{1,0:T(8,128)(2,1)S(1)}, bf16[20,4096]{1,0:T(8,128)(2,1)S(1)}, u32[]{:S(2)}, u32[]{:S(2)}) collective-permute-start(bf16[20,4096]{1,0:T(8,128)(2,1)S(1)} %get-tuple-element.89.refs_0_), channel_id=1, source_target_pairs={{0,6},{1,7},{2,4},{3,5},{4,2},{5,3},{6,0},{7,1},{8,14},{9,15},{10,... | collective-permute-start | bytes 491528 | tf_op jit(solution)/shard_map/ppermute | solution.py:428
  47.8 9.3 %collective-permute-start.9 = (bf16[20,4096]{1,0:T(8,128)(2,1)S(1)}, bf16[20,4096]{1,0:T(8,128)(2,1)S(1)}, u32[]{:S(2)}, u32[]{:S(2)}) collective-permute-start(bf16[20,4096]{1,0:T(8,128)(2,1)S(1)} %get-tuple-element.89.refs_0_), channel_id=1, source_target_pairs={{0,4},{1,5},{2,6},{3,7},{4,0},{5,1},{6,2},{7,3},{8,12},{9,13},{10,... | collective-permute-start | bytes 491528 | tf_op jit(solution)/shard_map/ppermute | solution.py:428
  57.2 3.6 %collective-permute-start.15 = (bf16[80,4096]{1,0:T(8,128)(2,1)S(1)}, bf16[80,4096]{1,0:T(8,128)(2,1)S(1)}, u32[]{:S(2)}, u32[]{:S(2)}) collective-permute-start(bf16[80,4096]{1,0:T(8,128)(2,1)S(1)} %pile.2.local), channel_id=1, source_target_pairs={{0,1},{1,0},{2,3},{3,2},{4,5},{5,4},{6,7},{7,6},{8,9},{9,8},{10,11... | collective-permute-start | bytes 1966088 | tf_op jit(solution)/shard_map/ppermute | solution.py:428
  57.3 8.7 %collective-permute-start.12 = (bf16[20,4096]{1,0:T(8,128)(2,1)S(1)}, bf16[20,4096]{1,0:T(8,128)(2,1)S(1)}, u32[]{:S(2)}, u32[]{:S(2)}) collective-permute-start(bf16[20,4096]{1,0:T(8,128)(2,1)S(1)} %collective-permute-done.11.refs_0_), channel_id=1, source_target_pairs={{0,6},{1,7},{2,4},{3,5},{4,2},{5,3},{6,0},{7,1},{8,14},{9,15},{10,... | collective-permute-start | bytes 491528 | tf_op jit(solution)/shard_map/ppermute | solution.py:428
  60.0 10.0 %collective-permute-start.13 = (bf16[20,4096]{1,0:T(8,128)(2,1)S(1)}, bf16[20,4096]{1,0:T(8,128)(2,1)S(1)}, u32[]{:S(2)}, u32[]{:S(2)}) collective-permute-start(bf16[20,4096]{1,0:T(8,128)(2,1)S(1)} %collective-permute-done.11.refs_0_), channel_id=1, source_target_pairs={{0,4},{1,5},{2,6},{3,7},{4,0},{5,1},{6,2},{7,3},{8,12},{9,13},{10,... | collective-permute-start | bytes 491528 | tf_op jit(solution)/shard_map/ppermute | solution.py:428
  60.5 9.5 %collective-permute-start.14 = (bf16[20,4096]{1,0:T(8,128)(2,1)S(1)}, bf16[20,4096]{1,0:T(8,128)(2,1)S(1)}, u32[]{:S(2)}, u32[]{:S(2)}) collective-permute-start(bf16[20,4096]{1,0:T(8,128)(2,1)S(1)} %collective-permute-done.11.refs_0_), channel_id=1, source_target_pairs={{0,2},{1,3},{2,0},{3,1},{4,6},{5,7},{6,4},{7,5},{8,10},{9,11},{10,... | collective-permute-start | bytes 491528 | tf_op jit(solution)/shard_map/ppermute | solution.py:428
  70.1 2.2 %collective-permute-start.16 = (bf16[80,4096]{1,0:T(8,128)(2,1)S(1)}, bf16[80,4096]{1,0:T(8,128)(2,1)S(1)}, u32[]{:S(2)}, u32[]{:S(2)}) collective-permute-start(bf16[80,4096]{1,0:T(8,128)(2,1)S(1)} %pile.3.local), channel_id=1, source_target_pairs={{0,1},{1,0},{2,3},{3,2},{4,5},{5,4},{6,7},{7,6},{8,9},{9,8},{10,11... | collective-permute-start | bytes 1966088 | tf_op jit(solution)/shard_map/ppermute | solution.py:428
  70.2 6.5 %collective-permute-start.18 = (bf16[80,4096]{1,0:T(8,128)(2,1)S(1)}, bf16[80,4096]{1,0:T(8,128)(2,1)S(1)}, u32[]{:S(2)}, u32[]{:S(2)}) collective-permute-start(bf16[80,4096]{1,0:T(8,128)(2,1)S(1)} %get-tuple-element.109), channel_id=1, source_target_pairs={{0,1},{1,0},{2,3},{3,2},{4,5},{5,4},{6,7},{7,6},{8,9},{9,8},{10,11... | collective-permute-start | bytes 1966088 | tf_op jit(solution)/shard_map/ppermute | solution.py:428
  78.9 7.0 %collective-permute-start.19 = (bf16[20,4096]{1,0:T(8,128)(2,1)S(1)}, bf16[20,4096]{1,0:T(8,128)(2,1)S(1)}, u32[]{:S(2)}, u32[]{:S(2)}) collective-permute-start(bf16[20,4096]{1,0:T(8,128)(2,1)S(1)} %get-tuple-element.115), channel_id=1, source_target_pairs={{0,2},{1,3},{2,0},{3,1},{4,6},{5,7},{6,4},{7,5},{8,10},{9,11},{10,... | collective-permute-start | bytes 491528 | tf_op jit(solution)/shard_map/ppermute | solution.py:428
  80.4 7.8 %collective-permute-start.20 = (bf16[20,4096]{1,0:T(8,128)(2,1)S(1)}, bf16[20,4096]{1,0:T(8,128)(2,1)S(1)}, u32[]{:S(2)}, u32[]{:S(2)}) collective-permute-start(bf16[20,4096]{1,0:T(8,128)(2,1)S(1)} %get-tuple-element.116), channel_id=1, source_target_pairs={{0,4},{1,5},{2,6},{3,7},{4,0},{5,1},{6,2},{7,3},{8,12},{9,13},{10,... | collective-permute-start | bytes 491528 | tf_op jit(solution)/shard_map/ppermute | solution.py:428
  81.8 10.6 %collective-permute-start.24 = (bf16[20,4096]{1,0:T(8,128)(2,1)S(1)}, bf16[20,4096]{1,0:T(8,128)(2,1)S(1)}, u32[]{:S(2)}, u32[]{:S(2)}) collective-permute-start(bf16[20,4096]{1,0:T(8,128)(2,1)S(1)} %get-tuple-element.128), channel_id=1, source_target_pairs={{0,6},{1,7},{2,4},{3,5},{4,2},{5,3},{6,0},{7,1},{8,14},{9,15},{10,... | collective-permute-start | bytes 491528 | tf_op jit(solution)/shard_map/ppermute | solution.py:428
  88.2 8.2 %collective-permute-start.21 = (bf16[20,4096]{1,0:T(8,128)(2,1)S(1)}, bf16[20,4096]{1,0:T(8,128)(2,1)S(1)}, u32[]{:S(2)}, u32[]{:S(2)}) collective-permute-start(bf16[20,4096]{1,0:T(8,128)(2,1)S(1)} %get-tuple-element.122), channel_id=1, source_target_pairs={{0,2},{1,3},{2,0},{3,1},{4,6},{5,7},{6,4},{7,5},{8,10},{9,11},{10,... | collective-permute-start | bytes 491528 | tf_op jit(solution)/shard_map/ppermute | solution.py:428
  88.8 12.1 %collective-permute-start.22 = (bf16[20,4096]{1,0:T(8,128)(2,1)S(1)}, bf16[20,4096]{1,0:T(8,128)(2,1)S(1)}, u32[]{:S(2)}, u32[]{:S(2)}) collective-permute-start(bf16[20,4096]{1,0:T(8,128)(2,1)S(1)} %get-tuple-element.123), channel_id=1, source_target_pairs={{0,4},{1,5},{2,6},{3,7},{4,0},{5,1},{6,2},{7,3},{8,12},{9,13},{10,... | collective-permute-start | bytes 491528 | tf_op jit(solution)/shard_map/ppermute | solution.py:428
  90.2 13.7 %collective-permute-start.23 = (bf16[20,4096]{1,0:T(8,128)(2,1)S(1)}, bf16[20,4096]{1,0:T(8,128)(2,1)S(1)}, u32[]{:S(2)}, u32[]{:S(2)}) collective-permute-start(bf16[20,4096]{1,0:T(8,128)(2,1)S(1)} %get-tuple-element.124), channel_id=1, source_target_pairs={{0,6},{1,7},{2,4},{3,5},{4,2},{5,3},{6,0},{7,1},{8,14},{9,15},{10,... | collective-permute-start | bytes 491528 | tf_op jit(solution)/shard_map/ppermute | solution.py:428
  92.5 11.7 %collective-permute-start.25 = (bf16[20,4096]{1,0:T(8,128)(2,1)S(1)}, bf16[20,4096]{1,0:T(8,128)(2,1)S(1)}, u32[]{:S(2)}, u32[]{:S(2)}) collective-permute-start(bf16[20,4096]{1,0:T(8,128)(2,1)S(1)} %total.1), channel_id=1, source_target_pairs={{0,8},{1,9},{2,10},{3,11},{4,12},{5,13},{6,14},{7,15},{8,0},{9,1},... | collective-permute-start | bytes 491528 | tf_op jit(solution)/shard_map/ppermute | solution.py:506
  (2 other events, 4.1 us)

commit v16 on v15

--- a/solution.py
+++ b/solution.py
@@ -452,9 +452,8 @@
         ],
         scalars,
     )
-    gate_held = fetch(w_gate, scalars)
     key_two = moved(key_one, passed)
-    value_one, gate_held, mine = lax.optimization_barrier((value_one, gate_held, mine))
+    value_one, mine = lax.optimization_barrier((value_one, mine))
     value_two = moved(value_one, passed)
     key_four = swapped(choose(scalars, [key_two, key_three, key_one]), 1)
     value_four = swapped(choose(scalars, [value_two, value_three, value_one]), 1)
@@ -469,7 +468,7 @@
         ],
         seg_own, resid, gain, routes_held, gates_held,
     )
-    up_held, down_held = fetch(w_up, weight), fetch(w_down, weight)
+    gate_held, up_held = fetch(w_gate, weight), fetch(w_up, weight)
     partner = [(i, (i + shard_count) % count) for i in range(count)]
     masks = list(range(2, shard_count, 2))[::-1]
     got = lax.ppermute(send, "expert", partner)
@@ -489,11 +488,12 @@
         return [blocks[0]] + moved[::-1]
 
     early_blocks = spread(keep)
-    early_blocks, got, up_held, down_held = lax.optimization_barrier(
-        (early_blocks, got, up_held, down_held)
-    )
-    held = [gate_held, up_held, down_held]
-    early_parts = experts(*both_cores(early_blocks), *held)
+    early_blocks, got, gate_held, up_held = lax.optimization_barrier(
+        (early_blocks, got, gate_held, up_held)
+    )
+    early_rows = both_cores(early_blocks)
+    held = [gate_held, up_held, fetch(w_down, early_rows[1])]
+    early_parts = experts(*early_rows, *held)
     late_blocks = spread(got)
     late_blocks, early_parts = lax.optimization_barrier((late_blocks, early_parts))
     late_blocks = summed(experts(*both_cores(late_blocks), *held))

time: 106 us -> 105 us (level)
  starting transfers between devices: 42.4 us -> 40.3 us
  waiting for transfers between devices: 34.6 us -> 36.5 us
    ppermute x6, waiting for transfers between devices: 7.83 us -> 13.7 us  [moved(): lax.ppermute(block, 'expert', [pair for pair in pairs if pair[1] < count])]
    ppermute x18, waiting for transfers between devices: 26.7 us -> 22.8 us  [swapped(): return lax.ppermute(block, 'expert', [(i, i ^ mask) for i in range(count)])]
    ppermute x18, starting transfers between devices: 18.8 us -> 16.4 us  [swapped(): return lax.ppermute(block, 'expert', [(i, i ^ mask) for i in range(count)])]
where the time goes in v16:
time: 105 us
  starting transfers between devices  40.3 us (38%)
  waiting for transfers between devices  36.5 us (35%)
  Pallas kernels  27.8 us (26%)
    ppermute x18, waiting for transfers between devices, swapped(): return lax.ppermute(block, 'expert', [(i, i ^ mask) for i in range(count)])  22.8 us
    ppermute x6, starting transfers between devices, moved(): lax.ppermute(block, 'expert', [pair for pair in pairs if pair[1] < count])  17.4 us
    ppermute x18, starting transfers between devices, swapped(): return lax.ppermute(block, 'expert', [(i, i ^ mask) for i in range(count)])  16.4 us
    ppermute x6, waiting for transfers between devices, moved(): lax.ppermute(block, 'expert', [pair for pair in pairs if pair[1] < count])  13.7 us
    pallas_call x3, Pallas kernels, fetch(): pl.pallas_call(functools.partial(fetch_kernel, parts), in_specs=[anywhere...  10.5 us
    pallas_call x2, Pallas kernels, experts(): pl.pallas_call(experts_kernel, in_specs=[NEAR] * 5, out_specs=[NEAR] * 2,...  8.47 us
    ppermute x1, starting transfers between devices, shards(): other = lax.ppermute(back, 'expert', partner)  3.78 us
    pallas_call x1, Pallas kernels, attention(): pl.pallas_call(attention_kernel, in_specs=[pl.BlockSpec(memory_space=pltp...  3 us
  transfers between devices with their start and end apart: 26, of which 15 were waited for; matrix products, arithmetic and copies ran while one was open for 0% of the time, Pallas kernels for 21%

profile of v16, /device:TPU:0, one launch (start us, length us, event | category | flops | bytes accessed | tf_op | source)
XLA Modules:
  0.0 105.0 jit_solution(1803371482698147566)
XLA Ops:
  1.1 4.3 %collective-permute-start.1 = (bf16[64,4224]{1,0:T(8,128)(2,1)S(1)}, bf16[64,4224]{1,0:T(8,128)(2,1)S(1)}, u32[]{:S(2)}, u32[]{:S(2)}) collective-permute-start(bf16[64,4224]{1,0:T(8,128)(2,1)S(1)} %bundle.1), channel_id=1, source_target_pairs={{0,3},{1,4},{2,1},{3,6},{4,7},{5,8},{6,5},{7,10},{8,11},{9,12},{10... | collective-permute-start | bytes 1622024 | tf_op jit(solution)/shard_map/ppermute | solution.py:421
  5.4 3.8 %collective-permute-start = (bf16[64,4096]{1,0:T(8,128)(2,1)}, bf16[64,4096]{1,0:T(8,128)(2,1)S(1)}, u32[]{:S(2)}, u32[]{:S(2)}) collective-permute-start(bf16[64,4096]{1,0:T(8,128)(2,1)} %refs_2_.1), channel_id=1, source_target_pairs={{0,3},{1,4},{2,1},{3,6},{4,7},{5,8},{6,5},{7,10},{8,11},{9,12},{10... | collective-permute-start | bytes 1572872 | tf_op jit(solution)/shard_map/ppermute | solution.py:421
  9.2 1.7 %collective-permute-start.4 = (bf16[64,4224]{1,0:T(8,128)(2,1)S(1)}, bf16[64,4224]{1,0:T(8,128)(2,1)S(1)}, u32[]{:S(2)}, u32[]{:S(2)}) collective-permute-start(bf16[64,4224]{1,0:T(8,128)(2,1)S(1)} %bundle.1), channel_id=1, source_target_pairs={{0,1},{1,2},{2,3},{4,5},{5,6},{6,7},{8,9},{9,10},{10,11},{12,13},{... | collective-permute-start | bytes 1622024 | tf_op jit(solution)/shard_map/ppermute | solution.py:421
  13.5 5.0 %collective-permute-start.5 = (bf16[64,4096]{1,0:T(8,128)(2,1)}, bf16[64,4096]{1,0:T(8,128)(2,1)S(1)}, u32[]{:S(2)}, u32[]{:S(2)}) collective-permute-start(bf16[64,4096]{1,0:T(8,128)(2,1)} %refs_2_.1), channel_id=1, source_target_pairs={{0,1},{1,2},{2,3},{4,5},{5,6},{6,7},{8,9},{9,10},{10,11},{12,13},{... | collective-permute-start | bytes 1572872 | tf_op jit(solution)/shard_map/ppermute | solution.py:421
  18.7 1.6 %bring.1 = (bf16[64,4096]{1,0:T(8,128)(2,1)S(1)}, bf16[64,4096]{1,0:T(8,128)(2,1)S(1)}, bf16[64,4096]{1,0:T(8,128)(2,1)S(1)}, s32[1,64]{1,0:T(1,128)S(1)}, bf16[...) custom-call(bf16[64,4096]{1,0:T(8,128)(2,1)} %refs_0_.1, ...), custom_call_target="tpu_custom_call" | custom-call | bytes 4211968 | tf_op jit(solution)/shard_map/bring/pallas_call | solution.py:215
  20.3 3.3 %collective-permute-done.third.v1 = bf16[64,4096]{1,0:T(8,128)(2,1)S(1)} collective-permute-done((bf16[64,4096]{1,0:T(8,128)(2,1)}, bf16[64,4096]{1,0:T(8,128)(2,1)S(1)}, u32[]{:S(2)}, u32[]{:S(2)}) %collective-permute-start) | collective-permute-done | bytes 524320 | tf_op jit(solution)/shard_map/ppermute | solution.py:421
  25.7 9.1 %collective-permute-done.3.first.v2 = bf16[64,4096]{1,0:T(8,128)(2,1)S(1)} collective-permute-done((bf16[64,4096]{1,0:T(8,128)(2,1)S(1)}, bf16[64,4096]{1,0:T(8,128)(2,1)S(1)}, u32[]{:S(2)}, u32[]{:S(2)}) %collective-permute-start.3) | collective-permute-done | bytes 524320 | tf_op jit(solution)/shard_map/ppermute | solution.py:421
  35.4 1.9 %collective-permute-done.7.v4 = bf16[64,4096]{1,0:T(8,128)(2,1)S(1)} collective-permute-done((bf16[64,4096]{1,0:T(8,128)(2,1)S(1)}, bf16[64,4096]{1,0:T(8,128)(2,1)S(1)}, u32[]{:S(2)}, u32[]{:S(2)}) %collective-permute-start.7) | collective-permute-done | bytes 524320 | tf_op jit(solution)/shard_map/ppermute | solution.py:428
  37.3 3.0 %attention.1 = (f32[64,4096]{1,0:T(8,128)S(1)}, bf16[20,4096]{1,0:T(8,128)(2,1)S(1)}, bf16[20,4096]{1,0:T(8,128)(2,1)S(1)}, bf16[2,64,32]{2,1,0:T(8,128)(2,1)S(1)}) custom-call(s32[7]{0:T(128)S(1)} %stack.31.refs_8_.flags.deltas, bf16[64,4096]{1,0:T(8,128)(2,1)S(1)} %get-tuple-element.74.q, bf16[64,4096]{1,0:T(8,128)(2,1)S(1)} %get-tuple-element.75.k0, ...), custom_call_target="tpu_custom_call" | custom-call | flops 335544320 | bytes 8388608 | tf_op jit(solution)/shard_map/attention/pallas_call | solution.py:178
  40.4 2.7 %collective-permute-start.11 = (bf16[20,4096]{1,0:T(8,128)(2,1)S(1)}, bf16[20,4096]{1,0:T(8,128)(2,1)S(1)}, u32[]{:S(2)}, u32[]{:S(2)}) collective-permute-start(bf16[20,4096]{1,0:T(8,128)(2,1)S(1)} %get-tuple-element.86), channel_id=1, source_target_pairs={{0,8},{1,9},{2,10},{3,11},{4,12},{5,13},{6,14},{7,15},{8,0},{9,1},... | collective-permute-start | bytes 491528 | tf_op jit(solution)/shard_map/ppermute | solution.py:474
  43.1 4.7 %collective-permute-start.8 = (bf16[20,4096]{1,0:T(8,128)(2,1)S(1)}, bf16[20,4096]{1,0:T(8,128)(2,1)S(1)}, u32[]{:S(2)}, u32[]{:S(2)}) collective-permute-start(bf16[20,4096]{1,0:T(8,128)(2,1)S(1)} %get-tuple-element.88.refs_0_), channel_id=1, source_target_pairs={{0,6},{1,7},{2,4},{3,5},{4,2},{5,3},{6,0},{7,1},{8,14},{9,15},{10,... | collective-permute-start | bytes 491528 | tf_op jit(solution)/shard_map/ppermute | solution.py:428
  47.8 3.5 %fetch.3.w_gate = bf16[4096,1024]{1,0:T(8,128)(2,1)S(1)} custom-call(bf16[4096,1024]{1,0:T(8,128)(2,1)} %source.3, bf16[2,64,32]{2,1,0:T(8,128)(2,1)S(1)} %get-tuple-element.84.after.weight), custom_call_target="tpu_custom_call" | custom-call | bytes 16777216 | tf_op jit(solution)/shard_map/fetch/pallas_call | solution.py:244
  51.3 3.5 %fetch.4.w_up = bf16[4096,1024]{1,0:T(8,128)(2,1)S(1)} custom-call(bf16[4096,1024]{1,0:T(8,128)(2,1)} %source.4, bf16[2,64,32]{2,1,0:T(8,128)(2,1)S(1)} %get-tuple-element.84.after.weight), custom_call_target="tpu_custom_call" | custom-call | bytes 16777216 | tf_op jit(solution)/shard_map/fetch/pallas_call | solution.py:244
  54.9 2.0 %collective-permute-done.9.refs_2_ = bf16[20,4096]{1,0:T(8,128)(2,1)S(1)} collective-permute-done((bf16[20,4096]{1,0:T(8,128)(2,1)S(1)}, bf16[20,4096]{1,0:T(8,128)(2,1)S(1)}, u32[]{:S(2)}, u32[]{:S(2)}) %collective-permute-start.9) | collective-permute-done | bytes 163872 | tf_op jit(solution)/shard_map/ppermute | solution.py:428
  57.1 2.7 %collective-permute-start.12 = (bf16[20,4096]{1,0:T(8,128)(2,1)S(1)}, bf16[20,4096]{1,0:T(8,128)(2,1)S(1)}, u32[]{:S(2)}, u32[]{:S(2)}) collective-permute-start(bf16[20,4096]{1,0:T(8,128)(2,1)S(1)} %collective-permute-done.11.refs_0_), channel_id=1, source_target_pairs={{0,6},{1,7},{2,4},{3,5},{4,2},{5,3},{6,0},{7,1},{8,14},{9,15},{10,... | collective-permute-start | bytes 491528 | tf_op jit(solution)/shard_map/ppermute | solution.py:428
  60.7 3.5 %fetch.5.w_down = bf16[1024,4096]{1,0:T(8,128)(2,1)S(1)} custom-call(bf16[1024,4096]{1,0:T(8,128)(2,1)} %source.5, bf16[80,4096]{1,0:T(8,128)(2,1)S(1)} %collective-permute-done.15.after.remote), custom_call_target="tpu_custom_call" | custom-call | bytes 16777216 | tf_op jit(solution)/shard_map/fetch/pallas_call | solution.py:244
  64.2 4.2 %experts.2 = (bf16[80,4096]{1,0:T(8,128)(2,1)S(1)}, bf16[80,4096]{1,0:T(8,128)(2,1)S(1)}) custom-call(bf16[80,4096]{1,0:T(8,128)(2,1)S(1)} %pile.2.local, bf16[80,4096]{1,0:T(8,128)(2,1)S(1)} %collective-permute-done.15.after.remote, bf16[4096,1024]{1,0:T(8,128)(2,1)S(1)} %fetch.3.w_gate, bf16[4096,1024]{1,0:T(8,128)(2,1)S(1)} %fetch.4.w_up, ...), custom_call_target="tpu_custom_call" | custom-call | flops 4026531840 | bytes 2621440 | tf_op jit(solution)/shard_map/experts/pallas_call | solution.py:280
  72.1 4.2 %experts.3 = (bf16[80,4096]{1,0:T(8,128)(2,1)S(1)}, bf16[80,4096]{1,0:T(8,128)(2,1)S(1)}) custom-call(bf16[80,4096]{1,0:T(8,128)(2,1)S(1)} %pile.3.local, bf16[80,4096]{1,0:T(8,128)(2,1)S(1)} %collective-permute-done.16.remote, bf16[4096,1024]{1,0:T(8,128)(2,1)S(1)} %fetch.3.w_gate, bf16[4096,1024]{1,0:T(8,128)(2,1)S(1)} %fetch.4.w_up, ...), custom_call_target="tpu_custom_call" | custom-call | flops 4026531840 | bytes 2621440 | tf_op jit(solution)/shard_map/experts/pallas_call | solution.py:280
  76.7 1.8 %collective-permute-done.17.second = bf16[80,4096]{1,0:T(8,128)(2,1)S(1)} collective-permute-done((bf16[80,4096]{1,0:T(8,128)(2,1)S(1)}, bf16[80,4096]{1,0:T(8,128)(2,1)S(1)}, u32[]{:S(2)}, u32[]{:S(2)}) %collective-permute-start.17) | collective-permute-done | bytes 655392 | tf_op jit(solution)/shard_map/ppermute | solution.py:428
  82.2 3.5 %collective-permute-done.19.refs_1_ = bf16[20,4096]{1,0:T(8,128)(2,1)S(1)} collective-permute-done((bf16[20,4096]{1,0:T(8,128)(2,1)S(1)}, bf16[20,4096]{1,0:T(8,128)(2,1)S(1)}, u32[]{:S(2)}, u32[]{:S(2)}) %collective-permute-start.19) | collective-permute-done | bytes 163872 | tf_op jit(solution)/shard_map/ppermute | solution.py:428
  85.7 2.3 %collective-permute-done.20.refs_2_ = bf16[20,4096]{1,0:T(8,128)(2,1)S(1)} collective-permute-done((bf16[20,4096]{1,0:T(8,128)(2,1)S(1)}, bf16[20,4096]{1,0:T(8,128)(2,1)S(1)}, u32[]{:S(2)}, u32[]{:S(2)}) %collective-permute-start.20) | collective-permute-done | bytes 163872 | tf_op jit(solution)/shard_map/ppermute | solution.py:428
  92.3 3.8 %collective-permute-start.25 = (bf16[20,4096]{1,0:T(8,128)(2,1)S(1)}, bf16[20,4096]{1,0:T(8,128)(2,1)S(1)}, u32[]{:S(2)}, u32[]{:S(2)}) collective-permute-start(bf16[20,4096]{1,0:T(8,128)(2,1)S(1)} %total.1), channel_id=1, source_target_pairs={{0,8},{1,9},{2,10},{3,11},{4,12},{5,13},{6,14},{7,15},{8,0},{9,1},... | collective-permute-start | bytes 491528 | tf_op jit(solution)/shard_map/ppermute | solution.py:506
  96.2 4.4 %collective-permute-done.22.refs_2_ = bf16[20,4096]{1,0:T(8,128)(2,1)S(1)} collective-permute-done((bf16[20,4096]{1,0:T(8,128)(2,1)S(1)}, bf16[20,4096]{1,0:T(8,128)(2,1)S(1)}, u32[]{:S(2)}, u32[]{:S(2)}) %collective-permute-start.22) | collective-permute-done | bytes 163872 | tf_op jit(solution)/shard_map/ppermute | solution.py:428
  100.6 3.1 %collective-permute-done.23.refs_3_ = bf16[20,4096]{1,0:T(8,128)(2,1)S(1)} collective-permute-done((bf16[20,4096]{1,0:T(8,128)(2,1)S(1)}, bf16[20,4096]{1,0:T(8,128)(2,1)S(1)}, u32[]{:S(2)}, u32[]{:S(2)}) %collective-permute-start.23) | collective-permute-done | bytes 163872 | tf_op jit(solution)/shard_map/ppermute | solution.py:428
  (46 shorter events, 21.1 us)
Async XLA Ops:
  1.1 11.2 %collective-permute-start.1 = (bf16[64,4224]{1,0:T(8,128)(2,1)S(1)}, bf16[64,4224]{1,0:T(8,128)(2,1)S(1)}, u32[]{:S(2)}, u32[]{:S(2)}) collective-permute-start(bf16[64,4224]{1,0:T(8,128)(2,1)S(1)} %bundle.1), channel_id=1, source_target_pairs={{0,3},{1,4},{2,1},{3,6},{4,7},{5,8},{6,5},{7,10},{8,11},{9,12},{10... | collective-permute-start | bytes 1622024 | tf_op jit(solution)/shard_map/ppermute | solution.py:421
  5.4 18.2 %collective-permute-start = (bf16[64,4096]{1,0:T(8,128)(2,1)}, bf16[64,4096]{1,0:T(8,128)(2,1)S(1)}, u32[]{:S(2)}, u32[]{:S(2)}) collective-permute-start(bf16[64,4096]{1,0:T(8,128)(2,1)} %refs_2_.1), channel_id=1, source_target_pairs={{0,3},{1,4},{2,1},{3,6},{4,7},{5,8},{6,5},{7,10},{8,11},{9,12},{10... | collective-permute-start | bytes 1572872 | tf_op jit(solution)/shard_map/ppermute | solution.py:421
  9.2 15.8 %collective-permute-start.4 = (bf16[64,4224]{1,0:T(8,128)(2,1)S(1)}, bf16[64,4224]{1,0:T(8,128)(2,1)S(1)}, u32[]{:S(2)}, u32[]{:S(2)}) collective-permute-start(bf16[64,4224]{1,0:T(8,128)(2,1)S(1)} %bundle.1), channel_id=1, source_target_pairs={{0,1},{1,2},{2,3},{4,5},{5,6},{6,7},{8,9},{9,10},{10,11},{12,13},{... | collective-permute-start | bytes 1622024 | tf_op jit(solution)/shard_map/ppermute | solution.py:421
  12.3 12.7 %collective-permute-start.2 = (bf16[64,4224]{1,0:T(8,128)(2,1)S(1)}, bf16[64,4224]{1,0:T(8,128)(2,1)S(1)}, u32[]{:S(2)}, u32[]{:S(2)}) collective-permute-start(bf16[64,4224]{1,0:T(8,128)(2,1)S(1)} %collective-permute-done.1.third.k1), channel_id=1, source_target_pairs={{1,5},{2,0},{5,9},{6,4},{9,13},{10,8},{14,12},{17,21},{18,16},{21,... | collective-permute-start | bytes 1622024 | tf_op jit(solution)/shard_map/ppermute | solution.py:421
  13.5 12.1 %collective-permute-start.5 = (bf16[64,4096]{1,0:T(8,128)(2,1)}, bf16[64,4096]{1,0:T(8,128)(2,1)S(1)}, u32[]{:S(2)}, u32[]{:S(2)}) collective-permute-start(bf16[64,4096]{1,0:T(8,128)(2,1)} %refs_2_.1), channel_id=1, source_target_pairs={{0,1},{1,2},{2,3},{4,5},{5,6},{6,7},{8,9},{9,10},{10,11},{12,13},{... | collective-permute-start | bytes 1572872 | tf_op jit(solution)/shard_map/ppermute | solution.py:421
  23.7 11.1 %collective-permute-start.3 = (bf16[64,4096]{1,0:T(8,128)(2,1)S(1)}, bf16[64,4096]{1,0:T(8,128)(2,1)S(1)}, u32[]{:S(2)}, u32[]{:S(2)}) collective-permute-start(bf16[64,4096]{1,0:T(8,128)(2,1)S(1)} %collective-permute-done.third.v1), channel_id=1, source_target_pairs={{1,5},{2,0},{5,9},{6,4},{9,13},{10,8},{14,12},{17,21},{18,16},{21,... | collective-permute-start | bytes 1572872 | tf_op jit(solution)/shard_map/ppermute | solution.py:421
  25.6 11.7 %collective-permute-start.6 = (bf16[64,4224]{1,0:T(8,128)(2,1)S(1)}, bf16[64,4224]{1,0:T(8,128)(2,1)S(1)}, u32[]{:S(2)}, u32[]{:S(2)}) collective-permute-start(bf16[64,4224]{1,0:T(8,128)(2,1)S(1)} %choose.2), channel_id=1, source_target_pairs={{0,1},{1,0},{2,3},{3,2},{4,5},{5,4},{6,7},{7,6},{8,9},{9,8},{10,11... | collective-permute-start | bytes 1622024 | tf_op jit(solution)/shard_map/ppermute | solution.py:428
  40.3 14.5 %collective-permute-start.10 = (bf16[20,4096]{1,0:T(8,128)(2,1)S(1)}, bf16[20,4096]{1,0:T(8,128)(2,1)S(1)}, u32[]{:S(2)}, u32[]{:S(2)}) collective-permute-start(bf16[20,4096]{1,0:T(8,128)(2,1)S(1)} %get-tuple-element.88.refs_0_), channel_id=1, source_target_pairs={{0,2},{1,3},{2,0},{3,1},{4,6},{5,7},{6,4},{7,5},{8,10},{9,11},{10,... | collective-permute-start | bytes 491528 | tf_op jit(solution)/shard_map/ppermute | solution.py:428
  40.4 14.5 %collective-permute-start.11 = (bf16[20,4096]{1,0:T(8,128)(2,1)S(1)}, bf16[20,4096]{1,0:T(8,128)(2,1)S(1)}, u32[]{:S(2)}, u32[]{:S(2)}) collective-permute-start(bf16[20,4096]{1,0:T(8,128)(2,1)S(1)} %get-tuple-element.86), channel_id=1, source_target_pairs={{0,8},{1,9},{2,10},{3,11},{4,12},{5,13},{6,14},{7,15},{8,0},{9,1},... | collective-permute-start | bytes 491528 | tf_op jit(solution)/shard_map/ppermute | solution.py:474
  43.1 11.8 %collective-permute-start.8 = (bf16[20,4096]{1,0:T(8,128)(2,1)S(1)}, bf16[20,4096]{1,0:T(8,128)(2,1)S(1)}, u32[]{:S(2)}, u32[]{:S(2)}) collective-permute-start(bf16[20,4096]{1,0:T(8,128)(2,1)S(1)} %get-tuple-element.88.refs_0_), channel_id=1, source_target_pairs={{0,6},{1,7},{2,4},{3,5},{4,2},{5,3},{6,0},{7,1},{8,14},{9,15},{10,... | collective-permute-start | bytes 491528 | tf_op jit(solution)/shard_map/ppermute | solution.py:428
  47.8 9.1 %collective-permute-start.9 = (bf16[20,4096]{1,0:T(8,128)(2,1)S(1)}, bf16[20,4096]{1,0:T(8,128)(2,1)S(1)}, u32[]{:S(2)}, u32[]{:S(2)}) collective-permute-start(bf16[20,4096]{1,0:T(8,128)(2,1)S(1)} %get-tuple-element.88.refs_0_), channel_id=1, source_target_pairs={{0,4},{1,5},{2,6},{3,7},{4,0},{5,1},{6,2},{7,3},{8,12},{9,13},{10,... | collective-permute-start | bytes 491528 | tf_op jit(solution)/shard_map/ppermute | solution.py:428
  57.0 3.6 %collective-permute-start.15 = (bf16[80,4096]{1,0:T(8,128)(2,1)S(1)}, bf16[80,4096]{1,0:T(8,128)(2,1)S(1)}, u32[]{:S(2)}, u32[]{:S(2)}) collective-permute-start(bf16[80,4096]{1,0:T(8,128)(2,1)S(1)} %pile.2.local), channel_id=1, source_target_pairs={{0,1},{1,0},{2,3},{3,2},{4,5},{5,4},{6,7},{7,6},{8,9},{9,8},{10,11... | collective-permute-start | bytes 1966088 | tf_op jit(solution)/shard_map/ppermute | solution.py:428
  57.1 11.3 %collective-permute-start.12 = (bf16[20,4096]{1,0:T(8,128)(2,1)S(1)}, bf16[20,4096]{1,0:T(8,128)(2,1)S(1)}, u32[]{:S(2)}, u32[]{:S(2)}) collective-permute-start(bf16[20,4096]{1,0:T(8,128)(2,1)S(1)} %collective-permute-done.11.refs_0_), channel_id=1, source_target_pairs={{0,6},{1,7},{2,4},{3,5},{4,2},{5,3},{6,0},{7,1},{8,14},{9,15},{10,... | collective-permute-start | bytes 491528 | tf_op jit(solution)/shard_map/ppermute | solution.py:428
  59.8 10.0 %collective-permute-start.13 = (bf16[20,4096]{1,0:T(8,128)(2,1)S(1)}, bf16[20,4096]{1,0:T(8,128)(2,1)S(1)}, u32[]{:S(2)}, u32[]{:S(2)}) collective-permute-start(bf16[20,4096]{1,0:T(8,128)(2,1)S(1)} %collective-permute-done.11.refs_0_), channel_id=1, source_target_pairs={{0,4},{1,5},{2,6},{3,7},{4,0},{5,1},{6,2},{7,3},{8,12},{9,13},{10,... | collective-permute-start | bytes 491528 | tf_op jit(solution)/shard_map/ppermute | solution.py:428
  60.3 9.5 %collective-permute-start.14 = (bf16[20,4096]{1,0:T(8,128)(2,1)S(1)}, bf16[20,4096]{1,0:T(8,128)(2,1)S(1)}, u32[]{:S(2)}, u32[]{:S(2)}) collective-permute-start(bf16[20,4096]{1,0:T(8,128)(2,1)S(1)} %collective-permute-done.11.refs_0_), channel_id=1, source_target_pairs={{0,2},{1,3},{2,0},{3,1},{4,6},{5,7},{6,4},{7,5},{8,10},{9,11},{10,... | collective-permute-start | bytes 491528 | tf_op jit(solution)/shard_map/ppermute | solution.py:428
  70.0 6.5 %collective-permute-start.18 = (bf16[80,4096]{1,0:T(8,128)(2,1)S(1)}, bf16[80,4096]{1,0:T(8,128)(2,1)S(1)}, u32[]{:S(2)}, u32[]{:S(2)}) collective-permute-start(bf16[80,4096]{1,0:T(8,128)(2,1)S(1)} %get-tuple-element.107), channel_id=1, source_target_pairs={{0,1},{1,0},{2,3},{3,2},{4,5},{5,4},{6,7},{7,6},{8,9},{9,8},{10,11... | collective-permute-start | bytes 1966088 | tf_op jit(solution)/shard_map/ppermute | solution.py:428
  76.3 2.2 %collective-permute-start.17 = (bf16[80,4096]{1,0:T(8,128)(2,1)S(1)}, bf16[80,4096]{1,0:T(8,128)(2,1)S(1)}, u32[]{:S(2)}, u32[]{:S(2)}) collective-permute-start(bf16[80,4096]{1,0:T(8,128)(2,1)S(1)} %get-tuple-element.101), channel_id=1, source_target_pairs={{0,1},{1,0},{2,3},{3,2},{4,5},{5,4},{6,7},{7,6},{8,9},{9,8},{10,11... | collective-permute-start | bytes 1966088 | tf_op jit(solution)/shard_map/ppermute | solution.py:428
  78.7 7.0 %collective-permute-start.19 = (bf16[20,4096]{1,0:T(8,128)(2,1)S(1)}, bf16[20,4096]{1,0:T(8,128)(2,1)S(1)}, u32[]{:S(2)}, u32[]{:S(2)}) collective-permute-start(bf16[20,4096]{1,0:T(8,128)(2,1)S(1)} %get-tuple-element.113), channel_id=1, source_target_pairs={{0,2},{1,3},{2,0},{3,1},{4,6},{5,7},{6,4},{7,5},{8,10},{9,11},{10,... | collective-permute-start | bytes 491528 | tf_op jit(solution)/shard_map/ppermute | solution.py:428
  80.2 7.8 %collective-permute-start.20 = (bf16[20,4096]{1,0:T(8,128)(2,1)S(1)}, bf16[20,4096]{1,0:T(8,128)(2,1)S(1)}, u32[]{:S(2)}, u32[]{:S(2)}) collective-permute-start(bf16[20,4096]{1,0:T(8,128)(2,1)S(1)} %get-tuple-element.114), channel_id=1, source_target_pairs={{0,4},{1,5},{2,6},{3,7},{4,0},{5,1},{6,2},{7,3},{8,12},{9,13},{10,... | collective-permute-start | bytes 491528 | tf_op jit(solution)/shard_map/ppermute | solution.py:428
  81.7 10.5 %collective-permute-start.24 = (bf16[20,4096]{1,0:T(8,128)(2,1)S(1)}, bf16[20,4096]{1,0:T(8,128)(2,1)S(1)}, u32[]{:S(2)}, u32[]{:S(2)}) collective-permute-start(bf16[20,4096]{1,0:T(8,128)(2,1)S(1)} %get-tuple-element.126), channel_id=1, source_target_pairs={{0,6},{1,7},{2,4},{3,5},{4,2},{5,3},{6,0},{7,1},{8,14},{9,15},{10,... | collective-permute-start | bytes 491528 | tf_op jit(solution)/shard_map/ppermute | solution.py:428
  87.9 8.3 %collective-permute-start.21 = (bf16[20,4096]{1,0:T(8,128)(2,1)S(1)}, bf16[20,4096]{1,0:T(8,128)(2,1)S(1)}, u32[]{:S(2)}, u32[]{:S(2)}) collective-permute-start(bf16[20,4096]{1,0:T(8,128)(2,1)S(1)} %get-tuple-element.120), channel_id=1, source_target_pairs={{0,2},{1,3},{2,0},{3,1},{4,6},{5,7},{6,4},{7,5},{8,10},{9,11},{10,... | collective-permute-start | bytes 491528 | tf_op jit(solution)/shard_map/ppermute | solution.py:428
  88.6 12.1 %collective-permute-start.22 = (bf16[20,4096]{1,0:T(8,128)(2,1)S(1)}, bf16[20,4096]{1,0:T(8,128)(2,1)S(1)}, u32[]{:S(2)}, u32[]{:S(2)}) collective-permute-start(bf16[20,4096]{1,0:T(8,128)(2,1)S(1)} %get-tuple-element.121), channel_id=1, source_target_pairs={{0,4},{1,5},{2,6},{3,7},{4,0},{5,1},{6,2},{7,3},{8,12},{9,13},{10,... | collective-permute-start | bytes 491528 | tf_op jit(solution)/shard_map/ppermute | solution.py:428
  90.1 13.6 %collective-permute-start.23 = (bf16[20,4096]{1,0:T(8,128)(2,1)S(1)}, bf16[20,4096]{1,0:T(8,128)(2,1)S(1)}, u32[]{:S(2)}, u32[]{:S(2)}) collective-permute-start(bf16[20,4096]{1,0:T(8,128)(2,1)S(1)} %get-tuple-element.122), channel_id=1, source_target_pairs={{0,6},{1,7},{2,4},{3,5},{4,2},{5,3},{6,0},{7,1},{8,14},{9,15},{10,... | collective-permute-start | bytes 491528 | tf_op jit(solution)/shard_map/ppermute | solution.py:428
  92.3 11.7 %collective-permute-start.25 = (bf16[20,4096]{1,0:T(8,128)(2,1)S(1)}, bf16[20,4096]{1,0:T(8,128)(2,1)S(1)}, u32[]{:S(2)}, u32[]{:S(2)}) collective-permute-start(bf16[20,4096]{1,0:T(8,128)(2,1)S(1)} %total.1), channel_id=1, source_target_pairs={{0,8},{1,9},{2,10},{3,11},{4,12},{5,13},{6,14},{7,15},{8,0},{9,1},... | collective-permute-start | bytes 491528 | tf_op jit(solution)/shard_map/ppermute | solution.py:506
  (2 other events, 4.1 us)

commit v17 on v16

--- a/solution.py
+++ b/solution.py
@@ -445,17 +445,17 @@
     key_block = bundle(keys, seg_own)
     key_one, value_one = moved(key_block, across), moved(values, across)
     key_three, value_three = moved(key_block, beside), moved(values, beside)
+    key_two = moved(key_one, passed)
     mine = bring(
         [
             queries, keys, values, seg_own, resid, norm_gain.reshape(1, -1), routes.T,
             route_gates.T,
         ],
-        scalars,
-    )
-    key_two = moved(key_one, passed)
-    value_one, mine = lax.optimization_barrier((value_one, mine))
+        key_two,
+    )
     value_two = moved(value_one, passed)
     key_four = swapped(choose(scalars, [key_two, key_three, key_one]), 1)
+    key_four, mine = lax.optimization_barrier((key_four, mine))
     value_four = swapped(choose(scalars, [value_two, value_three, value_one]), 1)
 
     queries, keys, values, seg_own, resid, gain, routes_held, gates_held = mine

time: 105 us -> 107 us (1.019)
    ppermute x6, waiting for transfers between devices: 13.7 us -> 15.7 us  [moved(): lax.ppermute(block, 'expert', [pair for pair in pairs if pair[1] < count])]
    ppermute x18, waiting for transfers between devices: 22.8 us -> 21.3 us  [swapped(): return lax.ppermute(block, 'expert', [(i, i ^ mask) for i in range(count)])]
  transfers between devices with their start and end apart: 26 -> 26, of which waited for: 15 -> 14; matrix products, arithmetic and copies ran while one was open for 0% -> 0% of each run, Pallas kernels for 21% -> 21%
where the time goes in v17:
time: 107 us; the launch traced here: 106 us
  starting transfers between devices  40.1 us (37%)
  waiting for transfers between devices  37 us (35%)
  Pallas kernels  28.6 us (27%)
    ppermute x18, waiting for transfers between devices, swapped(): return lax.ppermute(block, 'expert', [(i, i ^ mask) for i in range(count)])  21.3 us
    ppermute x6, starting transfers between devices, moved(): lax.ppermute(block, 'expert', [pair for pair in pairs if pair[1] < count])  17.2 us
    ppermute x18, starting transfers between devices, swapped(): return lax.ppermute(block, 'expert', [(i, i ^ mask) for i in range(count)])  16.4 us
    ppermute x6, waiting for transfers between devices, moved(): lax.ppermute(block, 'expert', [pair for pair in pairs if pair[1] < count])  15.7 us
    pallas_call x3, Pallas kernels, fetch(): pl.pallas_call(functools.partial(fetch_kernel, parts), in_specs=[anywhere...  10.5 us
    pallas_call x2, Pallas kernels, experts(): pl.pallas_call(experts_kernel, in_specs=[NEAR] * 5, out_specs=[NEAR] * 2,...  8.47 us
    ppermute x1, starting transfers between devices, shards(): other = lax.ppermute(back, 'expert', partner)  3.77 us
    pallas_call x1, Pallas kernels, attention(): pl.pallas_call(attention_kernel, in_specs=[pl.BlockSpec(memory_space=pltp...  2.96 us
  transfers between devices with their start and end apart: 26, of which 14 were waited for; matrix products, arithmetic and copies ran while one was open for 0% of the time, Pallas kernels for 21%

profile of v17, /device:TPU:0, one launch (start us, length us, event | category | flops | bytes accessed | tf_op | source)
XLA Modules:
  0.0 106.1 jit_solution(14454145358213382079)
XLA Ops:
  0.0 1.9 %bundle.1 = bf16[64,4224]{1,0:T(8,128)(2,1)} custom-call(bf16[64,4096]{1,0:T(8,128)(2,1)} %refs_1_.1, s32[1,64]{1,0:T(1,128)} %bitcast.12), custom_call_target="tpu_custom_call" | custom-call | bytes 1048576 | tf_op jit(solution)/shard_map/bundle/pallas_call | solution.py:43
  1.9 4.3 %collective-permute-start = (bf16[64,4224]{1,0:T(8,128)(2,1)}, bf16[64,4224]{1,0:T(8,128)(2,1)S(1)}, u32[]{:S(2)}, u32[]{:S(2)}) collective-permute-start(bf16[64,4224]{1,0:T(8,128)(2,1)} %bundle.1), channel_id=1, source_target_pairs={{0,3},{1,4},{2,1},{3,6},{4,7},{5,8},{6,5},{7,10},{8,11},{9,12},{10... | collective-permute-start | bytes 1622024 | tf_op jit(solution)/shard_map/ppermute | solution.py:421
  6.2 3.8 %collective-permute-start.4 = (bf16[64,4096]{1,0:T(8,128)(2,1)}, bf16[64,4096]{1,0:T(8,128)(2,1)S(1)}, u32[]{:S(2)}, u32[]{:S(2)}) collective-permute-start(bf16[64,4096]{1,0:T(8,128)(2,1)} %refs_2_.1), channel_id=1, source_target_pairs={{0,3},{1,4},{2,1},{3,6},{4,7},{5,8},{6,5},{7,10},{8,11},{9,12},{10... | collective-permute-start | bytes 1572872 | tf_op jit(solution)/shard_map/ppermute | solution.py:421
  10.0 1.7 %collective-permute-start.2 = (bf16[64,4224]{1,0:T(8,128)(2,1)}, bf16[64,4224]{1,0:T(8,128)(2,1)S(1)}, u32[]{:S(2)}, u32[]{:S(2)}) collective-permute-start(bf16[64,4224]{1,0:T(8,128)(2,1)} %bundle.1), channel_id=1, source_target_pairs={{0,1},{1,2},{2,3},{4,5},{5,6},{6,7},{8,9},{9,10},{10,11},{12,13},{... | collective-permute-start | bytes 1622024 | tf_op jit(solution)/shard_map/ppermute | solution.py:421
  11.8 1.7 %collective-permute-done.third.k1 = bf16[64,4224]{1,0:T(8,128)(2,1)S(1)} collective-permute-done((bf16[64,4224]{1,0:T(8,128)(2,1)}, bf16[64,4224]{1,0:T(8,128)(2,1)S(1)}, u32[]{:S(2)}, u32[]{:S(2)}) %collective-permute-start) | collective-permute-done | bytes 540704 | tf_op jit(solution)/shard_map/ppermute | solution.py:421
  14.7 4.8 %collective-permute-start.6 = (bf16[64,4096]{1,0:T(8,128)(2,1)}, bf16[64,4096]{1,0:T(8,128)(2,1)S(1)}, u32[]{:S(2)}, u32[]{:S(2)}) collective-permute-start(bf16[64,4096]{1,0:T(8,128)(2,1)} %refs_2_.1), channel_id=1, source_target_pairs={{0,1},{1,2},{2,3},{4,5},{5,6},{6,7},{8,9},{9,10},{10,11},{12,13},{... | collective-permute-start | bytes 1572872 | tf_op jit(solution)/shard_map/ppermute | solution.py:421
  19.6 5.1 %collective-permute-done.4.third.v1 = bf16[64,4096]{1,0:T(8,128)(2,1)S(1)} collective-permute-done((bf16[64,4096]{1,0:T(8,128)(2,1)}, bf16[64,4096]{1,0:T(8,128)(2,1)S(1)}, u32[]{:S(2)}, u32[]{:S(2)}) %collective-permute-start.4) | collective-permute-done | bytes 524320 | tf_op jit(solution)/shard_map/ppermute | solution.py:421
  26.8 8.9 %collective-permute-done.5.first.v2 = bf16[64,4096]{1,0:T(8,128)(2,1)S(1)} collective-permute-done((bf16[64,4096]{1,0:T(8,128)(2,1)S(1)}, bf16[64,4096]{1,0:T(8,128)(2,1)S(1)}, u32[]{:S(2)}, u32[]{:S(2)}) %collective-permute-start.5) | collective-permute-done | bytes 524320 | tf_op jit(solution)/shard_map/ppermute | solution.py:421
  38.3 3.0 %attention.1 = (f32[64,4096]{1,0:T(8,128)S(1)}, bf16[20,4096]{1,0:T(8,128)(2,1)S(1)}, bf16[20,4096]{1,0:T(8,128)(2,1)S(1)}, bf16[2,64,32]{2,1,0:T(8,128)(2,1)S(1)}) custom-call(s32[7]{0:T(128)S(1)} %stack.31.flags.deltas, bf16[64,4096]{1,0:T(8,128)(2,1)S(1)} %get-tuple-element.74.q, bf16[64,4096]{1,0:T(8,128)(2,1)S(1)} %get-tuple-element.75.k0, ...), custom_call_target="tpu_custom_call" | custom-call | flops 335544320 | bytes 8388608 | tf_op jit(solution)/shard_map/attention/pallas_call | solution.py:178
  41.4 2.7 %collective-permute-start.11 = (bf16[20,4096]{1,0:T(8,128)(2,1)S(1)}, bf16[20,4096]{1,0:T(8,128)(2,1)S(1)}, u32[]{:S(2)}, u32[]{:S(2)}) collective-permute-start(bf16[20,4096]{1,0:T(8,128)(2,1)S(1)} %get-tuple-element.86), channel_id=1, source_target_pairs={{0,8},{1,9},{2,10},{3,11},{4,12},{5,13},{6,14},{7,15},{8,0},{9,1},... | collective-permute-start | bytes 491528 | tf_op jit(solution)/shard_map/ppermute | solution.py:474
  44.0 4.7 %collective-permute-start.8 = (bf16[20,4096]{1,0:T(8,128)(2,1)S(1)}, bf16[20,4096]{1,0:T(8,128)(2,1)S(1)}, u32[]{:S(2)}, u32[]{:S(2)}) collective-permute-start(bf16[20,4096]{1,0:T(8,128)(2,1)S(1)} %get-tuple-element.88.refs_0_), channel_id=1, source_target_pairs={{0,6},{1,7},{2,4},{3,5},{4,2},{5,3},{6,0},{7,1},{8,14},{9,15},{10,... | collective-permute-start | bytes 491528 | tf_op jit(solution)/shard_map/ppermute | solution.py:428
  48.8 3.5 %fetch.3.w_gate = bf16[4096,1024]{1,0:T(8,128)(2,1)S(1)} custom-call(bf16[4096,1024]{1,0:T(8,128)(2,1)} %source.3, bf16[2,64,32]{2,1,0:T(8,128)(2,1)S(1)} %get-tuple-element.84.after.weight), custom_call_target="tpu_custom_call" | custom-call | bytes 16777216 | tf_op jit(solution)/shard_map/fetch/pallas_call | solution.py:244
  52.3 3.5 %fetch.4.w_up = bf16[4096,1024]{1,0:T(8,128)(2,1)S(1)} custom-call(bf16[4096,1024]{1,0:T(8,128)(2,1)} %source.4, bf16[2,64,32]{2,1,0:T(8,128)(2,1)S(1)} %get-tuple-element.84.after.weight), custom_call_target="tpu_custom_call" | custom-call | bytes 16777216 | tf_op jit(solution)/shard_map/fetch/pallas_call | solution.py:244
  55.9 2.1 %collective-permute-done.9.refs_2_ = bf16[20,4096]{1,0:T(8,128)(2,1)S(1)} collective-permute-done((bf16[20,4096]{1,0:T(8,128)(2,1)S(1)}, bf16[20,4096]{1,0:T(8,128)(2,1)S(1)}, u32[]{:S(2)}, u32[]{:S(2)}) %collective-permute-start.9) | collective-permute-done | bytes 163872 | tf_op jit(solution)/shard_map/ppermute | solution.py:428
  58.2 2.7 %collective-permute-start.12 = (bf16[20,4096]{1,0:T(8,128)(2,1)S(1)}, bf16[20,4096]{1,0:T(8,128)(2,1)S(1)}, u32[]{:S(2)}, u32[]{:S(2)}) collective-permute-start(bf16[20,4096]{1,0:T(8,128)(2,1)S(1)} %collective-permute-done.11.refs_0_), channel_id=1, source_target_pairs={{0,6},{1,7},{2,4},{3,5},{4,2},{5,3},{6,0},{7,1},{8,14},{9,15},{10,... | collective-permute-start | bytes 491528 | tf_op jit(solution)/shard_map/ppermute | solution.py:428
  61.7 3.5 %fetch.5.w_down = bf16[1024,4096]{1,0:T(8,128)(2,1)S(1)} custom-call(bf16[1024,4096]{1,0:T(8,128)(2,1)} %source.5, bf16[80,4096]{1,0:T(8,128)(2,1)S(1)} %collective-permute-done.15.after.remote), custom_call_target="tpu_custom_call" | custom-call | bytes 16777216 | tf_op jit(solution)/shard_map/fetch/pallas_call | solution.py:244
  65.2 4.2 %experts.2 = (bf16[80,4096]{1,0:T(8,128)(2,1)S(1)}, bf16[80,4096]{1,0:T(8,128)(2,1)S(1)}) custom-call(bf16[80,4096]{1,0:T(8,128)(2,1)S(1)} %pile.2.local, bf16[80,4096]{1,0:T(8,128)(2,1)S(1)} %collective-permute-done.15.after.remote, bf16[4096,1024]{1,0:T(8,128)(2,1)S(1)} %fetch.3.w_gate, bf16[4096,1024]{1,0:T(8,128)(2,1)S(1)} %fetch.4.w_up, ...), custom_call_target="tpu_custom_call" | custom-call | flops 4026531840 | bytes 2621440 | tf_op jit(solution)/shard_map/experts/pallas_call | solution.py:280
  73.1 4.2 %experts.3 = (bf16[80,4096]{1,0:T(8,128)(2,1)S(1)}, bf16[80,4096]{1,0:T(8,128)(2,1)S(1)}) custom-call(bf16[80,4096]{1,0:T(8,128)(2,1)S(1)} %pile.3.local, bf16[80,4096]{1,0:T(8,128)(2,1)S(1)} %collective-permute-done.16.remote, bf16[4096,1024]{1,0:T(8,128)(2,1)S(1)} %fetch.3.w_gate, bf16[4096,1024]{1,0:T(8,128)(2,1)S(1)} %fetch.4.w_up, ...), custom_call_target="tpu_custom_call" | custom-call | flops 4026531840 | bytes 2621440 | tf_op jit(solution)/shard_map/experts/pallas_call | solution.py:280
  77.8 1.8 %collective-permute-done.17.second = bf16[80,4096]{1,0:T(8,128)(2,1)S(1)} collective-permute-done((bf16[80,4096]{1,0:T(8,128)(2,1)S(1)}, bf16[80,4096]{1,0:T(8,128)(2,1)S(1)}, u32[]{:S(2)}, u32[]{:S(2)}) %collective-permute-start.17) | collective-permute-done | bytes 655392 | tf_op jit(solution)/shard_map/ppermute | solution.py:428
  83.3 3.5 %collective-permute-done.19.refs_1_ = bf16[20,4096]{1,0:T(8,128)(2,1)S(1)} collective-permute-done((bf16[20,4096]{1,0:T(8,128)(2,1)S(1)}, bf16[20,4096]{1,0:T(8,128)(2,1)S(1)}, u32[]{:S(2)}, u32[]{:S(2)}) %collective-permute-start.19) | collective-permute-done | bytes 163872 | tf_op jit(solution)/shard_map/ppermute | solution.py:428
  86.8 2.3 %collective-permute-done.20.refs_2_ = bf16[20,4096]{1,0:T(8,128)(2,1)S(1)} collective-permute-done((bf16[20,4096]{1,0:T(8,128)(2,1)S(1)}, bf16[20,4096]{1,0:T(8,128)(2,1)S(1)}, u32[]{:S(2)}, u32[]{:S(2)}) %collective-permute-start.20) | collective-permute-done | bytes 163872 | tf_op jit(solution)/shard_map/ppermute | solution.py:428
  93.4 3.8 %collective-permute-start.25 = (bf16[20,4096]{1,0:T(8,128)(2,1)S(1)}, bf16[20,4096]{1,0:T(8,128)(2,1)S(1)}, u32[]{:S(2)}, u32[]{:S(2)}) collective-permute-start(bf16[20,4096]{1,0:T(8,128)(2,1)S(1)} %total.1), channel_id=1, source_target_pairs={{0,8},{1,9},{2,10},{3,11},{4,12},{5,13},{6,14},{7,15},{8,0},{9,1},... | collective-permute-start | bytes 491528 | tf_op jit(solution)/shard_map/ppermute | solution.py:506
  97.3 4.4 %collective-permute-done.22.refs_2_ = bf16[20,4096]{1,0:T(8,128)(2,1)S(1)} collective-permute-done((bf16[20,4096]{1,0:T(8,128)(2,1)S(1)}, bf16[20,4096]{1,0:T(8,128)(2,1)S(1)}, u32[]{:S(2)}, u32[]{:S(2)}) %collective-permute-start.22) | collective-permute-done | bytes 163872 | tf_op jit(solution)/shard_map/ppermute | solution.py:428
  101.7 3.1 %collective-permute-done.23.refs_3_ = bf16[20,4096]{1,0:T(8,128)(2,1)S(1)} collective-permute-done((bf16[20,4096]{1,0:T(8,128)(2,1)S(1)}, bf16[20,4096]{1,0:T(8,128)(2,1)S(1)}, u32[]{:S(2)}, u32[]{:S(2)}) %collective-permute-start.23) | collective-permute-done | bytes 163872 | tf_op jit(solution)/shard_map/ppermute | solution.py:428
  (46 shorter events, 20.6 us)
Async XLA Ops:
  1.9 11.6 %collective-permute-start = (bf16[64,4224]{1,0:T(8,128)(2,1)}, bf16[64,4224]{1,0:T(8,128)(2,1)S(1)}, u32[]{:S(2)}, u32[]{:S(2)}) collective-permute-start(bf16[64,4224]{1,0:T(8,128)(2,1)} %bundle.1), channel_id=1, source_target_pairs={{0,3},{1,4},{2,1},{3,6},{4,7},{5,8},{6,5},{7,10},{8,11},{9,12},{10... | collective-permute-start | bytes 1622024 | tf_op jit(solution)/shard_map/ppermute | solution.py:421
  6.2 18.4 %collective-permute-start.4 = (bf16[64,4096]{1,0:T(8,128)(2,1)}, bf16[64,4096]{1,0:T(8,128)(2,1)S(1)}, u32[]{:S(2)}, u32[]{:S(2)}) collective-permute-start(bf16[64,4096]{1,0:T(8,128)(2,1)} %refs_2_.1), channel_id=1, source_target_pairs={{0,3},{1,4},{2,1},{3,6},{4,7},{5,8},{6,5},{7,10},{8,11},{9,12},{10... | collective-permute-start | bytes 1572872 | tf_op jit(solution)/shard_map/ppermute | solution.py:421
  10.0 16.1 %collective-permute-start.2 = (bf16[64,4224]{1,0:T(8,128)(2,1)}, bf16[64,4224]{1,0:T(8,128)(2,1)S(1)}, u32[]{:S(2)}, u32[]{:S(2)}) collective-permute-start(bf16[64,4224]{1,0:T(8,128)(2,1)} %bundle.1), channel_id=1, source_target_pairs={{0,1},{1,2},{2,3},{4,5},{5,6},{6,7},{8,9},{9,10},{10,11},{12,13},{... | collective-permute-start | bytes 1622024 | tf_op jit(solution)/shard_map/ppermute | solution.py:421
  13.4 12.7 %collective-permute-start.1 = (bf16[64,4224]{1,0:T(8,128)(2,1)S(1)}, bf16[64,4224]{1,0:T(8,128)(2,1)S(1)}, u32[]{:S(2)}, u32[]{:S(2)}) collective-permute-start(bf16[64,4224]{1,0:T(8,128)(2,1)S(1)} %collective-permute-done.third.k1), channel_id=1, source_target_pairs={{1,5},{2,0},{5,9},{6,4},{9,13},{10,8},{14,12},{17,21},{18,16},{21,... | collective-permute-start | bytes 1622024 | tf_op jit(solution)/shard_map/ppermute | solution.py:421
  14.7 12.1 %collective-permute-start.6 = (bf16[64,4096]{1,0:T(8,128)(2,1)}, bf16[64,4096]{1,0:T(8,128)(2,1)S(1)}, u32[]{:S(2)}, u32[]{:S(2)}) collective-permute-start(bf16[64,4096]{1,0:T(8,128)(2,1)} %refs_2_.1), channel_id=1, source_target_pairs={{0,1},{1,2},{2,3},{4,5},{5,6},{6,7},{8,9},{9,10},{10,11},{12,13},{... | collective-permute-start | bytes 1572872 | tf_op jit(solution)/shard_map/ppermute | solution.py:421
  24.7 11.1 %collective-permute-start.5 = (bf16[64,4096]{1,0:T(8,128)(2,1)S(1)}, bf16[64,4096]{1,0:T(8,128)(2,1)S(1)}, u32[]{:S(2)}, u32[]{:S(2)}) collective-permute-start(bf16[64,4096]{1,0:T(8,128)(2,1)S(1)} %collective-permute-done.4.third.v1), channel_id=1, source_target_pairs={{1,5},{2,0},{5,9},{6,4},{9,13},{10,8},{14,12},{17,21},{18,16},{21,... | collective-permute-start | bytes 1572872 | tf_op jit(solution)/shard_map/ppermute | solution.py:421
  26.7 11.3 %collective-permute-start.3 = (bf16[64,4224]{1,0:T(8,128)(2,1)S(1)}, bf16[64,4224]{1,0:T(8,128)(2,1)S(1)}, u32[]{:S(2)}, u32[]{:S(2)}) collective-permute-start(bf16[64,4224]{1,0:T(8,128)(2,1)S(1)} %choose.2), channel_id=1, source_target_pairs={{0,1},{1,0},{2,3},{3,2},{4,5},{5,4},{6,7},{7,6},{8,9},{9,8},{10,11... | collective-permute-start | bytes 1622024 | tf_op jit(solution)/shard_map/ppermute | solution.py:428
  41.3 14.5 %collective-permute-start.10 = (bf16[20,4096]{1,0:T(8,128)(2,1)S(1)}, bf16[20,4096]{1,0:T(8,128)(2,1)S(1)}, u32[]{:S(2)}, u32[]{:S(2)}) collective-permute-start(bf16[20,4096]{1,0:T(8,128)(2,1)S(1)} %get-tuple-element.88.refs_0_), channel_id=1, source_target_pairs={{0,2},{1,3},{2,0},{3,1},{4,6},{5,7},{6,4},{7,5},{8,10},{9,11},{10,... | collective-permute-start | bytes 491528 | tf_op jit(solution)/shard_map/ppermute | solution.py:428
  41.4 14.5 %collective-permute-start.11 = (bf16[20,4096]{1,0:T(8,128)(2,1)S(1)}, bf16[20,4096]{1,0:T(8,128)(2,1)S(1)}, u32[]{:S(2)}, u32[]{:S(2)}) collective-permute-start(bf16[20,4096]{1,0:T(8,128)(2,1)S(1)} %get-tuple-element.86), channel_id=1, source_target_pairs={{0,8},{1,9},{2,10},{3,11},{4,12},{5,13},{6,14},{7,15},{8,0},{9,1},... | collective-permute-start | bytes 491528 | tf_op jit(solution)/shard_map/ppermute | solution.py:474
  44.0 11.8 %collective-permute-start.8 = (bf16[20,4096]{1,0:T(8,128)(2,1)S(1)}, bf16[20,4096]{1,0:T(8,128)(2,1)S(1)}, u32[]{:S(2)}, u32[]{:S(2)}) collective-permute-start(bf16[20,4096]{1,0:T(8,128)(2,1)S(1)} %get-tuple-element.88.refs_0_), channel_id=1, source_target_pairs={{0,6},{1,7},{2,4},{3,5},{4,2},{5,3},{6,0},{7,1},{8,14},{9,15},{10,... | collective-permute-start | bytes 491528 | tf_op jit(solution)/shard_map/ppermute | solution.py:428
  48.8 9.2 %collective-permute-start.9 = (bf16[20,4096]{1,0:T(8,128)(2,1)S(1)}, bf16[20,4096]{1,0:T(8,128)(2,1)S(1)}, u32[]{:S(2)}, u32[]{:S(2)}) collective-permute-start(bf16[20,4096]{1,0:T(8,128)(2,1)S(1)} %get-tuple-element.88.refs_0_), channel_id=1, source_target_pairs={{0,4},{1,5},{2,6},{3,7},{4,0},{5,1},{6,2},{7,3},{8,12},{9,13},{10,... | collective-permute-start | bytes 491528 | tf_op jit(solution)/shard_map/ppermute | solution.py:428
  58.1 3.6 %collective-permute-start.15 = (bf16[80,4096]{1,0:T(8,128)(2,1)S(1)}, bf16[80,4096]{1,0:T(8,128)(2,1)S(1)}, u32[]{:S(2)}, u32[]{:S(2)}) collective-permute-start(bf16[80,4096]{1,0:T(8,128)(2,1)S(1)} %pile.2.local), channel_id=1, source_target_pairs={{0,1},{1,0},{2,3},{3,2},{4,5},{5,4},{6,7},{7,6},{8,9},{9,8},{10,11... | collective-permute-start | bytes 1966088 | tf_op jit(solution)/shard_map/ppermute | solution.py:428
  58.2 11.3 %collective-permute-start.12 = (bf16[20,4096]{1,0:T(8,128)(2,1)S(1)}, bf16[20,4096]{1,0:T(8,128)(2,1)S(1)}, u32[]{:S(2)}, u32[]{:S(2)}) collective-permute-start(bf16[20,4096]{1,0:T(8,128)(2,1)S(1)} %collective-permute-done.11.refs_0_), channel_id=1, source_target_pairs={{0,6},{1,7},{2,4},{3,5},{4,2},{5,3},{6,0},{7,1},{8,14},{9,15},{10,... | collective-permute-start | bytes 491528 | tf_op jit(solution)/shard_map/ppermute | solution.py:428
  60.9 10.0 %collective-permute-start.13 = (bf16[20,4096]{1,0:T(8,128)(2,1)S(1)}, bf16[20,4096]{1,0:T(8,128)(2,1)S(1)}, u32[]{:S(2)}, u32[]{:S(2)}) collective-permute-start(bf16[20,4096]{1,0:T(8,128)(2,1)S(1)} %collective-permute-done.11.refs_0_), channel_id=1, source_target_pairs={{0,4},{1,5},{2,6},{3,7},{4,0},{5,1},{6,2},{7,3},{8,12},{9,13},{10,... | collective-permute-start | bytes 491528 | tf_op jit(solution)/shard_map/ppermute | solution.py:428
  61.4 9.5 %collective-permute-start.14 = (bf16[20,4096]{1,0:T(8,128)(2,1)S(1)}, bf16[20,4096]{1,0:T(8,128)(2,1)S(1)}, u32[]{:S(2)}, u32[]{:S(2)}) collective-permute-start(bf16[20,4096]{1,0:T(8,128)(2,1)S(1)} %collective-permute-done.11.refs_0_), channel_id=1, source_target_pairs={{0,2},{1,3},{2,0},{3,1},{4,6},{5,7},{6,4},{7,5},{8,10},{9,11},{10,... | collective-permute-start | bytes 491528 | tf_op jit(solution)/shard_map/ppermute | solution.py:428
  71.0 2.2 %collective-permute-start.16 = (bf16[80,4096]{1,0:T(8,128)(2,1)S(1)}, bf16[80,4096]{1,0:T(8,128)(2,1)S(1)}, u32[]{:S(2)}, u32[]{:S(2)}) collective-permute-start(bf16[80,4096]{1,0:T(8,128)(2,1)S(1)} %pile.3.local), channel_id=1, source_target_pairs={{0,1},{1,0},{2,3},{3,2},{4,5},{5,4},{6,7},{7,6},{8,9},{9,8},{10,11... | collective-permute-start | bytes 1966088 | tf_op jit(solution)/shard_map/ppermute | solution.py:428
  71.1 6.5 %collective-permute-start.18 = (bf16[80,4096]{1,0:T(8,128)(2,1)S(1)}, bf16[80,4096]{1,0:T(8,128)(2,1)S(1)}, u32[]{:S(2)}, u32[]{:S(2)}) collective-permute-start(bf16[80,4096]{1,0:T(8,128)(2,1)S(1)} %get-tuple-element.107), channel_id=1, source_target_pairs={{0,1},{1,0},{2,3},{3,2},{4,5},{5,4},{6,7},{7,6},{8,9},{9,8},{10,11... | collective-permute-start | bytes 1966088 | tf_op jit(solution)/shard_map/ppermute | solution.py:428
  79.7 7.0 %collective-permute-start.19 = (bf16[20,4096]{1,0:T(8,128)(2,1)S(1)}, bf16[20,4096]{1,0:T(8,128)(2,1)S(1)}, u32[]{:S(2)}, u32[]{:S(2)}) collective-permute-start(bf16[20,4096]{1,0:T(8,128)(2,1)S(1)} %get-tuple-element.113), channel_id=1, source_target_pairs={{0,2},{1,3},{2,0},{3,1},{4,6},{5,7},{6,4},{7,5},{8,10},{9,11},{10,... | collective-permute-start | bytes 491528 | tf_op jit(solution)/shard_map/ppermute | solution.py:428
  81.2 7.8 %collective-permute-start.20 = (bf16[20,4096]{1,0:T(8,128)(2,1)S(1)}, bf16[20,4096]{1,0:T(8,128)(2,1)S(1)}, u32[]{:S(2)}, u32[]{:S(2)}) collective-permute-start(bf16[20,4096]{1,0:T(8,128)(2,1)S(1)} %get-tuple-element.114), channel_id=1, source_target_pairs={{0,4},{1,5},{2,6},{3,7},{4,0},{5,1},{6,2},{7,3},{8,12},{9,13},{10,... | collective-permute-start | bytes 491528 | tf_op jit(solution)/shard_map/ppermute | solution.py:428
  82.8 10.5 %collective-permute-start.24 = (bf16[20,4096]{1,0:T(8,128)(2,1)S(1)}, bf16[20,4096]{1,0:T(8,128)(2,1)S(1)}, u32[]{:S(2)}, u32[]{:S(2)}) collective-permute-start(bf16[20,4096]{1,0:T(8,128)(2,1)S(1)} %get-tuple-element.126), channel_id=1, source_target_pairs={{0,6},{1,7},{2,4},{3,5},{4,2},{5,3},{6,0},{7,1},{8,14},{9,15},{10,... | collective-permute-start | bytes 491528 | tf_op jit(solution)/shard_map/ppermute | solution.py:428
  89.0 8.3 %collective-permute-start.21 = (bf16[20,4096]{1,0:T(8,128)(2,1)S(1)}, bf16[20,4096]{1,0:T(8,128)(2,1)S(1)}, u32[]{:S(2)}, u32[]{:S(2)}) collective-permute-start(bf16[20,4096]{1,0:T(8,128)(2,1)S(1)} %get-tuple-element.120), channel_id=1, source_target_pairs={{0,2},{1,3},{2,0},{3,1},{4,6},{5,7},{6,4},{7,5},{8,10},{9,11},{10,... | collective-permute-start | bytes 491528 | tf_op jit(solution)/shard_map/ppermute | solution.py:428
  89.6 12.1 %collective-permute-start.22 = (bf16[20,4096]{1,0:T(8,128)(2,1)S(1)}, bf16[20,4096]{1,0:T(8,128)(2,1)S(1)}, u32[]{:S(2)}, u32[]{:S(2)}) collective-permute-start(bf16[20,4096]{1,0:T(8,128)(2,1)S(1)} %get-tuple-element.121), channel_id=1, source_target_pairs={{0,4},{1,5},{2,6},{3,7},{4,0},{5,1},{6,2},{7,3},{8,12},{9,13},{10,... | collective-permute-start | bytes 491528 | tf_op jit(solution)/shard_map/ppermute | solution.py:428
  91.2 13.6 %collective-permute-start.23 = (bf16[20,4096]{1,0:T(8,128)(2,1)S(1)}, bf16[20,4096]{1,0:T(8,128)(2,1)S(1)}, u32[]{:S(2)}, u32[]{:S(2)}) collective-permute-start(bf16[20,4096]{1,0:T(8,128)(2,1)S(1)} %get-tuple-element.122), channel_id=1, source_target_pairs={{0,6},{1,7},{2,4},{3,5},{4,2},{5,3},{6,0},{7,1},{8,14},{9,15},{10,... | collective-permute-start | bytes 491528 | tf_op jit(solution)/shard_map/ppermute | solution.py:428
  93.4 11.7 %collective-permute-start.25 = (bf16[20,4096]{1,0:T(8,128)(2,1)S(1)}, bf16[20,4096]{1,0:T(8,128)(2,1)S(1)}, u32[]{:S(2)}, u32[]{:S(2)}) collective-permute-start(bf16[20,4096]{1,0:T(8,128)(2,1)S(1)} %total.1), channel_id=1, source_target_pairs={{0,8},{1,9},{2,10},{3,11},{4,12},{5,13},{6,14},{7,15},{8,0},{9,1},... | collective-permute-start | bytes 491528 | tf_op jit(solution)/shard_map/ppermute | solution.py:506
  (2 other events, 4.1 us)
